TPU v7x, 32 devices: a whole 2x2x4 slice. The times are simulated.
32 devices in a mesh: rows: 2 (over x), chan: 16 (over z, y, core).
Axes of the slice: x: 2, y: 2, z: 4, core: 2. Of those that a mesh axis runs over, the one named last changes fastest.
Arguments:
- activations: bfloat16 [64, 7, 7, 512], P('rows', None, None, 'chan'), may hold values from 0 to 2
- cotangents: bfloat16 [64, 512, 49], P('rows', 'chan'), may hold values from -0.0005859375 to 0.0005859375
- ordering: int32 [2, 32], P('rows'), may hold values from 0 to 31, each once within a row
- ridge: float32 [32], replicated, may hold values from 0.2 to 2
Outputs:
- gram_panel: float32 [64, 32], P('rows')
- factor_panel: float32 [64, 32], P('rows')
Inputs may be any that keep to these rules, and one draw needn't show every extreme that they name: Each row of ordering lists every one of the group's 32 examples once.
All inputs are finite; a program needn't handle non-finite values.
Results may differ from a plain program's by a relative error of at most 0.0003.
Values may be sent and summed in bfloat16 or wider, within the bound.
No kernel may reach another device: no remote copies, remote signals or barrier semaphores. Data moves between devices by JAX's collectives and lax.ppermute only.
A program may use at most 64 MiB of HBM per device.

v0:
```python
import functools

import jax
import jax.numpy as jnp
from jax import lax
from jax.experimental import pallas as pl
from jax.experimental.pallas import tpu as pltpu
from jax.sharding import PartitionSpec as P

PIV_DEV = 16

SIDE = 7
PITCH = 8
GROUPS4 = 14
CH = 32
EX = 32
LANES = 128
F32 = jnp.float32
BF16 = jnp.bfloat16


def fetch(sources, targets, sems):
    copies = [pltpu.make_async_copy(a, b, sems.at[i]) for i, (a, b) in enumerate(zip(sources, targets))]
    for copy in copies:
        copy.start()
    return copies


def prep_kernel(order_hbm, x_hbm, g_hbm, xo_ref, go_ref, order_ref, x_ref, g_ref, sems, gs, gt, gout):
    for copy in fetch((order_hbm, x_hbm, g_hbm), (order_ref, x_ref, g_ref), sems):
        copy.wait()
    row_id = lax.broadcasted_iota(jnp.int32, (EX, EX), 0)
    col_id = lax.broadcasted_iota(jnp.int32, (EX, EX), 1)
    onehot = jnp.zeros((EX, EX), F32)
    for k in range(EX):
        example = order_ref[0, k]
        onehot = jnp.where((row_id == k) & (col_id == example), 1.0, onehot)
        gs[k * CH:(k + 1) * CH, 0:SIDE * SIDE] = g_ref[example].astype(F32)
    onehot = onehot.astype(BF16)
    zero_block = jnp.zeros((EX, CH), BF16)
    for group in range(GROUPS4):
        pieces = []
        for j in range(4):
            py, px = group // 2, (group % 2) * 4 + j
            pieces.append(x_ref[py * SIDE + px] if px < SIDE else zero_block)
        packed = jnp.concatenate(pieces, axis=1)
        xo_ref[group] = jnp.dot(onehot, packed, preferred_element_type=F32).astype(BF16)
    block_id = lax.broadcasted_iota(jnp.int32, (GROUPS4, LANES), 1) // CH
    for quad in range(EX // 4):
        flipped = jnp.transpose(gs[quad * LANES:(quad + 1) * LANES, :])
        for py in range(SIDE):
            gt[py * PITCH:py * PITCH + SIDE, :] = flipped[py * SIDE:(py + 1) * SIDE, :]
            gt[py * PITCH + SIDE:(py + 1) * PITCH, :] = jnp.zeros((1, LANES), F32)
        parts = [gt[pl.ds(j, GROUPS4, stride=4), :] for j in range(4)]
        for e in range(4):
            merged = jnp.zeros((GROUPS4, LANES), F32)
            for j in range(4):
                shift = (CH * (j - e)) % LANES
                moved = pltpu.roll(parts[j], shift, 1) if shift else parts[j]
                merged = jnp.where(block_id == j, moved, merged)
            gout[pl.ds(quad * 4 + e, GROUPS4, stride=EX), :] = merged
    for group in range(GROUPS4):
        go_ref[group] = gout[group * EX:(group + 1) * EX, :].astype(BF16)


def prep(order, x, g):
    full = jax.ShapeDtypeStruct((GROUPS4, EX, LANES), BF16)
    vmem = pl.BlockSpec(memory_space=pltpu.VMEM)
    return pl.pallas_call(
        prep_kernel,
        out_shape=(full, full),
        in_specs=[pl.BlockSpec(memory_space=pl.ANY)] * 3,
        out_specs=(vmem,) * 2,
        scratch_shapes=[
            pltpu.SMEM(order.shape, order.dtype),
            pltpu.VMEM(x.shape, x.dtype),
            pltpu.VMEM(g.shape, g.dtype),
            pltpu.SemaphoreType.DMA((3,)),
            pltpu.VMEM((EX * CH, LANES), F32),
            pltpu.VMEM((SIDE * PITCH, LANES), F32),
            pltpu.VMEM((GROUPS4 * EX, LANES), F32),
        ],
        compiler_params=pltpu.CompilerParams(vmem_limit_bytes=56 << 20),
        name="prep",
    )(order, x, g)


SPOTS = SIDE * SIDE
ROWB = SIDE * EX
COLB = PITCH * PIV_DEV


def cost(flops, moved):
    return pl.CostEstimate(flops=flops, bytes_accessed=moved, transcendentals=0)


def unpack_kernel(*refs):
    packed, all_ref, piv_ref = refs[:4], refs[4], refs[5]
    row = lax.broadcasted_iota(jnp.int32, (4 * LANES, 4 * LANES), 0)
    col = lax.broadcasted_iota(jnp.int32, (4 * LANES, 4 * LANES), 1)
    target = (row // CH) % 4 * LANES + row // LANES * CH + row % CH
    move = jnp.where(col == target, 1.0, 0.0).astype(BF16)
    flat = jnp.concatenate([packed[i][...].reshape(GROUPS4 * EX, LANES) for i in range(4)], axis=1)
    moved = jnp.dot(flat, move, preferred_element_type=F32).astype(BF16)
    for group in range(GROUPS4):
        for j in range(4):
            py, px = group // 2, (group % 2) * 4 + j
            if px == SIDE:
                continue
            spot = moved[group * EX:(group + 1) * EX, j * LANES:(j + 1) * LANES]
            all_ref[py * SIDE + px] = spot
            piv_ref[py * SIDE + px] = spot[:PIV_DEV]


def unpack(arrays, name):
    vmem = pl.BlockSpec(memory_space=pltpu.VMEM)
    return pl.pallas_call(
        unpack_kernel,
        out_shape=(
            jax.ShapeDtypeStruct((SPOTS, EX, LANES), BF16),
            jax.ShapeDtypeStruct((SPOTS, PIV_DEV, LANES), BF16),
        ),
        in_specs=[vmem] * len(arrays),
        out_specs=(vmem,) * 2,
        compiler_params=pltpu.CompilerParams(vmem_limit_bytes=8 << 20),
        cost_estimate=cost(0, 1 << 20),
        name=name,
    )(*arrays)


def panel_terms(x, g, xp, gp, lx, rx, rg, t):
    for py in range(SIDE):
        for px in range(PITCH):
            row, col = (py * SIDE + px) * EX, (py * PITCH + px) * PIV_DEV
            for d in range(3):
                from_x = px + d - 1
                inside = 0 <= from_x < SIDE and px < SIDE
                lanes = slice(d * LANES, (d + 1) * LANES)
                spot = py * SIDE + from_x
                rx[col:col + PIV_DEV, lanes] = xp[spot] if inside else jnp.zeros((PIV_DEV, LANES), BF16)
                if px < SIDE:
                    lx[row:row + EX, lanes] = x[spot] if inside else jnp.zeros((EX, LANES), BF16)
            rg[col:col + PIV_DEV, :] = gp[py * SIDE + px] if px < SIDE else jnp.zeros((PIV_DEV, LANES), BF16)

    contract = (((1,), (1,)), ((), ()))
    spans = [(qy, min(qy + 2, SIDE)) for qy in range(0, SIDE, 2)]
    for start, stop in spans:
        right = rx[start * COLB:stop * COLB, :]
        for py in range(SIDE):
            left = lx[py * ROWB:(py + 1) * ROWB, :]
            t[py, :, start * COLB:stop * COLB] = lax.dot_general(left, right, contract, preferred_element_type=F32)
    acc = jnp.zeros((EX, COLB), F32)
    for start, stop in spans:
        right = rg[start * COLB:stop * COLB, :]
        for py in range(SIDE):
            left = g[py * SIDE:(py + 1) * SIDE].reshape(ROWB, LANES)
            gg = lax.dot_general(left, right, contract, preferred_element_type=F32)
            for qy in range(start, stop):
                for px in range(SIDE):
                    rows = slice(px * EX, (px + 1) * EX)
                    total = t[py, rows, qy * COLB:(qy + 1) * COLB]
                    if py > 0 and qy > 0:
                        total = total + t[py - 1, rows, (qy - 1) * COLB:qy * COLB]
                    if py < SIDE - 1 and qy < SIDE - 1:
                        total = total + t[py + 1, rows, (qy + 1) * COLB:(qy + 2) * COLB]
                    acc = acc + gg[rows, (qy - start) * COLB:(qy - start + 1) * COLB] * total
    acc = acc + pltpu.roll(acc, 64, 1)
    acc = acc + pltpu.roll(acc, 32, 1)
    return acc + pltpu.roll(acc, 16, 1)


def own_kernel(x, g, xp, gp, out_ref, *work):
    out_ref[...] = panel_terms(x, g, xp, gp, *work)


def cross_kernel(x, g, xp, gp, own_ref, out_ref, *work):
    across = panel_terms(x, g, xp, gp, *work)
    lane = lax.broadcasted_iota(jnp.int32, (8, LANES), 1)
    is_own = (lane // PIV_DEV) % 2 == lax.axis_index("rows")
    packed = jnp.zeros((8, LANES), F32)
    for j in range(4):
        rows = slice(8 * j, 8 * j + 8)
        packed = jnp.where(lane // EX == j, jnp.where(is_own, own_ref[rows, :], across[rows]), packed)
    out_ref[...] = packed


def terms(kernel, arrays, shape, name):
    vmem = pl.BlockSpec(memory_space=pltpu.VMEM)
    rows, cols = SIDE * ROWB, SIDE * COLB
    return pl.pallas_call(
        kernel,
        out_shape=jax.ShapeDtypeStruct(shape, F32),
        in_specs=[vmem] * len(arrays),
        out_specs=vmem,
        scratch_shapes=[
            pltpu.VMEM((rows, 3 * LANES), BF16),
            pltpu.VMEM((cols, 3 * LANES), BF16),
            pltpu.VMEM((cols, LANES), BF16),
            pltpu.VMEM((SIDE, ROWB, cols), F32),
        ],
        compiler_params=pltpu.CompilerParams(vmem_limit_bytes=24 << 20),
        cost_estimate=cost(2 * rows * cols * 4 * LANES, 8 << 20),
        name=name,
    )(*arrays)


def rows_of(packed, count):
    return jnp.concatenate(
        [packed[:, EX * j:EX * (j + 1)] for j in range(count)], axis=0
    )


def final_kernel(own_ref, other_ref, ridge_ref, gram_ref, factor_ref):
    first = lax.axis_index("rows") == 0
    panel = rows_of(own_ref[...], 4)
    gram_ref[...] = panel
    mine, cross = panel[:PIV_DEV], rows_of(other_ref[...], 2)
    diag = jnp.concatenate([jnp.where(first, mine, cross), jnp.where(first, cross, mine)], axis=0)
    row_id = lax.broadcasted_iota(jnp.int32, (EX, EX), 0)
    col_id = lax.broadcasted_iota(jnp.int32, (EX, EX), 1)
    ridge = jnp.where(row_id == col_id, jnp.broadcast_to(ridge_ref[...], (EX, EX)), 0.0)
    system = 0.5 * (diag + jnp.transpose(diag)) + ridge
    factor = jnp.zeros((EX, EX), F32)
    step = 4
    for j in range(0, EX, step):
        sys_cols = [jnp.broadcast_to(system[:, j + k:j + k + 1], (EX, EX)) for k in range(step)]
        pan_cols = [jnp.broadcast_to(panel[:, j + k:j + k + 1], (EX, EX)) for k in range(step)]
        sys_rows = [system[j + k:j + k + 1, :] for k in range(step)]
        for k in range(step):
            scale = lax.rsqrt(sys_cols[k][j + k:j + k + 1, :])
            sys_cols[k], pan_cols[k], sys_rows[k] = sys_cols[k] * scale, pan_cols[k] * scale, sys_rows[k] * scale
            factor = jnp.where(col_id == j + k, pan_cols[k], factor)
            for m in range(k + 1, step):
                entry = sys_cols[k][j + m:j + m + 1, :]
                sys_cols[m] = sys_cols[m] - sys_cols[k] * entry
                pan_cols[m] = pan_cols[m] - pan_cols[k] * entry
                sys_rows[m] = sys_rows[m] - sys_rows[k] * entry
        if j + step < EX:
            for k in range(step):
                system = system - sys_cols[k] * sys_rows[k]
                panel = panel - pan_cols[k] * sys_rows[k]
    factor_ref[...] = factor


def final(own, other, ridge):
    vmem = pl.BlockSpec(memory_space=pltpu.VMEM)
    out = jax.ShapeDtypeStruct((EX, EX), F32)
    return pl.pallas_call(
        final_kernel,
        out_shape=(out, out),
        in_specs=[vmem] * 3,
        out_specs=(vmem, vmem),
        compiler_params=pltpu.CompilerParams(vmem_limit_bytes=8 << 20),
        name="solve",
    )(own, other, ridge.reshape(1, EX))


def exchange(value, count, flip):
    return lax.ppermute(value, "chan", [(i, i ^ flip) for i in range(count)])


def exchange_across(value, count):
    pairs = [(g * count + i, (1 - g) * count + i) for g in range(2) for i in range(count)]
    return lax.ppermute(value, ("rows", "chan"), pairs)


def local_packed(count, activations, cotangents, ordering, ridge):
    near, far = (1, 2, 3), (4, 8, 12)
    x = jnp.transpose(activations, (1, 2, 0, 3)).reshape(SIDE * SIDE, EX, CH)
    xo, go = prep(ordering, x, cotangents)
    own_g = [go] + [exchange(go, count, f) for f in near]
    own_x = [xo] + [exchange(xo, count, f) for f in far]
    x_all, x_piv = unpack(own_x, "unpack_x")
    x_cross = exchange_across(x_piv, count)
    g_all, g_piv = unpack(own_g, "unpack_g")
    g_cross = exchange_across(g_piv, count)
    own_term = terms(own_kernel, (x_all, g_all, x_piv, g_piv), (EX, LANES), "terms_own")
    term = terms(cross_kernel, (x_all, g_all, x_cross, g_cross, own_term), (8, LANES), "terms_cross")
    for flip in (1, 2, 4, 8):
        term = term + exchange(term, count, flip)
    return final(term, exchange_across(term, count), ridge)


def jacobian_block(grad_rows, input_rows):
    example_count = input_rows.shape[0]
    side_len = input_rows.shape[1]
    channel_count = input_rows.shape[3]
    grad_count = grad_rows.shape[1]
    grid_grads = grad_rows.reshape(example_count, grad_count, side_len, side_len)
    padded_grads = jnp.pad(grid_grads, ((0, 0), (0, 0), (1, 1), (1, 1)))
    shifted = []
    for row_shift in range(3):
        for col_shift in range(3):
            window = padded_grads[
                :,
                :,
                2 - row_shift : 2 - row_shift + side_len,
                2 - col_shift : 2 - col_shift + side_len,
            ]
            shifted.append(window.reshape(example_count, grad_count, side_len * side_len))
    stacked_grads = jnp.stack(shifted, axis=2).reshape(
        example_count, grad_count * 9, side_len * side_len
    )
    flat_inputs = input_rows.reshape(example_count, side_len * side_len, channel_count)
    product = jnp.einsum(
        "nkp,npq->nkq", stacked_grads, flat_inputs, preferred_element_type=jnp.float32
    )
    return product.astype(jnp.bfloat16).reshape(example_count, -1)


def gram_block(left_rows, right_rows):
    return lax.dot_general(
        left_rows, right_rows, (((1,), (1,)), ((), ())), preferred_element_type=jnp.float32
    )


def local(activations, cotangents, ordering, ridge):
    local_order = ordering[0]
    own_inputs = jnp.take(activations, local_order, axis=0)
    own_grads = jnp.take(cotangents, local_order, axis=0)
    pivot_count = PIV_DEV
    pivot_inputs, pivot_grads = (
        lax.all_gather(own_inputs[:pivot_count], "rows", axis=0, tiled=True),
        lax.all_gather(own_grads[:pivot_count], "rows", axis=0, tiled=True),
    )
    full_own, full_pivot = (
        lax.all_gather(own_inputs, "chan", axis=3, tiled=True),
        lax.all_gather(pivot_inputs, "chan", axis=3, tiled=True),
    )
    own_jac = jacobian_block(own_grads, full_own)
    pivot_jac = jacobian_block(pivot_grads, full_pivot)
    partial_panel = gram_block(own_jac, pivot_jac)
    gram_panel = lax.psum(partial_panel, "chan")
    diag_block = lax.all_gather(gram_panel[:pivot_count], "rows", axis=0, tiled=True)
    system = 0.5 * (diag_block + diag_block.T) + jnp.diag(ridge)
    lower = jnp.linalg.cholesky(system)
    factor_panel = jax.scipy.linalg.solve_triangular(lower, gram_panel.T, lower=True).T
    return (gram_panel, factor_panel)


def solution(mesh):
    row_groups, count = mesh.shape["rows"], mesh.shape["chan"]
    packed = row_groups == 2 and count == 16
    return jax.shard_map(
        functools.partial(local_packed, count) if packed else local,
        mesh=mesh,
        in_specs=(P("rows", None, None, "chan"), P("rows", "chan", None), P("rows", None), P()),
        out_specs=(P("rows", None), P("rows", None)),
        check_vma=False,
    )
```

profile of v0, /device:TPU:0, one launch (start us, length us, event | category | flops | bytes accessed | tf_op | source)
XLA Modules:
  0.0 51.1 jit_solution(14199340756016330119)
XLA Ops:
  0.6 2.3 %prep.1 = (bf16[14,32,128]{2,1,0:T(8,128)(2,1)}, bf16[14,32,128]{2,1,0:T(8,128)(2,1)}) custom-call(s32[1,32]{1,0:T(1,128)} %order_hbm.1, bf16[49,32,32]{2,1,0:T(8,128)(2,1)} %bitcast.5, bf16[32,32,49]{2,1,0:T(8,128)(2,1)} %g_hbm.1), custom_call_target="tpu_custom_call" | custom-call | tf_op jit(solution)/shard_map/prep/pallas_call | solution.py:69
  3.0 5.1 %collective-permute-start.2 = (bf16[14,32,128]{2,1,0:T(8,128)(2,1)}, bf16[14,32,128]{2,1,0:T(8,128)(2,1)S(1)}, u32[]{:S(2)}, u32[]{:S(2)}) collective-permute-start(bf16[14,32,128]{2,1,0:T(8,128)(2,1)} %get-tuple-element.8.refs_0_), channel_id=1, source_target_pairs={{0,12},{1,13},{2,14},{3,15},{4,8},{5,9},{6,10},{7,11},{8,4},{9,5},... | collective-permute-start | bytes 344072 | tf_op jit(solution)/shard_map/ppermute | solution.py:259
  8.1 0.6 %collective-permute-start = (bf16[14,32,128]{2,1,0:T(8,128)(2,1)}, bf16[14,32,128]{2,1,0:T(8,128)(2,1)S(1)}, u32[]{:S(2)}, u32[]{:S(2)}) collective-permute-start(bf16[14,32,128]{2,1,0:T(8,128)(2,1)} %get-tuple-element.8.refs_0_), channel_id=1, source_target_pairs={{0,4},{1,5},{2,6},{3,7},{4,0},{5,1},{6,2},{7,3},{8,12},{9,13},{10,... | collective-permute-start | bytes 344072 | tf_op jit(solution)/shard_map/ppermute | solution.py:259
  9.1 1.3 %collective-permute-start.4 = (bf16[14,32,128]{2,1,0:T(8,128)(2,1)}, bf16[14,32,128]{2,1,0:T(8,128)(2,1)S(1)}, u32[]{:S(2)}, u32[]{:S(2)}) collective-permute-start(bf16[14,32,128]{2,1,0:T(8,128)(2,1)} %get-tuple-element.10.refs_0_), channel_id=1, source_target_pairs={{0,2},{1,3},{2,0},{3,1},{4,6},{5,7},{6,4},{7,5},{8,10},{9,11},{10,... | collective-permute-start | bytes 344072 | tf_op jit(solution)/shard_map/ppermute | solution.py:259
  10.4 1.9 %collective-permute-done.2.refs_3_ = bf16[14,32,128]{2,1,0:T(8,128)(2,1)S(1)} collective-permute-done((bf16[14,32,128]{2,1,0:T(8,128)(2,1)}, bf16[14,32,128]{2,1,0:T(8,128)(2,1)S(1)}, u32[]{:S(2)}, u32[]{:S(2)}) %collective-permute-start.2) | collective-permute-done | bytes 114720 | tf_op jit(solution)/shard_map/ppermute | solution.py:259
  12.4 5.6 %collective-permute-done.1.refs_2_ = bf16[14,32,128]{2,1,0:T(8,128)(2,1)S(1)} collective-permute-done((bf16[14,32,128]{2,1,0:T(8,128)(2,1)}, bf16[14,32,128]{2,1,0:T(8,128)(2,1)S(1)}, u32[]{:S(2)}, u32[]{:S(2)}) %collective-permute-start.1) | collective-permute-done | bytes 114720 | tf_op jit(solution)/shard_map/ppermute | solution.py:259
  18.0 0.9 %copy-done.1 = bf16[14,32,128]{2,1,0:T(8,128)(2,1)S(1)} copy-done((bf16[14,32,128]{2,1,0:T(8,128)(2,1)S(1)}, bf16[14,32,128]{2,1,0:T(8,128)(2,1)}, u32[]{:S(2)}) %copy-start.1) | copy-done | bytes 114712
  19.3 1.6 %collective-permute-start.6 = (bf16[49,16,128]{2,1,0:T(8,128)(2,1)S(1)}, bf16[49,16,128]{2,1,0:T(8,128)(2,1)S(1)}, u32[]{:S(2)}, u32[]{:S(2)}) collective-permute-start(bf16[49,16,128]{2,1,0:T(8,128)(2,1)S(1)} %get-tuple-element.12.xp), channel_id=1, source_target_pairs={{0,16},{1,17},{2,18},{3,19},{4,20},{5,21},{6,22},{7,23},{8,24},{9,... | collective-permute-start | bytes 602120 | tf_op jit(solution)/shard_map/ppermute | solution.py:264
  20.9 0.4 unpack_g.1
  21.3 0.6 %collective-permute-start.7 = (bf16[49,16,128]{2,1,0:T(8,128)(2,1)S(1)}, bf16[49,16,128]{2,1,0:T(8,128)(2,1)S(1)}, u32[]{:S(2)}, u32[]{:S(2)}) collective-permute-start(bf16[49,16,128]{2,1,0:T(8,128)(2,1)S(1)} %get-tuple-element.13.gp), channel_id=1, source_target_pairs={{0,16},{1,17},{2,18},{3,19},{4,20},{5,21},{6,22},{7,23},{8,24},{9,... | collective-permute-start | bytes 602120 | tf_op jit(solution)/shard_map/ppermute | solution.py:264
  21.9 3.0 %terms_own.1.own_ref = f32[32,128]{1,0:T(8,128)S(1)} custom-call(bf16[49,32,128]{2,1,0:T(8,128)(2,1)S(1)} %get-tuple-element.9.x, bf16[49,32,128]{2,1,0:T(8,128)(2,1)S(1)} %get-tuple-element.11.g, bf16[49,16,128]{2,1,0:T(8,128)(2,1)S(1)} %get-tuple-element.12.xp, bf16[49,16,128]{2,1,0:T(8,128)(2,1)S(1)} %get-tuple-element.13.gp), custom_call_target="tpu_custom_call" | custom-call | flops 1438646272 | bytes 8388608 | tf_op jit(solution)/shard_map/terms_own/pallas_call | solution.py:190
  24.9 2.4 %collective-permute-done.6.xp = bf16[49,16,128]{2,1,0:T(8,128)(2,1)S(1)} collective-permute-done((bf16[49,16,128]{2,1,0:T(8,128)(2,1)S(1)}, bf16[49,16,128]{2,1,0:T(8,128)(2,1)S(1)}, u32[]{:S(2)}, u32[]{:S(2)}) %collective-permute-start.6) | collective-permute-done | bytes 200736 | tf_op jit(solution)/shard_map/ppermute | solution.py:264
  27.3 2.4 %collective-permute-done.7.gp = bf16[49,16,128]{2,1,0:T(8,128)(2,1)S(1)} collective-permute-done((bf16[49,16,128]{2,1,0:T(8,128)(2,1)S(1)}, bf16[49,16,128]{2,1,0:T(8,128)(2,1)S(1)}, u32[]{:S(2)}, u32[]{:S(2)}) %collective-permute-start.7) | collective-permute-done | bytes 200736 | tf_op jit(solution)/shard_map/ppermute | solution.py:264
  29.7 3.0 %terms_cross.1 = f32[8,128]{1,0:T(8,128)S(1)} custom-call(bf16[49,32,128]{2,1,0:T(8,128)(2,1)S(1)} %get-tuple-element.9.x, bf16[49,32,128]{2,1,0:T(8,128)(2,1)S(1)} %get-tuple-element.11.g, bf16[49,16,128]{2,1,0:T(8,128)(2,1)S(1)} %collective-permute-done.6.xp, bf16[49,16,128]{2,1,0:T(8,128)(2,1)S(1)} %collective-permute-done.7.gp, ...), custom_call_target="tpu_custom_call" | custom-call | flops 1438646272 | bytes 8388608 | tf_op jit(solution)/shard_map/terms_cross/pallas_call | solution.py:190
  32.7 1.2 %collective-permute-done.8 = f32[8,128]{1,0:T(8,128)S(1)} collective-permute-done((f32[8,128]{1,0:T(8,128)S(1)}, f32[8,128]{1,0:T(8,128)S(1)}, u32[]{:S(2)}, u32[]{:S(2)}) %collective-permute-start.8) | collective-permute-done | bytes 4128 | tf_op jit(solution)/shard_map/ppermute | solution.py:259
  33.9 1.5 %collective-permute-start.9 = (f32[8,128]{1,0:T(8,128)S(1)}, f32[8,128]{1,0:T(8,128)S(1)}, u32[]{:S(2)}, u32[]{:S(2)}) collective-permute-start(f32[8,128]{1,0:T(8,128)S(1)} %add.12), channel_id=1, source_target_pairs={{0,2},{1,3},{2,0},{3,1},{4,6},{5,7},{6,4},{7,5},{8,10},{9,11},{10,... | collective-permute-start | bytes 12296 | tf_op jit(solution)/shard_map/ppermute | solution.py:259
  35.4 2.1 %collective-permute-done.9 = f32[8,128]{1,0:T(8,128)S(1)} collective-permute-done((f32[8,128]{1,0:T(8,128)S(1)}, f32[8,128]{1,0:T(8,128)S(1)}, u32[]{:S(2)}, u32[]{:S(2)}) %collective-permute-start.9) | collective-permute-done | bytes 4128 | tf_op jit(solution)/shard_map/ppermute | solution.py:259
  37.5 0.5 collective-permute-start.10
  38.0 3.1 %collective-permute-done.10 = f32[8,128]{1,0:T(8,128)S(1)} collective-permute-done((f32[8,128]{1,0:T(8,128)S(1)}, f32[8,128]{1,0:T(8,128)S(1)}, u32[]{:S(2)}, u32[]{:S(2)}) %collective-permute-start.10) | collective-permute-done | bytes 4128 | tf_op jit(solution)/shard_map/ppermute | solution.py:259
  41.1 1.6 %collective-permute-start.11 = (f32[8,128]{1,0:T(8,128)S(1)}, f32[8,128]{1,0:T(8,128)S(1)}, u32[]{:S(2)}, u32[]{:S(2)}) collective-permute-start(f32[8,128]{1,0:T(8,128)S(1)} %add.14), channel_id=1, source_target_pairs={{0,8},{1,9},{2,10},{3,11},{4,12},{5,13},{6,14},{7,15},{8,0},{9,1},... | collective-permute-start | bytes 12296 | tf_op jit(solution)/shard_map/ppermute | solution.py:259
  42.8 2.9 %collective-permute-done.11 = f32[8,128]{1,0:T(8,128)S(1)} collective-permute-done((f32[8,128]{1,0:T(8,128)S(1)}, f32[8,128]{1,0:T(8,128)S(1)}, u32[]{:S(2)}, u32[]{:S(2)}) %collective-permute-start.11) | collective-permute-done | bytes 4128 | tf_op jit(solution)/shard_map/ppermute | solution.py:259
  45.6 1.5 %collective-permute-start.12 = (f32[8,128]{1,0:T(8,128)S(1)}, f32[8,128]{1,0:T(8,128)S(1)}, u32[]{:S(2)}, u32[]{:S(2)}) collective-permute-start(f32[8,128]{1,0:T(8,128)S(1)} %add.15.own_ref), channel_id=1, source_target_pairs={{0,16},{1,17},{2,18},{3,19},{4,20},{5,21},{6,22},{7,23},{8,24},{9,... | collective-permute-start | bytes 12296 | tf_op jit(solution)/shard_map/ppermute | solution.py:264
  47.2 2.1 %collective-permute-done.12.other_ref = f32[8,128]{1,0:T(8,128)S(1)} collective-permute-done((f32[8,128]{1,0:T(8,128)S(1)}, f32[8,128]{1,0:T(8,128)S(1)}, u32[]{:S(2)}, u32[]{:S(2)}) %collective-permute-start.12) | collective-permute-done | bytes 4128 | tf_op jit(solution)/shard_map/ppermute | solution.py:264
  49.2 1.8 %solve.1 = (f32[32,32]{1,0:T(8,128)}, f32[32,32]{1,0:T(8,128)}) custom-call(f32[8,128]{1,0:T(8,128)S(1)} %add.15.own_ref, f32[8,128]{1,0:T(8,128)S(1)} %collective-permute-done.12.other_ref, f32[1,32]{1,0:T(1,128)S(1)} %bitcast.4), custom_call_target="tpu_custom_call" | custom-call | tf_op jit(solution)/shard_map/solve/pallas_call | solution.py:248
  (18 shorter events, 0.9 us)
Async XLA Ops:
  3.0 9.4 %collective-permute-start.2 = (bf16[14,32,128]{2,1,0:T(8,128)(2,1)}, bf16[14,32,128]{2,1,0:T(8,128)(2,1)S(1)}, u32[]{:S(2)}, u32[]{:S(2)}) collective-permute-start(bf16[14,32,128]{2,1,0:T(8,128)(2,1)} %get-tuple-element.8.refs_0_), channel_id=1, source_target_pairs={{0,12},{1,13},{2,14},{3,15},{4,8},{5,9},{6,10},{7,11},{8,4},{9,5},... | collective-permute-start | bytes 344072 | tf_op jit(solution)/shard_map/ppermute | solution.py:259
  8.1 9.9 %collective-permute-start.1 = (bf16[14,32,128]{2,1,0:T(8,128)(2,1)}, bf16[14,32,128]{2,1,0:T(8,128)(2,1)S(1)}, u32[]{:S(2)}, u32[]{:S(2)}) collective-permute-start(bf16[14,32,128]{2,1,0:T(8,128)(2,1)} %get-tuple-element.8.refs_0_), channel_id=1, source_target_pairs={{0,8},{1,9},{2,10},{3,11},{4,12},{5,13},{6,14},{7,15},{8,0},{9,1},... | collective-permute-start | bytes 344072 | tf_op jit(solution)/shard_map/ppermute | solution.py:259
  8.1 9.9 %collective-permute-start = (bf16[14,32,128]{2,1,0:T(8,128)(2,1)}, bf16[14,32,128]{2,1,0:T(8,128)(2,1)S(1)}, u32[]{:S(2)}, u32[]{:S(2)}) collective-permute-start(bf16[14,32,128]{2,1,0:T(8,128)(2,1)} %get-tuple-element.8.refs_0_), channel_id=1, source_target_pairs={{0,4},{1,5},{2,6},{3,7},{4,0},{5,1},{6,2},{7,3},{8,12},{9,13},{10,... | collective-permute-start | bytes 344072 | tf_op jit(solution)/shard_map/ppermute | solution.py:259
  8.7 12.2 %copy-start = (bf16[14,32,128]{2,1,0:T(8,128)(2,1)S(1)}, bf16[14,32,128]{2,1,0:T(8,128)(2,1)}, u32[]{:S(2)}) copy-start(bf16[14,32,128]{2,1,0:T(8,128)(2,1)} %get-tuple-element.10.refs_0_) | copy-start | bytes 344068
  8.7 12.1 %collective-permute-start.5 = (bf16[14,32,128]{2,1,0:T(8,128)(2,1)}, bf16[14,32,128]{2,1,0:T(8,128)(2,1)S(1)}, u32[]{:S(2)}, u32[]{:S(2)}) collective-permute-start(bf16[14,32,128]{2,1,0:T(8,128)(2,1)} %get-tuple-element.10.refs_0_), channel_id=1, source_target_pairs={{0,3},{1,2},{2,1},{3,0},{4,7},{5,6},{6,5},{7,4},{8,11},{9,10},{10,... | collective-permute-start | bytes 344072 | tf_op jit(solution)/shard_map/ppermute | solution.py:259
  9.1 11.8 %collective-permute-start.4 = (bf16[14,32,128]{2,1,0:T(8,128)(2,1)}, bf16[14,32,128]{2,1,0:T(8,128)(2,1)S(1)}, u32[]{:S(2)}, u32[]{:S(2)}) collective-permute-start(bf16[14,32,128]{2,1,0:T(8,128)(2,1)} %get-tuple-element.10.refs_0_), channel_id=1, source_target_pairs={{0,2},{1,3},{2,0},{3,1},{4,6},{5,7},{6,4},{7,5},{8,10},{9,11},{10,... | collective-permute-start | bytes 344072 | tf_op jit(solution)/shard_map/ppermute | solution.py:259
  12.4 8.5 %collective-permute-start.3 = (bf16[14,32,128]{2,1,0:T(8,128)(2,1)}, bf16[14,32,128]{2,1,0:T(8,128)(2,1)S(1)}, u32[]{:S(2)}, u32[]{:S(2)}) collective-permute-start(bf16[14,32,128]{2,1,0:T(8,128)(2,1)} %get-tuple-element.10.refs_0_), channel_id=1, source_target_pairs={{0,1},{1,0},{2,3},{3,2},{4,5},{5,4},{6,7},{7,6},{8,9},{9,8},{10,11... | collective-permute-start | bytes 344072 | tf_op jit(solution)/shard_map/ppermute | solution.py:259
  18.0 0.9 %copy-start.1 = (bf16[14,32,128]{2,1,0:T(8,128)(2,1)S(1)}, bf16[14,32,128]{2,1,0:T(8,128)(2,1)}, u32[]{:S(2)}) copy-start(bf16[14,32,128]{2,1,0:T(8,128)(2,1)} %get-tuple-element.8.refs_0_) | copy-start | bytes 344068
  19.3 8.0 %collective-permute-start.6 = (bf16[49,16,128]{2,1,0:T(8,128)(2,1)S(1)}, bf16[49,16,128]{2,1,0:T(8,128)(2,1)S(1)}, u32[]{:S(2)}, u32[]{:S(2)}) collective-permute-start(bf16[49,16,128]{2,1,0:T(8,128)(2,1)S(1)} %get-tuple-element.12.xp), channel_id=1, source_target_pairs={{0,16},{1,17},{2,18},{3,19},{4,20},{5,21},{6,22},{7,23},{8,24},{9,... | collective-permute-start | bytes 602120 | tf_op jit(solution)/shard_map/ppermute | solution.py:264
  21.3 8.4 %collective-permute-start.7 = (bf16[49,16,128]{2,1,0:T(8,128)(2,1)S(1)}, bf16[49,16,128]{2,1,0:T(8,128)(2,1)S(1)}, u32[]{:S(2)}, u32[]{:S(2)}) collective-permute-start(bf16[49,16,128]{2,1,0:T(8,128)(2,1)S(1)} %get-tuple-element.13.gp), channel_id=1, source_target_pairs={{0,16},{1,17},{2,18},{3,19},{4,20},{5,21},{6,22},{7,23},{8,24},{9,... | collective-permute-start | bytes 602120 | tf_op jit(solution)/shard_map/ppermute | solution.py:264
  32.7 1.2 %collective-permute-start.8 = (f32[8,128]{1,0:T(8,128)S(1)}, f32[8,128]{1,0:T(8,128)S(1)}, u32[]{:S(2)}, u32[]{:S(2)}) collective-permute-start(f32[8,128]{1,0:T(8,128)S(1)} %terms_cross.1), channel_id=1, source_target_pairs={{0,1},{1,0},{2,3},{3,2},{4,5},{5,4},{6,7},{7,6},{8,9},{9,8},{10,11... | collective-permute-start | bytes 12296 | tf_op jit(solution)/shard_map/ppermute | solution.py:259
  33.9 3.6 %collective-permute-start.9 = (f32[8,128]{1,0:T(8,128)S(1)}, f32[8,128]{1,0:T(8,128)S(1)}, u32[]{:S(2)}, u32[]{:S(2)}) collective-permute-start(f32[8,128]{1,0:T(8,128)S(1)} %add.12), channel_id=1, source_target_pairs={{0,2},{1,3},{2,0},{3,1},{4,6},{5,7},{6,4},{7,5},{8,10},{9,11},{10,... | collective-permute-start | bytes 12296 | tf_op jit(solution)/shard_map/ppermute | solution.py:259
  37.5 3.6 %collective-permute-start.10 = (f32[8,128]{1,0:T(8,128)S(1)}, f32[8,128]{1,0:T(8,128)S(1)}, u32[]{:S(2)}, u32[]{:S(2)}) collective-permute-start(f32[8,128]{1,0:T(8,128)S(1)} %add.13), channel_id=1, source_target_pairs={{0,4},{1,5},{2,6},{3,7},{4,0},{5,1},{6,2},{7,3},{8,12},{9,13},{10,... | collective-permute-start | bytes 12296 | tf_op jit(solution)/shard_map/ppermute | solution.py:259
  41.1 4.5 %collective-permute-start.11 = (f32[8,128]{1,0:T(8,128)S(1)}, f32[8,128]{1,0:T(8,128)S(1)}, u32[]{:S(2)}, u32[]{:S(2)}) collective-permute-start(f32[8,128]{1,0:T(8,128)S(1)} %add.14), channel_id=1, source_target_pairs={{0,8},{1,9},{2,10},{3,11},{4,12},{5,13},{6,14},{7,15},{8,0},{9,1},... | collective-permute-start | bytes 12296 | tf_op jit(solution)/shard_map/ppermute | solution.py:259
  45.6 3.6 %copy-start.2 = (f32[32]{0:T(128)S(1)}, f32[32]{0:T(128)}, u32[]{:S(2)}) copy-start(f32[32]{0:T(128)} %param.7) | copy-start | bytes 388
  45.6 3.6 %collective-permute-start.12 = (f32[8,128]{1,0:T(8,128)S(1)}, f32[8,128]{1,0:T(8,128)S(1)}, u32[]{:S(2)}, u32[]{:S(2)}) collective-permute-start(f32[8,128]{1,0:T(8,128)S(1)} %add.15.own_ref), channel_id=1, source_target_pairs={{0,16},{1,17},{2,18},{3,19},{4,20},{5,21},{6,22},{7,23},{8,24},{9,... | collective-permute-start | bytes 12296 | tf_op jit(solution)/shard_map/ppermute | solution.py:264
where the time goes:
time: 51.2 us; the launch traced here: 51.1 us
  waiting for transfers between devices  23.6 us (46%)
  starting transfers between devices  14.8 us (29%)
  Pallas kernels  11.1 us (22%)
  local copies, waits for them, and re-layouts  0.91 us (2%)
  between operations  0.69 us (1%)
    ppermute x10, waiting for transfers between devices, exchange(): return lax.ppermute(value, 'chan', [(i, i ^ flip) for i in range(count)])  16.8 us
    ppermute x10, starting transfers between devices, exchange(): return lax.ppermute(value, 'chan', [(i, i ^ flip) for i in range(count)])  11.1 us
    ppermute x3, waiting for transfers between devices, exchange_across(): return lax.ppermute(value, ('rows', 'chan'), pairs)  6.85 us
    pallas_call x2, Pallas kernels, terms(): pl.pallas_call(kernel, out_shape=jax.ShapeDtypeStruct(shape, F32), in_spe...  6.01 us
    ppermute x3, starting transfers between devices, exchange_across(): return lax.ppermute(value, ('rows', 'chan'), pairs)  3.68 us
    pallas_call x1, Pallas kernels, prep(): pl.pallas_call(prep_kernel, out_shape=(full, full), in_specs=[pl.BlockSpe...  2.33 us
    pallas_call x1, Pallas kernels, final(): pl.pallas_call(final_kernel, out_shape=(out, out), in_specs=[vmem] * 3, o...  1.84 us
  transfers between devices with their start and end apart: 13, of which 9 were waited for; matrix products, arithmetic and copies ran while one was open for 0% of the time, Pallas kernels for 8%

commit v1 on v0

--- a/solution.py
+++ b/solution.py
@@ -26,7 +26,7 @@
     return copies
 
 
-def prep_kernel(order_hbm, x_hbm, g_hbm, xo_ref, go_ref, order_ref, x_ref, g_ref, sems, gs, gt, gout):
+def prep_kernel(order_hbm, x_hbm, g_hbm, xo_ref, go_ref, gp_ref, order_ref, x_ref, g_ref, sems, gs, gt, gout):
     for copy in fetch((order_hbm, x_hbm, g_hbm), (order_ref, x_ref, g_ref), sems):
         copy.wait()
     row_id = lax.broadcasted_iota(jnp.int32, (EX, EX), 0)
@@ -60,7 +60,9 @@
                 merged = jnp.where(block_id == j, moved, merged)
             gout[pl.ds(quad * 4 + e, GROUPS4, stride=EX), :] = merged
     for group in range(GROUPS4):
-        go_ref[group] = gout[group * EX:(group + 1) * EX, :].astype(BF16)
+        ordered = gout[group * EX:(group + 1) * EX, :].astype(BF16)
+        go_ref[group] = ordered
+        gp_ref[group] = ordered[:PIV_DEV]
 
 
 def prep(order, x, g):
@@ -68,9 +70,9 @@
     vmem = pl.BlockSpec(memory_space=pltpu.VMEM)
     return pl.pallas_call(
         prep_kernel,
-        out_shape=(full, full),
+        out_shape=(full, full, jax.ShapeDtypeStruct((GROUPS4, PIV_DEV, LANES), BF16)),
         in_specs=[pl.BlockSpec(memory_space=pl.ANY)] * 3,
-        out_specs=(vmem,) * 2,
+        out_specs=(vmem,) * 3,
         scratch_shapes=[
             pltpu.SMEM(order.shape, order.dtype),
             pltpu.VMEM(x.shape, x.dtype),
@@ -94,35 +96,55 @@
     return pl.CostEstimate(flops=flops, bytes_accessed=moved, transcendentals=0)
 
 
+def merge_kernel(own_ref, cross_ref, out_ref):
+    out_ref[:, :EX, :] = own_ref[...]
+    out_ref[:, EX:, :] = cross_ref[...]
+
+
+def merge(own, cross):
+    vmem = pl.BlockSpec(memory_space=pltpu.VMEM)
+    return pl.pallas_call(
+        merge_kernel,
+        out_shape=jax.ShapeDtypeStruct((GROUPS4, EX + PIV_DEV, LANES), BF16),
+        in_specs=[vmem] * 2,
+        out_specs=vmem,
+        compiler_params=pltpu.CompilerParams(vmem_limit_bytes=8 << 20),
+        cost_estimate=cost(0, 1 << 18),
+        name="merge",
+    )(own, cross)
+
+
 def unpack_kernel(*refs):
-    packed, all_ref, piv_ref = refs[:4], refs[4], refs[5]
+    packed, all_ref, piv_refs = refs[:4], refs[4], refs[5:]
+    examples = packed[0].shape[1]
     row = lax.broadcasted_iota(jnp.int32, (4 * LANES, 4 * LANES), 0)
     col = lax.broadcasted_iota(jnp.int32, (4 * LANES, 4 * LANES), 1)
     target = (row // CH) % 4 * LANES + row // LANES * CH + row % CH
     move = jnp.where(col == target, 1.0, 0.0).astype(BF16)
-    flat = jnp.concatenate([packed[i][...].reshape(GROUPS4 * EX, LANES) for i in range(4)], axis=1)
+    flat = jnp.concatenate([ref[...].reshape(GROUPS4 * examples, LANES) for ref in packed], axis=1)
     moved = jnp.dot(flat, move, preferred_element_type=F32).astype(BF16)
     for group in range(GROUPS4):
         for j in range(4):
             py, px = group // 2, (group % 2) * 4 + j
             if px == SIDE:
                 continue
-            spot = moved[group * EX:(group + 1) * EX, j * LANES:(j + 1) * LANES]
-            all_ref[py * SIDE + px] = spot
-            piv_ref[py * SIDE + px] = spot[:PIV_DEV]
+            spot = moved[group * examples:(group + 1) * examples, j * LANES:(j + 1) * LANES]
+            all_ref[py * SIDE + px] = spot[:EX]
+            piv_refs[0][py * SIDE + px] = spot[:PIV_DEV]
+            if examples > EX:
+                piv_refs[1][py * SIDE + px] = spot[EX:]
 
 
 def unpack(arrays, name):
     vmem = pl.BlockSpec(memory_space=pltpu.VMEM)
+    pivots = jax.ShapeDtypeStruct((SPOTS, PIV_DEV, LANES), BF16)
+    pivot_sets = arrays[0].shape[1] // PIV_DEV - 1
     return pl.pallas_call(
         unpack_kernel,
-        out_shape=(
-            jax.ShapeDtypeStruct((SPOTS, EX, LANES), BF16),
-            jax.ShapeDtypeStruct((SPOTS, PIV_DEV, LANES), BF16),
-        ),
-        in_specs=[vmem] * len(arrays),
-        out_specs=(vmem,) * 2,
-        compiler_params=pltpu.CompilerParams(vmem_limit_bytes=8 << 20),
+        out_shape=(jax.ShapeDtypeStruct((SPOTS, EX, LANES), BF16),) + (pivots,) * pivot_sets,
+        in_specs=[vmem] * 4,
+        out_specs=(vmem,) * (1 + pivot_sets),
+        compiler_params=pltpu.CompilerParams(vmem_limit_bytes=12 << 20),
         cost_estimate=cost(0, 1 << 20),
         name=name,
     )(*arrays)
@@ -169,11 +191,14 @@
     return acc + pltpu.roll(acc, 16, 1)
 
 
-def own_kernel(x, g, xp, gp, out_ref, *work):
-    out_ref[...] = panel_terms(x, g, xp, gp, *work)
-
-
-def cross_kernel(x, g, xp, gp, own_ref, out_ref, *work):
+def own_kernel(x, g, xp, gp, out_ref, block_ref, *work):
+    folded = panel_terms(x, g, xp, gp, *work)
+    out_ref[...] = folded
+    lane = lax.broadcasted_iota(jnp.int32, (8, LANES), 1)
+    block_ref[...] = jnp.where(lane // PIV_DEV == 0, folded[:8], folded[8:PIV_DEV])
+
+
+def cross_kernel(x, g, xp, gp, own_ref, block_ref, out_ref, *work):
     across = panel_terms(x, g, xp, gp, *work)
     lane = lax.broadcasted_iota(jnp.int32, (8, LANES), 1)
     is_own = (lane // PIV_DEV) % 2 == lax.axis_index("rows")
@@ -181,17 +206,18 @@
     for j in range(4):
         rows = slice(8 * j, 8 * j + 8)
         packed = jnp.where(lane // EX == j, jnp.where(is_own, own_ref[rows, :], across[rows]), packed)
-    out_ref[...] = packed
-
-
-def terms(kernel, arrays, shape, name):
+    out_ref[0:8, :] = packed
+    out_ref[8:16, :] = block_ref[...]
+
+
+def terms(kernel, arrays, shapes, name):
     vmem = pl.BlockSpec(memory_space=pltpu.VMEM)
     rows, cols = SIDE * ROWB, SIDE * COLB
     return pl.pallas_call(
         kernel,
-        out_shape=jax.ShapeDtypeStruct(shape, F32),
+        out_shape=tuple(jax.ShapeDtypeStruct(shape, F32) for shape in shapes),
         in_specs=[vmem] * len(arrays),
-        out_specs=vmem,
+        out_specs=(vmem,) * len(shapes),
         scratch_shapes=[
             pltpu.VMEM((rows, 3 * LANES), BF16),
             pltpu.VMEM((cols, 3 * LANES), BF16),
@@ -210,14 +236,21 @@
     )
 
 
-def final_kernel(own_ref, other_ref, ridge_ref, gram_ref, factor_ref):
-    first = lax.axis_index("rows") == 0
-    panel = rows_of(own_ref[...], 4)
+def final_kernel(*refs):
+    total_refs, (ridge_ref, gram_ref, factor_ref) = refs[:4], refs[4:]
+    total = (total_refs[0][...] + total_refs[1][...]) + (total_refs[2][...] + total_refs[3][...])
+    panel = rows_of(total[:8], 4)
     gram_ref[...] = panel
-    mine, cross = panel[:PIV_DEV], rows_of(other_ref[...], 2)
-    diag = jnp.concatenate([jnp.where(first, mine, cross), jnp.where(first, cross, mine)], axis=0)
+    group = lax.axis_index("rows")
+    mine, zero = panel[:PIV_DEV], jnp.zeros((PIV_DEV, EX), F32)
+    upper = jnp.concatenate([jnp.where(group == 0, mine, zero), jnp.where(group == 0, zero, mine)], axis=0)
+    block = jnp.concatenate([total[8:, :PIV_DEV], total[8:, PIV_DEV:2 * PIV_DEV]], axis=0)
+    block = jnp.concatenate([block, block], axis=1)
+    block = jnp.concatenate([block, block], axis=0)
     row_id = lax.broadcasted_iota(jnp.int32, (EX, EX), 0)
     col_id = lax.broadcasted_iota(jnp.int32, (EX, EX), 1)
+    diag = jnp.where(col_id // PIV_DEV == group, jnp.transpose(upper), block)
+    diag = jnp.where(row_id // PIV_DEV == group, upper, diag)
     ridge = jnp.where(row_id == col_id, jnp.broadcast_to(ridge_ref[...], (EX, EX)), 0.0)
     system = 0.5 * (diag + jnp.transpose(diag)) + ridge
     factor = jnp.zeros((EX, EX), F32)
@@ -242,17 +275,17 @@
     factor_ref[...] = factor
 
 
-def final(own, other, ridge):
+def final(totals, ridge):
     vmem = pl.BlockSpec(memory_space=pltpu.VMEM)
     out = jax.ShapeDtypeStruct((EX, EX), F32)
     return pl.pallas_call(
         final_kernel,
         out_shape=(out, out),
-        in_specs=[vmem] * 3,
+        in_specs=[vmem] * 5,
         out_specs=(vmem, vmem),
         compiler_params=pltpu.CompilerParams(vmem_limit_bytes=8 << 20),
         name="solve",
-    )(own, other, ridge.reshape(1, EX))
+    )(*totals, ridge.reshape(1, EX))
 
 
 def exchange(value, count, flip):
@@ -267,18 +300,19 @@
 def local_packed(count, activations, cotangents, ordering, ridge):
     near, far = (1, 2, 3), (4, 8, 12)
     x = jnp.transpose(activations, (1, 2, 0, 3)).reshape(SIDE * SIDE, EX, CH)
-    xo, go = prep(ordering, x, cotangents)
-    own_g = [go] + [exchange(go, count, f) for f in near]
+    xo, go, gp = prep(ordering, x, cotangents)
+    gm = merge(go, exchange_across(gp, count))
+    own_g = [gm] + [exchange(gm, count, f) for f in near]
     own_x = [xo] + [exchange(xo, count, f) for f in far]
     x_all, x_piv = unpack(own_x, "unpack_x")
     x_cross = exchange_across(x_piv, count)
-    g_all, g_piv = unpack(own_g, "unpack_g")
-    g_cross = exchange_across(g_piv, count)
-    own_term = terms(own_kernel, (x_all, g_all, x_piv, g_piv), (EX, LANES), "terms_own")
-    term = terms(cross_kernel, (x_all, g_all, x_cross, g_cross, own_term), (8, LANES), "terms_cross")
-    for flip in (1, 2, 4, 8):
-        term = term + exchange(term, count, flip)
-    return final(term, exchange_across(term, count), ridge)
+    g_all, g_piv, g_cross = unpack(own_g, "unpack_g")
+    own_term, block = terms(own_kernel, (x_all, g_all, x_piv, g_piv), ((EX, LANES), (8, LANES)), "terms_own")
+    block = exchange_across(block, count)
+    term, = terms(cross_kernel, (x_all, g_all, x_cross, g_cross, own_term, block), ((16, LANES),), "terms_cross")
+    terms_near = [term] + [exchange(term, count, f) for f in near]
+    part = (terms_near[0] + terms_near[1]) + (terms_near[2] + terms_near[3])
+    return final([part] + [exchange(part, count, f) for f in far], ridge)
 
 
 def jacobian_block(grad_rows, input_rows):

time: 51.2 us -> 48 us (0.938)
  waiting for transfers between devices: 23.6 us -> 16.6 us
  starting transfers between devices: 14.8 us -> 18.4 us
    ppermute x3, waiting for transfers between devices: 6.85 us -> 2.23 us  [exchange_across(): return lax.ppermute(value, ('rows', 'chan'), pairs)]
    ppermute x10 -> x12, starting transfers between devices: 11.1 us -> 14.4 us  [exchange(): return lax.ppermute(value, 'chan', [(i, i ^ flip) for i in range(count)])]
    ppermute x10 -> x12, waiting for transfers between devices: 16.8 us -> 14.3 us  [exchange(): return lax.ppermute(value, 'chan', [(i, i ^ flip) for i in range(count)])]
    pallas_call x4 -> x5, Pallas kernels: 10.2 us -> 10.3 us  [the longest x2 6.05 us: terms(): pl.pallas_call(kernel, out_shape=tuple((jax.ShapeDtypeStruct(shape, F32)...]
  transfers between devices with their start and end apart: 13 -> 15, of which waited for: 9 -> 8; matrix products, arithmetic and copies ran while one was open for 0% -> 0% of each run, Pallas kernels for 8% -> 8%
where the time goes in v1:
time: 48 us; the launch traced here: 47.9 us
  starting transfers between devices  18.4 us (38%)
  waiting for transfers between devices  16.6 us (35%)
  Pallas kernels  11.3 us (24%)
  local copies, waits for them, and re-layouts  0.91 us (2%)
  between operations  0.69 us (1%)
    ppermute x12, starting transfers between devices, exchange(): return lax.ppermute(value, 'chan', [(i, i ^ flip) for i in range(count)])  14.4 us
    ppermute x12, waiting for transfers between devices, exchange(): return lax.ppermute(value, 'chan', [(i, i ^ flip) for i in range(count)])  14.3 us
    pallas_call x2, Pallas kernels, terms(): pl.pallas_call(kernel, out_shape=tuple((jax.ShapeDtypeStruct(shape, F32)...  6.05 us
    ppermute x3, starting transfers between devices, exchange_across(): return lax.ppermute(value, ('rows', 'chan'), pairs)  3.92 us
    pallas_call x1, Pallas kernels, prep(): pl.pallas_call(prep_kernel, out_shape=(full, full, jax.ShapeDtypeStruct((...  2.37 us
    ppermute x3, waiting for transfers between devices, exchange_across(): return lax.ppermute(value, ('rows', 'chan'), pairs)  2.23 us
    pallas_call x1, Pallas kernels, final(): pl.pallas_call(final_kernel, out_shape=(out, out), in_specs=[vmem] * 5, o...  1.91 us
    pallas_call x2, Pallas kernels, unpack(): pl.pallas_call(unpack_kernel, out_shape=(jax.ShapeDtypeStruct((SPOTS, EX,...  1 us
  transfers between devices with their start and end apart: 15, of which 8 were waited for; matrix products, arithmetic and copies ran while one was open for 0% of the time, Pallas kernels for 8%

profile of v1, /device:TPU:0, one launch (start us, length us, event | category | flops | bytes accessed | tf_op | source)
XLA Modules:
  0.0 47.9 jit_solution(4540528614781844533)
XLA Ops:
  0.6 2.4 %prep.1 = (bf16[14,32,128]{2,1,0:T(8,128)(2,1)}, bf16[14,32,128]{2,1,0:T(8,128)(2,1)}, bf16[14,16,128]{2,1,0:T(8,128)(2,1)}) custom-call(s32[1,32]{1,0:T(1,128)} %order_hbm.1, bf16[49,32,32]{2,1,0:T(8,128)(2,1)} %bitcast.5, bf16[32,32,49]{2,1,0:T(8,128)(2,1)} %g_hbm.1), custom_call_target="tpu_custom_call" | custom-call | tf_op jit(solution)/shard_map/prep/pallas_call | solution.py:71
  3.0 3.1 %collective-permute-start = (bf16[14,32,128]{2,1,0:T(8,128)(2,1)}, bf16[14,32,128]{2,1,0:T(8,128)(2,1)S(1)}, u32[]{:S(2)}, u32[]{:S(2)}) collective-permute-start(bf16[14,32,128]{2,1,0:T(8,128)(2,1)} %get-tuple-element.12.refs_0_), channel_id=1, source_target_pairs={{0,4},{1,5},{2,6},{3,7},{4,0},{5,1},{6,2},{7,3},{8,12},{9,13},{10,... | collective-permute-start | bytes 344072 | tf_op jit(solution)/shard_map/ppermute | solution.py:292
  6.1 1.5 %collective-permute-start.3 = (bf16[14,16,128]{2,1,0:T(8,128)(2,1)}, bf16[14,16,128]{2,1,0:T(8,128)(2,1)S(1)}, u32[]{:S(2)}, u32[]{:S(2)}) collective-permute-start(bf16[14,16,128]{2,1,0:T(8,128)(2,1)} %get-tuple-element.15), channel_id=1, source_target_pairs={{0,16},{1,17},{2,18},{3,19},{4,20},{5,21},{6,22},{7,23},{8,24},{9,... | collective-permute-start | bytes 172040 | tf_op jit(solution)/shard_map/ppermute | solution.py:297
  7.6 2.6 %collective-permute-start.1 = (bf16[14,32,128]{2,1,0:T(8,128)(2,1)}, bf16[14,32,128]{2,1,0:T(8,128)(2,1)S(1)}, u32[]{:S(2)}, u32[]{:S(2)}) collective-permute-start(bf16[14,32,128]{2,1,0:T(8,128)(2,1)} %get-tuple-element.12.refs_0_), channel_id=1, source_target_pairs={{0,8},{1,9},{2,10},{3,11},{4,12},{5,13},{6,14},{7,15},{8,0},{9,1},... | collective-permute-start | bytes 344072 | tf_op jit(solution)/shard_map/ppermute | solution.py:292
  10.5 0.9 %copy-done.1 = bf16[14,32,128]{2,1,0:T(8,128)(2,1)S(1)} copy-done((bf16[14,32,128]{2,1,0:T(8,128)(2,1)S(1)}, bf16[14,32,128]{2,1,0:T(8,128)(2,1)}, u32[]{:S(2)}) %copy-start.1) | copy-done | bytes 114712
  11.5 1.6 %collective-permute-start.5 = (bf16[14,48,128]{2,1,0:T(8,128)(2,1)S(1)}, bf16[14,48,128]{2,1,0:T(8,128)(2,1)S(1)}, u32[]{:S(2)}, u32[]{:S(2)}) collective-permute-start(bf16[14,48,128]{2,1,0:T(8,128)(2,1)S(1)} %merge.1.refs_0_), channel_id=1, source_target_pairs={{0,2},{1,3},{2,0},{3,1},{4,6},{5,7},{6,4},{7,5},{8,10},{9,11},{10,... | collective-permute-start | bytes 516104 | tf_op jit(solution)/shard_map/ppermute | solution.py:292
  13.3 5.5 %collective-permute-done.1.refs_2_ = bf16[14,32,128]{2,1,0:T(8,128)(2,1)S(1)} collective-permute-done((bf16[14,32,128]{2,1,0:T(8,128)(2,1)}, bf16[14,32,128]{2,1,0:T(8,128)(2,1)S(1)}, u32[]{:S(2)}, u32[]{:S(2)}) %collective-permute-start.1) | collective-permute-done | bytes 114720 | tf_op jit(solution)/shard_map/ppermute | solution.py:292
  18.8 0.4 unpack_x.1
  19.3 1.0 %collective-permute-start.7 = (bf16[49,16,128]{2,1,0:T(8,128)(2,1)S(1)}, bf16[49,16,128]{2,1,0:T(8,128)(2,1)S(1)}, u32[]{:S(2)}, u32[]{:S(2)}) collective-permute-start(bf16[49,16,128]{2,1,0:T(8,128)(2,1)S(1)} %get-tuple-element.17.xp), channel_id=1, source_target_pairs={{0,16},{1,17},{2,18},{3,19},{4,20},{5,21},{6,22},{7,23},{8,24},{9,... | collective-permute-start | bytes 602120 | tf_op jit(solution)/shard_map/ppermute | solution.py:297
  20.2 1.3 %collective-permute-done.6.refs_3_ = bf16[14,48,128]{2,1,0:T(8,128)(2,1)S(1)} collective-permute-done((bf16[14,48,128]{2,1,0:T(8,128)(2,1)S(1)}, bf16[14,48,128]{2,1,0:T(8,128)(2,1)S(1)}, u32[]{:S(2)}, u32[]{:S(2)}) %collective-permute-start.6) | collective-permute-done | bytes 172064 | tf_op jit(solution)/shard_map/ppermute | solution.py:292
  21.5 0.6 %unpack_g.1 = (bf16[49,32,128]{2,1,0:T(8,128)(2,1)S(1)}, bf16[49,16,128]{2,1,0:T(8,128)(2,1)S(1)}, bf16[49,16,128]{2,1,0:T(8,128)(2,1)S(1)}) custom-call(bf16[14,48,128]{2,1,0:T(8,128)(2,1)S(1)} %merge.1.refs_0_, bf16[14,48,128]{2,1,0:T(8,128)(2,1)S(1)} %collective-permute-done.4.refs_1_, bf16[14,48,128]{2,1,0:T(8,128)(2,1)S(1)} %collective-permute-done.5.refs_2_, ...), custom_call_target="tpu_custom_call" | custom-call | bytes 1048576 | tf_op jit(solution)/shard_map/unpack_g/pallas_call | solution.py:142
  22.1 3.0 %terms_own.1 = (f32[32,128]{1,0:T(8,128)S(1)}, f32[8,128]{1,0:T(8,128)S(1)}) custom-call(bf16[49,32,128]{2,1,0:T(8,128)(2,1)S(1)} %get-tuple-element.13.x, bf16[49,32,128]{2,1,0:T(8,128)(2,1)S(1)} %get-tuple-element.16.g, bf16[49,16,128]{2,1,0:T(8,128)(2,1)S(1)} %get-tuple-element.17.xp, bf16[49,16,128]{2,1,0:T(8,128)(2,1)S(1)} %get-tuple-element.19.gp), custom_call_target="tpu_custom_call" | custom-call | flops 1438646272 | bytes 8388608 | tf_op jit(solution)/shard_map/terms_own/pallas_call | solution.py:216
  25.1 1.5 %collective-permute-start.8 = (f32[8,128]{1,0:T(8,128)S(1)}, f32[8,128]{1,0:T(8,128)S(1)}, u32[]{:S(2)}, u32[]{:S(2)}) collective-permute-start(f32[8,128]{1,0:T(8,128)S(1)} %get-tuple-element.21), channel_id=1, source_target_pairs={{0,16},{1,17},{2,18},{3,19},{4,20},{5,21},{6,22},{7,23},{8,24},{9,... | collective-permute-start | bytes 12296 | tf_op jit(solution)/shard_map/ppermute | solution.py:297
  26.6 2.1 %collective-permute-done.8.block_ref = f32[8,128]{1,0:T(8,128)S(1)} collective-permute-done((f32[8,128]{1,0:T(8,128)S(1)}, f32[8,128]{1,0:T(8,128)S(1)}, u32[]{:S(2)}, u32[]{:S(2)}) %collective-permute-start.8) | collective-permute-done | bytes 4128 | tf_op jit(solution)/shard_map/ppermute | solution.py:297
  28.7 3.0 %terms_cross.1 = f32[16,128]{1,0:T(8,128)S(1)} custom-call(bf16[49,32,128]{2,1,0:T(8,128)(2,1)S(1)} %get-tuple-element.13.x, bf16[49,32,128]{2,1,0:T(8,128)(2,1)S(1)} %get-tuple-element.16.g, bf16[49,16,128]{2,1,0:T(8,128)(2,1)S(1)} %collective-permute-done.7.xp, bf16[49,16,128]{2,1,0:T(8,128)(2,1)S(1)} %get-tuple-element.18.gp, ...), custom_call_target="tpu_custom_call" | custom-call | flops 1438646272 | bytes 8388608 | tf_op jit(solution)/shard_map/terms_cross/pallas_call | solution.py:216
  31.7 1.5 %collective-permute-start.10 = (f32[16,128]{1,0:T(8,128)S(1)}, f32[16,128]{1,0:T(8,128)S(1)}, u32[]{:S(2)}, u32[]{:S(2)}) collective-permute-start(f32[16,128]{1,0:T(8,128)S(1)} %terms_cross.1), channel_id=1, source_target_pairs={{0,2},{1,3},{2,0},{3,1},{4,6},{5,7},{6,4},{7,5},{8,10},{9,11},{10,... | collective-permute-start | bytes 24584 | tf_op jit(solution)/shard_map/ppermute | solution.py:292
  33.3 0.6 %collective-permute-start.9 = (f32[16,128]{1,0:T(8,128)S(1)}, f32[16,128]{1,0:T(8,128)S(1)}, u32[]{:S(2)}, u32[]{:S(2)}) collective-permute-start(f32[16,128]{1,0:T(8,128)S(1)} %terms_cross.1), channel_id=1, source_target_pairs={{0,1},{1,0},{2,3},{3,2},{4,5},{5,4},{6,7},{7,6},{8,9},{9,8},{10,11... | collective-permute-start | bytes 24584 | tf_op jit(solution)/shard_map/ppermute | solution.py:292
  33.9 1.5 %collective-permute-done.10 = f32[16,128]{1,0:T(8,128)S(1)} collective-permute-done((f32[16,128]{1,0:T(8,128)S(1)}, f32[16,128]{1,0:T(8,128)S(1)}, u32[]{:S(2)}, u32[]{:S(2)}) %collective-permute-start.10) | collective-permute-done | bytes 8224 | tf_op jit(solution)/shard_map/ppermute | solution.py:292
  35.4 1.0 %collective-permute-done.11 = f32[16,128]{1,0:T(8,128)S(1)} collective-permute-done((f32[16,128]{1,0:T(8,128)S(1)}, f32[16,128]{1,0:T(8,128)S(1)}, u32[]{:S(2)}, u32[]{:S(2)}) %collective-permute-start.11) | collective-permute-done | bytes 8224 | tf_op jit(solution)/shard_map/ppermute | solution.py:292
  36.4 0.7 %collective-permute-start.12 = (f32[16,128]{1,0:T(8,128)S(1)}, f32[16,128]{1,0:T(8,128)S(1)}, u32[]{:S(2)}, u32[]{:S(2)}) collective-permute-start(f32[16,128]{1,0:T(8,128)S(1)} %add_add_fusion.refs_0_), channel_id=1, source_target_pairs={{0,4},{1,5},{2,6},{3,7},{4,0},{5,1},{6,2},{7,3},{8,12},{9,13},{10,... | collective-permute-start | bytes 24584 | tf_op jit(solution)/shard_map/ppermute | solution.py:292
  37.0 3.5 %collective-permute-start.13 = (f32[16,128]{1,0:T(8,128)S(1)}, f32[16,128]{1,0:T(8,128)S(1)}, u32[]{:S(2)}, u32[]{:S(2)}) collective-permute-start(f32[16,128]{1,0:T(8,128)S(1)} %add_add_fusion.refs_0_), channel_id=1, source_target_pairs={{0,8},{1,9},{2,10},{3,11},{4,12},{5,13},{6,14},{7,15},{8,0},{9,1},... | collective-permute-start | bytes 24584 | tf_op jit(solution)/shard_map/ppermute | solution.py:292
  40.8 1.3 %collective-permute-done.13.refs_2_ = f32[16,128]{1,0:T(8,128)S(1)} collective-permute-done((f32[16,128]{1,0:T(8,128)S(1)}, f32[16,128]{1,0:T(8,128)S(1)}, u32[]{:S(2)}, u32[]{:S(2)}) %collective-permute-start.13) | collective-permute-done | bytes 8224 | tf_op jit(solution)/shard_map/ppermute | solution.py:292
  42.1 3.8 %collective-permute-done.14.refs_3_ = f32[16,128]{1,0:T(8,128)S(1)} collective-permute-done((f32[16,128]{1,0:T(8,128)S(1)}, f32[16,128]{1,0:T(8,128)S(1)}, u32[]{:S(2)}, u32[]{:S(2)}) %collective-permute-start.14) | collective-permute-done | bytes 8224 | tf_op jit(solution)/shard_map/ppermute | solution.py:292
  46.0 1.9 %solve.1 = (f32[32,32]{1,0:T(8,128)}, f32[32,32]{1,0:T(8,128)}) custom-call(f32[16,128]{1,0:T(8,128)S(1)} %add_add_fusion.refs_0_, f32[16,128]{1,0:T(8,128)S(1)} %collective-permute-done.12.refs_1_, f32[16,128]{1,0:T(8,128)S(1)} %collective-permute-done.13.refs_2_, f32[16,128]{1,0:T(8,128)S(1)} %collective-permute-done.14.refs_3_, f32[1,32]{1,0:T(1,128)S(1)} %bitcast.4), custom_call_target="tpu_custom_call" | custom-call | tf_op jit(solution)/shard_map/solve/pallas_call | solution.py:281
  (20 shorter events, 1.0 us)
Async XLA Ops:
  3.0 10.1 %collective-permute-start = (bf16[14,32,128]{2,1,0:T(8,128)(2,1)}, bf16[14,32,128]{2,1,0:T(8,128)(2,1)S(1)}, u32[]{:S(2)}, u32[]{:S(2)}) collective-permute-start(bf16[14,32,128]{2,1,0:T(8,128)(2,1)} %get-tuple-element.12.refs_0_), channel_id=1, source_target_pairs={{0,4},{1,5},{2,6},{3,7},{4,0},{5,1},{6,2},{7,3},{8,12},{9,13},{10,... | collective-permute-start | bytes 344072 | tf_op jit(solution)/shard_map/ppermute | solution.py:292
  6.1 4.4 %collective-permute-start.3 = (bf16[14,16,128]{2,1,0:T(8,128)(2,1)}, bf16[14,16,128]{2,1,0:T(8,128)(2,1)S(1)}, u32[]{:S(2)}, u32[]{:S(2)}) collective-permute-start(bf16[14,16,128]{2,1,0:T(8,128)(2,1)} %get-tuple-element.15), channel_id=1, source_target_pairs={{0,16},{1,17},{2,18},{3,19},{4,20},{5,21},{6,22},{7,23},{8,24},{9,... | collective-permute-start | bytes 172040 | tf_op jit(solution)/shard_map/ppermute | solution.py:297
  7.6 11.2 %collective-permute-start.1 = (bf16[14,32,128]{2,1,0:T(8,128)(2,1)}, bf16[14,32,128]{2,1,0:T(8,128)(2,1)S(1)}, u32[]{:S(2)}, u32[]{:S(2)}) collective-permute-start(bf16[14,32,128]{2,1,0:T(8,128)(2,1)} %get-tuple-element.12.refs_0_), channel_id=1, source_target_pairs={{0,8},{1,9},{2,10},{3,11},{4,12},{5,13},{6,14},{7,15},{8,0},{9,1},... | collective-permute-start | bytes 344072 | tf_op jit(solution)/shard_map/ppermute | solution.py:292
  10.2 8.6 %collective-permute-start.2 = (bf16[14,32,128]{2,1,0:T(8,128)(2,1)}, bf16[14,32,128]{2,1,0:T(8,128)(2,1)S(1)}, u32[]{:S(2)}, u32[]{:S(2)}) collective-permute-start(bf16[14,32,128]{2,1,0:T(8,128)(2,1)} %get-tuple-element.12.refs_0_), channel_id=1, source_target_pairs={{0,12},{1,13},{2,14},{3,15},{4,8},{5,9},{6,10},{7,11},{8,4},{9,5},... | collective-permute-start | bytes 344072 | tf_op jit(solution)/shard_map/ppermute | solution.py:292
  10.5 0.9 %copy-start.1 = (bf16[14,32,128]{2,1,0:T(8,128)(2,1)S(1)}, bf16[14,32,128]{2,1,0:T(8,128)(2,1)}, u32[]{:S(2)}) copy-start(bf16[14,32,128]{2,1,0:T(8,128)(2,1)} %get-tuple-element.14.own_ref) | copy-start | bytes 344068
  11.4 7.4 %copy-start = (bf16[14,32,128]{2,1,0:T(8,128)(2,1)S(1)}, bf16[14,32,128]{2,1,0:T(8,128)(2,1)}, u32[]{:S(2)}) copy-start(bf16[14,32,128]{2,1,0:T(8,128)(2,1)} %get-tuple-element.12.refs_0_) | copy-start | bytes 344068
  11.4 8.8 %collective-permute-start.4 = (bf16[14,48,128]{2,1,0:T(8,128)(2,1)S(1)}, bf16[14,48,128]{2,1,0:T(8,128)(2,1)S(1)}, u32[]{:S(2)}, u32[]{:S(2)}) collective-permute-start(bf16[14,48,128]{2,1,0:T(8,128)(2,1)S(1)} %merge.1.refs_0_), channel_id=1, source_target_pairs={{0,1},{1,0},{2,3},{3,2},{4,5},{5,4},{6,7},{7,6},{8,9},{9,8},{10,11... | collective-permute-start | bytes 516104 | tf_op jit(solution)/shard_map/ppermute | solution.py:292
  11.5 8.7 %collective-permute-start.5 = (bf16[14,48,128]{2,1,0:T(8,128)(2,1)S(1)}, bf16[14,48,128]{2,1,0:T(8,128)(2,1)S(1)}, u32[]{:S(2)}, u32[]{:S(2)}) collective-permute-start(bf16[14,48,128]{2,1,0:T(8,128)(2,1)S(1)} %merge.1.refs_0_), channel_id=1, source_target_pairs={{0,2},{1,3},{2,0},{3,1},{4,6},{5,7},{6,4},{7,5},{8,10},{9,11},{10,... | collective-permute-start | bytes 516104 | tf_op jit(solution)/shard_map/ppermute | solution.py:292
  13.1 8.4 %collective-permute-start.6 = (bf16[14,48,128]{2,1,0:T(8,128)(2,1)S(1)}, bf16[14,48,128]{2,1,0:T(8,128)(2,1)S(1)}, u32[]{:S(2)}, u32[]{:S(2)}) collective-permute-start(bf16[14,48,128]{2,1,0:T(8,128)(2,1)S(1)} %merge.1.refs_0_), channel_id=1, source_target_pairs={{0,3},{1,2},{2,1},{3,0},{4,7},{5,6},{6,5},{7,4},{8,11},{9,10},{10,... | collective-permute-start | bytes 516104 | tf_op jit(solution)/shard_map/ppermute | solution.py:292
  19.3 9.5 %collective-permute-start.7 = (bf16[49,16,128]{2,1,0:T(8,128)(2,1)S(1)}, bf16[49,16,128]{2,1,0:T(8,128)(2,1)S(1)}, u32[]{:S(2)}, u32[]{:S(2)}) collective-permute-start(bf16[49,16,128]{2,1,0:T(8,128)(2,1)S(1)} %get-tuple-element.17.xp), channel_id=1, source_target_pairs={{0,16},{1,17},{2,18},{3,19},{4,20},{5,21},{6,22},{7,23},{8,24},{9,... | collective-permute-start | bytes 602120 | tf_op jit(solution)/shard_map/ppermute | solution.py:297
  25.1 3.6 %collective-permute-start.8 = (f32[8,128]{1,0:T(8,128)S(1)}, f32[8,128]{1,0:T(8,128)S(1)}, u32[]{:S(2)}, u32[]{:S(2)}) collective-permute-start(f32[8,128]{1,0:T(8,128)S(1)} %get-tuple-element.21), channel_id=1, source_target_pairs={{0,16},{1,17},{2,18},{3,19},{4,20},{5,21},{6,22},{7,23},{8,24},{9,... | collective-permute-start | bytes 12296 | tf_op jit(solution)/shard_map/ppermute | solution.py:297
  31.7 3.7 %collective-permute-start.10 = (f32[16,128]{1,0:T(8,128)S(1)}, f32[16,128]{1,0:T(8,128)S(1)}, u32[]{:S(2)}, u32[]{:S(2)}) collective-permute-start(f32[16,128]{1,0:T(8,128)S(1)} %terms_cross.1), channel_id=1, source_target_pairs={{0,2},{1,3},{2,0},{3,1},{4,6},{5,7},{6,4},{7,5},{8,10},{9,11},{10,... | collective-permute-start | bytes 24584 | tf_op jit(solution)/shard_map/ppermute | solution.py:292
  33.3 3.1 %collective-permute-start.11 = (f32[16,128]{1,0:T(8,128)S(1)}, f32[16,128]{1,0:T(8,128)S(1)}, u32[]{:S(2)}, u32[]{:S(2)}) collective-permute-start(f32[16,128]{1,0:T(8,128)S(1)} %terms_cross.1), channel_id=1, source_target_pairs={{0,3},{1,2},{2,1},{3,0},{4,7},{5,6},{6,5},{7,4},{8,11},{9,10},{10,... | collective-permute-start | bytes 24584 | tf_op jit(solution)/shard_map/ppermute | solution.py:292
  33.3 3.1 %collective-permute-start.9 = (f32[16,128]{1,0:T(8,128)S(1)}, f32[16,128]{1,0:T(8,128)S(1)}, u32[]{:S(2)}, u32[]{:S(2)}) collective-permute-start(f32[16,128]{1,0:T(8,128)S(1)} %terms_cross.1), channel_id=1, source_target_pairs={{0,1},{1,0},{2,3},{3,2},{4,5},{5,4},{6,7},{7,6},{8,9},{9,8},{10,11... | collective-permute-start | bytes 24584 | tf_op jit(solution)/shard_map/ppermute | solution.py:292
  36.4 9.6 %copy-start.2 = (f32[32]{0:T(128)S(1)}, f32[32]{0:T(128)}, u32[]{:S(2)}) copy-start(f32[32]{0:T(128)} %param.7) | copy-start | bytes 388
  36.4 4.5 %collective-permute-start.12 = (f32[16,128]{1,0:T(8,128)S(1)}, f32[16,128]{1,0:T(8,128)S(1)}, u32[]{:S(2)}, u32[]{:S(2)}) collective-permute-start(f32[16,128]{1,0:T(8,128)S(1)} %add_add_fusion.refs_0_), channel_id=1, source_target_pairs={{0,4},{1,5},{2,6},{3,7},{4,0},{5,1},{6,2},{7,3},{8,12},{9,13},{10,... | collective-permute-start | bytes 24584 | tf_op jit(solution)/shard_map/ppermute | solution.py:292
  37.0 5.1 %collective-permute-start.13 = (f32[16,128]{1,0:T(8,128)S(1)}, f32[16,128]{1,0:T(8,128)S(1)}, u32[]{:S(2)}, u32[]{:S(2)}) collective-permute-start(f32[16,128]{1,0:T(8,128)S(1)} %add_add_fusion.refs_0_), channel_id=1, source_target_pairs={{0,8},{1,9},{2,10},{3,11},{4,12},{5,13},{6,14},{7,15},{8,0},{9,1},... | collective-permute-start | bytes 24584 | tf_op jit(solution)/shard_map/ppermute | solution.py:292
  40.5 5.4 %collective-permute-start.14 = (f32[16,128]{1,0:T(8,128)S(1)}, f32[16,128]{1,0:T(8,128)S(1)}, u32[]{:S(2)}, u32[]{:S(2)}) collective-permute-start(f32[16,128]{1,0:T(8,128)S(1)} %add_add_fusion.refs_0_), channel_id=1, source_target_pairs={{0,12},{1,13},{2,14},{3,15},{4,8},{5,9},{6,10},{7,11},{8,4},{9,5},... | collective-permute-start | bytes 24584 | tf_op jit(solution)/shard_map/ppermute | solution.py:292

commit v2 on v1

--- a/solution.py
+++ b/solution.py
@@ -88,7 +88,6 @@
 
 
 SPOTS = SIDE * SIDE
-ROWB = SIDE * EX
 COLB = PITCH * PIV_DEV
 
 
@@ -114,8 +113,7 @@
     )(own, cross)
 
 
-def unpack_kernel(*refs):
-    packed, all_ref, piv_refs = refs[:4], refs[4], refs[5:]
+def unpack_body(packed, all_ref, piv_refs):
     examples = packed[0].shape[1]
     row = lax.broadcasted_iota(jnp.int32, (4 * LANES, 4 * LANES), 0)
     col = lax.broadcasted_iota(jnp.int32, (4 * LANES, 4 * LANES), 1)
@@ -135,14 +133,23 @@
                 piv_refs[1][py * SIDE + px] = spot[EX:]
 
 
+def unpack_kernel(*refs):
+    unpack_body(refs[:4], refs[4], refs[5:])
+
+
+def unpack_gathered_kernel(gathered, all_ref, piv_ref):
+    unpack_body([gathered.at[i] for i in range(4)], all_ref, (piv_ref,))
+
+
 def unpack(arrays, name):
     vmem = pl.BlockSpec(memory_space=pltpu.VMEM)
     pivots = jax.ShapeDtypeStruct((SPOTS, PIV_DEV, LANES), BF16)
-    pivot_sets = arrays[0].shape[1] // PIV_DEV - 1
+    pivot_sets = arrays[0].shape[-2] // PIV_DEV - 1
+    gathered = len(arrays) == 1
     return pl.pallas_call(
-        unpack_kernel,
+        unpack_gathered_kernel if gathered else unpack_kernel,
         out_shape=(jax.ShapeDtypeStruct((SPOTS, EX, LANES), BF16),) + (pivots,) * pivot_sets,
-        in_specs=[vmem] * 4,
+        in_specs=[vmem] * len(arrays),
         out_specs=(vmem,) * (1 + pivot_sets),
         compiler_params=pltpu.CompilerParams(vmem_limit_bytes=12 << 20),
         cost_estimate=cost(0, 1 << 20),
@@ -150,10 +157,13 @@
     )(*arrays)
 
 
-def panel_terms(x, g, xp, gp, lx, rx, rg, t):
+def panel_terms(rows_x, rows_g, xp, gp, lx, lg, rx, rg, t):
+    heights = [ref.shape[1] for ref in rows_x]
+    height = sum(heights)
+    block = SIDE * height
     for py in range(SIDE):
         for px in range(PITCH):
-            row, col = (py * SIDE + px) * EX, (py * PITCH + px) * PIV_DEV
+            row, col = (py * SIDE + px) * height, (py * PITCH + px) * PIV_DEV
             for d in range(3):
                 from_x = px + d - 1
                 inside = 0 <= from_x < SIDE and px < SIDE
@@ -161,25 +171,33 @@
                 spot = py * SIDE + from_x
                 rx[col:col + PIV_DEV, lanes] = xp[spot] if inside else jnp.zeros((PIV_DEV, LANES), BF16)
                 if px < SIDE:
-                    lx[row:row + EX, lanes] = x[spot] if inside else jnp.zeros((EX, LANES), BF16)
+                    first = row
+                    for ref, count in zip(rows_x, heights):
+                        lx[first:first + count, lanes] = ref[spot] if inside else jnp.zeros((count, LANES), BF16)
+                        first += count
             rg[col:col + PIV_DEV, :] = gp[py * SIDE + px] if px < SIDE else jnp.zeros((PIV_DEV, LANES), BF16)
+            if px < SIDE:
+                first = row
+                for ref, count in zip(rows_g, heights):
+                    lg[first:first + count, :] = ref[py * SIDE + px]
+                    first += count
 
     contract = (((1,), (1,)), ((), ()))
     spans = [(qy, min(qy + 2, SIDE)) for qy in range(0, SIDE, 2)]
     for start, stop in spans:
         right = rx[start * COLB:stop * COLB, :]
         for py in range(SIDE):
-            left = lx[py * ROWB:(py + 1) * ROWB, :]
+            left = lx[py * block:(py + 1) * block, :]
             t[py, :, start * COLB:stop * COLB] = lax.dot_general(left, right, contract, preferred_element_type=F32)
-    acc = jnp.zeros((EX, COLB), F32)
+    acc = jnp.zeros((height, COLB), F32)
     for start, stop in spans:
         right = rg[start * COLB:stop * COLB, :]
         for py in range(SIDE):
-            left = g[py * SIDE:(py + 1) * SIDE].reshape(ROWB, LANES)
+            left = lg[py * block:(py + 1) * block, :]
             gg = lax.dot_general(left, right, contract, preferred_element_type=F32)
             for qy in range(start, stop):
                 for px in range(SIDE):
-                    rows = slice(px * EX, (px + 1) * EX)
+                    rows = slice(px * height, (px + 1) * height)
                     total = t[py, rows, qy * COLB:(qy + 1) * COLB]
                     if py > 0 and qy > 0:
                         total = total + t[py - 1, rows, (qy - 1) * COLB:qy * COLB]
@@ -191,15 +209,12 @@
     return acc + pltpu.roll(acc, 16, 1)
 
 
-def own_kernel(x, g, xp, gp, out_ref, block_ref, *work):
-    folded = panel_terms(x, g, xp, gp, *work)
-    out_ref[...] = folded
-    lane = lax.broadcasted_iota(jnp.int32, (8, LANES), 1)
-    block_ref[...] = jnp.where(lane // PIV_DEV == 0, folded[:8], folded[8:PIV_DEV])
-
-
-def cross_kernel(x, g, xp, gp, own_ref, block_ref, out_ref, *work):
-    across = panel_terms(x, g, xp, gp, *work)
+def own_kernel(x, g, xp, gp, out_ref, *work):
+    out_ref[...] = panel_terms([x], [g], xp, gp, *work)
+
+
+def cross_kernel(x, g, xp, gp, own_ref, out_ref, *work):
+    across = panel_terms([x, xp], [g, gp], xp, gp, *work)
     lane = lax.broadcasted_iota(jnp.int32, (8, LANES), 1)
     is_own = (lane // PIV_DEV) % 2 == lax.axis_index("rows")
     packed = jnp.zeros((8, LANES), F32)
@@ -207,24 +222,25 @@
         rows = slice(8 * j, 8 * j + 8)
         packed = jnp.where(lane // EX == j, jnp.where(is_own, own_ref[rows, :], across[rows]), packed)
     out_ref[0:8, :] = packed
-    out_ref[8:16, :] = block_ref[...]
-
-
-def terms(kernel, arrays, shapes, name):
+    out_ref[8:16, :] = jnp.where(lane // PIV_DEV == 0, across[EX:EX + 8], across[EX + 8:EX + PIV_DEV])
+
+
+def terms(kernel, arrays, height, shape, name):
     vmem = pl.BlockSpec(memory_space=pltpu.VMEM)
-    rows, cols = SIDE * ROWB, SIDE * COLB
+    rows, cols = SPOTS * height, SIDE * COLB
     return pl.pallas_call(
         kernel,
-        out_shape=tuple(jax.ShapeDtypeStruct(shape, F32) for shape in shapes),
+        out_shape=jax.ShapeDtypeStruct(shape, F32),
         in_specs=[vmem] * len(arrays),
-        out_specs=(vmem,) * len(shapes),
+        out_specs=vmem,
         scratch_shapes=[
             pltpu.VMEM((rows, 3 * LANES), BF16),
+            pltpu.VMEM((rows, LANES), BF16),
             pltpu.VMEM((cols, 3 * LANES), BF16),
             pltpu.VMEM((cols, LANES), BF16),
-            pltpu.VMEM((SIDE, ROWB, cols), F32),
+            pltpu.VMEM((SIDE, SIDE * height, cols), F32),
         ],
-        compiler_params=pltpu.CompilerParams(vmem_limit_bytes=24 << 20),
+        compiler_params=pltpu.CompilerParams(vmem_limit_bytes=28 << 20),
         cost_estimate=cost(2 * rows * cols * 4 * LANES, 8 << 20),
         name=name,
     )(*arrays)
@@ -303,13 +319,13 @@
     xo, go, gp = prep(ordering, x, cotangents)
     gm = merge(go, exchange_across(gp, count))
     own_g = [gm] + [exchange(gm, count, f) for f in near]
-    own_x = [xo] + [exchange(xo, count, f) for f in far]
-    x_all, x_piv = unpack(own_x, "unpack_x")
+    lines = [[4 * i + k for i in range(count // 4)] for k in range(4)]
+    x_all, x_piv = unpack([lax.all_gather(xo, "chan", axis_index_groups=lines)], "unpack_x")
     x_cross = exchange_across(x_piv, count)
     g_all, g_piv, g_cross = unpack(own_g, "unpack_g")
-    own_term, block = terms(own_kernel, (x_all, g_all, x_piv, g_piv), ((EX, LANES), (8, LANES)), "terms_own")
-    block = exchange_across(block, count)
-    term, = terms(cross_kernel, (x_all, g_all, x_cross, g_cross, own_term, block), ((16, LANES),), "terms_cross")
+    own_term = terms(own_kernel, (x_all, g_all, x_piv, g_piv), EX, (EX, LANES), "terms_own")
+    arrays = (x_all, g_all, x_cross, g_cross, own_term)
+    term = terms(cross_kernel, arrays, EX + PIV_DEV, (16, LANES), "terms_cross")
     terms_near = [term] + [exchange(term, count, f) for f in near]
     part = (terms_near[0] + terms_near[1]) + (terms_near[2] + terms_near[3])
     return final([part] + [exchange(part, count, f) for f in far], ridge)

time: 48 us -> 52.3 us (1.090)
  blocking collectives: 0 us -> 15.7 us
  waiting for transfers between devices: 16.6 us -> 8.87 us
  starting transfers between devices: 18.4 us -> 13.4 us
  Pallas kernels: 11.3 us -> 12.6 us
    all_gather x0 -> x1, blocking collectives: none -> 15.7 us  [local_packed(): lax.all_gather(xo, 'chan', axis_index_groups=lines)]
    ppermute x12 -> x9, waiting for transfers between devices: 14.3 us -> 5.79 us  [exchange(): return lax.ppermute(value, 'chan', [(i, i ^ flip) for i in range(count)])]
    ppermute x12 -> x9, starting transfers between devices: 14.4 us -> 8.8 us  [exchange(): return lax.ppermute(value, 'chan', [(i, i ^ flip) for i in range(count)])]
    pallas_call x4, Pallas kernels: 7.05 us -> 8.31 us  [the longest x2 7.31 us: terms(): pl.pallas_call(kernel, out_shape=jax.ShapeDtypeStruct(shape, F32), in_spe...]
    ppermute x3 -> x2, waiting for transfers between devices: 2.23 us -> 3.08 us  [exchange_across(): return lax.ppermute(value, ('rows', 'chan'), pairs)]
    ppermute x3 -> x2, starting transfers between devices: 3.92 us -> 4.56 us  [exchange_across(): return lax.ppermute(value, ('rows', 'chan'), pairs)]
  transfers between devices with their start and end apart: 15 -> 11, of which waited for: 8 -> 6; matrix products, arithmetic and copies ran while one was open for 0% -> 0% of each run, Pallas kernels for 8% -> 8%
where the time goes in v2:
time: 52.3 us; the launch traced here: 52.1 us
  blocking collectives  15.7 us (30%)
  starting transfers between devices  13.4 us (26%)
  Pallas kernels  12.6 us (24%)
  waiting for transfers between devices  8.87 us (17%)
  local copies, waits for them, and re-layouts  0.91 us (2%)
  between operations  0.69 us (1%)
    all_gather x1, blocking collectives, local_packed(): lax.all_gather(xo, 'chan', axis_index_groups=lines)  15.7 us
    ppermute x9, starting transfers between devices, exchange(): return lax.ppermute(value, 'chan', [(i, i ^ flip) for i in range(count)])  8.8 us
    pallas_call x2, Pallas kernels, terms(): pl.pallas_call(kernel, out_shape=jax.ShapeDtypeStruct(shape, F32), in_spe...  7.31 us
    ppermute x9, waiting for transfers between devices, exchange(): return lax.ppermute(value, 'chan', [(i, i ^ flip) for i in range(count)])  5.79 us
    ppermute x2, starting transfers between devices, exchange_across(): return lax.ppermute(value, ('rows', 'chan'), pairs)  4.56 us
    ppermute x2, waiting for transfers between devices, exchange_across(): return lax.ppermute(value, ('rows', 'chan'), pairs)  3.08 us
    pallas_call x1, Pallas kernels, prep(): pl.pallas_call(prep_kernel, out_shape=(full, full, jax.ShapeDtypeStruct((...  2.36 us
    pallas_call x1, Pallas kernels, final(): pl.pallas_call(final_kernel, out_shape=(out, out), in_specs=[vmem] * 5, o...  1.91 us
  transfers between devices with their start and end apart: 11, of which 6 were waited for; matrix products, arithmetic and copies ran while one was open for 0% of the time, Pallas kernels for 8%

profile of v2, /device:TPU:0, one launch (start us, length us, event | category | flops | bytes accessed | tf_op | source)
XLA Modules:
  0.0 52.1 jit_solution(15171584702582607779)
XLA Ops:
  0.6 2.4 %prep.1 = (bf16[14,32,128]{2,1,0:T(8,128)(2,1)}, bf16[14,32,128]{2,1,0:T(8,128)(2,1)}, bf16[14,16,128]{2,1,0:T(8,128)(2,1)}) custom-call(s32[1,32]{1,0:T(1,128)} %order_hbm.1, bf16[49,32,32]{2,1,0:T(8,128)(2,1)} %bitcast.7, bf16[32,32,49]{2,1,0:T(8,128)(2,1)} %g_hbm.1), custom_call_target="tpu_custom_call" | custom-call | tf_op jit(solution)/shard_map/prep/pallas_call | solution.py:71
  3.0 3.0 %collective-permute-start = (bf16[14,16,128]{2,1,0:T(8,128)(2,1)}, bf16[14,16,128]{2,1,0:T(8,128)(2,1)S(1)}, u32[]{:S(2)}, u32[]{:S(2)}) collective-permute-start(bf16[14,16,128]{2,1,0:T(8,128)(2,1)} %get-tuple-element.13), channel_id=1, source_target_pairs={{0,16},{1,17},{2,18},{3,19},{4,20},{5,21},{6,22},{7,23},{8,24},{9,... | collective-permute-start | bytes 172040 | tf_op jit(solution)/shard_map/ppermute | solution.py:313
  6.0 2.4 %collective-permute-done.cross_ref = bf16[14,16,128]{2,1,0:T(8,128)(2,1)S(1)} collective-permute-done((bf16[14,16,128]{2,1,0:T(8,128)(2,1)}, bf16[14,16,128]{2,1,0:T(8,128)(2,1)S(1)}, u32[]{:S(2)}, u32[]{:S(2)}) %collective-permute-start) | collective-permute-done | bytes 57376 | tf_op jit(solution)/shard_map/ppermute | solution.py:313
  8.4 0.9 %copy-done = bf16[14,32,128]{2,1,0:T(8,128)(2,1)S(1)} copy-done((bf16[14,32,128]{2,1,0:T(8,128)(2,1)S(1)}, bf16[14,32,128]{2,1,0:T(8,128)(2,1)}, u32[]{:S(2)}) %copy-start) | copy-done | bytes 114712
  9.3 0.4 collective-permute-start.3
  9.7 1.8 %collective-permute-start.2 = (bf16[14,48,128]{2,1,0:T(8,128)(2,1)S(1)}, bf16[14,48,128]{2,1,0:T(8,128)(2,1)S(1)}, u32[]{:S(2)}, u32[]{:S(2)}) collective-permute-start(bf16[14,48,128]{2,1,0:T(8,128)(2,1)S(1)} %merge.1.refs_0_), channel_id=1, source_target_pairs={{0,2},{1,3},{2,0},{3,1},{4,6},{5,7},{6,4},{7,5},{8,10},{9,11},{10,... | collective-permute-start | bytes 516104 | tf_op jit(solution)/shard_map/ppermute | solution.py:308
  11.5 0.0 collective-permute-start.1
  11.5 15.7 %all-gather = bf16[56,32,128]{2,1,0:T(8,128)(2,1)S(1)} all-gather(bf16[14,32,128]{2,1,0:T(8,128)(2,1)S(1)} %copy-done.2), channel_id=2, replica_groups={{0,4,8,12},{1,5,9,13},{2,6,10,14},{3,7,11,15},{16,20,24,28},{17,21,25,2..., dimensions={0}, use_global_device_ids=true | all-gather | bytes 573440 | tf_op jit(solution)/shard_map/all_gather | solution.py:323
  27.2 0.4 unpack_x.1
  27.7 1.6 %collective-permute-start.4 = (bf16[49,16,128]{2,1,0:T(8,128)(2,1)S(1)}, bf16[49,16,128]{2,1,0:T(8,128)(2,1)S(1)}, u32[]{:S(2)}, u32[]{:S(2)}) collective-permute-start(bf16[49,16,128]{2,1,0:T(8,128)(2,1)S(1)} %get-tuple-element.15.xp), channel_id=1, source_target_pairs={{0,16},{1,17},{2,18},{3,19},{4,20},{5,21},{6,22},{7,23},{8,24},{9,... | collective-permute-start | bytes 602120 | tf_op jit(solution)/shard_map/ppermute | solution.py:313
  29.2 0.6 %unpack_g.1 = (bf16[49,32,128]{2,1,0:T(8,128)(2,1)S(1)}, bf16[49,16,128]{2,1,0:T(8,128)(2,1)S(1)}, bf16[49,16,128]{2,1,0:T(8,128)(2,1)S(1)}) custom-call(bf16[14,48,128]{2,1,0:T(8,128)(2,1)S(1)} %merge.1.refs_0_, bf16[14,48,128]{2,1,0:T(8,128)(2,1)S(1)} %collective-permute-done.1.refs_1_, bf16[14,48,128]{2,1,0:T(8,128)(2,1)S(1)} %collective-permute-done.2.refs_2_, ...), custom_call_target="tpu_custom_call" | custom-call | bytes 1048576 | tf_op jit(solution)/shard_map/unpack_g/pallas_call | solution.py:149
  29.8 3.0 %terms_own.1.own_ref = f32[32,128]{1,0:T(8,128)S(1)} custom-call(bf16[49,32,128]{2,1,0:T(8,128)(2,1)S(1)} %get-tuple-element.11.x, bf16[49,32,128]{2,1,0:T(8,128)(2,1)S(1)} %get-tuple-element.14.g, bf16[49,16,128]{2,1,0:T(8,128)(2,1)S(1)} %get-tuple-element.15.xp, bf16[49,16,128]{2,1,0:T(8,128)(2,1)S(1)} %get-tuple-element.17.gp), custom_call_target="tpu_custom_call" | custom-call | flops 1438646272 | bytes 8388608 | tf_op jit(solution)/shard_map/terms_own/pallas_call | solution.py:231
  32.8 0.7 %collective-permute-done.4.xp = bf16[49,16,128]{2,1,0:T(8,128)(2,1)S(1)} collective-permute-done((bf16[49,16,128]{2,1,0:T(8,128)(2,1)S(1)}, bf16[49,16,128]{2,1,0:T(8,128)(2,1)S(1)}, u32[]{:S(2)}, u32[]{:S(2)}) %collective-permute-start.4) | collective-permute-done | bytes 200736 | tf_op jit(solution)/shard_map/ppermute | solution.py:313
  33.5 4.3 %terms_cross.1 = f32[16,128]{1,0:T(8,128)S(1)} custom-call(bf16[49,32,128]{2,1,0:T(8,128)(2,1)S(1)} %get-tuple-element.11.x, bf16[49,32,128]{2,1,0:T(8,128)(2,1)S(1)} %get-tuple-element.14.g, bf16[49,16,128]{2,1,0:T(8,128)(2,1)S(1)} %collective-permute-done.4.xp, bf16[49,16,128]{2,1,0:T(8,128)(2,1)S(1)} %get-tuple-element.16.gp, f32[32,128]{1,0:T(8,128)S(1)} %terms_own.1.own_ref), custom_call_target="tpu_custom_call" | custom-call | flops 2157969408 | bytes 8388608 | tf_op jit(solution)/shard_map/terms_cross/pallas_call | solution.py:231
  37.9 0.1 collective-permute-start.7
  37.9 1.5 %collective-permute-start.6 = (f32[16,128]{1,0:T(8,128)S(1)}, f32[16,128]{1,0:T(8,128)S(1)}, u32[]{:S(2)}, u32[]{:S(2)}) collective-permute-start(f32[16,128]{1,0:T(8,128)S(1)} %terms_cross.1), channel_id=1, source_target_pairs={{0,2},{1,3},{2,0},{3,1},{4,6},{5,7},{6,4},{7,5},{8,10},{9,11},{10,... | collective-permute-start | bytes 24584 | tf_op jit(solution)/shard_map/ppermute | solution.py:308
  39.4 0.4 collective-permute-start.5
  39.8 1.3 %collective-permute-done.7 = f32[16,128]{1,0:T(8,128)S(1)} collective-permute-done((f32[16,128]{1,0:T(8,128)S(1)}, f32[16,128]{1,0:T(8,128)S(1)}, u32[]{:S(2)}, u32[]{:S(2)}) %collective-permute-start.7) | collective-permute-done | bytes 8224 | tf_op jit(solution)/shard_map/ppermute | solution.py:308
  41.0 0.6 %collective-permute-done.6 = f32[16,128]{1,0:T(8,128)S(1)} collective-permute-done((f32[16,128]{1,0:T(8,128)S(1)}, f32[16,128]{1,0:T(8,128)S(1)}, u32[]{:S(2)}, u32[]{:S(2)}) %collective-permute-start.6) | collective-permute-done | bytes 8224 | tf_op jit(solution)/shard_map/ppermute | solution.py:308
  41.7 4.0 %collective-permute-start.10 = (f32[16,128]{1,0:T(8,128)S(1)}, f32[16,128]{1,0:T(8,128)S(1)}, u32[]{:S(2)}, u32[]{:S(2)}) collective-permute-start(f32[16,128]{1,0:T(8,128)S(1)} %add_add_fusion.refs_0_), channel_id=1, source_target_pairs={{0,12},{1,13},{2,14},{3,15},{4,8},{5,9},{6,10},{7,11},{8,4},{9,5},... | collective-permute-start | bytes 24584 | tf_op jit(solution)/shard_map/ppermute | solution.py:308
  45.7 0.6 %collective-permute-start.8 = (f32[16,128]{1,0:T(8,128)S(1)}, f32[16,128]{1,0:T(8,128)S(1)}, u32[]{:S(2)}, u32[]{:S(2)}) collective-permute-start(f32[16,128]{1,0:T(8,128)S(1)} %add_add_fusion.refs_0_), channel_id=1, source_target_pairs={{0,4},{1,5},{2,6},{3,7},{4,0},{5,1},{6,2},{7,3},{8,12},{9,13},{10,... | collective-permute-start | bytes 24584 | tf_op jit(solution)/shard_map/ppermute | solution.py:308
  46.3 1.0 %collective-permute-done.10.refs_3_ = f32[16,128]{1,0:T(8,128)S(1)} collective-permute-done((f32[16,128]{1,0:T(8,128)S(1)}, f32[16,128]{1,0:T(8,128)S(1)}, u32[]{:S(2)}, u32[]{:S(2)}) %collective-permute-start.10) | collective-permute-done | bytes 8224 | tf_op jit(solution)/shard_map/ppermute | solution.py:308
  47.3 2.9 %collective-permute-done.9.refs_2_ = f32[16,128]{1,0:T(8,128)S(1)} collective-permute-done((f32[16,128]{1,0:T(8,128)S(1)}, f32[16,128]{1,0:T(8,128)S(1)}, u32[]{:S(2)}, u32[]{:S(2)}) %collective-permute-start.9) | collective-permute-done | bytes 8224 | tf_op jit(solution)/shard_map/ppermute | solution.py:308
  50.2 1.9 %solve.1 = (f32[32,32]{1,0:T(8,128)}, f32[32,32]{1,0:T(8,128)}) custom-call(f32[16,128]{1,0:T(8,128)S(1)} %add_add_fusion.refs_0_, f32[16,128]{1,0:T(8,128)S(1)} %collective-permute-done.8.refs_1_, f32[16,128]{1,0:T(8,128)S(1)} %collective-permute-done.9.refs_2_, f32[16,128]{1,0:T(8,128)S(1)} %collective-permute-done.10.refs_3_, f32[1,32]{1,0:T(1,128)S(1)} %bitcast.6), custom_call_target="tpu_custom_call" | custom-call | tf_op jit(solution)/shard_map/solve/pallas_call | solution.py:297
  (13 shorter events, 0.0 us)
Async XLA Ops:
  3.0 5.4 %collective-permute-start = (bf16[14,16,128]{2,1,0:T(8,128)(2,1)}, bf16[14,16,128]{2,1,0:T(8,128)(2,1)S(1)}, u32[]{:S(2)}, u32[]{:S(2)}) collective-permute-start(bf16[14,16,128]{2,1,0:T(8,128)(2,1)} %get-tuple-element.13), channel_id=1, source_target_pairs={{0,16},{1,17},{2,18},{3,19},{4,20},{5,21},{6,22},{7,23},{8,24},{9,... | collective-permute-start | bytes 172040 | tf_op jit(solution)/shard_map/ppermute | solution.py:313
  8.4 0.9 %copy-start = (bf16[14,32,128]{2,1,0:T(8,128)(2,1)S(1)}, bf16[14,32,128]{2,1,0:T(8,128)(2,1)}, u32[]{:S(2)}) copy-start(bf16[14,32,128]{2,1,0:T(8,128)(2,1)} %get-tuple-element.12.own_ref) | copy-start | bytes 344068
  9.3 2.3 %copy-start.2 = (bf16[14,32,128]{2,1,0:T(8,128)(2,1)S(1)}, bf16[14,32,128]{2,1,0:T(8,128)(2,1)}, u32[]{:S(2)}) copy-start(bf16[14,32,128]{2,1,0:T(8,128)(2,1)} %get-tuple-element.10) | copy-start | bytes 344068
  9.3 20.0 %collective-permute-start.3 = (bf16[14,48,128]{2,1,0:T(8,128)(2,1)S(1)}, bf16[14,48,128]{2,1,0:T(8,128)(2,1)S(1)}, u32[]{:S(2)}, u32[]{:S(2)}) collective-permute-start(bf16[14,48,128]{2,1,0:T(8,128)(2,1)S(1)} %merge.1.refs_0_), channel_id=1, source_target_pairs={{0,3},{1,2},{2,1},{3,0},{4,7},{5,6},{6,5},{7,4},{8,11},{9,10},{10,... | collective-permute-start | bytes 516104 | tf_op jit(solution)/shard_map/ppermute | solution.py:308
  9.7 19.6 %collective-permute-start.2 = (bf16[14,48,128]{2,1,0:T(8,128)(2,1)S(1)}, bf16[14,48,128]{2,1,0:T(8,128)(2,1)S(1)}, u32[]{:S(2)}, u32[]{:S(2)}) collective-permute-start(bf16[14,48,128]{2,1,0:T(8,128)(2,1)S(1)} %merge.1.refs_0_), channel_id=1, source_target_pairs={{0,2},{1,3},{2,0},{3,1},{4,6},{5,7},{6,4},{7,5},{8,10},{9,11},{10,... | collective-permute-start | bytes 516104 | tf_op jit(solution)/shard_map/ppermute | solution.py:308
  11.5 17.8 %collective-permute-start.1 = (bf16[14,48,128]{2,1,0:T(8,128)(2,1)S(1)}, bf16[14,48,128]{2,1,0:T(8,128)(2,1)S(1)}, u32[]{:S(2)}, u32[]{:S(2)}) collective-permute-start(bf16[14,48,128]{2,1,0:T(8,128)(2,1)S(1)} %merge.1.refs_0_), channel_id=1, source_target_pairs={{0,1},{1,0},{2,3},{3,2},{4,5},{5,4},{6,7},{7,6},{8,9},{9,8},{10,11... | collective-permute-start | bytes 516104 | tf_op jit(solution)/shard_map/ppermute | solution.py:308
  27.7 5.9 %collective-permute-start.4 = (bf16[49,16,128]{2,1,0:T(8,128)(2,1)S(1)}, bf16[49,16,128]{2,1,0:T(8,128)(2,1)S(1)}, u32[]{:S(2)}, u32[]{:S(2)}) collective-permute-start(bf16[49,16,128]{2,1,0:T(8,128)(2,1)S(1)} %get-tuple-element.15.xp), channel_id=1, source_target_pairs={{0,16},{1,17},{2,18},{3,19},{4,20},{5,21},{6,22},{7,23},{8,24},{9,... | collective-permute-start | bytes 602120 | tf_op jit(solution)/shard_map/ppermute | solution.py:313
  37.9 3.2 %collective-permute-start.7 = (f32[16,128]{1,0:T(8,128)S(1)}, f32[16,128]{1,0:T(8,128)S(1)}, u32[]{:S(2)}, u32[]{:S(2)}) collective-permute-start(f32[16,128]{1,0:T(8,128)S(1)} %terms_cross.1), channel_id=1, source_target_pairs={{0,3},{1,2},{2,1},{3,0},{4,7},{5,6},{6,5},{7,4},{8,11},{9,10},{10,... | collective-permute-start | bytes 24584 | tf_op jit(solution)/shard_map/ppermute | solution.py:308
  37.9 3.7 %collective-permute-start.6 = (f32[16,128]{1,0:T(8,128)S(1)}, f32[16,128]{1,0:T(8,128)S(1)}, u32[]{:S(2)}, u32[]{:S(2)}) collective-permute-start(f32[16,128]{1,0:T(8,128)S(1)} %terms_cross.1), channel_id=1, source_target_pairs={{0,2},{1,3},{2,0},{3,1},{4,6},{5,7},{6,4},{7,5},{8,10},{9,11},{10,... | collective-permute-start | bytes 24584 | tf_op jit(solution)/shard_map/ppermute | solution.py:308
  39.4 2.3 %collective-permute-start.5 = (f32[16,128]{1,0:T(8,128)S(1)}, f32[16,128]{1,0:T(8,128)S(1)}, u32[]{:S(2)}, u32[]{:S(2)}) collective-permute-start(f32[16,128]{1,0:T(8,128)S(1)} %terms_cross.1), channel_id=1, source_target_pairs={{0,1},{1,0},{2,3},{3,2},{4,5},{5,4},{6,7},{7,6},{8,9},{9,8},{10,11... | collective-permute-start | bytes 24584 | tf_op jit(solution)/shard_map/ppermute | solution.py:308
  41.6 8.6 %copy-start.1 = (f32[32]{0:T(128)S(1)}, f32[32]{0:T(128)}, u32[]{:S(2)}) copy-start(f32[32]{0:T(128)} %param.7) | copy-start | bytes 388
  41.7 5.7 %collective-permute-start.10 = (f32[16,128]{1,0:T(8,128)S(1)}, f32[16,128]{1,0:T(8,128)S(1)}, u32[]{:S(2)}, u32[]{:S(2)}) collective-permute-start(f32[16,128]{1,0:T(8,128)S(1)} %add_add_fusion.refs_0_), channel_id=1, source_target_pairs={{0,12},{1,13},{2,14},{3,15},{4,8},{5,9},{6,10},{7,11},{8,4},{9,5},... | collective-permute-start | bytes 24584 | tf_op jit(solution)/shard_map/ppermute | solution.py:308
  45.7 4.5 %collective-permute-start.9 = (f32[16,128]{1,0:T(8,128)S(1)}, f32[16,128]{1,0:T(8,128)S(1)}, u32[]{:S(2)}, u32[]{:S(2)}) collective-permute-start(f32[16,128]{1,0:T(8,128)S(1)} %add_add_fusion.refs_0_), channel_id=1, source_target_pairs={{0,8},{1,9},{2,10},{3,11},{4,12},{5,13},{6,14},{7,15},{8,0},{9,1},... | collective-permute-start | bytes 24584 | tf_op jit(solution)/shard_map/ppermute | solution.py:308
  45.7 4.5 %collective-permute-start.8 = (f32[16,128]{1,0:T(8,128)S(1)}, f32[16,128]{1,0:T(8,128)S(1)}, u32[]{:S(2)}, u32[]{:S(2)}) collective-permute-start(f32[16,128]{1,0:T(8,128)S(1)} %add_add_fusion.refs_0_), channel_id=1, source_target_pairs={{0,4},{1,5},{2,6},{3,7},{4,0},{5,1},{6,2},{7,3},{8,12},{9,13},{10,... | collective-permute-start | bytes 24584 | tf_op jit(solution)/shard_map/ppermute | solution.py:308

commit v3 on v2

--- a/solution.py
+++ b/solution.py
@@ -27,8 +27,9 @@
 
 
 def prep_kernel(order_hbm, x_hbm, g_hbm, xo_ref, go_ref, gp_ref, order_ref, x_ref, g_ref, sems, gs, gt, gout):
-    for copy in fetch((order_hbm, x_hbm, g_hbm), (order_ref, x_ref, g_ref), sems):
-        copy.wait()
+    copies = fetch((order_hbm, g_hbm, x_hbm), (order_ref, g_ref, x_ref), sems)
+    copies[0].wait()
+    copies[1].wait()
     row_id = lax.broadcasted_iota(jnp.int32, (EX, EX), 0)
     col_id = lax.broadcasted_iota(jnp.int32, (EX, EX), 1)
     onehot = jnp.zeros((EX, EX), F32)
@@ -36,15 +37,6 @@
         example = order_ref[0, k]
         onehot = jnp.where((row_id == k) & (col_id == example), 1.0, onehot)
         gs[k * CH:(k + 1) * CH, 0:SIDE * SIDE] = g_ref[example].astype(F32)
-    onehot = onehot.astype(BF16)
-    zero_block = jnp.zeros((EX, CH), BF16)
-    for group in range(GROUPS4):
-        pieces = []
-        for j in range(4):
-            py, px = group // 2, (group % 2) * 4 + j
-            pieces.append(x_ref[py * SIDE + px] if px < SIDE else zero_block)
-        packed = jnp.concatenate(pieces, axis=1)
-        xo_ref[group] = jnp.dot(onehot, packed, preferred_element_type=F32).astype(BF16)
     block_id = lax.broadcasted_iota(jnp.int32, (GROUPS4, LANES), 1) // CH
     for quad in range(EX // 4):
         flipped = jnp.transpose(gs[quad * LANES:(quad + 1) * LANES, :])
@@ -63,6 +55,16 @@
         ordered = gout[group * EX:(group + 1) * EX, :].astype(BF16)
         go_ref[group] = ordered
         gp_ref[group] = ordered[:PIV_DEV]
+    copies[2].wait()
+    onehot = onehot.astype(BF16)
+    zero_block = jnp.zeros((EX, CH), BF16)
+    for group in range(GROUPS4):
+        pieces = []
+        for j in range(4):
+            py, px = group // 2, (group % 2) * 4 + j
+            pieces.append(x_ref[py * SIDE + px] if px < SIDE else zero_block)
+        packed = jnp.concatenate(pieces, axis=1)
+        xo_ref[group] = jnp.dot(onehot, packed, preferred_element_type=F32).astype(BF16)
 
 
 def prep(order, x, g):
@@ -71,7 +73,7 @@
     return pl.pallas_call(
         prep_kernel,
         out_shape=(full, full, jax.ShapeDtypeStruct((GROUPS4, PIV_DEV, LANES), BF16)),
-        in_specs=[pl.BlockSpec(memory_space=pl.ANY)] * 3,
+        in_specs=[pl.BlockSpec(memory_space=pltpu.HBM)] * 3,
         out_specs=(vmem,) * 3,
         scratch_shapes=[
             pltpu.SMEM(order.shape, order.dtype),
@@ -82,7 +84,7 @@
             pltpu.VMEM((SIDE * PITCH, LANES), F32),
             pltpu.VMEM((GROUPS4 * EX, LANES), F32),
         ],
-        compiler_params=pltpu.CompilerParams(vmem_limit_bytes=56 << 20),
+        compiler_params=pltpu.CompilerParams(vmem_limit_bytes=54848 << 10),
         name="prep",
     )(order, x, g)
 
@@ -113,7 +115,8 @@
     )(own, cross)
 
 
-def unpack_body(packed, all_ref, piv_refs):
+def unpack_kernel(*refs):
+    packed, all_ref, piv_refs = refs[:4], refs[4], refs[5:]
     examples = packed[0].shape[1]
     row = lax.broadcasted_iota(jnp.int32, (4 * LANES, 4 * LANES), 0)
     col = lax.broadcasted_iota(jnp.int32, (4 * LANES, 4 * LANES), 1)
@@ -133,23 +136,14 @@
                 piv_refs[1][py * SIDE + px] = spot[EX:]
 
 
-def unpack_kernel(*refs):
-    unpack_body(refs[:4], refs[4], refs[5:])
-
-
-def unpack_gathered_kernel(gathered, all_ref, piv_ref):
-    unpack_body([gathered.at[i] for i in range(4)], all_ref, (piv_ref,))
-
-
 def unpack(arrays, name):
     vmem = pl.BlockSpec(memory_space=pltpu.VMEM)
     pivots = jax.ShapeDtypeStruct((SPOTS, PIV_DEV, LANES), BF16)
-    pivot_sets = arrays[0].shape[-2] // PIV_DEV - 1
-    gathered = len(arrays) == 1
-    return pl.pallas_call(
-        unpack_gathered_kernel if gathered else unpack_kernel,
+    pivot_sets = arrays[0].shape[1] // PIV_DEV - 1
+    return pl.pallas_call(
+        unpack_kernel,
         out_shape=(jax.ShapeDtypeStruct((SPOTS, EX, LANES), BF16),) + (pivots,) * pivot_sets,
-        in_specs=[vmem] * len(arrays),
+        in_specs=[vmem] * 4,
         out_specs=(vmem,) * (1 + pivot_sets),
         compiler_params=pltpu.CompilerParams(vmem_limit_bytes=12 << 20),
         cost_estimate=cost(0, 1 << 20),
@@ -214,15 +208,14 @@
 
 
 def cross_kernel(x, g, xp, gp, own_ref, out_ref, *work):
-    across = panel_terms([x, xp], [g, gp], xp, gp, *work)
+    across = panel_terms([x], [g], xp, gp, *work)
     lane = lax.broadcasted_iota(jnp.int32, (8, LANES), 1)
     is_own = (lane // PIV_DEV) % 2 == lax.axis_index("rows")
     packed = jnp.zeros((8, LANES), F32)
     for j in range(4):
         rows = slice(8 * j, 8 * j + 8)
         packed = jnp.where(lane // EX == j, jnp.where(is_own, own_ref[rows, :], across[rows]), packed)
-    out_ref[0:8, :] = packed
-    out_ref[8:16, :] = jnp.where(lane // PIV_DEV == 0, across[EX:EX + 8], across[EX + 8:EX + PIV_DEV])
+    out_ref[...] = packed
 
 
 def terms(kernel, arrays, height, shape, name):
@@ -252,21 +245,20 @@
     )
 
 
-def final_kernel(*refs):
-    total_refs, (ridge_ref, gram_ref, factor_ref) = refs[:4], refs[4:]
-    total = (total_refs[0][...] + total_refs[1][...]) + (total_refs[2][...] + total_refs[3][...])
-    panel = rows_of(total[:8], 4)
+def tree_sum(values):
+    while len(values) > 1:
+        values = [a + b for a, b in zip(values[0::2], values[1::2])]
+    return values[0]
+
+
+def final_kernel(terms_ref, ridge_ref, gram_ref, factor_ref):
+    count = terms_ref.shape[0] // 2
+    sums = [tree_sum([terms_ref[g * count + i] for i in range(count)]) for g in range(2)]
+    panel = rows_of(jnp.where(lax.axis_index("rows") == 0, sums[0], sums[1]), 4)
     gram_ref[...] = panel
-    group = lax.axis_index("rows")
-    mine, zero = panel[:PIV_DEV], jnp.zeros((PIV_DEV, EX), F32)
-    upper = jnp.concatenate([jnp.where(group == 0, mine, zero), jnp.where(group == 0, zero, mine)], axis=0)
-    block = jnp.concatenate([total[8:, :PIV_DEV], total[8:, PIV_DEV:2 * PIV_DEV]], axis=0)
-    block = jnp.concatenate([block, block], axis=1)
-    block = jnp.concatenate([block, block], axis=0)
+    diag = jnp.concatenate([rows_of(total, 2) for total in sums], axis=0)
     row_id = lax.broadcasted_iota(jnp.int32, (EX, EX), 0)
     col_id = lax.broadcasted_iota(jnp.int32, (EX, EX), 1)
-    diag = jnp.where(col_id // PIV_DEV == group, jnp.transpose(upper), block)
-    diag = jnp.where(row_id // PIV_DEV == group, upper, diag)
     ridge = jnp.where(row_id == col_id, jnp.broadcast_to(ridge_ref[...], (EX, EX)), 0.0)
     system = 0.5 * (diag + jnp.transpose(diag)) + ridge
     factor = jnp.zeros((EX, EX), F32)
@@ -291,21 +283,26 @@
     factor_ref[...] = factor
 
 
-def final(totals, ridge):
+def final(terms_of_all, ridge):
     vmem = pl.BlockSpec(memory_space=pltpu.VMEM)
     out = jax.ShapeDtypeStruct((EX, EX), F32)
     return pl.pallas_call(
         final_kernel,
         out_shape=(out, out),
-        in_specs=[vmem] * 5,
+        in_specs=[vmem] * 2,
         out_specs=(vmem, vmem),
         compiler_params=pltpu.CompilerParams(vmem_limit_bytes=8 << 20),
         name="solve",
-    )(*totals, ridge.reshape(1, EX))
+    )(terms_of_all, ridge.reshape(1, EX))
 
 
 def exchange(value, count, flip):
     return lax.ppermute(value, "chan", [(i, i ^ flip) for i in range(count)])
+
+
+def gather(value, count, first, second):
+    received = exchange(value, count, first)
+    return [value, exchange(value, count, second), received, exchange(received, count, second)]
 
 
 def exchange_across(value, count):
@@ -314,21 +311,16 @@
 
 
 def local_packed(count, activations, cotangents, ordering, ridge):
-    near, far = (1, 2, 3), (4, 8, 12)
     x = jnp.transpose(activations, (1, 2, 0, 3)).reshape(SIDE * SIDE, EX, CH)
     xo, go, gp = prep(ordering, x, cotangents)
     gm = merge(go, exchange_across(gp, count))
-    own_g = [gm] + [exchange(gm, count, f) for f in near]
-    lines = [[4 * i + k for i in range(count // 4)] for k in range(4)]
-    x_all, x_piv = unpack([lax.all_gather(xo, "chan", axis_index_groups=lines)], "unpack_x")
+    x_all, x_piv = unpack(gather(xo, count, 8, 4), "unpack_x")
     x_cross = exchange_across(x_piv, count)
-    g_all, g_piv, g_cross = unpack(own_g, "unpack_g")
+    g_all, g_piv, g_cross = unpack([gm] + [exchange(gm, count, f) for f in (1, 2, 3)], "unpack_g")
     own_term = terms(own_kernel, (x_all, g_all, x_piv, g_piv), EX, (EX, LANES), "terms_own")
-    arrays = (x_all, g_all, x_cross, g_cross, own_term)
-    term = terms(cross_kernel, arrays, EX + PIV_DEV, (16, LANES), "terms_cross")
-    terms_near = [term] + [exchange(term, count, f) for f in near]
-    part = (terms_near[0] + terms_near[1]) + (terms_near[2] + terms_near[3])
-    return final([part] + [exchange(part, count, f) for f in far], ridge)
+    term = terms(cross_kernel, (x_all, g_all, x_cross, g_cross, own_term), EX, (8, LANES), "terms_cross")
+    copies = jnp.broadcast_to(term, (2 * count, 8, LANES))
+    return final(lax.all_to_all(copies, ("rows", "chan"), 0, 0), ridge)
 
 
 def jacobian_block(grad_rows, input_rows):

time: 52.3 us -> 46.6 us (0.89)
  blocking collectives: 15.7 us -> 13.6 us
  starting transfers between devices: 13.4 us -> 11.4 us
  Pallas kernels: 12.6 us -> 10.7 us
    all_gather x1 -> x0, blocking collectives: 15.7 us -> none  [local_packed(): lax.all_gather(xo, 'chan', axis_index_groups=lines)]
    all_to_all x0 -> x1, blocking collectives: none -> 13.6 us  [local_packed(): return final(lax.all_to_all(copies, ('rows', 'chan'), 0, 0), ridge)]
    ppermute x2, waiting for transfers between devices: 3.08 us -> 0.01 us  [exchange_across(): return lax.ppermute(value, ('rows', 'chan'), pairs)]
    ppermute x9 -> x6, waiting for transfers between devices: 5.79 us -> 8.75 us  [exchange(): return lax.ppermute(value, 'chan', [(i, i ^ flip) for i in range(count)])]
    ppermute x2, starting transfers between devices: 4.56 us -> 3.09 us  [exchange_across(): return lax.ppermute(value, ('rows', 'chan'), pairs)]
    pallas_call x2, Pallas kernels: 7.31 us -> 6.07 us  [terms(): pl.pallas_call(kernel, out_shape=jax.ShapeDtypeStruct(shape, F32), in_spe...]
    pallas_call x1, Pallas kernels: 2.36 us -> 1.76 us  [prep(): pl.pallas_call(prep_kernel, out_shape=(full, full, jax.ShapeDtypeStruct((...]
    ppermute x9 -> x6, starting transfers between devices: 8.8 us -> 8.28 us  [exchange(): return lax.ppermute(value, 'chan', [(i, i ^ flip) for i in range(count)])]
  transfers between devices with their start and end apart: 11 -> 8, of which waited for: 6 -> 4; matrix products, arithmetic and copies ran while one was open for 0% -> 0% of each run, Pallas kernels for 8% -> 9%
where the time goes in v3:
time: 46.6 us; the launch traced here: 46.5 us
  blocking collectives  13.6 us (29%)
  starting transfers between devices  11.4 us (24%)
  Pallas kernels  10.7 us (23%)
  waiting for transfers between devices  8.75 us (19%)
  local copies, waits for them, and re-layouts  1.32 us (3%)
  between operations  0.69 us (1%)
    all_to_all x1, blocking collectives, local_packed(): return final(lax.all_to_all(copies, ('rows', 'chan'), 0, 0), ridge)  13.6 us
    ppermute x6, waiting for transfers between devices, exchange(): return lax.ppermute(value, 'chan', [(i, i ^ flip) for i in range(count)])  8.75 us
    ppermute x6, starting transfers between devices, exchange(): return lax.ppermute(value, 'chan', [(i, i ^ flip) for i in range(count)])  8.28 us
    pallas_call x2, Pallas kernels, terms(): pl.pallas_call(kernel, out_shape=jax.ShapeDtypeStruct(shape, F32), in_spe...  6.07 us
    ppermute x2, starting transfers between devices, exchange_across(): return lax.ppermute(value, ('rows', 'chan'), pairs)  3.09 us
    pallas_call x1, Pallas kernels, final(): pl.pallas_call(final_kernel, out_shape=(out, out), in_specs=[vmem] * 2, o...  1.85 us
    pallas_call x1, Pallas kernels, prep(): pl.pallas_call(prep_kernel, out_shape=(full, full, jax.ShapeDtypeStruct((...  1.76 us
    unnamed x4, local copies, waits for them, and re-layouts  1.3 us
  transfers between devices with their start and end apart: 8, of which 4 were waited for; matrix products, arithmetic and copies ran while one was open for 0% of the time, Pallas kernels for 9%

profile of v3, /device:TPU:0, one launch (start us, length us, event | category | flops | bytes accessed | tf_op | source)
XLA Modules:
  0.0 46.5 jit_solution(8602596175765527648)
XLA Ops:
  0.6 0.6 %copy-done = s32[1,32]{1,0:T(1,128)S(1)} copy-done((s32[1,32]{1,0:T(1,128)S(1)}, s32[1,32]{1,0:T(1,128)}, u32[]{:S(2)}) %copy-start) | copy-done | bytes 152
  1.3 1.8 %prep.1 = (bf16[14,32,128]{2,1,0:T(8,128)(2,1)S(1)}, bf16[14,32,128]{2,1,0:T(8,128)(2,1)S(1)}, bf16[14,16,128]{2,1,0:T(8,128)(2,1)S(1)}) custom-call(s32[1,32]{1,0:T(1,128)S(1)} %copy-done, bf16[49,32,32]{2,1,0:T(8,128)(2,1)} %bitcast.5, bf16[32,32,49]{2,1,0:T(8,128)(2,1)} %g_hbm.1), custom_call_target="tpu_custom_call" | custom-call | tf_op jit(solution)/shard_map/prep/pallas_call | solution.py:73
  3.1 4.1 %collective-permute-start.1 = (bf16[14,32,128]{2,1,0:T(8,128)(2,1)S(1)}, bf16[14,32,128]{2,1,0:T(8,128)(2,1)S(1)}, u32[]{:S(2)}, u32[]{:S(2)}) collective-permute-start(bf16[14,32,128]{2,1,0:T(8,128)(2,1)S(1)} %get-tuple-element.10.refs_0_), channel_id=1, source_target_pairs={{0,8},{1,9},{2,10},{3,11},{4,12},{5,13},{6,14},{7,15},{8,0},{9,1},... | collective-permute-start | bytes 344072 | tf_op jit(solution)/shard_map/ppermute | solution.py:300
  7.2 1.5 %collective-permute-start.3 = (bf16[14,16,128]{2,1,0:T(8,128)(2,1)S(1)}, bf16[14,16,128]{2,1,0:T(8,128)(2,1)S(1)}, u32[]{:S(2)}, u32[]{:S(2)}) collective-permute-start(bf16[14,16,128]{2,1,0:T(8,128)(2,1)S(1)} %get-tuple-element.13), channel_id=1, source_target_pairs={{0,16},{1,17},{2,18},{3,19},{4,20},{5,21},{6,22},{7,23},{8,24},{9,... | collective-permute-start | bytes 172040 | tf_op jit(solution)/shard_map/ppermute | solution.py:310
  8.6 1.6 %collective-permute-start = (bf16[14,32,128]{2,1,0:T(8,128)(2,1)S(1)}, bf16[14,32,128]{2,1,0:T(8,128)(2,1)S(1)}, u32[]{:S(2)}, u32[]{:S(2)}) collective-permute-start(bf16[14,32,128]{2,1,0:T(8,128)(2,1)S(1)} %get-tuple-element.10.refs_0_), channel_id=1, source_target_pairs={{0,4},{1,5},{2,6},{3,7},{4,0},{5,1},{6,2},{7,3},{8,12},{9,13},{10,... | collective-permute-start | bytes 344072 | tf_op jit(solution)/shard_map/ppermute | solution.py:300
  10.2 2.6 %collective-permute-done.1.refs_2_ = bf16[14,32,128]{2,1,0:T(8,128)(2,1)S(1)} collective-permute-done((bf16[14,32,128]{2,1,0:T(8,128)(2,1)S(1)}, bf16[14,32,128]{2,1,0:T(8,128)(2,1)S(1)}, u32[]{:S(2)}, u32[]{:S(2)}) %collective-permute-start.1) | collective-permute-done | bytes 114720 | tf_op jit(solution)/shard_map/ppermute | solution.py:300
  12.9 0.7 %collective-permute-start.2 = (bf16[14,32,128]{2,1,0:T(8,128)(2,1)S(1)}, bf16[14,32,128]{2,1,0:T(8,128)(2,1)S(1)}, u32[]{:S(2)}, u32[]{:S(2)}) collective-permute-start(bf16[14,32,128]{2,1,0:T(8,128)(2,1)S(1)} %collective-permute-done.1.refs_2_), channel_id=1, source_target_pairs={{0,4},{1,5},{2,6},{3,7},{4,0},{5,1},{6,2},{7,3},{8,12},{9,13},{10,... | collective-permute-start | bytes 344072 | tf_op jit(solution)/shard_map/ppermute | solution.py:300
  13.5 0.0 collective-permute-done.3.cross_ref
  13.6 0.1 collective-permute-start.4
  13.6 1.6 %collective-permute-start.5 = (bf16[14,48,128]{2,1,0:T(8,128)(2,1)S(1)}, bf16[14,48,128]{2,1,0:T(8,128)(2,1)S(1)}, u32[]{:S(2)}, u32[]{:S(2)}) collective-permute-start(bf16[14,48,128]{2,1,0:T(8,128)(2,1)S(1)} %merge.1.refs_0_), channel_id=1, source_target_pairs={{0,2},{1,3},{2,0},{3,1},{4,6},{5,7},{6,4},{7,5},{8,10},{9,11},{10,... | collective-permute-start | bytes 516104 | tf_op jit(solution)/shard_map/ppermute | solution.py:300
  15.2 0.3 collective-permute-start.6
  15.5 0.0 collective-permute-done.refs_1_
  15.5 2.2 %collective-permute-done.2.refs_3_ = bf16[14,32,128]{2,1,0:T(8,128)(2,1)S(1)} collective-permute-done((bf16[14,32,128]{2,1,0:T(8,128)(2,1)S(1)}, bf16[14,32,128]{2,1,0:T(8,128)(2,1)S(1)}, u32[]{:S(2)}, u32[]{:S(2)}) %collective-permute-start.2) | collective-permute-done | bytes 114720 | tf_op jit(solution)/shard_map/ppermute | solution.py:300
  17.7 0.4 unpack_x.1
  18.1 1.6 %collective-permute-start.7 = (bf16[49,16,128]{2,1,0:T(8,128)(2,1)S(1)}, bf16[49,16,128]{2,1,0:T(8,128)(2,1)S(1)}, u32[]{:S(2)}, u32[]{:S(2)}) collective-permute-start(bf16[49,16,128]{2,1,0:T(8,128)(2,1)S(1)} %get-tuple-element.15.xp), channel_id=1, source_target_pairs={{0,16},{1,17},{2,18},{3,19},{4,20},{5,21},{6,22},{7,23},{8,24},{9,... | collective-permute-start | bytes 602120 | tf_op jit(solution)/shard_map/ppermute | solution.py:310
  19.7 0.0 collective-permute-done.4.refs_1_
  19.7 1.2 %collective-permute-done.5.refs_2_ = bf16[14,48,128]{2,1,0:T(8,128)(2,1)S(1)} collective-permute-done((bf16[14,48,128]{2,1,0:T(8,128)(2,1)S(1)}, bf16[14,48,128]{2,1,0:T(8,128)(2,1)S(1)}, u32[]{:S(2)}, u32[]{:S(2)}) %collective-permute-start.5) | collective-permute-done | bytes 172064 | tf_op jit(solution)/shard_map/ppermute | solution.py:300
  20.9 2.8 %collective-permute-done.6.refs_3_ = bf16[14,48,128]{2,1,0:T(8,128)(2,1)S(1)} collective-permute-done((bf16[14,48,128]{2,1,0:T(8,128)(2,1)S(1)}, bf16[14,48,128]{2,1,0:T(8,128)(2,1)S(1)}, u32[]{:S(2)}, u32[]{:S(2)}) %collective-permute-start.6) | collective-permute-done | bytes 172064 | tf_op jit(solution)/shard_map/ppermute | solution.py:300
  23.7 0.6 %unpack_g.1 = (bf16[49,32,128]{2,1,0:T(8,128)(2,1)S(1)}, bf16[49,16,128]{2,1,0:T(8,128)(2,1)S(1)}, bf16[49,16,128]{2,1,0:T(8,128)(2,1)S(1)}) custom-call(bf16[14,48,128]{2,1,0:T(8,128)(2,1)S(1)} %merge.1.refs_0_, bf16[14,48,128]{2,1,0:T(8,128)(2,1)S(1)} %collective-permute-done.4.refs_1_, bf16[14,48,128]{2,1,0:T(8,128)(2,1)S(1)} %collective-permute-done.5.refs_2_, ...), custom_call_target="tpu_custom_call" | custom-call | bytes 1048576 | tf_op jit(solution)/shard_map/unpack_g/pallas_call | solution.py:143
  24.2 3.0 %terms_own.1.own_ref = f32[32,128]{1,0:T(8,128)S(1)} custom-call(bf16[49,32,128]{2,1,0:T(8,128)(2,1)S(1)} %get-tuple-element.11.x, bf16[49,32,128]{2,1,0:T(8,128)(2,1)S(1)} %get-tuple-element.14.g, bf16[49,16,128]{2,1,0:T(8,128)(2,1)S(1)} %get-tuple-element.15.xp, bf16[49,16,128]{2,1,0:T(8,128)(2,1)S(1)} %get-tuple-element.17.gp), custom_call_target="tpu_custom_call" | custom-call | flops 1438646272 | bytes 8388608 | tf_op jit(solution)/shard_map/terms_own/pallas_call | solution.py:224
  27.3 3.0 %terms_cross.1 = f32[8,128]{1,0:T(8,128)S(1)} custom-call(bf16[49,32,128]{2,1,0:T(8,128)(2,1)S(1)} %get-tuple-element.11.x, bf16[49,32,128]{2,1,0:T(8,128)(2,1)S(1)} %get-tuple-element.14.g, bf16[49,16,128]{2,1,0:T(8,128)(2,1)S(1)} %collective-permute-done.7.xp, bf16[49,16,128]{2,1,0:T(8,128)(2,1)S(1)} %get-tuple-element.16.gp, f32[32,128]{1,0:T(8,128)S(1)} %terms_own.1.own_ref), custom_call_target="tpu_custom_call" | custom-call | flops 1438646272 | bytes 8388608 | tf_op jit(solution)/shard_map/terms_cross/pallas_call | solution.py:224
  30.3 13.6 %all_to_all.5.terms_ref = f32[32,8,128]{2,1,0:T(8,128)S(1)} all-to-all(f32[32,8,128]{2,1,0:T(8,128)S(1)} %broadcast_in_dim.3), channel_id=1, replica_groups=mesh['rows'=2,'chan'=16] {'rows','chan'}, dimensions={0} | all-to-all | bytes 262144 | tf_op jit(solution)/shard_map/all_to_all | solution.py:323
  44.0 0.7 %copy-done.1 = f32[32]{0:T(128)S(1)} copy-done((f32[32]{0:T(128)S(1)}, f32[32]{0:T(128)}, u32[]{:S(2)}) %copy-start.1) | copy-done | bytes 152
  44.6 1.8 %solve.1 = (f32[32,32]{1,0:T(8,128)}, f32[32,32]{1,0:T(8,128)}) custom-call(f32[32,8,128]{2,1,0:T(8,128)S(1)} %all_to_all.5.terms_ref, f32[1,32]{1,0:T(1,128)S(1)} %bitcast.4), custom_call_target="tpu_custom_call" | custom-call | tf_op jit(solution)/shard_map/solve/pallas_call | solution.py:289
  (5 shorter events, 0.0 us)
Async XLA Ops:
  0.6 0.7 %copy-start = (s32[1,32]{1,0:T(1,128)S(1)}, s32[1,32]{1,0:T(1,128)}, u32[]{:S(2)}) copy-start(s32[1,32]{1,0:T(1,128)} %order_hbm.1) | copy-start | bytes 388
  3.1 9.8 %collective-permute-start.1 = (bf16[14,32,128]{2,1,0:T(8,128)(2,1)S(1)}, bf16[14,32,128]{2,1,0:T(8,128)(2,1)S(1)}, u32[]{:S(2)}, u32[]{:S(2)}) collective-permute-start(bf16[14,32,128]{2,1,0:T(8,128)(2,1)S(1)} %get-tuple-element.10.refs_0_), channel_id=1, source_target_pairs={{0,8},{1,9},{2,10},{3,11},{4,12},{5,13},{6,14},{7,15},{8,0},{9,1},... | collective-permute-start | bytes 344072 | tf_op jit(solution)/shard_map/ppermute | solution.py:300
  7.2 6.4 %collective-permute-start.3 = (bf16[14,16,128]{2,1,0:T(8,128)(2,1)S(1)}, bf16[14,16,128]{2,1,0:T(8,128)(2,1)S(1)}, u32[]{:S(2)}, u32[]{:S(2)}) collective-permute-start(bf16[14,16,128]{2,1,0:T(8,128)(2,1)S(1)} %get-tuple-element.13), channel_id=1, source_target_pairs={{0,16},{1,17},{2,18},{3,19},{4,20},{5,21},{6,22},{7,23},{8,24},{9,... | collective-permute-start | bytes 172040 | tf_op jit(solution)/shard_map/ppermute | solution.py:310
  8.6 6.8 %collective-permute-start = (bf16[14,32,128]{2,1,0:T(8,128)(2,1)S(1)}, bf16[14,32,128]{2,1,0:T(8,128)(2,1)S(1)}, u32[]{:S(2)}, u32[]{:S(2)}) collective-permute-start(bf16[14,32,128]{2,1,0:T(8,128)(2,1)S(1)} %get-tuple-element.10.refs_0_), channel_id=1, source_target_pairs={{0,4},{1,5},{2,6},{3,7},{4,0},{5,1},{6,2},{7,3},{8,12},{9,13},{10,... | collective-permute-start | bytes 344072 | tf_op jit(solution)/shard_map/ppermute | solution.py:300
  12.9 4.8 %collective-permute-start.2 = (bf16[14,32,128]{2,1,0:T(8,128)(2,1)S(1)}, bf16[14,32,128]{2,1,0:T(8,128)(2,1)S(1)}, u32[]{:S(2)}, u32[]{:S(2)}) collective-permute-start(bf16[14,32,128]{2,1,0:T(8,128)(2,1)S(1)} %collective-permute-done.1.refs_2_), channel_id=1, source_target_pairs={{0,4},{1,5},{2,6},{3,7},{4,0},{5,1},{6,2},{7,3},{8,12},{9,13},{10,... | collective-permute-start | bytes 344072 | tf_op jit(solution)/shard_map/ppermute | solution.py:300
  13.6 6.2 %collective-permute-start.4 = (bf16[14,48,128]{2,1,0:T(8,128)(2,1)S(1)}, bf16[14,48,128]{2,1,0:T(8,128)(2,1)S(1)}, u32[]{:S(2)}, u32[]{:S(2)}) collective-permute-start(bf16[14,48,128]{2,1,0:T(8,128)(2,1)S(1)} %merge.1.refs_0_), channel_id=1, source_target_pairs={{0,1},{1,0},{2,3},{3,2},{4,5},{5,4},{6,7},{7,6},{8,9},{9,8},{10,11... | collective-permute-start | bytes 516104 | tf_op jit(solution)/shard_map/ppermute | solution.py:300
  13.6 7.2 %collective-permute-start.5 = (bf16[14,48,128]{2,1,0:T(8,128)(2,1)S(1)}, bf16[14,48,128]{2,1,0:T(8,128)(2,1)S(1)}, u32[]{:S(2)}, u32[]{:S(2)}) collective-permute-start(bf16[14,48,128]{2,1,0:T(8,128)(2,1)S(1)} %merge.1.refs_0_), channel_id=1, source_target_pairs={{0,2},{1,3},{2,0},{3,1},{4,6},{5,7},{6,4},{7,5},{8,10},{9,11},{10,... | collective-permute-start | bytes 516104 | tf_op jit(solution)/shard_map/ppermute | solution.py:300
  15.2 8.4 %collective-permute-start.6 = (bf16[14,48,128]{2,1,0:T(8,128)(2,1)S(1)}, bf16[14,48,128]{2,1,0:T(8,128)(2,1)S(1)}, u32[]{:S(2)}, u32[]{:S(2)}) collective-permute-start(bf16[14,48,128]{2,1,0:T(8,128)(2,1)S(1)} %merge.1.refs_0_), channel_id=1, source_target_pairs={{0,3},{1,2},{2,1},{3,0},{4,7},{5,6},{6,5},{7,4},{8,11},{9,10},{10,... | collective-permute-start | bytes 516104 | tf_op jit(solution)/shard_map/ppermute | solution.py:300
  18.1 9.2 %collective-permute-start.7 = (bf16[49,16,128]{2,1,0:T(8,128)(2,1)S(1)}, bf16[49,16,128]{2,1,0:T(8,128)(2,1)S(1)}, u32[]{:S(2)}, u32[]{:S(2)}) collective-permute-start(bf16[49,16,128]{2,1,0:T(8,128)(2,1)S(1)} %get-tuple-element.15.xp), channel_id=1, source_target_pairs={{0,16},{1,17},{2,18},{3,19},{4,20},{5,21},{6,22},{7,23},{8,24},{9,... | collective-permute-start | bytes 602120 | tf_op jit(solution)/shard_map/ppermute | solution.py:310
  44.0 0.7 %copy-start.1 = (f32[32]{0:T(128)S(1)}, f32[32]{0:T(128)}, u32[]{:S(2)}) copy-start(f32[32]{0:T(128)} %param.7) | copy-start | bytes 388

commit v4 on v3

--- a/solution.py
+++ b/solution.py
@@ -26,7 +26,7 @@
     return copies
 
 
-def prep_kernel(order_hbm, x_hbm, g_hbm, xo_ref, go_ref, gp_ref, order_ref, x_ref, g_ref, sems, gs, gt, gout):
+def prep_kernel(order_hbm, x_hbm, g_hbm, xo_ref, go_ref, order_ref, x_ref, g_ref, sems, gs, gt, gout):
     copies = fetch((order_hbm, g_hbm, x_hbm), (order_ref, g_ref, x_ref), sems)
     copies[0].wait()
     copies[1].wait()
@@ -52,9 +52,7 @@
                 merged = jnp.where(block_id == j, moved, merged)
             gout[pl.ds(quad * 4 + e, GROUPS4, stride=EX), :] = merged
     for group in range(GROUPS4):
-        ordered = gout[group * EX:(group + 1) * EX, :].astype(BF16)
-        go_ref[group] = ordered
-        gp_ref[group] = ordered[:PIV_DEV]
+        go_ref[group] = gout[group * EX:(group + 1) * EX, :].astype(BF16)
     copies[2].wait()
     onehot = onehot.astype(BF16)
     zero_block = jnp.zeros((EX, CH), BF16)
@@ -72,9 +70,9 @@
     vmem = pl.BlockSpec(memory_space=pltpu.VMEM)
     return pl.pallas_call(
         prep_kernel,
-        out_shape=(full, full, jax.ShapeDtypeStruct((GROUPS4, PIV_DEV, LANES), BF16)),
+        out_shape=(full, full),
         in_specs=[pl.BlockSpec(memory_space=pltpu.HBM)] * 3,
-        out_specs=(vmem,) * 3,
+        out_specs=(vmem,) * 2,
         scratch_shapes=[
             pltpu.SMEM(order.shape, order.dtype),
             pltpu.VMEM(x.shape, x.dtype),
@@ -97,54 +95,32 @@
     return pl.CostEstimate(flops=flops, bytes_accessed=moved, transcendentals=0)
 
 
-def merge_kernel(own_ref, cross_ref, out_ref):
-    out_ref[:, :EX, :] = own_ref[...]
-    out_ref[:, EX:, :] = cross_ref[...]
-
-
-def merge(own, cross):
-    vmem = pl.BlockSpec(memory_space=pltpu.VMEM)
-    return pl.pallas_call(
-        merge_kernel,
-        out_shape=jax.ShapeDtypeStruct((GROUPS4, EX + PIV_DEV, LANES), BF16),
-        in_specs=[vmem] * 2,
-        out_specs=vmem,
-        compiler_params=pltpu.CompilerParams(vmem_limit_bytes=8 << 20),
-        cost_estimate=cost(0, 1 << 18),
-        name="merge",
-    )(own, cross)
-
-
 def unpack_kernel(*refs):
-    packed, all_ref, piv_refs = refs[:4], refs[4], refs[5:]
-    examples = packed[0].shape[1]
+    packed, all_ref, piv_ref = refs[:4], refs[4], refs[5]
     row = lax.broadcasted_iota(jnp.int32, (4 * LANES, 4 * LANES), 0)
     col = lax.broadcasted_iota(jnp.int32, (4 * LANES, 4 * LANES), 1)
     target = (row // CH) % 4 * LANES + row // LANES * CH + row % CH
     move = jnp.where(col == target, 1.0, 0.0).astype(BF16)
-    flat = jnp.concatenate([ref[...].reshape(GROUPS4 * examples, LANES) for ref in packed], axis=1)
+    flat = jnp.concatenate([ref[...].reshape(GROUPS4 * EX, LANES) for ref in packed], axis=1)
     moved = jnp.dot(flat, move, preferred_element_type=F32).astype(BF16)
     for group in range(GROUPS4):
         for j in range(4):
             py, px = group // 2, (group % 2) * 4 + j
             if px == SIDE:
                 continue
-            spot = moved[group * examples:(group + 1) * examples, j * LANES:(j + 1) * LANES]
-            all_ref[py * SIDE + px] = spot[:EX]
-            piv_refs[0][py * SIDE + px] = spot[:PIV_DEV]
-            if examples > EX:
-                piv_refs[1][py * SIDE + px] = spot[EX:]
+            spot = moved[group * EX:(group + 1) * EX, j * LANES:(j + 1) * LANES]
+            all_ref[py * SIDE + px] = spot
+            piv_ref[py * SIDE + px] = spot[:PIV_DEV]
 
 
 def unpack(arrays, name):
     vmem = pl.BlockSpec(memory_space=pltpu.VMEM)
     pivots = jax.ShapeDtypeStruct((SPOTS, PIV_DEV, LANES), BF16)
-    pivot_sets = arrays[0].shape[1] // PIV_DEV - 1
     return pl.pallas_call(
         unpack_kernel,
-        out_shape=(jax.ShapeDtypeStruct((SPOTS, EX, LANES), BF16),) + (pivots,) * pivot_sets,
+        out_shape=(jax.ShapeDtypeStruct((SPOTS, EX, LANES), BF16), pivots),
         in_specs=[vmem] * 4,
-        out_specs=(vmem,) * (1 + pivot_sets),
+        out_specs=(vmem,) * 2,
         compiler_params=pltpu.CompilerParams(vmem_limit_bytes=12 << 20),
         cost_estimate=cost(0, 1 << 20),
         name=name,
@@ -312,11 +288,11 @@
 
 def local_packed(count, activations, cotangents, ordering, ridge):
     x = jnp.transpose(activations, (1, 2, 0, 3)).reshape(SIDE * SIDE, EX, CH)
-    xo, go, gp = prep(ordering, x, cotangents)
-    gm = merge(go, exchange_across(gp, count))
-    x_all, x_piv = unpack(gather(xo, count, 8, 4), "unpack_x")
+    xo, go = prep(ordering, x, cotangents)
+    x_all, x_piv = unpack(gather(xo, count, 2, 1), "unpack_x")
     x_cross = exchange_across(x_piv, count)
-    g_all, g_piv, g_cross = unpack([gm] + [exchange(gm, count, f) for f in (1, 2, 3)], "unpack_g")
+    g_all, g_piv = unpack(gather(go, count, 8, 4), "unpack_g")
+    g_cross = exchange_across(g_piv, count)
     own_term = terms(own_kernel, (x_all, g_all, x_piv, g_piv), EX, (EX, LANES), "terms_own")
     term = terms(cross_kernel, (x_all, g_all, x_cross, g_cross, own_term), EX, (8, LANES), "terms_cross")
     copies = jnp.broadcast_to(term, (2 * count, 8, LANES))

time: 46.6 us -> 44.5 us (0.955)
  blocking collectives: 13.6 us -> 12.7 us
  waiting for transfers between devices: 8.75 us -> 8.03 us
    ppermute x6, waiting for transfers between devices: 8.75 us -> 5.9 us  [exchange(): return lax.ppermute(value, 'chan', [(i, i ^ flip) for i in range(count)])]
    ppermute x2, waiting for transfers between devices: 0.01 us -> 2.13 us  [exchange_across(): return lax.ppermute(value, ('rows', 'chan'), pairs)]
    all_to_all x1, blocking collectives: 13.6 us -> 12.7 us  [local_packed(): return final(lax.all_to_all(copies, ('rows', 'chan'), 0, 0), ridge)]
    pallas_call x2 -> x1, Pallas kernels: 1.77 us -> 1.76 us  [prep(): pl.pallas_call(prep_kernel, out_shape=(full, full), in_specs=[pl.BlockSpe...]
where the time goes in v4:
time: 44.5 us; the launch traced here: 44.4 us
  blocking collectives  12.7 us (29%)
  starting transfers between devices  11.1 us (25%)
  Pallas kernels  10.5 us (24%)
  waiting for transfers between devices  8.03 us (18%)
  local copies, waits for them, and re-layouts  1.32 us (3%)
  between operations  0.68 us (2%)
    all_to_all x1, blocking collectives, local_packed(): return final(lax.all_to_all(copies, ('rows', 'chan'), 0, 0), ridge)  12.7 us
    ppermute x6, starting transfers between devices, exchange(): return lax.ppermute(value, 'chan', [(i, i ^ flip) for i in range(count)])  7.99 us
    pallas_call x2, Pallas kernels, terms(): pl.pallas_call(kernel, out_shape=jax.ShapeDtypeStruct(shape, F32), in_spe...  6.03 us
    ppermute x6, waiting for transfers between devices, exchange(): return lax.ppermute(value, 'chan', [(i, i ^ flip) for i in range(count)])  5.9 us
    ppermute x2, starting transfers between devices, exchange_across(): return lax.ppermute(value, ('rows', 'chan'), pairs)  3.11 us
    ppermute x2, waiting for transfers between devices, exchange_across(): return lax.ppermute(value, ('rows', 'chan'), pairs)  2.13 us
    pallas_call x1, Pallas kernels, final(): pl.pallas_call(final_kernel, out_shape=(out, out), in_specs=[vmem] * 2, o...  1.85 us
    pallas_call x1, Pallas kernels, prep(): pl.pallas_call(prep_kernel, out_shape=(full, full), in_specs=[pl.BlockSpe...  1.76 us
  transfers between devices with their start and end apart: 8, of which 4 were waited for; matrix products, arithmetic and copies ran while one was open for 0% of the time, Pallas kernels for 9%

profile of v4, /device:TPU:0, one launch (start us, length us, event | category | flops | bytes accessed | tf_op | source)
XLA Modules:
  0.0 44.4 jit_solution(15196693452482159231)
XLA Ops:
  0.6 0.6 %copy-done = s32[1,32]{1,0:T(1,128)S(1)} copy-done((s32[1,32]{1,0:T(1,128)S(1)}, s32[1,32]{1,0:T(1,128)}, u32[]{:S(2)}) %copy-start) | copy-done | bytes 152
  1.3 1.8 %prep.1 = (bf16[14,32,128]{2,1,0:T(8,128)(2,1)S(1)}, bf16[14,32,128]{2,1,0:T(8,128)(2,1)S(1)}) custom-call(s32[1,32]{1,0:T(1,128)S(1)} %copy-done, bf16[49,32,32]{2,1,0:T(8,128)(2,1)} %bitcast.5, bf16[32,32,49]{2,1,0:T(8,128)(2,1)} %g_hbm.1), custom_call_target="tpu_custom_call" | custom-call | tf_op jit(solution)/shard_map/prep/pallas_call | solution.py:71
  3.1 3.0 %collective-permute-start.1 = (bf16[14,32,128]{2,1,0:T(8,128)(2,1)S(1)}, bf16[14,32,128]{2,1,0:T(8,128)(2,1)S(1)}, u32[]{:S(2)}, u32[]{:S(2)}) collective-permute-start(bf16[14,32,128]{2,1,0:T(8,128)(2,1)S(1)} %get-tuple-element.8.refs_0_), channel_id=1, source_target_pairs={{0,2},{1,3},{2,0},{3,1},{4,6},{5,7},{6,4},{7,5},{8,10},{9,11},{10,... | collective-permute-start | bytes 344072 | tf_op jit(solution)/shard_map/ppermute | solution.py:276
  6.1 2.6 %collective-permute-start.4 = (bf16[14,32,128]{2,1,0:T(8,128)(2,1)S(1)}, bf16[14,32,128]{2,1,0:T(8,128)(2,1)S(1)}, u32[]{:S(2)}, u32[]{:S(2)}) collective-permute-start(bf16[14,32,128]{2,1,0:T(8,128)(2,1)S(1)} %get-tuple-element.10.refs_0_), channel_id=1, source_target_pairs={{0,8},{1,9},{2,10},{3,11},{4,12},{5,13},{6,14},{7,15},{8,0},{9,1},... | collective-permute-start | bytes 344072 | tf_op jit(solution)/shard_map/ppermute | solution.py:276
  8.7 0.0 collective-permute-start
  8.7 0.6 %collective-permute-done.1.refs_2_ = bf16[14,32,128]{2,1,0:T(8,128)(2,1)S(1)} collective-permute-done((bf16[14,32,128]{2,1,0:T(8,128)(2,1)S(1)}, bf16[14,32,128]{2,1,0:T(8,128)(2,1)S(1)}, u32[]{:S(2)}, u32[]{:S(2)}) %collective-permute-start.1) | collective-permute-done | bytes 114720 | tf_op jit(solution)/shard_map/ppermute | solution.py:276
  9.2 0.0 collective-permute-start.2
  9.2 1.8 %collective-permute-start.3 = (bf16[14,32,128]{2,1,0:T(8,128)(2,1)S(1)}, bf16[14,32,128]{2,1,0:T(8,128)(2,1)S(1)}, u32[]{:S(2)}, u32[]{:S(2)}) collective-permute-start(bf16[14,32,128]{2,1,0:T(8,128)(2,1)S(1)} %get-tuple-element.10.refs_0_), channel_id=1, source_target_pairs={{0,4},{1,5},{2,6},{3,7},{4,0},{5,1},{6,2},{7,3},{8,12},{9,13},{10,... | collective-permute-start | bytes 344072 | tf_op jit(solution)/shard_map/ppermute | solution.py:276
  11.0 3.1 %collective-permute-done.4.refs_2_ = bf16[14,32,128]{2,1,0:T(8,128)(2,1)S(1)} collective-permute-done((bf16[14,32,128]{2,1,0:T(8,128)(2,1)S(1)}, bf16[14,32,128]{2,1,0:T(8,128)(2,1)S(1)}, u32[]{:S(2)}, u32[]{:S(2)}) %collective-permute-start.4) | collective-permute-done | bytes 114720 | tf_op jit(solution)/shard_map/ppermute | solution.py:276
  14.2 0.6 %collective-permute-start.5 = (bf16[14,32,128]{2,1,0:T(8,128)(2,1)S(1)}, bf16[14,32,128]{2,1,0:T(8,128)(2,1)S(1)}, u32[]{:S(2)}, u32[]{:S(2)}) collective-permute-start(bf16[14,32,128]{2,1,0:T(8,128)(2,1)S(1)} %collective-permute-done.4.refs_2_), channel_id=1, source_target_pairs={{0,4},{1,5},{2,6},{3,7},{4,0},{5,1},{6,2},{7,3},{8,12},{9,13},{10,... | collective-permute-start | bytes 344072 | tf_op jit(solution)/shard_map/ppermute | solution.py:276
  14.7 0.0 collective-permute-done.2.refs_3_
  14.7 0.4 unpack_x.1
  15.2 1.6 %collective-permute-start.6 = (bf16[49,16,128]{2,1,0:T(8,128)(2,1)S(1)}, bf16[49,16,128]{2,1,0:T(8,128)(2,1)S(1)}, u32[]{:S(2)}, u32[]{:S(2)}) collective-permute-start(bf16[49,16,128]{2,1,0:T(8,128)(2,1)S(1)} %get-tuple-element.12.xp), channel_id=1, source_target_pairs={{0,16},{1,17},{2,18},{3,19},{4,20},{5,21},{6,22},{7,23},{8,24},{9,... | collective-permute-start | bytes 602120 | tf_op jit(solution)/shard_map/ppermute | solution.py:286
  16.7 0.0 collective-permute-done.3.refs_1_
  16.7 2.2 %collective-permute-done.5.refs_3_ = bf16[14,32,128]{2,1,0:T(8,128)(2,1)S(1)} collective-permute-done((bf16[14,32,128]{2,1,0:T(8,128)(2,1)S(1)}, bf16[14,32,128]{2,1,0:T(8,128)(2,1)S(1)}, u32[]{:S(2)}, u32[]{:S(2)}) %collective-permute-start.5) | collective-permute-done | bytes 114720 | tf_op jit(solution)/shard_map/ppermute | solution.py:276
  19.0 0.4 unpack_g.1
  19.4 1.6 %collective-permute-start.7 = (bf16[49,16,128]{2,1,0:T(8,128)(2,1)S(1)}, bf16[49,16,128]{2,1,0:T(8,128)(2,1)S(1)}, u32[]{:S(2)}, u32[]{:S(2)}) collective-permute-start(bf16[49,16,128]{2,1,0:T(8,128)(2,1)S(1)} %get-tuple-element.13.gp), channel_id=1, source_target_pairs={{0,16},{1,17},{2,18},{3,19},{4,20},{5,21},{6,22},{7,23},{8,24},{9,... | collective-permute-start | bytes 602120 | tf_op jit(solution)/shard_map/ppermute | solution.py:286
  21.0 3.0 %terms_own.1.own_ref = f32[32,128]{1,0:T(8,128)S(1)} custom-call(bf16[49,32,128]{2,1,0:T(8,128)(2,1)S(1)} %get-tuple-element.9.x, bf16[49,32,128]{2,1,0:T(8,128)(2,1)S(1)} %get-tuple-element.11.g, bf16[49,16,128]{2,1,0:T(8,128)(2,1)S(1)} %get-tuple-element.12.xp, bf16[49,16,128]{2,1,0:T(8,128)(2,1)S(1)} %get-tuple-element.13.gp), custom_call_target="tpu_custom_call" | custom-call | flops 1438646272 | bytes 8388608 | tf_op jit(solution)/shard_map/terms_own/pallas_call | solution.py:200
  24.0 0.0 collective-permute-done.6.xp
  24.0 2.1 %collective-permute-done.7.gp = bf16[49,16,128]{2,1,0:T(8,128)(2,1)S(1)} collective-permute-done((bf16[49,16,128]{2,1,0:T(8,128)(2,1)S(1)}, bf16[49,16,128]{2,1,0:T(8,128)(2,1)S(1)}, u32[]{:S(2)}, u32[]{:S(2)}) %collective-permute-start.7) | collective-permute-done | bytes 200736 | tf_op jit(solution)/shard_map/ppermute | solution.py:286
  26.1 3.0 %terms_cross.1 = f32[8,128]{1,0:T(8,128)S(1)} custom-call(bf16[49,32,128]{2,1,0:T(8,128)(2,1)S(1)} %get-tuple-element.9.x, bf16[49,32,128]{2,1,0:T(8,128)(2,1)S(1)} %get-tuple-element.11.g, bf16[49,16,128]{2,1,0:T(8,128)(2,1)S(1)} %collective-permute-done.6.xp, bf16[49,16,128]{2,1,0:T(8,128)(2,1)S(1)} %collective-permute-done.7.gp, ...), custom_call_target="tpu_custom_call" | custom-call | flops 1438646272 | bytes 8388608 | tf_op jit(solution)/shard_map/terms_cross/pallas_call | solution.py:200
  29.1 12.7 %all_to_all.5.terms_ref = f32[32,8,128]{2,1,0:T(8,128)S(1)} all-to-all(f32[32,8,128]{2,1,0:T(8,128)S(1)} %broadcast_in_dim.3), channel_id=1, replica_groups=mesh['rows'=2,'chan'=16] {'rows','chan'}, dimensions={0} | all-to-all | bytes 262144 | tf_op jit(solution)/shard_map/all_to_all | solution.py:299
  41.8 0.7 %copy-done.1 = f32[32]{0:T(128)S(1)} copy-done((f32[32]{0:T(128)S(1)}, f32[32]{0:T(128)}, u32[]{:S(2)}) %copy-start.1) | copy-done | bytes 152
  42.5 1.8 %solve.1 = (f32[32,32]{1,0:T(8,128)}, f32[32,32]{1,0:T(8,128)}) custom-call(f32[32,8,128]{2,1,0:T(8,128)S(1)} %all_to_all.5.terms_ref, f32[1,32]{1,0:T(1,128)S(1)} %bitcast.4), custom_call_target="tpu_custom_call" | custom-call | tf_op jit(solution)/shard_map/solve/pallas_call | solution.py:265
  (4 shorter events, 0.0 us)
Async XLA Ops:
  0.6 0.7 %copy-start = (s32[1,32]{1,0:T(1,128)S(1)}, s32[1,32]{1,0:T(1,128)}, u32[]{:S(2)}) copy-start(s32[1,32]{1,0:T(1,128)} %order_hbm.1) | copy-start | bytes 388
  3.1 6.2 %collective-permute-start.1 = (bf16[14,32,128]{2,1,0:T(8,128)(2,1)S(1)}, bf16[14,32,128]{2,1,0:T(8,128)(2,1)S(1)}, u32[]{:S(2)}, u32[]{:S(2)}) collective-permute-start(bf16[14,32,128]{2,1,0:T(8,128)(2,1)S(1)} %get-tuple-element.8.refs_0_), channel_id=1, source_target_pairs={{0,2},{1,3},{2,0},{3,1},{4,6},{5,7},{6,4},{7,5},{8,10},{9,11},{10,... | collective-permute-start | bytes 344072 | tf_op jit(solution)/shard_map/ppermute | solution.py:276
  6.1 8.1 %collective-permute-start.4 = (bf16[14,32,128]{2,1,0:T(8,128)(2,1)S(1)}, bf16[14,32,128]{2,1,0:T(8,128)(2,1)S(1)}, u32[]{:S(2)}, u32[]{:S(2)}) collective-permute-start(bf16[14,32,128]{2,1,0:T(8,128)(2,1)S(1)} %get-tuple-element.10.refs_0_), channel_id=1, source_target_pairs={{0,8},{1,9},{2,10},{3,11},{4,12},{5,13},{6,14},{7,15},{8,0},{9,1},... | collective-permute-start | bytes 344072 | tf_op jit(solution)/shard_map/ppermute | solution.py:276
  8.7 6.0 %collective-permute-start = (bf16[14,32,128]{2,1,0:T(8,128)(2,1)S(1)}, bf16[14,32,128]{2,1,0:T(8,128)(2,1)S(1)}, u32[]{:S(2)}, u32[]{:S(2)}) collective-permute-start(bf16[14,32,128]{2,1,0:T(8,128)(2,1)S(1)} %get-tuple-element.8.refs_0_), channel_id=1, source_target_pairs={{0,1},{1,0},{2,3},{3,2},{4,5},{5,4},{6,7},{7,6},{8,9},{9,8},{10,11... | collective-permute-start | bytes 344072 | tf_op jit(solution)/shard_map/ppermute | solution.py:276
  9.2 5.5 %collective-permute-start.2 = (bf16[14,32,128]{2,1,0:T(8,128)(2,1)S(1)}, bf16[14,32,128]{2,1,0:T(8,128)(2,1)S(1)}, u32[]{:S(2)}, u32[]{:S(2)}) collective-permute-start(bf16[14,32,128]{2,1,0:T(8,128)(2,1)S(1)} %collective-permute-done.1.refs_2_), channel_id=1, source_target_pairs={{0,1},{1,0},{2,3},{3,2},{4,5},{5,4},{6,7},{7,6},{8,9},{9,8},{10,11... | collective-permute-start | bytes 344072 | tf_op jit(solution)/shard_map/ppermute | solution.py:276
  9.2 7.5 %collective-permute-start.3 = (bf16[14,32,128]{2,1,0:T(8,128)(2,1)S(1)}, bf16[14,32,128]{2,1,0:T(8,128)(2,1)S(1)}, u32[]{:S(2)}, u32[]{:S(2)}) collective-permute-start(bf16[14,32,128]{2,1,0:T(8,128)(2,1)S(1)} %get-tuple-element.10.refs_0_), channel_id=1, source_target_pairs={{0,4},{1,5},{2,6},{3,7},{4,0},{5,1},{6,2},{7,3},{8,12},{9,13},{10,... | collective-permute-start | bytes 344072 | tf_op jit(solution)/shard_map/ppermute | solution.py:276
  14.2 4.8 %collective-permute-start.5 = (bf16[14,32,128]{2,1,0:T(8,128)(2,1)S(1)}, bf16[14,32,128]{2,1,0:T(8,128)(2,1)S(1)}, u32[]{:S(2)}, u32[]{:S(2)}) collective-permute-start(bf16[14,32,128]{2,1,0:T(8,128)(2,1)S(1)} %collective-permute-done.4.refs_2_), channel_id=1, source_target_pairs={{0,4},{1,5},{2,6},{3,7},{4,0},{5,1},{6,2},{7,3},{8,12},{9,13},{10,... | collective-permute-start | bytes 344072 | tf_op jit(solution)/shard_map/ppermute | solution.py:276
  15.2 8.8 %collective-permute-start.6 = (bf16[49,16,128]{2,1,0:T(8,128)(2,1)S(1)}, bf16[49,16,128]{2,1,0:T(8,128)(2,1)S(1)}, u32[]{:S(2)}, u32[]{:S(2)}) collective-permute-start(bf16[49,16,128]{2,1,0:T(8,128)(2,1)S(1)} %get-tuple-element.12.xp), channel_id=1, source_target_pairs={{0,16},{1,17},{2,18},{3,19},{4,20},{5,21},{6,22},{7,23},{8,24},{9,... | collective-permute-start | bytes 602120 | tf_op jit(solution)/shard_map/ppermute | solution.py:286
  19.4 6.7 %collective-permute-start.7 = (bf16[49,16,128]{2,1,0:T(8,128)(2,1)S(1)}, bf16[49,16,128]{2,1,0:T(8,128)(2,1)S(1)}, u32[]{:S(2)}, u32[]{:S(2)}) collective-permute-start(bf16[49,16,128]{2,1,0:T(8,128)(2,1)S(1)} %get-tuple-element.13.gp), channel_id=1, source_target_pairs={{0,16},{1,17},{2,18},{3,19},{4,20},{5,21},{6,22},{7,23},{8,24},{9,... | collective-permute-start | bytes 602120 | tf_op jit(solution)/shard_map/ppermute | solution.py:286
  41.8 0.7 %copy-start.1 = (f32[32]{0:T(128)S(1)}, f32[32]{0:T(128)}, u32[]{:S(2)}) copy-start(f32[32]{0:T(128)} %param.7) | copy-start | bytes 388

commit v5 on v4

--- a/solution.py
+++ b/solution.py
@@ -127,10 +127,13 @@
     )(*arrays)
 
 
-def panel_terms(rows_x, rows_g, xp, gp, lx, lg, rx, rg, t):
+CONTRACT = (((1,), (1,)), ((), ()))
+SPANS = [(qy, min(qy + 2, SIDE)) for qy in range(0, SIDE, 2)]
+
+
+def input_products(rows_x, xp, lx, rx, t):
     heights = [ref.shape[1] for ref in rows_x]
     height = sum(heights)
-    block = SIDE * height
     for py in range(SIDE):
         for px in range(PITCH):
             row, col = (py * SIDE + px) * height, (py * PITCH + px) * PIV_DEV
@@ -145,26 +148,33 @@
                     for ref, count in zip(rows_x, heights):
                         lx[first:first + count, lanes] = ref[spot] if inside else jnp.zeros((count, LANES), BF16)
                         first += count
+    block = SIDE * height
+    for start, stop in SPANS:
+        right = rx[start * COLB:stop * COLB, :]
+        for py in range(SIDE):
+            left = lx[py * block:(py + 1) * block, :]
+            t[py, :, start * COLB:stop * COLB] = lax.dot_general(left, right, CONTRACT, preferred_element_type=F32)
+
+
+def panel_terms(rows_g, gp, lg, rg, t):
+    heights = [ref.shape[1] for ref in rows_g]
+    height = sum(heights)
+    for py in range(SIDE):
+        for px in range(PITCH):
+            row, col = (py * SIDE + px) * height, (py * PITCH + px) * PIV_DEV
             rg[col:col + PIV_DEV, :] = gp[py * SIDE + px] if px < SIDE else jnp.zeros((PIV_DEV, LANES), BF16)
             if px < SIDE:
                 first = row
                 for ref, count in zip(rows_g, heights):
                     lg[first:first + count, :] = ref[py * SIDE + px]
                     first += count
-
-    contract = (((1,), (1,)), ((), ()))
-    spans = [(qy, min(qy + 2, SIDE)) for qy in range(0, SIDE, 2)]
-    for start, stop in spans:
-        right = rx[start * COLB:stop * COLB, :]
-        for py in range(SIDE):
-            left = lx[py * block:(py + 1) * block, :]
-            t[py, :, start * COLB:stop * COLB] = lax.dot_general(left, right, contract, preferred_element_type=F32)
+    block = SIDE * height
     acc = jnp.zeros((height, COLB), F32)
-    for start, stop in spans:
+    for start, stop in SPANS:
         right = rg[start * COLB:stop * COLB, :]
         for py in range(SIDE):
             left = lg[py * block:(py + 1) * block, :]
-            gg = lax.dot_general(left, right, contract, preferred_element_type=F32)
+            gg = lax.dot_general(left, right, CONTRACT, preferred_element_type=F32)
             for qy in range(start, stop):
                 for px in range(SIDE):
                     rows = slice(px * height, (px + 1) * height)
@@ -179,38 +189,46 @@
     return acc + pltpu.roll(acc, 16, 1)
 
 
-def own_kernel(x, g, xp, gp, out_ref, *work):
-    out_ref[...] = panel_terms([x], [g], xp, gp, *work)
-
-
-def cross_kernel(x, g, xp, gp, own_ref, out_ref, *work):
-    across = panel_terms([x], [g], xp, gp, *work)
+def own_kernel(x, g, xp, gp, ridge, out_ref, ridge_out, lx, rx, lg, rg, t):
+    ridge_out[...] = ridge[...]
+    input_products([x], xp, lx, rx, t)
+    out_ref[...] = panel_terms([g], gp, lg, rg, t)
+
+
+def cross_inputs_kernel(x, xp, t_out, lx, rx):
+    input_products([x, xp], xp, lx, rx, t_out)
+
+
+def cross_kernel(t, g, gp, own_ref, out_ref, lg, rg):
+    across = panel_terms([g, gp], gp, lg, rg, t)
     lane = lax.broadcasted_iota(jnp.int32, (8, LANES), 1)
     is_own = (lane // PIV_DEV) % 2 == lax.axis_index("rows")
     packed = jnp.zeros((8, LANES), F32)
     for j in range(4):
         rows = slice(8 * j, 8 * j + 8)
         packed = jnp.where(lane // EX == j, jnp.where(is_own, own_ref[rows, :], across[rows]), packed)
-    out_ref[...] = packed
-
-
-def terms(kernel, arrays, height, shape, name):
+    out_ref[0:8, :] = packed
+    out_ref[8:16, :] = jnp.where(lane // PIV_DEV == 0, across[EX:EX + 8], across[EX + 8:EX + PIV_DEV])
+
+
+def product_shape(height):
+    return (SIDE, SIDE * height, SIDE * COLB)
+
+
+def scratch_of(height, width):
+    return [pltpu.VMEM((SPOTS * height, width), BF16), pltpu.VMEM((SIDE * COLB, width), BF16)]
+
+
+def terms(kernel, arrays, shapes, scratch, flops, name):
     vmem = pl.BlockSpec(memory_space=pltpu.VMEM)
-    rows, cols = SPOTS * height, SIDE * COLB
     return pl.pallas_call(
         kernel,
-        out_shape=jax.ShapeDtypeStruct(shape, F32),
+        out_shape=tuple(jax.ShapeDtypeStruct(shape, F32) for shape in shapes),
         in_specs=[vmem] * len(arrays),
-        out_specs=vmem,
-        scratch_shapes=[
-            pltpu.VMEM((rows, 3 * LANES), BF16),
-            pltpu.VMEM((rows, LANES), BF16),
-            pltpu.VMEM((cols, 3 * LANES), BF16),
-            pltpu.VMEM((cols, LANES), BF16),
-            pltpu.VMEM((SIDE, SIDE * height, cols), F32),
-        ],
-        compiler_params=pltpu.CompilerParams(vmem_limit_bytes=28 << 20),
-        cost_estimate=cost(2 * rows * cols * 4 * LANES, 8 << 20),
+        out_specs=(vmem,) * len(shapes),
+        scratch_shapes=scratch,
+        compiler_params=pltpu.CompilerParams(vmem_limit_bytes=20 << 20),
+        cost_estimate=cost(flops, 4 << 20),
         name=name,
     )(*arrays)
 
@@ -221,20 +239,20 @@
     )
 
 
-def tree_sum(values):
-    while len(values) > 1:
-        values = [a + b for a, b in zip(values[0::2], values[1::2])]
-    return values[0]
-
-
-def final_kernel(terms_ref, ridge_ref, gram_ref, factor_ref):
-    count = terms_ref.shape[0] // 2
-    sums = [tree_sum([terms_ref[g * count + i] for i in range(count)]) for g in range(2)]
-    panel = rows_of(jnp.where(lax.axis_index("rows") == 0, sums[0], sums[1]), 4)
+def final_kernel(total_ref, ridge_ref, gram_ref, factor_ref):
+    total = (total_ref[0] + total_ref[1]) + (total_ref[2] + total_ref[3])
+    panel = rows_of(total[:8], 4)
     gram_ref[...] = panel
-    diag = jnp.concatenate([rows_of(total, 2) for total in sums], axis=0)
+    group = lax.axis_index("rows")
+    mine, zero = panel[:PIV_DEV], jnp.zeros((PIV_DEV, EX), F32)
+    upper = jnp.concatenate([jnp.where(group == 0, mine, zero), jnp.where(group == 0, zero, mine)], axis=0)
+    block = jnp.concatenate([total[8:, :PIV_DEV], total[8:, PIV_DEV:2 * PIV_DEV]], axis=0)
+    block = jnp.concatenate([block, block], axis=1)
+    block = jnp.concatenate([block, block], axis=0)
     row_id = lax.broadcasted_iota(jnp.int32, (EX, EX), 0)
     col_id = lax.broadcasted_iota(jnp.int32, (EX, EX), 1)
+    diag = jnp.where(col_id // PIV_DEV == group, jnp.transpose(upper), block)
+    diag = jnp.where(row_id // PIV_DEV == group, upper, diag)
     ridge = jnp.where(row_id == col_id, jnp.broadcast_to(ridge_ref[...], (EX, EX)), 0.0)
     system = 0.5 * (diag + jnp.transpose(diag)) + ridge
     factor = jnp.zeros((EX, EX), F32)
@@ -259,7 +277,7 @@
     factor_ref[...] = factor
 
 
-def final(terms_of_all, ridge):
+def final(totals, ridge):
     vmem = pl.BlockSpec(memory_space=pltpu.VMEM)
     out = jax.ShapeDtypeStruct((EX, EX), F32)
     return pl.pallas_call(
@@ -269,7 +287,7 @@
         out_specs=(vmem, vmem),
         compiler_params=pltpu.CompilerParams(vmem_limit_bytes=8 << 20),
         name="solve",
-    )(terms_of_all, ridge.reshape(1, EX))
+    )(totals, ridge)
 
 
 def exchange(value, count, flip):
@@ -293,10 +311,26 @@
     x_cross = exchange_across(x_piv, count)
     g_all, g_piv = unpack(gather(go, count, 8, 4), "unpack_g")
     g_cross = exchange_across(g_piv, count)
-    own_term = terms(own_kernel, (x_all, g_all, x_piv, g_piv), EX, (EX, LANES), "terms_own")
-    term = terms(cross_kernel, (x_all, g_all, x_cross, g_cross, own_term), EX, (8, LANES), "terms_cross")
-    copies = jnp.broadcast_to(term, (2 * count, 8, LANES))
-    return final(lax.all_to_all(copies, ("rows", "chan"), 0, 0), ridge)
+    height = EX + PIV_DEV
+    own_term, ridge = terms(
+        own_kernel,
+        (x_all, g_all, x_piv, g_piv, ridge.reshape(1, EX)),
+        ((EX, LANES), (1, EX)),
+        scratch_of(EX, 3 * LANES) + scratch_of(EX, LANES) + [pltpu.VMEM(product_shape(EX), F32)],
+        11 * 10**9,
+        "terms_own",
+    )
+    products, = terms(
+        cross_inputs_kernel, (x_all, x_cross), (product_shape(height),), scratch_of(height, 3 * LANES), 8 * 10**9, "cross_inputs"
+    )
+    term, = terms(
+        cross_kernel, (products, g_all, g_cross, own_term), ((16, LANES),), scratch_of(height, LANES), 8 * 10**9, "terms_cross"
+    )
+    quads = [[4 * i + k for k in range(4)] for i in range(count // 4)]
+    lines = [[4 * i + k for i in range(count // 4)] for k in range(4)]
+    parts = lax.all_gather(term, "chan", axis_index_groups=quads)
+    part = (parts[0] + parts[1]) + (parts[2] + parts[3])
+    return final(lax.all_gather(part, "chan", axis_index_groups=lines), ridge)
 
 
 def jacobian_block(grad_rows, input_rows):

time: 44.5 us -> 50.4 us (1.13)
  blocking collectives: 12.7 us -> 18.3 us
  Pallas kernels: 10.5 us -> 12.9 us
  waiting for transfers between devices: 8.03 us -> 5.9 us
    all_gather x0 -> x2, blocking collectives: none -> 18.3 us  [the longest x1 13.1 us: local_packed(): return final(lax.all_gather(part, 'chan', axis_index_groups=lines), ridge)]
    all_to_all x1 -> x0, blocking collectives: 12.7 us -> none  [local_packed(): return final(lax.all_to_all(copies, ('rows', 'chan'), 0, 0), ridge)]
    pallas_call x2 -> x3, Pallas kernels: 6.03 us -> 8.36 us  [terms(): pl.pallas_call(kernel, out_shape=tuple((jax.ShapeDtypeStruct(shape, F32)...]
    ppermute x2, waiting for transfers between devices: 2.13 us -> 0.01 us  [exchange_across(): return lax.ppermute(value, ('rows', 'chan'), pairs)]
  transfers between devices with their start and end apart: 8 -> 8, of which waited for: 4 -> 3; matrix products, arithmetic and copies ran while one was open for 0% -> 0% of each run, Pallas kernels for 9% -> 13%
where the time goes in v5:
time: 50.4 us; the launch traced here: 50.2 us
  blocking collectives  18.3 us (36%)
  Pallas kernels  12.9 us (26%)
  starting transfers between devices  11.1 us (22%)
  waiting for transfers between devices  5.9 us (12%)
  local copies, waits for them, and re-layouts  1.3 us (3%)
  between operations  0.69 us (1%)
    all_gather x1, blocking collectives, local_packed(): return final(lax.all_gather(part, 'chan', axis_index_groups=lines), ridge)  13.1 us
    pallas_call x3, Pallas kernels, terms(): pl.pallas_call(kernel, out_shape=tuple((jax.ShapeDtypeStruct(shape, F32)...  8.36 us
    ppermute x6, starting transfers between devices, exchange(): return lax.ppermute(value, 'chan', [(i, i ^ flip) for i in range(count)])  7.99 us
    ppermute x6, waiting for transfers between devices, exchange(): return lax.ppermute(value, 'chan', [(i, i ^ flip) for i in range(count)])  5.9 us
    all_gather x1, blocking collectives, local_packed(): parts = lax.all_gather(term, 'chan', axis_index_groups=quads)  5.18 us
    ppermute x2, starting transfers between devices, exchange_across(): return lax.ppermute(value, ('rows', 'chan'), pairs)  3.11 us
    pallas_call x1, Pallas kernels, final(): pl.pallas_call(final_kernel, out_shape=(out, out), in_specs=[vmem] * 2, o...  1.91 us
    pallas_call x1, Pallas kernels, prep(): pl.pallas_call(prep_kernel, out_shape=(full, full), in_specs=[pl.BlockSpe...  1.76 us
  transfers between devices with their start and end apart: 8, of which 3 were waited for; matrix products, arithmetic and copies ran while one was open for 0% of the time, Pallas kernels for 13%

profile of v5, /device:TPU:0, one launch (start us, length us, event | category | flops | bytes accessed | tf_op | source)
XLA Modules:
  0.0 50.2 jit_solution(17999373077494999202)
XLA Ops:
  0.6 0.6 %copy-done = s32[1,32]{1,0:T(1,128)S(1)} copy-done((s32[1,32]{1,0:T(1,128)S(1)}, s32[1,32]{1,0:T(1,128)}, u32[]{:S(2)}) %copy-start) | copy-done | bytes 152
  1.3 1.8 %prep.1 = (bf16[14,32,128]{2,1,0:T(8,128)(2,1)S(1)}, bf16[14,32,128]{2,1,0:T(8,128)(2,1)S(1)}) custom-call(s32[1,32]{1,0:T(1,128)S(1)} %copy-done, bf16[49,32,32]{2,1,0:T(8,128)(2,1)} %bitcast.7, bf16[32,32,49]{2,1,0:T(8,128)(2,1)} %g_hbm.1), custom_call_target="tpu_custom_call" | custom-call | tf_op jit(solution)/shard_map/prep/pallas_call | solution.py:71
  3.1 3.0 %collective-permute-start.1 = (bf16[14,32,128]{2,1,0:T(8,128)(2,1)S(1)}, bf16[14,32,128]{2,1,0:T(8,128)(2,1)S(1)}, u32[]{:S(2)}, u32[]{:S(2)}) collective-permute-start(bf16[14,32,128]{2,1,0:T(8,128)(2,1)S(1)} %get-tuple-element.10.refs_0_), channel_id=1, source_target_pairs={{0,2},{1,3},{2,0},{3,1},{4,6},{5,7},{6,4},{7,5},{8,10},{9,11},{10,... | collective-permute-start | bytes 344072 | tf_op jit(solution)/shard_map/ppermute | solution.py:294
  6.1 2.6 %collective-permute-start.5 = (bf16[14,32,128]{2,1,0:T(8,128)(2,1)S(1)}, bf16[14,32,128]{2,1,0:T(8,128)(2,1)S(1)}, u32[]{:S(2)}, u32[]{:S(2)}) collective-permute-start(bf16[14,32,128]{2,1,0:T(8,128)(2,1)S(1)} %get-tuple-element.13.refs_0_), channel_id=1, source_target_pairs={{0,8},{1,9},{2,10},{3,11},{4,12},{5,13},{6,14},{7,15},{8,0},{9,1},... | collective-permute-start | bytes 344072 | tf_op jit(solution)/shard_map/ppermute | solution.py:294
  8.7 0.0 collective-permute-start
  8.7 0.6 %collective-permute-done.1.refs_2_ = bf16[14,32,128]{2,1,0:T(8,128)(2,1)S(1)} collective-permute-done((bf16[14,32,128]{2,1,0:T(8,128)(2,1)S(1)}, bf16[14,32,128]{2,1,0:T(8,128)(2,1)S(1)}, u32[]{:S(2)}, u32[]{:S(2)}) %collective-permute-start.1) | collective-permute-done | bytes 114720 | tf_op jit(solution)/shard_map/ppermute | solution.py:294
  9.2 1.8 %collective-permute-start.4 = (bf16[14,32,128]{2,1,0:T(8,128)(2,1)S(1)}, bf16[14,32,128]{2,1,0:T(8,128)(2,1)S(1)}, u32[]{:S(2)}, u32[]{:S(2)}) collective-permute-start(bf16[14,32,128]{2,1,0:T(8,128)(2,1)S(1)} %get-tuple-element.13.refs_0_), channel_id=1, source_target_pairs={{0,4},{1,5},{2,6},{3,7},{4,0},{5,1},{6,2},{7,3},{8,12},{9,13},{10,... | collective-permute-start | bytes 344072 | tf_op jit(solution)/shard_map/ppermute | solution.py:294
  11.0 3.1 %collective-permute-done.5.refs_2_ = bf16[14,32,128]{2,1,0:T(8,128)(2,1)S(1)} collective-permute-done((bf16[14,32,128]{2,1,0:T(8,128)(2,1)S(1)}, bf16[14,32,128]{2,1,0:T(8,128)(2,1)S(1)}, u32[]{:S(2)}, u32[]{:S(2)}) %collective-permute-start.5) | collective-permute-done | bytes 114720 | tf_op jit(solution)/shard_map/ppermute | solution.py:294
  14.2 0.6 %collective-permute-start.6 = (bf16[14,32,128]{2,1,0:T(8,128)(2,1)S(1)}, bf16[14,32,128]{2,1,0:T(8,128)(2,1)S(1)}, u32[]{:S(2)}, u32[]{:S(2)}) collective-permute-start(bf16[14,32,128]{2,1,0:T(8,128)(2,1)S(1)} %collective-permute-done.5.refs_2_), channel_id=1, source_target_pairs={{0,4},{1,5},{2,6},{3,7},{4,0},{5,1},{6,2},{7,3},{8,12},{9,13},{10,... | collective-permute-start | bytes 344072 | tf_op jit(solution)/shard_map/ppermute | solution.py:294
  14.7 0.0 collective-permute-done.2.refs_3_
  14.7 0.4 unpack_x.1
  15.2 1.6 %collective-permute-start.3 = (bf16[49,16,128]{2,1,0:T(8,128)(2,1)S(1)}, bf16[49,16,128]{2,1,0:T(8,128)(2,1)S(1)}, u32[]{:S(2)}, u32[]{:S(2)}) collective-permute-start(bf16[49,16,128]{2,1,0:T(8,128)(2,1)S(1)} %get-tuple-element.12.xp), channel_id=1, source_target_pairs={{0,16},{1,17},{2,18},{3,19},{4,20},{5,21},{6,22},{7,23},{8,24},{9,... | collective-permute-start | bytes 602120 | tf_op jit(solution)/shard_map/ppermute | solution.py:304
  16.7 0.0 collective-permute-done.4.refs_1_
  16.7 2.2 %collective-permute-done.6.refs_3_ = bf16[14,32,128]{2,1,0:T(8,128)(2,1)S(1)} collective-permute-done((bf16[14,32,128]{2,1,0:T(8,128)(2,1)S(1)}, bf16[14,32,128]{2,1,0:T(8,128)(2,1)S(1)}, u32[]{:S(2)}, u32[]{:S(2)}) %collective-permute-start.6) | collective-permute-done | bytes 114720 | tf_op jit(solution)/shard_map/ppermute | solution.py:294
  19.0 0.4 unpack_g.1
  19.4 1.6 %collective-permute-start.7 = (bf16[49,16,128]{2,1,0:T(8,128)(2,1)S(1)}, bf16[49,16,128]{2,1,0:T(8,128)(2,1)S(1)}, u32[]{:S(2)}, u32[]{:S(2)}) collective-permute-start(bf16[49,16,128]{2,1,0:T(8,128)(2,1)S(1)} %get-tuple-element.15.gp), channel_id=1, source_target_pairs={{0,16},{1,17},{2,18},{3,19},{4,20},{5,21},{6,22},{7,23},{8,24},{9,... | collective-permute-start | bytes 602120 | tf_op jit(solution)/shard_map/ppermute | solution.py:304
  21.0 0.7 %copy-done.1 = f32[32]{0:T(128)S(1)} copy-done((f32[32]{0:T(128)S(1)}, f32[32]{0:T(128)}, u32[]{:S(2)}) %copy-start.1) | copy-done | bytes 152
  21.6 3.0 %terms_own.1 = (f32[32,128]{1,0:T(8,128)S(1)}, f32[1,32]{1,0:T(1,128)S(1)}) custom-call(bf16[49,32,128]{2,1,0:T(8,128)(2,1)S(1)} %get-tuple-element.11.x, bf16[49,32,128]{2,1,0:T(8,128)(2,1)S(1)} %get-tuple-element.14.g, bf16[49,16,128]{2,1,0:T(8,128)(2,1)S(1)} %get-tuple-element.12.xp, bf16[49,16,128]{2,1,0:T(8,128)(2,1)S(1)} %get-tuple-element.15.gp, ...), custom_call_target="tpu_custom_call" | custom-call | flops 11000000512 | bytes 4194304 | tf_op jit(solution)/shard_map/terms_own/pallas_call | solution.py:224
  24.6 0.0 collective-permute-done.3.xp
  24.6 2.8 %cross_inputs.1.t = f32[7,336,896]{2,1,0:T(8,128)S(1)} custom-call(bf16[49,32,128]{2,1,0:T(8,128)(2,1)S(1)} %get-tuple-element.11.x, bf16[49,16,128]{2,1,0:T(8,128)(2,1)S(1)} %collective-permute-done.3.xp), custom_call_target="tpu_custom_call" | custom-call | flops 8000000000 | bytes 4194304 | tf_op jit(solution)/shard_map/cross_inputs/pallas_call | solution.py:224
  27.4 2.6 %terms_cross.1 = f32[16,128]{1,0:T(8,128)S(1)} custom-call(f32[7,336,896]{2,1,0:T(8,128)S(1)} %cross_inputs.1.t, bf16[49,32,128]{2,1,0:T(8,128)(2,1)S(1)} %get-tuple-element.14.g, bf16[49,16,128]{2,1,0:T(8,128)(2,1)S(1)} %collective-permute-done.7.gp, f32[32,128]{1,0:T(8,128)S(1)} %get-tuple-element.16.own_ref), custom_call_target="tpu_custom_call" | custom-call | flops 8000000000 | bytes 4194304 | tf_op jit(solution)/shard_map/terms_cross/pallas_call | solution.py:224
  30.0 5.2 %all-gather = f32[64,128]{1,0:T(8,128)S(1)} all-gather(f32[16,128]{1,0:T(8,128)S(1)} %terms_cross.1), channel_id=2, replica_groups={{0,1,2,3},{4,5,6,7},{8,9,10,11},{12,13,14,15},{16,17,18,19},{20,21,22,2..., dimensions={0}, use_global_device_ids=true | all-gather | bytes 40960 | tf_op jit(solution)/shard_map/all_gather | solution.py:331
  35.2 13.1 %all-gather.1 = f32[64,128]{1,0:T(8,128)S(1)} all-gather(f32[16,128]{1,0:T(8,128)S(1)} %fusion), channel_id=3, replica_groups={{0,4,8,12},{1,5,9,13},{2,6,10,14},{3,7,11,15},{16,20,24,28},{17,21,25,2..., dimensions={0}, use_global_device_ids=true | all-gather | bytes 40960 | tf_op jit(solution)/shard_map/all_gather | solution.py:333
  48.3 1.9 %solve.1 = (f32[32,32]{1,0:T(8,128)}, f32[32,32]{1,0:T(8,128)}) custom-call(f32[4,16,128]{2,1,0:T(8,128)S(1)} %bitcast.5, f32[1,32]{1,0:T(1,128)S(1)} %get-tuple-element.17.ridge_ref), custom_call_target="tpu_custom_call" | custom-call | tf_op jit(solution)/shard_map/solve/pallas_call | solution.py:283
  (6 shorter events, 0.0 us)
Async XLA Ops:
  0.6 0.7 %copy-start = (s32[1,32]{1,0:T(1,128)S(1)}, s32[1,32]{1,0:T(1,128)}, u32[]{:S(2)}) copy-start(s32[1,32]{1,0:T(1,128)} %order_hbm.1) | copy-start | bytes 388
  3.1 6.2 %collective-permute-start.1 = (bf16[14,32,128]{2,1,0:T(8,128)(2,1)S(1)}, bf16[14,32,128]{2,1,0:T(8,128)(2,1)S(1)}, u32[]{:S(2)}, u32[]{:S(2)}) collective-permute-start(bf16[14,32,128]{2,1,0:T(8,128)(2,1)S(1)} %get-tuple-element.10.refs_0_), channel_id=1, source_target_pairs={{0,2},{1,3},{2,0},{3,1},{4,6},{5,7},{6,4},{7,5},{8,10},{9,11},{10,... | collective-permute-start | bytes 344072 | tf_op jit(solution)/shard_map/ppermute | solution.py:294
  6.1 8.1 %collective-permute-start.5 = (bf16[14,32,128]{2,1,0:T(8,128)(2,1)S(1)}, bf16[14,32,128]{2,1,0:T(8,128)(2,1)S(1)}, u32[]{:S(2)}, u32[]{:S(2)}) collective-permute-start(bf16[14,32,128]{2,1,0:T(8,128)(2,1)S(1)} %get-tuple-element.13.refs_0_), channel_id=1, source_target_pairs={{0,8},{1,9},{2,10},{3,11},{4,12},{5,13},{6,14},{7,15},{8,0},{9,1},... | collective-permute-start | bytes 344072 | tf_op jit(solution)/shard_map/ppermute | solution.py:294
  8.7 6.0 %collective-permute-start = (bf16[14,32,128]{2,1,0:T(8,128)(2,1)S(1)}, bf16[14,32,128]{2,1,0:T(8,128)(2,1)S(1)}, u32[]{:S(2)}, u32[]{:S(2)}) collective-permute-start(bf16[14,32,128]{2,1,0:T(8,128)(2,1)S(1)} %get-tuple-element.10.refs_0_), channel_id=1, source_target_pairs={{0,1},{1,0},{2,3},{3,2},{4,5},{5,4},{6,7},{7,6},{8,9},{9,8},{10,11... | collective-permute-start | bytes 344072 | tf_op jit(solution)/shard_map/ppermute | solution.py:294
  9.2 5.5 %collective-permute-start.2 = (bf16[14,32,128]{2,1,0:T(8,128)(2,1)S(1)}, bf16[14,32,128]{2,1,0:T(8,128)(2,1)S(1)}, u32[]{:S(2)}, u32[]{:S(2)}) collective-permute-start(bf16[14,32,128]{2,1,0:T(8,128)(2,1)S(1)} %collective-permute-done.1.refs_2_), channel_id=1, source_target_pairs={{0,1},{1,0},{2,3},{3,2},{4,5},{5,4},{6,7},{7,6},{8,9},{9,8},{10,11... | collective-permute-start | bytes 344072 | tf_op jit(solution)/shard_map/ppermute | solution.py:294
  9.2 7.5 %collective-permute-start.4 = (bf16[14,32,128]{2,1,0:T(8,128)(2,1)S(1)}, bf16[14,32,128]{2,1,0:T(8,128)(2,1)S(1)}, u32[]{:S(2)}, u32[]{:S(2)}) collective-permute-start(bf16[14,32,128]{2,1,0:T(8,128)(2,1)S(1)} %get-tuple-element.13.refs_0_), channel_id=1, source_target_pairs={{0,4},{1,5},{2,6},{3,7},{4,0},{5,1},{6,2},{7,3},{8,12},{9,13},{10,... | collective-permute-start | bytes 344072 | tf_op jit(solution)/shard_map/ppermute | solution.py:294
  14.2 4.8 %collective-permute-start.6 = (bf16[14,32,128]{2,1,0:T(8,128)(2,1)S(1)}, bf16[14,32,128]{2,1,0:T(8,128)(2,1)S(1)}, u32[]{:S(2)}, u32[]{:S(2)}) collective-permute-start(bf16[14,32,128]{2,1,0:T(8,128)(2,1)S(1)} %collective-permute-done.5.refs_2_), channel_id=1, source_target_pairs={{0,4},{1,5},{2,6},{3,7},{4,0},{5,1},{6,2},{7,3},{8,12},{9,13},{10,... | collective-permute-start | bytes 344072 | tf_op jit(solution)/shard_map/ppermute | solution.py:294
  15.2 9.5 %collective-permute-start.3 = (bf16[49,16,128]{2,1,0:T(8,128)(2,1)S(1)}, bf16[49,16,128]{2,1,0:T(8,128)(2,1)S(1)}, u32[]{:S(2)}, u32[]{:S(2)}) collective-permute-start(bf16[49,16,128]{2,1,0:T(8,128)(2,1)S(1)} %get-tuple-element.12.xp), channel_id=1, source_target_pairs={{0,16},{1,17},{2,18},{3,19},{4,20},{5,21},{6,22},{7,23},{8,24},{9,... | collective-permute-start | bytes 602120 | tf_op jit(solution)/shard_map/ppermute | solution.py:304
  19.4 8.0 %collective-permute-start.7 = (bf16[49,16,128]{2,1,0:T(8,128)(2,1)S(1)}, bf16[49,16,128]{2,1,0:T(8,128)(2,1)S(1)}, u32[]{:S(2)}, u32[]{:S(2)}) collective-permute-start(bf16[49,16,128]{2,1,0:T(8,128)(2,1)S(1)} %get-tuple-element.15.gp), channel_id=1, source_target_pairs={{0,16},{1,17},{2,18},{3,19},{4,20},{5,21},{6,22},{7,23},{8,24},{9,... | collective-permute-start | bytes 602120 | tf_op jit(solution)/shard_map/ppermute | solution.py:304
  21.0 0.7 %copy-start.1 = (f32[32]{0:T(128)S(1)}, f32[32]{0:T(128)}, u32[]{:S(2)}) copy-start(f32[32]{0:T(128)} %param.7) | copy-start | bytes 388

commit v6 on v5

--- a/solution.py
+++ b/solution.py
@@ -189,26 +189,25 @@
     return acc + pltpu.roll(acc, 16, 1)
 
 
-def own_kernel(x, g, xp, gp, ridge, out_ref, ridge_out, lx, rx, lg, rg, t):
-    ridge_out[...] = ridge[...]
+def own_kernel(x, g, xp, gp, out_ref, lx, rx, lg, rg, t):
     input_products([x], xp, lx, rx, t)
     out_ref[...] = panel_terms([g], gp, lg, rg, t)
 
 
 def cross_inputs_kernel(x, xp, t_out, lx, rx):
-    input_products([x, xp], xp, lx, rx, t_out)
-
-
-def cross_kernel(t, g, gp, own_ref, out_ref, lg, rg):
-    across = panel_terms([g, gp], gp, lg, rg, t)
+    input_products([x], xp, lx, rx, t_out)
+
+
+def cross_kernel(t, g, gp, own_ref, ridge, out_ref, ridge_out, lg, rg):
+    ridge_out[...] = ridge[...]
+    across = panel_terms([g], gp, lg, rg, t)
     lane = lax.broadcasted_iota(jnp.int32, (8, LANES), 1)
     is_own = (lane // PIV_DEV) % 2 == lax.axis_index("rows")
     packed = jnp.zeros((8, LANES), F32)
     for j in range(4):
         rows = slice(8 * j, 8 * j + 8)
         packed = jnp.where(lane // EX == j, jnp.where(is_own, own_ref[rows, :], across[rows]), packed)
-    out_ref[0:8, :] = packed
-    out_ref[8:16, :] = jnp.where(lane // PIV_DEV == 0, across[EX:EX + 8], across[EX + 8:EX + PIV_DEV])
+    out_ref[...] = packed
 
 
 def product_shape(height):
@@ -239,20 +238,20 @@
     )
 
 
-def final_kernel(total_ref, ridge_ref, gram_ref, factor_ref):
-    total = (total_ref[0] + total_ref[1]) + (total_ref[2] + total_ref[3])
-    panel = rows_of(total[:8], 4)
+def tree_sum(values):
+    while len(values) > 1:
+        values = [a + b for a, b in zip(values[0::2], values[1::2])]
+    return values[0]
+
+
+def final_kernel(terms_ref, ridge_ref, gram_ref, factor_ref):
+    count = terms_ref.shape[0] // 2
+    sums = [tree_sum([terms_ref[g * count + i] for i in range(count)]) for g in range(2)]
+    panel = rows_of(jnp.where(lax.axis_index("rows") == 0, sums[0], sums[1]), 4)
     gram_ref[...] = panel
-    group = lax.axis_index("rows")
-    mine, zero = panel[:PIV_DEV], jnp.zeros((PIV_DEV, EX), F32)
-    upper = jnp.concatenate([jnp.where(group == 0, mine, zero), jnp.where(group == 0, zero, mine)], axis=0)
-    block = jnp.concatenate([total[8:, :PIV_DEV], total[8:, PIV_DEV:2 * PIV_DEV]], axis=0)
-    block = jnp.concatenate([block, block], axis=1)
-    block = jnp.concatenate([block, block], axis=0)
+    diag = jnp.concatenate([rows_of(total, 2) for total in sums], axis=0)
     row_id = lax.broadcasted_iota(jnp.int32, (EX, EX), 0)
     col_id = lax.broadcasted_iota(jnp.int32, (EX, EX), 1)
-    diag = jnp.where(col_id // PIV_DEV == group, jnp.transpose(upper), block)
-    diag = jnp.where(row_id // PIV_DEV == group, upper, diag)
     ridge = jnp.where(row_id == col_id, jnp.broadcast_to(ridge_ref[...], (EX, EX)), 0.0)
     system = 0.5 * (diag + jnp.transpose(diag)) + ridge
     factor = jnp.zeros((EX, EX), F32)
@@ -277,7 +276,7 @@
     factor_ref[...] = factor
 
 
-def final(totals, ridge):
+def final(terms_of_all, ridge):
     vmem = pl.BlockSpec(memory_space=pltpu.VMEM)
     out = jax.ShapeDtypeStruct((EX, EX), F32)
     return pl.pallas_call(
@@ -287,7 +286,7 @@
         out_specs=(vmem, vmem),
         compiler_params=pltpu.CompilerParams(vmem_limit_bytes=8 << 20),
         name="solve",
-    )(totals, ridge)
+    )(terms_of_all, ridge)
 
 
 def exchange(value, count, flip):
@@ -311,26 +310,15 @@
     x_cross = exchange_across(x_piv, count)
     g_all, g_piv = unpack(gather(go, count, 8, 4), "unpack_g")
     g_cross = exchange_across(g_piv, count)
-    height = EX + PIV_DEV
-    own_term, ridge = terms(
-        own_kernel,
-        (x_all, g_all, x_piv, g_piv, ridge.reshape(1, EX)),
-        ((EX, LANES), (1, EX)),
-        scratch_of(EX, 3 * LANES) + scratch_of(EX, LANES) + [pltpu.VMEM(product_shape(EX), F32)],
-        11 * 10**9,
-        "terms_own",
-    )
-    products, = terms(
-        cross_inputs_kernel, (x_all, x_cross), (product_shape(height),), scratch_of(height, 3 * LANES), 8 * 10**9, "cross_inputs"
-    )
-    term, = terms(
-        cross_kernel, (products, g_all, g_cross, own_term), ((16, LANES),), scratch_of(height, LANES), 8 * 10**9, "terms_cross"
-    )
-    quads = [[4 * i + k for k in range(4)] for i in range(count // 4)]
-    lines = [[4 * i + k for i in range(count // 4)] for k in range(4)]
-    parts = lax.all_gather(term, "chan", axis_index_groups=quads)
-    part = (parts[0] + parts[1]) + (parts[2] + parts[3])
-    return final(lax.all_gather(part, "chan", axis_index_groups=lines), ridge)
+    wide, narrow = scratch_of(EX, 3 * LANES), scratch_of(EX, LANES)
+    shape, flops = product_shape(EX), 6 * 10**9
+    arrays = (x_all, g_all, x_piv, g_piv)
+    own_term, = terms(own_kernel, arrays, ((EX, LANES),), wide + narrow + [pltpu.VMEM(shape, F32)], 2 * flops, "terms_own")
+    products, = terms(cross_inputs_kernel, (x_all, x_cross), (shape,), wide, flops, "cross_inputs")
+    arrays = (products, g_all, g_cross, own_term, ridge.reshape(1, EX))
+    term, ridge = terms(cross_kernel, arrays, ((8, LANES), (1, EX)), narrow, flops, "terms_cross")
+    copies = jnp.broadcast_to(term, (2 * count, 8, LANES))
+    return final(lax.all_to_all(copies, ("rows", "chan"), 0, 0), ridge)
 
 
 def jacobian_block(grad_rows, input_rows):

time: 50.4 us -> 42.4 us (0.84)
  blocking collectives: 18.3 us -> 12.7 us
  Pallas kernels: 12.9 us -> 11.1 us
  local copies, waits for them, and re-layouts: 1.3 us -> 0.67 us
    all_gather x2 -> x0, blocking collectives: 18.3 us -> none  [the longest x1 13.1 us: local_packed(): return final(lax.all_gather(part, 'chan', axis_index_groups=lines), ridge)]
    all_to_all x0 -> x1, blocking collectives: none -> 12.7 us  [local_packed(): return final(lax.all_to_all(copies, ('rows', 'chan'), 0, 0), ridge)]
    pallas_call x3, Pallas kernels: 8.36 us -> 6.62 us  [terms(): pl.pallas_call(kernel, out_shape=tuple((jax.ShapeDtypeStruct(shape, F32)...]
    unnamed x4, local copies, waits for them, and re-layouts: 1.3 us -> 0.65 us
  transfers between devices with their start and end apart: 8 -> 8, of which waited for: 3 -> 4; matrix products, arithmetic and copies ran while one was open for 0% -> 0% of each run, Pallas kernels for 13% -> 14%
where the time goes in v6:
time: 42.4 us; the launch traced here: 42.3 us
  blocking collectives  12.7 us (30%)
  Pallas kernels  11.1 us (26%)
  starting transfers between devices  11.1 us (26%)
  waiting for transfers between devices  5.99 us (14%)
  between operations  0.69 us (2%)
  local copies, waits for them, and re-layouts  0.67 us (2%)
    all_to_all x1, blocking collectives, local_packed(): return final(lax.all_to_all(copies, ('rows', 'chan'), 0, 0), ridge)  12.7 us
    ppermute x6, starting transfers between devices, exchange(): return lax.ppermute(value, 'chan', [(i, i ^ flip) for i in range(count)])  7.99 us
    pallas_call x3, Pallas kernels, terms(): pl.pallas_call(kernel, out_shape=tuple((jax.ShapeDtypeStruct(shape, F32)...  6.62 us
    ppermute x6, waiting for transfers between devices, exchange(): return lax.ppermute(value, 'chan', [(i, i ^ flip) for i in range(count)])  5.89 us
    ppermute x2, starting transfers between devices, exchange_across(): return lax.ppermute(value, ('rows', 'chan'), pairs)  3.11 us
    pallas_call x1, Pallas kernels, final(): pl.pallas_call(final_kernel, out_shape=(out, out), in_specs=[vmem] * 2, o...  1.85 us
    pallas_call x1, Pallas kernels, prep(): pl.pallas_call(prep_kernel, out_shape=(full, full), in_specs=[pl.BlockSpe...  1.76 us
    pallas_call x2, Pallas kernels, unpack(): pl.pallas_call(unpack_kernel, out_shape=(jax.ShapeDtypeStruct((SPOTS, EX,...  0.88 us
  transfers between devices with their start and end apart: 8, of which 4 were waited for; matrix products, arithmetic and copies ran while one was open for 0% of the time, Pallas kernels for 14%

profile of v6, /device:TPU:0, one launch (start us, length us, event | category | flops | bytes accessed | tf_op | source)
XLA Modules:
  0.0 42.3 jit_solution(8598276600152926899)
XLA Ops:
  0.6 0.6 %copy-done = s32[1,32]{1,0:T(1,128)S(1)} copy-done((s32[1,32]{1,0:T(1,128)S(1)}, s32[1,32]{1,0:T(1,128)}, u32[]{:S(2)}) %copy-start) | copy-done | bytes 152
  1.3 1.8 %prep.1 = (bf16[14,32,128]{2,1,0:T(8,128)(2,1)S(1)}, bf16[14,32,128]{2,1,0:T(8,128)(2,1)S(1)}) custom-call(s32[1,32]{1,0:T(1,128)S(1)} %copy-done, bf16[49,32,32]{2,1,0:T(8,128)(2,1)} %bitcast.5, bf16[32,32,49]{2,1,0:T(8,128)(2,1)} %g_hbm.1), custom_call_target="tpu_custom_call" | custom-call | tf_op jit(solution)/shard_map/prep/pallas_call | solution.py:71
  3.1 3.0 %collective-permute-start.1 = (bf16[14,32,128]{2,1,0:T(8,128)(2,1)S(1)}, bf16[14,32,128]{2,1,0:T(8,128)(2,1)S(1)}, u32[]{:S(2)}, u32[]{:S(2)}) collective-permute-start(bf16[14,32,128]{2,1,0:T(8,128)(2,1)S(1)} %get-tuple-element.10.refs_0_), channel_id=1, source_target_pairs={{0,2},{1,3},{2,0},{3,1},{4,6},{5,7},{6,4},{7,5},{8,10},{9,11},{10,... | collective-permute-start | bytes 344072 | tf_op jit(solution)/shard_map/ppermute | solution.py:293
  6.1 2.6 %collective-permute-start.5 = (bf16[14,32,128]{2,1,0:T(8,128)(2,1)S(1)}, bf16[14,32,128]{2,1,0:T(8,128)(2,1)S(1)}, u32[]{:S(2)}, u32[]{:S(2)}) collective-permute-start(bf16[14,32,128]{2,1,0:T(8,128)(2,1)S(1)} %get-tuple-element.13.refs_0_), channel_id=1, source_target_pairs={{0,8},{1,9},{2,10},{3,11},{4,12},{5,13},{6,14},{7,15},{8,0},{9,1},... | collective-permute-start | bytes 344072 | tf_op jit(solution)/shard_map/ppermute | solution.py:293
  8.7 0.0 collective-permute-start
  8.7 0.6 %collective-permute-done.1.refs_2_ = bf16[14,32,128]{2,1,0:T(8,128)(2,1)S(1)} collective-permute-done((bf16[14,32,128]{2,1,0:T(8,128)(2,1)S(1)}, bf16[14,32,128]{2,1,0:T(8,128)(2,1)S(1)}, u32[]{:S(2)}, u32[]{:S(2)}) %collective-permute-start.1) | collective-permute-done | bytes 114720 | tf_op jit(solution)/shard_map/ppermute | solution.py:293
  9.2 0.0 collective-permute-start.2
  9.2 1.8 %collective-permute-start.4 = (bf16[14,32,128]{2,1,0:T(8,128)(2,1)S(1)}, bf16[14,32,128]{2,1,0:T(8,128)(2,1)S(1)}, u32[]{:S(2)}, u32[]{:S(2)}) collective-permute-start(bf16[14,32,128]{2,1,0:T(8,128)(2,1)S(1)} %get-tuple-element.13.refs_0_), channel_id=1, source_target_pairs={{0,4},{1,5},{2,6},{3,7},{4,0},{5,1},{6,2},{7,3},{8,12},{9,13},{10,... | collective-permute-start | bytes 344072 | tf_op jit(solution)/shard_map/ppermute | solution.py:293
  11.0 3.1 %collective-permute-done.5.refs_2_ = bf16[14,32,128]{2,1,0:T(8,128)(2,1)S(1)} collective-permute-done((bf16[14,32,128]{2,1,0:T(8,128)(2,1)S(1)}, bf16[14,32,128]{2,1,0:T(8,128)(2,1)S(1)}, u32[]{:S(2)}, u32[]{:S(2)}) %collective-permute-start.5) | collective-permute-done | bytes 114720 | tf_op jit(solution)/shard_map/ppermute | solution.py:293
  14.2 0.6 %collective-permute-start.6 = (bf16[14,32,128]{2,1,0:T(8,128)(2,1)S(1)}, bf16[14,32,128]{2,1,0:T(8,128)(2,1)S(1)}, u32[]{:S(2)}, u32[]{:S(2)}) collective-permute-start(bf16[14,32,128]{2,1,0:T(8,128)(2,1)S(1)} %collective-permute-done.5.refs_2_), channel_id=1, source_target_pairs={{0,4},{1,5},{2,6},{3,7},{4,0},{5,1},{6,2},{7,3},{8,12},{9,13},{10,... | collective-permute-start | bytes 344072 | tf_op jit(solution)/shard_map/ppermute | solution.py:293
  14.7 0.0 collective-permute-done.refs_1_
  14.7 0.0 collective-permute-done.2.refs_3_
  14.7 0.4 %unpack_x.1 = (bf16[49,32,128]{2,1,0:T(8,128)(2,1)S(1)}, bf16[49,16,128]{2,1,0:T(8,128)(2,1)S(1)}) custom-call(bf16[14,32,128]{2,1,0:T(8,128)(2,1)S(1)} %get-tuple-element.10.refs_0_, bf16[14,32,128]{2,1,0:T(8,128)(2,1)S(1)} %collective-permute-done.refs_1_, bf16[14,32,128]{2,1,0:T(8,128)(2,1)S(1)} %collective-permute-done.1.refs_2_, ...), custom_call_target="tpu_custom_call" | custom-call | bytes 1048576 | tf_op jit(solution)/shard_map/unpack_x/pallas_call | solution.py:119
  15.2 1.6 %collective-permute-start.3 = (bf16[49,16,128]{2,1,0:T(8,128)(2,1)S(1)}, bf16[49,16,128]{2,1,0:T(8,128)(2,1)S(1)}, u32[]{:S(2)}, u32[]{:S(2)}) collective-permute-start(bf16[49,16,128]{2,1,0:T(8,128)(2,1)S(1)} %get-tuple-element.12.xp), channel_id=1, source_target_pairs={{0,16},{1,17},{2,18},{3,19},{4,20},{5,21},{6,22},{7,23},{8,24},{9,... | collective-permute-start | bytes 602120 | tf_op jit(solution)/shard_map/ppermute | solution.py:303
  16.7 2.2 %collective-permute-done.6.refs_3_ = bf16[14,32,128]{2,1,0:T(8,128)(2,1)S(1)} collective-permute-done((bf16[14,32,128]{2,1,0:T(8,128)(2,1)S(1)}, bf16[14,32,128]{2,1,0:T(8,128)(2,1)S(1)}, u32[]{:S(2)}, u32[]{:S(2)}) %collective-permute-start.6) | collective-permute-done | bytes 114720 | tf_op jit(solution)/shard_map/ppermute | solution.py:293
  19.0 0.4 %unpack_g.1 = (bf16[49,32,128]{2,1,0:T(8,128)(2,1)S(1)}, bf16[49,16,128]{2,1,0:T(8,128)(2,1)S(1)}) custom-call(bf16[14,32,128]{2,1,0:T(8,128)(2,1)S(1)} %get-tuple-element.13.refs_0_, bf16[14,32,128]{2,1,0:T(8,128)(2,1)S(1)} %collective-permute-done.4.refs_1_, bf16[14,32,128]{2,1,0:T(8,128)(2,1)S(1)} %collective-permute-done.5.refs_2_, ...), custom_call_target="tpu_custom_call" | custom-call | bytes 1048576 | tf_op jit(solution)/shard_map/unpack_g/pallas_call | solution.py:119
  19.4 1.6 %collective-permute-start.7 = (bf16[49,16,128]{2,1,0:T(8,128)(2,1)S(1)}, bf16[49,16,128]{2,1,0:T(8,128)(2,1)S(1)}, u32[]{:S(2)}, u32[]{:S(2)}) collective-permute-start(bf16[49,16,128]{2,1,0:T(8,128)(2,1)S(1)} %get-tuple-element.15.gp), channel_id=1, source_target_pairs={{0,16},{1,17},{2,18},{3,19},{4,20},{5,21},{6,22},{7,23},{8,24},{9,... | collective-permute-start | bytes 602120 | tf_op jit(solution)/shard_map/ppermute | solution.py:303
  21.0 3.0 %terms_own.1.own_ref = f32[32,128]{1,0:T(8,128)S(1)} custom-call(bf16[49,32,128]{2,1,0:T(8,128)(2,1)S(1)} %get-tuple-element.11.x, bf16[49,32,128]{2,1,0:T(8,128)(2,1)S(1)} %get-tuple-element.14.g, bf16[49,16,128]{2,1,0:T(8,128)(2,1)S(1)} %get-tuple-element.12.xp, bf16[49,16,128]{2,1,0:T(8,128)(2,1)S(1)} %get-tuple-element.15.gp), custom_call_target="tpu_custom_call" | custom-call | flops 12000000000 | bytes 4194304 | tf_op jit(solution)/shard_map/terms_own/pallas_call | solution.py:223
  24.0 0.0 collective-permute-done.3.xp
  24.0 2.0 %cross_inputs.1.t = f32[7,224,896]{2,1,0:T(8,128)S(1)} custom-call(bf16[49,32,128]{2,1,0:T(8,128)(2,1)S(1)} %get-tuple-element.11.x, bf16[49,16,128]{2,1,0:T(8,128)(2,1)S(1)} %collective-permute-done.3.xp), custom_call_target="tpu_custom_call" | custom-call | flops 6000000000 | bytes 4194304 | tf_op jit(solution)/shard_map/cross_inputs/pallas_call | solution.py:223
  26.0 0.1 collective-permute-done.7.gp
  26.1 1.6 %terms_cross.1 = (f32[8,128]{1,0:T(8,128)S(1)}, f32[1,32]{1,0:T(1,128)S(1)}) custom-call(f32[7,224,896]{2,1,0:T(8,128)S(1)} %cross_inputs.1.t, bf16[49,32,128]{2,1,0:T(8,128)(2,1)S(1)} %get-tuple-element.14.g, bf16[49,16,128]{2,1,0:T(8,128)(2,1)S(1)} %collective-permute-done.7.gp, f32[32,128]{1,0:T(8,128)S(1)} %terms_own.1.own_ref, f32[1,32]{1,0:T(1,128)S(1)} %bitcast.4), custom_call_target="tpu_custom_call" | custom-call | flops 6000000000 | bytes 4194304 | tf_op jit(solution)/shard_map/terms_cross/pallas_call | solution.py:223
  27.7 12.7 %all_to_all.5.terms_ref = f32[32,8,128]{2,1,0:T(8,128)S(1)} all-to-all(f32[32,8,128]{2,1,0:T(8,128)S(1)} %broadcast_in_dim.3), channel_id=1, replica_groups=mesh['rows'=2,'chan'=16] {'rows','chan'}, dimensions={0} | all-to-all | bytes 262144 | tf_op jit(solution)/shard_map/all_to_all | solution.py:321
  40.4 1.8 %solve.1 = (f32[32,32]{1,0:T(8,128)}, f32[32,32]{1,0:T(8,128)}) custom-call(f32[32,8,128]{2,1,0:T(8,128)S(1)} %all_to_all.5.terms_ref, f32[1,32]{1,0:T(1,128)S(1)} %get-tuple-element.17.ridge_ref), custom_call_target="tpu_custom_call" | custom-call | tf_op jit(solution)/shard_map/solve/pallas_call | solution.py:282
  (5 shorter events, 0.0 us)
Async XLA Ops:
  0.6 0.7 %copy-start = (s32[1,32]{1,0:T(1,128)S(1)}, s32[1,32]{1,0:T(1,128)}, u32[]{:S(2)}) copy-start(s32[1,32]{1,0:T(1,128)} %order_hbm.1) | copy-start | bytes 388
  3.1 6.2 %collective-permute-start.1 = (bf16[14,32,128]{2,1,0:T(8,128)(2,1)S(1)}, bf16[14,32,128]{2,1,0:T(8,128)(2,1)S(1)}, u32[]{:S(2)}, u32[]{:S(2)}) collective-permute-start(bf16[14,32,128]{2,1,0:T(8,128)(2,1)S(1)} %get-tuple-element.10.refs_0_), channel_id=1, source_target_pairs={{0,2},{1,3},{2,0},{3,1},{4,6},{5,7},{6,4},{7,5},{8,10},{9,11},{10,... | collective-permute-start | bytes 344072 | tf_op jit(solution)/shard_map/ppermute | solution.py:293
  6.1 8.1 %collective-permute-start.5 = (bf16[14,32,128]{2,1,0:T(8,128)(2,1)S(1)}, bf16[14,32,128]{2,1,0:T(8,128)(2,1)S(1)}, u32[]{:S(2)}, u32[]{:S(2)}) collective-permute-start(bf16[14,32,128]{2,1,0:T(8,128)(2,1)S(1)} %get-tuple-element.13.refs_0_), channel_id=1, source_target_pairs={{0,8},{1,9},{2,10},{3,11},{4,12},{5,13},{6,14},{7,15},{8,0},{9,1},... | collective-permute-start | bytes 344072 | tf_op jit(solution)/shard_map/ppermute | solution.py:293
  8.7 6.0 %collective-permute-start = (bf16[14,32,128]{2,1,0:T(8,128)(2,1)S(1)}, bf16[14,32,128]{2,1,0:T(8,128)(2,1)S(1)}, u32[]{:S(2)}, u32[]{:S(2)}) collective-permute-start(bf16[14,32,128]{2,1,0:T(8,128)(2,1)S(1)} %get-tuple-element.10.refs_0_), channel_id=1, source_target_pairs={{0,1},{1,0},{2,3},{3,2},{4,5},{5,4},{6,7},{7,6},{8,9},{9,8},{10,11... | collective-permute-start | bytes 344072 | tf_op jit(solution)/shard_map/ppermute | solution.py:293
  9.2 5.5 %collective-permute-start.2 = (bf16[14,32,128]{2,1,0:T(8,128)(2,1)S(1)}, bf16[14,32,128]{2,1,0:T(8,128)(2,1)S(1)}, u32[]{:S(2)}, u32[]{:S(2)}) collective-permute-start(bf16[14,32,128]{2,1,0:T(8,128)(2,1)S(1)} %collective-permute-done.1.refs_2_), channel_id=1, source_target_pairs={{0,1},{1,0},{2,3},{3,2},{4,5},{5,4},{6,7},{7,6},{8,9},{9,8},{10,11... | collective-permute-start | bytes 344072 | tf_op jit(solution)/shard_map/ppermute | solution.py:293
  9.2 7.5 %collective-permute-start.4 = (bf16[14,32,128]{2,1,0:T(8,128)(2,1)S(1)}, bf16[14,32,128]{2,1,0:T(8,128)(2,1)S(1)}, u32[]{:S(2)}, u32[]{:S(2)}) collective-permute-start(bf16[14,32,128]{2,1,0:T(8,128)(2,1)S(1)} %get-tuple-element.13.refs_0_), channel_id=1, source_target_pairs={{0,4},{1,5},{2,6},{3,7},{4,0},{5,1},{6,2},{7,3},{8,12},{9,13},{10,... | collective-permute-start | bytes 344072 | tf_op jit(solution)/shard_map/ppermute | solution.py:293
  14.2 4.8 %collective-permute-start.6 = (bf16[14,32,128]{2,1,0:T(8,128)(2,1)S(1)}, bf16[14,32,128]{2,1,0:T(8,128)(2,1)S(1)}, u32[]{:S(2)}, u32[]{:S(2)}) collective-permute-start(bf16[14,32,128]{2,1,0:T(8,128)(2,1)S(1)} %collective-permute-done.5.refs_2_), channel_id=1, source_target_pairs={{0,4},{1,5},{2,6},{3,7},{4,0},{5,1},{6,2},{7,3},{8,12},{9,13},{10,... | collective-permute-start | bytes 344072 | tf_op jit(solution)/shard_map/ppermute | solution.py:293
  15.2 8.8 %collective-permute-start.3 = (bf16[49,16,128]{2,1,0:T(8,128)(2,1)S(1)}, bf16[49,16,128]{2,1,0:T(8,128)(2,1)S(1)}, u32[]{:S(2)}, u32[]{:S(2)}) collective-permute-start(bf16[49,16,128]{2,1,0:T(8,128)(2,1)S(1)} %get-tuple-element.12.xp), channel_id=1, source_target_pairs={{0,16},{1,17},{2,18},{3,19},{4,20},{5,21},{6,22},{7,23},{8,24},{9,... | collective-permute-start | bytes 602120 | tf_op jit(solution)/shard_map/ppermute | solution.py:303
  19.4 6.7 %collective-permute-start.7 = (bf16[49,16,128]{2,1,0:T(8,128)(2,1)S(1)}, bf16[49,16,128]{2,1,0:T(8,128)(2,1)S(1)}, u32[]{:S(2)}, u32[]{:S(2)}) collective-permute-start(bf16[49,16,128]{2,1,0:T(8,128)(2,1)S(1)} %get-tuple-element.15.gp), channel_id=1, source_target_pairs={{0,16},{1,17},{2,18},{3,19},{4,20},{5,21},{6,22},{7,23},{8,24},{9,... | collective-permute-start | bytes 602120 | tf_op jit(solution)/shard_map/ppermute | solution.py:303
  24.0 2.1 %copy-start.1 = (f32[32]{0:T(128)S(1)}, f32[32]{0:T(128)}, u32[]{:S(2)}) copy-start(f32[32]{0:T(128)} %param.7) | copy-start | bytes 388

commit v7 on v6

--- a/solution.py
+++ b/solution.py
@@ -189,13 +189,12 @@
     return acc + pltpu.roll(acc, 16, 1)
 
 
-def own_kernel(x, g, xp, gp, out_ref, lx, rx, lg, rg, t):
-    input_products([x], xp, lx, rx, t)
+def products_kernel(x, xp, t_out, lx, rx):
+    input_products([x], xp, lx, rx, t_out)
+
+
+def own_kernel(t, g, gp, out_ref, lg, rg):
     out_ref[...] = panel_terms([g], gp, lg, rg, t)
-
-
-def cross_inputs_kernel(x, xp, t_out, lx, rx):
-    input_products([x], xp, lx, rx, t_out)
 
 
 def cross_kernel(t, g, gp, own_ref, ridge, out_ref, ridge_out, lg, rg):
@@ -312,13 +311,12 @@
     g_cross = exchange_across(g_piv, count)
     wide, narrow = scratch_of(EX, 3 * LANES), scratch_of(EX, LANES)
     shape, flops = product_shape(EX), 6 * 10**9
-    arrays = (x_all, g_all, x_piv, g_piv)
-    own_term, = terms(own_kernel, arrays, ((EX, LANES),), wide + narrow + [pltpu.VMEM(shape, F32)], 2 * flops, "terms_own")
-    products, = terms(cross_inputs_kernel, (x_all, x_cross), (shape,), wide, flops, "cross_inputs")
+    products, = terms(products_kernel, (x_all, x_piv), (shape,), wide, flops, "own_inputs")
+    own_term, = terms(own_kernel, (products, g_all, g_piv), ((EX, LANES),), narrow, flops, "terms_own")
+    products, = terms(products_kernel, (x_all, x_cross), (shape,), wide, flops, "cross_inputs")
     arrays = (products, g_all, g_cross, own_term, ridge.reshape(1, EX))
     term, ridge = terms(cross_kernel, arrays, ((8, LANES), (1, EX)), narrow, flops, "terms_cross")
-    copies = jnp.broadcast_to(term, (2 * count, 8, LANES))
-    return final(lax.all_to_all(copies, ("rows", "chan"), 0, 0), ridge)
+    return final(lax.all_gather(term, ("rows", "chan")), ridge)
 
 
 def jacobian_block(grad_rows, input_rows):

time: 42.4 us -> 70.3 us (1.66)
  blocking collectives: 12.7 us -> 40.6 us
    all_gather x0 -> x1, blocking collectives: none -> 40.6 us  [local_packed(): return final(lax.all_gather(term, ('rows', 'chan')), ridge)]
    all_to_all x1 -> x0, blocking collectives: 12.7 us -> none  [local_packed(): return final(lax.all_to_all(copies, ('rows', 'chan'), 0, 0), ridge)]
    ppermute x6, waiting for transfers between devices: 5.89 us -> 3.85 us  [exchange(): return lax.ppermute(value, 'chan', [(i, i ^ flip) for i in range(count)])]
    ppermute x2, waiting for transfers between devices: 0.09 us -> 1.48 us  [exchange_across(): return lax.ppermute(value, ('rows', 'chan'), pairs)]
    pallas_call x3 -> x4, Pallas kernels: 6.62 us -> 7.27 us  [terms(): pl.pallas_call(kernel, out_shape=tuple((jax.ShapeDtypeStruct(shape, F32)...]
  transfers between devices with their start and end apart: 8 -> 8, of which waited for: 4 -> 4; matrix products, arithmetic and copies ran while one was open for 0% -> 0% of each run, Pallas kernels for 14% -> 9%
where the time goes in v7:
time: 70.3 us; the launch traced here: 70.1 us
  blocking collectives  40.6 us (58%)
  Pallas kernels  11.8 us (17%)
  starting transfers between devices  11.1 us (16%)
  waiting for transfers between devices  5.33 us (8%)
    all_gather x1, blocking collectives, local_packed(): return final(lax.all_gather(term, ('rows', 'chan')), ridge)  40.6 us
    ppermute x6, starting transfers between devices, exchange(): return lax.ppermute(value, 'chan', [(i, i ^ flip) for i in range(count)])  7.99 us
    pallas_call x4, Pallas kernels, terms(): pl.pallas_call(kernel, out_shape=tuple((jax.ShapeDtypeStruct(shape, F32)...  7.27 us
    ppermute x6, waiting for transfers between devices, exchange(): return lax.ppermute(value, 'chan', [(i, i ^ flip) for i in range(count)])  3.85 us
    ppermute x2, starting transfers between devices, exchange_across(): return lax.ppermute(value, ('rows', 'chan'), pairs)  3.11 us
    pallas_call x1, Pallas kernels, final(): pl.pallas_call(final_kernel, out_shape=(out, out), in_specs=[vmem] * 2, o...  1.85 us
    pallas_call x1, Pallas kernels, prep(): pl.pallas_call(prep_kernel, out_shape=(full, full), in_specs=[pl.BlockSpe...  1.76 us
    ppermute x2, waiting for transfers between devices, exchange_across(): return lax.ppermute(value, ('rows', 'chan'), pairs)  1.48 us
  transfers between devices with their start and end apart: 8, of which 4 were waited for; matrix products, arithmetic and copies ran while one was open for 0% of the time, Pallas kernels for 9%

profile of v7, /device:TPU:0, one launch (start us, length us, event | category | flops | bytes accessed | tf_op | source)
XLA Modules:
  0.0 70.1 jit_solution(7134778331851268139)
XLA Ops:
  0.6 0.6 copy-done
  1.3 1.8 %prep.1 = (bf16[14,32,128]{2,1,0:T(8,128)(2,1)S(1)}, bf16[14,32,128]{2,1,0:T(8,128)(2,1)S(1)}) custom-call(s32[1,32]{1,0:T(1,128)S(1)} %copy-done, bf16[49,32,32]{2,1,0:T(8,128)(2,1)} %bitcast.7, bf16[32,32,49]{2,1,0:T(8,128)(2,1)} %g_hbm.1), custom_call_target="tpu_custom_call" | custom-call | tf_op jit(solution)/shard_map/prep/pallas_call | solution.py:71
  3.1 3.0 %collective-permute-start.1 = (bf16[14,32,128]{2,1,0:T(8,128)(2,1)S(1)}, bf16[14,32,128]{2,1,0:T(8,128)(2,1)S(1)}, u32[]{:S(2)}, u32[]{:S(2)}) collective-permute-start(bf16[14,32,128]{2,1,0:T(8,128)(2,1)S(1)} %get-tuple-element.10.refs_0_), channel_id=1, source_target_pairs={{0,2},{1,3},{2,0},{3,1},{4,6},{5,7},{6,4},{7,5},{8,10},{9,11},{10,... | collective-permute-start | bytes 344072 | tf_op jit(solution)/shard_map/ppermute | solution.py:292
  6.1 2.6 %collective-permute-start.5 = (bf16[14,32,128]{2,1,0:T(8,128)(2,1)S(1)}, bf16[14,32,128]{2,1,0:T(8,128)(2,1)S(1)}, u32[]{:S(2)}, u32[]{:S(2)}) collective-permute-start(bf16[14,32,128]{2,1,0:T(8,128)(2,1)S(1)} %get-tuple-element.13.refs_0_), channel_id=1, source_target_pairs={{0,8},{1,9},{2,10},{3,11},{4,12},{5,13},{6,14},{7,15},{8,0},{9,1},... | collective-permute-start | bytes 344072 | tf_op jit(solution)/shard_map/ppermute | solution.py:292
  8.7 0.6 collective-permute-done.1.refs_2_
  9.2 0.0 collective-permute-start.2
  9.2 1.8 %collective-permute-start.4 = (bf16[14,32,128]{2,1,0:T(8,128)(2,1)S(1)}, bf16[14,32,128]{2,1,0:T(8,128)(2,1)S(1)}, u32[]{:S(2)}, u32[]{:S(2)}) collective-permute-start(bf16[14,32,128]{2,1,0:T(8,128)(2,1)S(1)} %get-tuple-element.13.refs_0_), channel_id=1, source_target_pairs={{0,4},{1,5},{2,6},{3,7},{4,0},{5,1},{6,2},{7,3},{8,12},{9,13},{10,... | collective-permute-start | bytes 344072 | tf_op jit(solution)/shard_map/ppermute | solution.py:292
  11.0 3.1 %collective-permute-done.5.refs_2_ = bf16[14,32,128]{2,1,0:T(8,128)(2,1)S(1)} collective-permute-done((bf16[14,32,128]{2,1,0:T(8,128)(2,1)S(1)}, bf16[14,32,128]{2,1,0:T(8,128)(2,1)S(1)}, u32[]{:S(2)}, u32[]{:S(2)}) %collective-permute-start.5) | collective-permute-done | bytes 114720 | tf_op jit(solution)/shard_map/ppermute | solution.py:292
  14.2 0.6 collective-permute-start.6
  14.7 0.0 collective-permute-done.refs_1_
  14.7 0.0 collective-permute-done.2.refs_3_
  14.7 0.4 unpack_x.1
  15.2 1.6 %collective-permute-start.3 = (bf16[49,16,128]{2,1,0:T(8,128)(2,1)S(1)}, bf16[49,16,128]{2,1,0:T(8,128)(2,1)S(1)}, u32[]{:S(2)}, u32[]{:S(2)}) collective-permute-start(bf16[49,16,128]{2,1,0:T(8,128)(2,1)S(1)} %get-tuple-element.12.xp), channel_id=1, source_target_pairs={{0,16},{1,17},{2,18},{3,19},{4,20},{5,21},{6,22},{7,23},{8,24},{9,... | collective-permute-start | bytes 602120 | tf_op jit(solution)/shard_map/ppermute | solution.py:302
  16.7 2.0 %own_inputs.1.t = f32[7,224,896]{2,1,0:T(8,128)S(1)} custom-call(bf16[49,32,128]{2,1,0:T(8,128)(2,1)S(1)} %get-tuple-element.11.x, bf16[49,16,128]{2,1,0:T(8,128)(2,1)S(1)} %get-tuple-element.12.xp), custom_call_target="tpu_custom_call" | custom-call | flops 6000000000 | bytes 4194304 | tf_op jit(solution)/shard_map/own_inputs/pallas_call | solution.py:222
  18.8 0.2 collective-permute-done.6.refs_3_
  19.0 0.4 unpack_g.1
  19.4 1.6 %collective-permute-start.7 = (bf16[49,16,128]{2,1,0:T(8,128)(2,1)S(1)}, bf16[49,16,128]{2,1,0:T(8,128)(2,1)S(1)}, u32[]{:S(2)}, u32[]{:S(2)}) collective-permute-start(bf16[49,16,128]{2,1,0:T(8,128)(2,1)S(1)} %get-tuple-element.15.gp), channel_id=1, source_target_pairs={{0,16},{1,17},{2,18},{3,19},{4,20},{5,21},{6,22},{7,23},{8,24},{9,... | collective-permute-start | bytes 602120 | tf_op jit(solution)/shard_map/ppermute | solution.py:302
  21.0 1.6 %terms_own.1.own_ref = f32[32,128]{1,0:T(8,128)S(1)} custom-call(f32[7,224,896]{2,1,0:T(8,128)S(1)} %own_inputs.1.t, bf16[49,32,128]{2,1,0:T(8,128)(2,1)S(1)} %get-tuple-element.14.g, bf16[49,16,128]{2,1,0:T(8,128)(2,1)S(1)} %get-tuple-element.15.gp), custom_call_target="tpu_custom_call" | custom-call | flops 6000000000 | bytes 4194304 | tf_op jit(solution)/shard_map/terms_own/pallas_call | solution.py:222
  22.5 0.0 collective-permute-done.3.xp
  22.6 2.1 %cross_inputs.1.t = f32[7,224,896]{2,1,0:T(8,128)S(1)} custom-call(bf16[49,32,128]{2,1,0:T(8,128)(2,1)S(1)} %get-tuple-element.11.x, bf16[49,16,128]{2,1,0:T(8,128)(2,1)S(1)} %collective-permute-done.3.xp), custom_call_target="tpu_custom_call" | custom-call | flops 6000000000 | bytes 4194304 | tf_op jit(solution)/shard_map/cross_inputs/pallas_call | solution.py:222
  24.6 1.5 %collective-permute-done.7.gp = bf16[49,16,128]{2,1,0:T(8,128)(2,1)S(1)} collective-permute-done((bf16[49,16,128]{2,1,0:T(8,128)(2,1)S(1)}, bf16[49,16,128]{2,1,0:T(8,128)(2,1)S(1)}, u32[]{:S(2)}, u32[]{:S(2)}) %collective-permute-start.7) | collective-permute-done | bytes 200736 | tf_op jit(solution)/shard_map/ppermute | solution.py:302
  26.1 1.6 %terms_cross.1 = (f32[8,128]{1,0:T(8,128)S(1)}, f32[1,32]{1,0:T(1,128)S(1)}) custom-call(f32[7,224,896]{2,1,0:T(8,128)S(1)} %cross_inputs.1.t, bf16[49,32,128]{2,1,0:T(8,128)(2,1)S(1)} %get-tuple-element.14.g, bf16[49,16,128]{2,1,0:T(8,128)(2,1)S(1)} %collective-permute-done.7.gp, f32[32,128]{1,0:T(8,128)S(1)} %terms_own.1.own_ref, f32[1,32]{1,0:T(1,128)S(1)} %bitcast.6), custom_call_target="tpu_custom_call" | custom-call | flops 6000000000 | bytes 4194304 | tf_op jit(solution)/shard_map/terms_cross/pallas_call | solution.py:222
  27.7 40.6 %all-gather = f32[256,128]{1,0:T(8,128)S(1)} all-gather(f32[8,128]{1,0:T(8,128)S(1)} %get-tuple-element.16), channel_id=2, replica_groups=mesh['rows'=2,'chan'=16] {'rows','chan'}, dimensions={0}, use_global_device_ids=true | all-gather | bytes 135168 | tf_op jit(solution)/shard_map/all_gather | solution.py:319
  68.3 1.8 %solve.1 = (f32[32,32]{1,0:T(8,128)}, f32[32,32]{1,0:T(8,128)}) custom-call(f32[32,8,128]{2,1,0:T(8,128)S(1)} %bitcast.5, f32[1,32]{1,0:T(1,128)S(1)} %get-tuple-element.17.ridge_ref), custom_call_target="tpu_custom_call" | custom-call | tf_op jit(solution)/shard_map/solve/pallas_call | solution.py:281
  (5 shorter events, 0.0 us)
Async XLA Ops:
  0.6 0.7 copy-start
  3.1 6.2 %collective-permute-start.1 = (bf16[14,32,128]{2,1,0:T(8,128)(2,1)S(1)}, bf16[14,32,128]{2,1,0:T(8,128)(2,1)S(1)}, u32[]{:S(2)}, u32[]{:S(2)}) collective-permute-start(bf16[14,32,128]{2,1,0:T(8,128)(2,1)S(1)} %get-tuple-element.10.refs_0_), channel_id=1, source_target_pairs={{0,2},{1,3},{2,0},{3,1},{4,6},{5,7},{6,4},{7,5},{8,10},{9,11},{10,... | collective-permute-start | bytes 344072 | tf_op jit(solution)/shard_map/ppermute | solution.py:292
  6.1 8.1 %collective-permute-start.5 = (bf16[14,32,128]{2,1,0:T(8,128)(2,1)S(1)}, bf16[14,32,128]{2,1,0:T(8,128)(2,1)S(1)}, u32[]{:S(2)}, u32[]{:S(2)}) collective-permute-start(bf16[14,32,128]{2,1,0:T(8,128)(2,1)S(1)} %get-tuple-element.13.refs_0_), channel_id=1, source_target_pairs={{0,8},{1,9},{2,10},{3,11},{4,12},{5,13},{6,14},{7,15},{8,0},{9,1},... | collective-permute-start | bytes 344072 | tf_op jit(solution)/shard_map/ppermute | solution.py:292
  8.7 6.0 %collective-permute-start = (bf16[14,32,128]{2,1,0:T(8,128)(2,1)S(1)}, bf16[14,32,128]{2,1,0:T(8,128)(2,1)S(1)}, u32[]{:S(2)}, u32[]{:S(2)}) collective-permute-start(bf16[14,32,128]{2,1,0:T(8,128)(2,1)S(1)} %get-tuple-element.10.refs_0_), channel_id=1, source_target_pairs={{0,1},{1,0},{2,3},{3,2},{4,5},{5,4},{6,7},{7,6},{8,9},{9,8},{10,11... | collective-permute-start | bytes 344072 | tf_op jit(solution)/shard_map/ppermute | solution.py:292
  9.2 5.5 %collective-permute-start.2 = (bf16[14,32,128]{2,1,0:T(8,128)(2,1)S(1)}, bf16[14,32,128]{2,1,0:T(8,128)(2,1)S(1)}, u32[]{:S(2)}, u32[]{:S(2)}) collective-permute-start(bf16[14,32,128]{2,1,0:T(8,128)(2,1)S(1)} %collective-permute-done.1.refs_2_), channel_id=1, source_target_pairs={{0,1},{1,0},{2,3},{3,2},{4,5},{5,4},{6,7},{7,6},{8,9},{9,8},{10,11... | collective-permute-start | bytes 344072 | tf_op jit(solution)/shard_map/ppermute | solution.py:292
  9.2 9.5 %collective-permute-start.4 = (bf16[14,32,128]{2,1,0:T(8,128)(2,1)S(1)}, bf16[14,32,128]{2,1,0:T(8,128)(2,1)S(1)}, u32[]{:S(2)}, u32[]{:S(2)}) collective-permute-start(bf16[14,32,128]{2,1,0:T(8,128)(2,1)S(1)} %get-tuple-element.13.refs_0_), channel_id=1, source_target_pairs={{0,4},{1,5},{2,6},{3,7},{4,0},{5,1},{6,2},{7,3},{8,12},{9,13},{10,... | collective-permute-start | bytes 344072 | tf_op jit(solution)/shard_map/ppermute | solution.py:292
  14.2 4.8 %collective-permute-start.6 = (bf16[14,32,128]{2,1,0:T(8,128)(2,1)S(1)}, bf16[14,32,128]{2,1,0:T(8,128)(2,1)S(1)}, u32[]{:S(2)}, u32[]{:S(2)}) collective-permute-start(bf16[14,32,128]{2,1,0:T(8,128)(2,1)S(1)} %collective-permute-done.5.refs_2_), channel_id=1, source_target_pairs={{0,4},{1,5},{2,6},{3,7},{4,0},{5,1},{6,2},{7,3},{8,12},{9,13},{10,... | collective-permute-start | bytes 344072 | tf_op jit(solution)/shard_map/ppermute | solution.py:292
  15.2 7.4 %collective-permute-start.3 = (bf16[49,16,128]{2,1,0:T(8,128)(2,1)S(1)}, bf16[49,16,128]{2,1,0:T(8,128)(2,1)S(1)}, u32[]{:S(2)}, u32[]{:S(2)}) collective-permute-start(bf16[49,16,128]{2,1,0:T(8,128)(2,1)S(1)} %get-tuple-element.12.xp), channel_id=1, source_target_pairs={{0,16},{1,17},{2,18},{3,19},{4,20},{5,21},{6,22},{7,23},{8,24},{9,... | collective-permute-start | bytes 602120 | tf_op jit(solution)/shard_map/ppermute | solution.py:302
  19.4 6.7 %collective-permute-start.7 = (bf16[49,16,128]{2,1,0:T(8,128)(2,1)S(1)}, bf16[49,16,128]{2,1,0:T(8,128)(2,1)S(1)}, u32[]{:S(2)}, u32[]{:S(2)}) collective-permute-start(bf16[49,16,128]{2,1,0:T(8,128)(2,1)S(1)} %get-tuple-element.15.gp), channel_id=1, source_target_pairs={{0,16},{1,17},{2,18},{3,19},{4,20},{5,21},{6,22},{7,23},{8,24},{9,... | collective-permute-start | bytes 602120 | tf_op jit(solution)/shard_map/ppermute | solution.py:302
  22.5 3.6 %copy-start.1 = (f32[32]{0:T(128)S(1)}, f32[32]{0:T(128)}, u32[]{:S(2)}) copy-start(f32[32]{0:T(128)} %param.7) | copy-start | bytes 388

commit v8 on v7

--- a/solution.py
+++ b/solution.py
@@ -96,7 +96,7 @@
 
 
 def unpack_kernel(*refs):
-    packed, all_ref, piv_ref = refs[:4], refs[4], refs[5]
+    packed, (all_ref, piv_ref) = refs[:4], refs[-2:]
     row = lax.broadcasted_iota(jnp.int32, (4 * LANES, 4 * LANES), 0)
     col = lax.broadcasted_iota(jnp.int32, (4 * LANES, 4 * LANES), 1)
     target = (row // CH) % 4 * LANES + row // LANES * CH + row % CH
@@ -113,18 +113,18 @@
             piv_ref[py * SIDE + px] = spot[:PIV_DEV]
 
 
-def unpack(arrays, name):
+def unpack(arrays, name, after=()):
     vmem = pl.BlockSpec(memory_space=pltpu.VMEM)
     pivots = jax.ShapeDtypeStruct((SPOTS, PIV_DEV, LANES), BF16)
     return pl.pallas_call(
         unpack_kernel,
         out_shape=(jax.ShapeDtypeStruct((SPOTS, EX, LANES), BF16), pivots),
-        in_specs=[vmem] * 4,
+        in_specs=[vmem] * 4 + [pl.BlockSpec(memory_space=pl.ANY)] * len(after),
         out_specs=(vmem,) * 2,
         compiler_params=pltpu.CompilerParams(vmem_limit_bytes=12 << 20),
         cost_estimate=cost(0, 1 << 20),
         name=name,
-    )(*arrays)
+    )(*arrays, *after)
 
 
 CONTRACT = (((1,), (1,)), ((), ()))
@@ -305,9 +305,10 @@
 def local_packed(count, activations, cotangents, ordering, ridge):
     x = jnp.transpose(activations, (1, 2, 0, 3)).reshape(SIDE * SIDE, EX, CH)
     xo, go = prep(ordering, x, cotangents)
-    x_all, x_piv = unpack(gather(xo, count, 2, 1), "unpack_x")
+    own_g = gather(go, count, 8, 4)
+    x_all, x_piv = unpack(gather(xo, count, 2, 1), "unpack_x", (own_g[1],))
     x_cross = exchange_across(x_piv, count)
-    g_all, g_piv = unpack(gather(go, count, 8, 4), "unpack_g")
+    g_all, g_piv = unpack(own_g, "unpack_g")
     g_cross = exchange_across(g_piv, count)
     wide, narrow = scratch_of(EX, 3 * LANES), scratch_of(EX, LANES)
     shape, flops = product_shape(EX), 6 * 10**9
@@ -316,7 +317,8 @@
     products, = terms(products_kernel, (x_all, x_cross), (shape,), wide, flops, "cross_inputs")
     arrays = (products, g_all, g_cross, own_term, ridge.reshape(1, EX))
     term, ridge = terms(cross_kernel, arrays, ((8, LANES), (1, EX)), narrow, flops, "terms_cross")
-    return final(lax.all_gather(term, ("rows", "chan")), ridge)
+    copies = jnp.broadcast_to(term, (2 * count, 8, LANES))
+    return final(lax.all_to_all(copies, ("rows", "chan"), 0, 0), ridge)
 
 
 def jacobian_block(grad_rows, input_rows):

time: 70.3 us -> 42.4 us (0.60)
  blocking collectives: 40.6 us -> 12.7 us
    all_gather x1 -> x0, blocking collectives: 40.6 us -> none  [local_packed(): return final(lax.all_gather(term, ('rows', 'chan')), ridge)]
    all_to_all x0 -> x1, blocking collectives: none -> 12.7 us  [local_packed(): return final(lax.all_to_all(copies, ('rows', 'chan'), 0, 0), ridge)]
  transfers between devices with their start and end apart: 8 -> 8, of which waited for: 4 -> 3; matrix products, arithmetic and copies ran while one was open for 0% -> 0% of each run, Pallas kernels for 9% -> 15%
where the time goes in v8:
time: 42.4 us; the launch traced here: 42.2 us
  blocking collectives  12.7 us (30%)
  Pallas kernels  11.7 us (28%)
  starting transfers between devices  11.5 us (27%)
  waiting for transfers between devices  4.95 us (12%)
  between operations  0.69 us (2%)
  local copies, waits for them, and re-layouts  0.67 us (2%)
    all_to_all x1, blocking collectives, local_packed(): return final(lax.all_to_all(copies, ('rows', 'chan'), 0, 0), ridge)  12.7 us
    ppermute x6, starting transfers between devices, exchange(): return lax.ppermute(value, 'chan', [(i, i ^ flip) for i in range(count)])  8.36 us
    pallas_call x4, Pallas kernels, terms(): pl.pallas_call(kernel, out_shape=tuple((jax.ShapeDtypeStruct(shape, F32)...  7.23 us
    ppermute x6, waiting for transfers between devices, exchange(): return lax.ppermute(value, 'chan', [(i, i ^ flip) for i in range(count)])  3.41 us
    ppermute x2, starting transfers between devices, exchange_across(): return lax.ppermute(value, ('rows', 'chan'), pairs)  3.11 us
    pallas_call x1, Pallas kernels, final(): pl.pallas_call(final_kernel, out_shape=(out, out), in_specs=[vmem] * 2, o...  1.85 us
    pallas_call x1, Pallas kernels, prep(): pl.pallas_call(prep_kernel, out_shape=(full, full), in_specs=[pl.BlockSpe...  1.76 us
    ppermute x2, waiting for transfers between devices, exchange_across(): return lax.ppermute(value, ('rows', 'chan'), pairs)  1.54 us
  transfers between devices with their start and end apart: 8, of which 3 were waited for; matrix products, arithmetic and copies ran while one was open for 0% of the time, Pallas kernels for 15%

profile of v8, /device:TPU:0, one launch (start us, length us, event | category | flops | bytes accessed | tf_op | source)
XLA Modules:
  0.0 42.2 jit_solution(14680874699430467150)
XLA Ops:
  0.6 0.6 %copy-done = s32[1,32]{1,0:T(1,128)S(1)} copy-done((s32[1,32]{1,0:T(1,128)S(1)}, s32[1,32]{1,0:T(1,128)}, u32[]{:S(2)}) %copy-start) | copy-done | bytes 152
  1.3 1.8 %prep.1 = (bf16[14,32,128]{2,1,0:T(8,128)(2,1)S(1)}, bf16[14,32,128]{2,1,0:T(8,128)(2,1)S(1)}) custom-call(s32[1,32]{1,0:T(1,128)S(1)} %copy-done, bf16[49,32,32]{2,1,0:T(8,128)(2,1)} %bitcast.5, bf16[32,32,49]{2,1,0:T(8,128)(2,1)} %g_hbm.1), custom_call_target="tpu_custom_call" | custom-call | tf_op jit(solution)/shard_map/prep/pallas_call | solution.py:71
  3.1 3.0 %collective-permute-start.1 = (bf16[14,32,128]{2,1,0:T(8,128)(2,1)S(1)}, bf16[14,32,128]{2,1,0:T(8,128)(2,1)S(1)}, u32[]{:S(2)}, u32[]{:S(2)}) collective-permute-start(bf16[14,32,128]{2,1,0:T(8,128)(2,1)S(1)} %get-tuple-element.10.refs_0_), channel_id=1, source_target_pairs={{0,2},{1,3},{2,0},{3,1},{4,6},{5,7},{6,4},{7,5},{8,10},{9,11},{10,... | collective-permute-start | bytes 344072 | tf_op jit(solution)/shard_map/ppermute | solution.py:292
  6.1 2.6 %collective-permute-start.5 = (bf16[14,32,128]{2,1,0:T(8,128)(2,1)S(1)}, bf16[14,32,128]{2,1,0:T(8,128)(2,1)S(1)}, u32[]{:S(2)}, u32[]{:S(2)}) collective-permute-start(bf16[14,32,128]{2,1,0:T(8,128)(2,1)S(1)} %get-tuple-element.11.refs_0_), channel_id=1, source_target_pairs={{0,8},{1,9},{2,10},{3,11},{4,12},{5,13},{6,14},{7,15},{8,0},{9,1},... | collective-permute-start | bytes 344072 | tf_op jit(solution)/shard_map/ppermute | solution.py:292
  8.7 1.6 %collective-permute-start.3 = (bf16[14,32,128]{2,1,0:T(8,128)(2,1)S(1)}, bf16[14,32,128]{2,1,0:T(8,128)(2,1)S(1)}, u32[]{:S(2)}, u32[]{:S(2)}) collective-permute-start(bf16[14,32,128]{2,1,0:T(8,128)(2,1)S(1)} %get-tuple-element.11.refs_0_), channel_id=1, source_target_pairs={{0,4},{1,5},{2,6},{3,7},{4,0},{5,1},{6,2},{7,3},{8,12},{9,13},{10,... | collective-permute-start | bytes 344072 | tf_op jit(solution)/shard_map/ppermute | solution.py:292
  10.3 0.0 collective-permute-start
  10.3 0.0 collective-permute-done.1.refs_2_
  10.3 0.5 %collective-permute-start.2 = (bf16[14,32,128]{2,1,0:T(8,128)(2,1)S(1)}, bf16[14,32,128]{2,1,0:T(8,128)(2,1)S(1)}, u32[]{:S(2)}, u32[]{:S(2)}) collective-permute-start(bf16[14,32,128]{2,1,0:T(8,128)(2,1)S(1)} %collective-permute-done.1.refs_2_), channel_id=1, source_target_pairs={{0,1},{1,0},{2,3},{3,2},{4,5},{5,4},{6,7},{7,6},{8,9},{9,8},{10,11... | collective-permute-start | bytes 344072 | tf_op jit(solution)/shard_map/ppermute | solution.py:292
  10.8 3.3 %collective-permute-done.5.refs_2_ = bf16[14,32,128]{2,1,0:T(8,128)(2,1)S(1)} collective-permute-done((bf16[14,32,128]{2,1,0:T(8,128)(2,1)S(1)}, bf16[14,32,128]{2,1,0:T(8,128)(2,1)S(1)}, u32[]{:S(2)}, u32[]{:S(2)}) %collective-permute-start.5) | collective-permute-done | bytes 114720 | tf_op jit(solution)/shard_map/ppermute | solution.py:292
  14.1 0.7 %collective-permute-start.6 = (bf16[14,32,128]{2,1,0:T(8,128)(2,1)S(1)}, bf16[14,32,128]{2,1,0:T(8,128)(2,1)S(1)}, u32[]{:S(2)}, u32[]{:S(2)}) collective-permute-start(bf16[14,32,128]{2,1,0:T(8,128)(2,1)S(1)} %collective-permute-done.5.refs_2_), channel_id=1, source_target_pairs={{0,4},{1,5},{2,6},{3,7},{4,0},{5,1},{6,2},{7,3},{8,12},{9,13},{10,... | collective-permute-start | bytes 344072 | tf_op jit(solution)/shard_map/ppermute | solution.py:292
  14.7 0.0 collective-permute-done.3.refs_4_.refs_1_
  14.7 0.4 %unpack_x.1 = (bf16[49,32,128]{2,1,0:T(8,128)(2,1)S(1)}, bf16[49,16,128]{2,1,0:T(8,128)(2,1)S(1)}) custom-call(bf16[14,32,128]{2,1,0:T(8,128)(2,1)S(1)} %get-tuple-element.10.refs_0_, bf16[14,32,128]{2,1,0:T(8,128)(2,1)S(1)} %collective-permute-done.refs_1_, bf16[14,32,128]{2,1,0:T(8,128)(2,1)S(1)} %collective-permute-done.1.refs_2_, ...), custom_call_target="tpu_custom_call" | custom-call | bytes 1048576 | tf_op jit(solution)/shard_map/unpack_x/pallas_call | solution.py:119
  15.2 1.6 %collective-permute-start.4 = (bf16[49,16,128]{2,1,0:T(8,128)(2,1)S(1)}, bf16[49,16,128]{2,1,0:T(8,128)(2,1)S(1)}, u32[]{:S(2)}, u32[]{:S(2)}) collective-permute-start(bf16[49,16,128]{2,1,0:T(8,128)(2,1)S(1)} %get-tuple-element.13.xp), channel_id=1, source_target_pairs={{0,16},{1,17},{2,18},{3,19},{4,20},{5,21},{6,22},{7,23},{8,24},{9,... | collective-permute-start | bytes 602120 | tf_op jit(solution)/shard_map/ppermute | solution.py:302
  16.7 2.0 %own_inputs.1.t = f32[7,224,896]{2,1,0:T(8,128)S(1)} custom-call(bf16[49,32,128]{2,1,0:T(8,128)(2,1)S(1)} %get-tuple-element.12.x, bf16[49,16,128]{2,1,0:T(8,128)(2,1)S(1)} %get-tuple-element.13.xp), custom_call_target="tpu_custom_call" | custom-call | flops 6000000000 | bytes 4194304 | tf_op jit(solution)/shard_map/own_inputs/pallas_call | solution.py:222
  18.8 0.1 collective-permute-done.6.refs_3_
  18.9 0.4 %unpack_g.1 = (bf16[49,32,128]{2,1,0:T(8,128)(2,1)S(1)}, bf16[49,16,128]{2,1,0:T(8,128)(2,1)S(1)}) custom-call(bf16[14,32,128]{2,1,0:T(8,128)(2,1)S(1)} %get-tuple-element.11.refs_0_, bf16[14,32,128]{2,1,0:T(8,128)(2,1)S(1)} %collective-permute-done.3.refs_4_.refs_1_, bf16[14,32,128]{2,1,0:T(8,128)(2,1)S(1)} %collective-permute-done.5.refs_2_, ...), custom_call_target="tpu_custom_call" | custom-call | bytes 1048576 | tf_op jit(solution)/shard_map/unpack_g/pallas_call | solution.py:119
  19.3 1.6 %collective-permute-start.7 = (bf16[49,16,128]{2,1,0:T(8,128)(2,1)S(1)}, bf16[49,16,128]{2,1,0:T(8,128)(2,1)S(1)}, u32[]{:S(2)}, u32[]{:S(2)}) collective-permute-start(bf16[49,16,128]{2,1,0:T(8,128)(2,1)S(1)} %get-tuple-element.15.gp), channel_id=1, source_target_pairs={{0,16},{1,17},{2,18},{3,19},{4,20},{5,21},{6,22},{7,23},{8,24},{9,... | collective-permute-start | bytes 602120 | tf_op jit(solution)/shard_map/ppermute | solution.py:302
  20.9 1.6 %terms_own.1.own_ref = f32[32,128]{1,0:T(8,128)S(1)} custom-call(f32[7,224,896]{2,1,0:T(8,128)S(1)} %own_inputs.1.t, bf16[49,32,128]{2,1,0:T(8,128)(2,1)S(1)} %get-tuple-element.14.g, bf16[49,16,128]{2,1,0:T(8,128)(2,1)S(1)} %get-tuple-element.15.gp), custom_call_target="tpu_custom_call" | custom-call | flops 6000000000 | bytes 4194304 | tf_op jit(solution)/shard_map/terms_own/pallas_call | solution.py:222
  22.5 0.0 collective-permute-done.4.xp
  22.5 2.0 %cross_inputs.1.t = f32[7,224,896]{2,1,0:T(8,128)S(1)} custom-call(bf16[49,32,128]{2,1,0:T(8,128)(2,1)S(1)} %get-tuple-element.12.x, bf16[49,16,128]{2,1,0:T(8,128)(2,1)S(1)} %collective-permute-done.4.xp), custom_call_target="tpu_custom_call" | custom-call | flops 6000000000 | bytes 4194304 | tf_op jit(solution)/shard_map/cross_inputs/pallas_call | solution.py:222
  24.5 1.5 %collective-permute-done.7.gp = bf16[49,16,128]{2,1,0:T(8,128)(2,1)S(1)} collective-permute-done((bf16[49,16,128]{2,1,0:T(8,128)(2,1)S(1)}, bf16[49,16,128]{2,1,0:T(8,128)(2,1)S(1)}, u32[]{:S(2)}, u32[]{:S(2)}) %collective-permute-start.7) | collective-permute-done | bytes 200736 | tf_op jit(solution)/shard_map/ppermute | solution.py:302
  26.0 1.6 %terms_cross.1 = (f32[8,128]{1,0:T(8,128)S(1)}, f32[1,32]{1,0:T(1,128)S(1)}) custom-call(f32[7,224,896]{2,1,0:T(8,128)S(1)} %cross_inputs.1.t, bf16[49,32,128]{2,1,0:T(8,128)(2,1)S(1)} %get-tuple-element.14.g, bf16[49,16,128]{2,1,0:T(8,128)(2,1)S(1)} %collective-permute-done.7.gp, f32[32,128]{1,0:T(8,128)S(1)} %terms_own.1.own_ref, f32[1,32]{1,0:T(1,128)S(1)} %bitcast.4), custom_call_target="tpu_custom_call" | custom-call | flops 6000000000 | bytes 4194304 | tf_op jit(solution)/shard_map/terms_cross/pallas_call | solution.py:222
  27.7 12.7 %all_to_all.5.terms_ref = f32[32,8,128]{2,1,0:T(8,128)S(1)} all-to-all(f32[32,8,128]{2,1,0:T(8,128)S(1)} %broadcast_in_dim.3), channel_id=1, replica_groups=mesh['rows'=2,'chan'=16] {'rows','chan'}, dimensions={0} | all-to-all | bytes 262144 | tf_op jit(solution)/shard_map/all_to_all | solution.py:321
  40.4 1.8 %solve.1 = (f32[32,32]{1,0:T(8,128)}, f32[32,32]{1,0:T(8,128)}) custom-call(f32[32,8,128]{2,1,0:T(8,128)S(1)} %all_to_all.5.terms_ref, f32[1,32]{1,0:T(1,128)S(1)} %get-tuple-element.17.ridge_ref), custom_call_target="tpu_custom_call" | custom-call | tf_op jit(solution)/shard_map/solve/pallas_call | solution.py:281
  (6 shorter events, 0.0 us)
Async XLA Ops:
  0.6 0.7 %copy-start = (s32[1,32]{1,0:T(1,128)S(1)}, s32[1,32]{1,0:T(1,128)}, u32[]{:S(2)}) copy-start(s32[1,32]{1,0:T(1,128)} %order_hbm.1) | copy-start | bytes 388
  3.1 7.2 %collective-permute-start.1 = (bf16[14,32,128]{2,1,0:T(8,128)(2,1)S(1)}, bf16[14,32,128]{2,1,0:T(8,128)(2,1)S(1)}, u32[]{:S(2)}, u32[]{:S(2)}) collective-permute-start(bf16[14,32,128]{2,1,0:T(8,128)(2,1)S(1)} %get-tuple-element.10.refs_0_), channel_id=1, source_target_pairs={{0,2},{1,3},{2,0},{3,1},{4,6},{5,7},{6,4},{7,5},{8,10},{9,11},{10,... | collective-permute-start | bytes 344072 | tf_op jit(solution)/shard_map/ppermute | solution.py:292
  6.1 8.0 %collective-permute-start.5 = (bf16[14,32,128]{2,1,0:T(8,128)(2,1)S(1)}, bf16[14,32,128]{2,1,0:T(8,128)(2,1)S(1)}, u32[]{:S(2)}, u32[]{:S(2)}) collective-permute-start(bf16[14,32,128]{2,1,0:T(8,128)(2,1)S(1)} %get-tuple-element.11.refs_0_), channel_id=1, source_target_pairs={{0,8},{1,9},{2,10},{3,11},{4,12},{5,13},{6,14},{7,15},{8,0},{9,1},... | collective-permute-start | bytes 344072 | tf_op jit(solution)/shard_map/ppermute | solution.py:292
  8.7 6.0 %collective-permute-start.3 = (bf16[14,32,128]{2,1,0:T(8,128)(2,1)S(1)}, bf16[14,32,128]{2,1,0:T(8,128)(2,1)S(1)}, u32[]{:S(2)}, u32[]{:S(2)}) collective-permute-start(bf16[14,32,128]{2,1,0:T(8,128)(2,1)S(1)} %get-tuple-element.11.refs_0_), channel_id=1, source_target_pairs={{0,4},{1,5},{2,6},{3,7},{4,0},{5,1},{6,2},{7,3},{8,12},{9,13},{10,... | collective-permute-start | bytes 344072 | tf_op jit(solution)/shard_map/ppermute | solution.py:292
  10.3 4.5 %collective-permute-start = (bf16[14,32,128]{2,1,0:T(8,128)(2,1)S(1)}, bf16[14,32,128]{2,1,0:T(8,128)(2,1)S(1)}, u32[]{:S(2)}, u32[]{:S(2)}) collective-permute-start(bf16[14,32,128]{2,1,0:T(8,128)(2,1)S(1)} %get-tuple-element.10.refs_0_), channel_id=1, source_target_pairs={{0,1},{1,0},{2,3},{3,2},{4,5},{5,4},{6,7},{7,6},{8,9},{9,8},{10,11... | collective-permute-start | bytes 344072 | tf_op jit(solution)/shard_map/ppermute | solution.py:292
  10.3 4.5 %collective-permute-start.2 = (bf16[14,32,128]{2,1,0:T(8,128)(2,1)S(1)}, bf16[14,32,128]{2,1,0:T(8,128)(2,1)S(1)}, u32[]{:S(2)}, u32[]{:S(2)}) collective-permute-start(bf16[14,32,128]{2,1,0:T(8,128)(2,1)S(1)} %collective-permute-done.1.refs_2_), channel_id=1, source_target_pairs={{0,1},{1,0},{2,3},{3,2},{4,5},{5,4},{6,7},{7,6},{8,9},{9,8},{10,11... | collective-permute-start | bytes 344072 | tf_op jit(solution)/shard_map/ppermute | solution.py:292
  14.1 4.8 %collective-permute-start.6 = (bf16[14,32,128]{2,1,0:T(8,128)(2,1)S(1)}, bf16[14,32,128]{2,1,0:T(8,128)(2,1)S(1)}, u32[]{:S(2)}, u32[]{:S(2)}) collective-permute-start(bf16[14,32,128]{2,1,0:T(8,128)(2,1)S(1)} %collective-permute-done.5.refs_2_), channel_id=1, source_target_pairs={{0,4},{1,5},{2,6},{3,7},{4,0},{5,1},{6,2},{7,3},{8,12},{9,13},{10,... | collective-permute-start | bytes 344072 | tf_op jit(solution)/shard_map/ppermute | solution.py:292
  15.2 7.3 %collective-permute-start.4 = (bf16[49,16,128]{2,1,0:T(8,128)(2,1)S(1)}, bf16[49,16,128]{2,1,0:T(8,128)(2,1)S(1)}, u32[]{:S(2)}, u32[]{:S(2)}) collective-permute-start(bf16[49,16,128]{2,1,0:T(8,128)(2,1)S(1)} %get-tuple-element.13.xp), channel_id=1, source_target_pairs={{0,16},{1,17},{2,18},{3,19},{4,20},{5,21},{6,22},{7,23},{8,24},{9,... | collective-permute-start | bytes 602120 | tf_op jit(solution)/shard_map/ppermute | solution.py:302
  19.3 6.7 %collective-permute-start.7 = (bf16[49,16,128]{2,1,0:T(8,128)(2,1)S(1)}, bf16[49,16,128]{2,1,0:T(8,128)(2,1)S(1)}, u32[]{:S(2)}, u32[]{:S(2)}) collective-permute-start(bf16[49,16,128]{2,1,0:T(8,128)(2,1)S(1)} %get-tuple-element.15.gp), channel_id=1, source_target_pairs={{0,16},{1,17},{2,18},{3,19},{4,20},{5,21},{6,22},{7,23},{8,24},{9,... | collective-permute-start | bytes 602120 | tf_op jit(solution)/shard_map/ppermute | solution.py:302
  22.4 3.6 %copy-start.1 = (f32[32]{0:T(128)S(1)}, f32[32]{0:T(128)}, u32[]{:S(2)}) copy-start(f32[32]{0:T(128)} %param.7) | copy-start | bytes 388

commit v9 on v8

--- a/solution.py
+++ b/solution.py
@@ -10,8 +10,9 @@
 PIV_DEV = 16
 
 SIDE = 7
+SPOTS = SIDE * SIDE
 PITCH = 8
-GROUPS4 = 14
+GROUPS4 = 13
 CH = 32
 EX = 32
 LANES = 128
@@ -36,13 +37,11 @@
     for k in range(EX):
         example = order_ref[0, k]
         onehot = jnp.where((row_id == k) & (col_id == example), 1.0, onehot)
-        gs[k * CH:(k + 1) * CH, 0:SIDE * SIDE] = g_ref[example].astype(F32)
+        gs[k * CH:(k + 1) * CH, 0:SPOTS] = g_ref[example].astype(F32)
+    gt[SPOTS:, :] = jnp.zeros((4 * GROUPS4 - SPOTS, LANES), F32)
     block_id = lax.broadcasted_iota(jnp.int32, (GROUPS4, LANES), 1) // CH
     for quad in range(EX // 4):
-        flipped = jnp.transpose(gs[quad * LANES:(quad + 1) * LANES, :])
-        for py in range(SIDE):
-            gt[py * PITCH:py * PITCH + SIDE, :] = flipped[py * SIDE:(py + 1) * SIDE, :]
-            gt[py * PITCH + SIDE:(py + 1) * PITCH, :] = jnp.zeros((1, LANES), F32)
+        gt[0:SPOTS, :] = jnp.transpose(gs[quad * LANES:(quad + 1) * LANES, :])[0:SPOTS, :]
         parts = [gt[pl.ds(j, GROUPS4, stride=4), :] for j in range(4)]
         for e in range(4):
             merged = jnp.zeros((GROUPS4, LANES), F32)
@@ -57,11 +56,8 @@
     onehot = onehot.astype(BF16)
     zero_block = jnp.zeros((EX, CH), BF16)
     for group in range(GROUPS4):
-        pieces = []
-        for j in range(4):
-            py, px = group // 2, (group % 2) * 4 + j
-            pieces.append(x_ref[py * SIDE + px] if px < SIDE else zero_block)
-        packed = jnp.concatenate(pieces, axis=1)
+        spots = [4 * group + j for j in range(4)]
+        packed = jnp.concatenate([x_ref[p] if p < SPOTS else zero_block for p in spots], axis=1)
         xo_ref[group] = jnp.dot(onehot, packed, preferred_element_type=F32).astype(BF16)
 
 
@@ -79,7 +75,7 @@
             pltpu.VMEM(g.shape, g.dtype),
             pltpu.SemaphoreType.DMA((3,)),
             pltpu.VMEM((EX * CH, LANES), F32),
-            pltpu.VMEM((SIDE * PITCH, LANES), F32),
+            pltpu.VMEM((4 * GROUPS4, LANES), F32),
             pltpu.VMEM((GROUPS4 * EX, LANES), F32),
         ],
         compiler_params=pltpu.CompilerParams(vmem_limit_bytes=54848 << 10),
@@ -87,7 +83,7 @@
     )(order, x, g)
 
 
-SPOTS = SIDE * SIDE
+ROWB = SIDE * EX
 COLB = PITCH * PIV_DEV
 
 
@@ -105,12 +101,10 @@
     moved = jnp.dot(flat, move, preferred_element_type=F32).astype(BF16)
     for group in range(GROUPS4):
         for j in range(4):
-            py, px = group // 2, (group % 2) * 4 + j
-            if px == SIDE:
-                continue
-            spot = moved[group * EX:(group + 1) * EX, j * LANES:(j + 1) * LANES]
-            all_ref[py * SIDE + px] = spot
-            piv_ref[py * SIDE + px] = spot[:PIV_DEV]
+            if 4 * group + j < SPOTS:
+                spot = moved[group * EX:(group + 1) * EX, j * LANES:(j + 1) * LANES]
+                all_ref[4 * group + j] = spot
+                piv_ref[4 * group + j] = spot[:PIV_DEV]
 
 
 def unpack(arrays, name, after=()):
@@ -131,53 +125,40 @@
 SPANS = [(qy, min(qy + 2, SIDE)) for qy in range(0, SIDE, 2)]
 
 
-def input_products(rows_x, xp, lx, rx, t):
-    heights = [ref.shape[1] for ref in rows_x]
-    height = sum(heights)
+def place_windows(values, window, pitch):
+    count = values.shape[1]
+    zero = jnp.zeros((count, LANES), BF16)
     for py in range(SIDE):
-        for px in range(PITCH):
-            row, col = (py * SIDE + px) * height, (py * PITCH + px) * PIV_DEV
+        for px in range(pitch):
+            first = (py * pitch + px) * count
             for d in range(3):
                 from_x = px + d - 1
                 inside = 0 <= from_x < SIDE and px < SIDE
-                lanes = slice(d * LANES, (d + 1) * LANES)
-                spot = py * SIDE + from_x
-                rx[col:col + PIV_DEV, lanes] = xp[spot] if inside else jnp.zeros((PIV_DEV, LANES), BF16)
-                if px < SIDE:
-                    first = row
-                    for ref, count in zip(rows_x, heights):
-                        lx[first:first + count, lanes] = ref[spot] if inside else jnp.zeros((count, LANES), BF16)
-                        first += count
-    block = SIDE * height
+                window[first:first + count, d * LANES:(d + 1) * LANES] = values[py * SIDE + from_x] if inside else zero
+
+
+def input_products(lx, rx, t):
     for start, stop in SPANS:
         right = rx[start * COLB:stop * COLB, :]
         for py in range(SIDE):
-            left = lx[py * block:(py + 1) * block, :]
+            left = lx[py * ROWB:(py + 1) * ROWB, :]
             t[py, :, start * COLB:stop * COLB] = lax.dot_general(left, right, CONTRACT, preferred_element_type=F32)
 
 
-def panel_terms(rows_g, gp, lg, rg, t):
-    heights = [ref.shape[1] for ref in rows_g]
-    height = sum(heights)
+def panel_terms(g, gp, rg, t):
     for py in range(SIDE):
         for px in range(PITCH):
-            row, col = (py * SIDE + px) * height, (py * PITCH + px) * PIV_DEV
+            col = (py * PITCH + px) * PIV_DEV
             rg[col:col + PIV_DEV, :] = gp[py * SIDE + px] if px < SIDE else jnp.zeros((PIV_DEV, LANES), BF16)
-            if px < SIDE:
-                first = row
-                for ref, count in zip(rows_g, heights):
-                    lg[first:first + count, :] = ref[py * SIDE + px]
-                    first += count
-    block = SIDE * height
-    acc = jnp.zeros((height, COLB), F32)
+    acc = jnp.zeros((EX, COLB), F32)
     for start, stop in SPANS:
         right = rg[start * COLB:stop * COLB, :]
         for py in range(SIDE):
-            left = lg[py * block:(py + 1) * block, :]
+            left = g[py * SIDE:(py + 1) * SIDE].reshape(ROWB, LANES)
             gg = lax.dot_general(left, right, CONTRACT, preferred_element_type=F32)
             for qy in range(start, stop):
                 for px in range(SIDE):
-                    rows = slice(px * height, (px + 1) * height)
+                    rows = slice(px * EX, (px + 1) * EX)
                     total = t[py, rows, qy * COLB:(qy + 1) * COLB]
                     if py > 0 and qy > 0:
                         total = total + t[py - 1, rows, (qy - 1) * COLB:qy * COLB]
@@ -189,17 +170,24 @@
     return acc + pltpu.roll(acc, 16, 1)
 
 
-def products_kernel(x, xp, t_out, lx, rx):
-    input_products([x], xp, lx, rx, t_out)
-
-
-def own_kernel(t, g, gp, out_ref, lg, rg):
-    out_ref[...] = panel_terms([g], gp, lg, rg, t)
-
-
-def cross_kernel(t, g, gp, own_ref, ridge, out_ref, ridge_out, lg, rg):
+def own_inputs_kernel(x, xp, t_out, lx_out, rx):
+    place_windows(x, lx_out, SIDE)
+    place_windows(xp, rx, PITCH)
+    input_products(lx_out, rx, t_out)
+
+
+def cross_inputs_kernel(lx, xp, t_out, rx):
+    place_windows(xp, rx, PITCH)
+    input_products(lx, rx, t_out)
+
+
+def own_kernel(t, g, gp, out_ref, rg):
+    out_ref[...] = panel_terms(g, gp, rg, t)
+
+
+def cross_kernel(t, g, gp, own_ref, ridge, out_ref, ridge_out, rg):
     ridge_out[...] = ridge[...]
-    across = panel_terms([g], gp, lg, rg, t)
+    across = panel_terms(g, gp, rg, t)
     lane = lax.broadcasted_iota(jnp.int32, (8, LANES), 1)
     is_own = (lane // PIV_DEV) % 2 == lax.axis_index("rows")
     packed = jnp.zeros((8, LANES), F32)
@@ -209,22 +197,14 @@
     out_ref[...] = packed
 
 
-def product_shape(height):
-    return (SIDE, SIDE * height, SIDE * COLB)
-
-
-def scratch_of(height, width):
-    return [pltpu.VMEM((SPOTS * height, width), BF16), pltpu.VMEM((SIDE * COLB, width), BF16)]
-
-
-def terms(kernel, arrays, shapes, scratch, flops, name):
+def terms(kernel, arrays, outs, width, flops, name):
     vmem = pl.BlockSpec(memory_space=pltpu.VMEM)
     return pl.pallas_call(
         kernel,
-        out_shape=tuple(jax.ShapeDtypeStruct(shape, F32) for shape in shapes),
+        out_shape=tuple(jax.ShapeDtypeStruct(*out) for out in outs),
         in_specs=[vmem] * len(arrays),
-        out_specs=(vmem,) * len(shapes),
-        scratch_shapes=scratch,
+        out_specs=(vmem,) * len(outs),
+        scratch_shapes=[pltpu.VMEM((SIDE * COLB, width), BF16)],
         compiler_params=pltpu.CompilerParams(vmem_limit_bytes=20 << 20),
         cost_estimate=cost(flops, 4 << 20),
         name=name,
@@ -303,20 +283,20 @@
 
 
 def local_packed(count, activations, cotangents, ordering, ridge):
-    x = jnp.transpose(activations, (1, 2, 0, 3)).reshape(SIDE * SIDE, EX, CH)
+    x = jnp.transpose(activations, (1, 2, 0, 3)).reshape(SPOTS, EX, CH)
     xo, go = prep(ordering, x, cotangents)
     own_g = gather(go, count, 8, 4)
     x_all, x_piv = unpack(gather(xo, count, 2, 1), "unpack_x", (own_g[1],))
     x_cross = exchange_across(x_piv, count)
-    g_all, g_piv = unpack(own_g, "unpack_g")
+    g_all, g_piv = unpack(own_g, "unpack_g", (x_piv,))
     g_cross = exchange_across(g_piv, count)
-    wide, narrow = scratch_of(EX, 3 * LANES), scratch_of(EX, LANES)
-    shape, flops = product_shape(EX), 6 * 10**9
-    products, = terms(products_kernel, (x_all, x_piv), (shape,), wide, flops, "own_inputs")
-    own_term, = terms(own_kernel, (products, g_all, g_piv), ((EX, LANES),), narrow, flops, "terms_own")
-    products, = terms(products_kernel, (x_all, x_cross), (shape,), wide, flops, "cross_inputs")
+    flops, product = 6 * 10**9, ((SIDE, ROWB, SIDE * COLB), F32)
+    windows = ((SPOTS * EX, 3 * LANES), BF16)
+    products, lx = terms(own_inputs_kernel, (x_all, x_piv), (product, windows), 3 * LANES, flops, "own_inputs")
+    own_term, = terms(own_kernel, (products, g_all, g_piv), (((EX, LANES), F32),), LANES, flops, "terms_own")
+    products, = terms(cross_inputs_kernel, (lx, x_cross), (product,), 3 * LANES, flops, "cross_inputs")
     arrays = (products, g_all, g_cross, own_term, ridge.reshape(1, EX))
-    term, ridge = terms(cross_kernel, arrays, ((8, LANES), (1, EX)), narrow, flops, "terms_cross")
+    term, ridge = terms(cross_kernel, arrays, (((8, LANES), F32), ((1, EX), F32)), LANES, flops, "terms_cross")
     copies = jnp.broadcast_to(term, (2 * count, 8, LANES))
     return final(lax.all_to_all(copies, ("rows", "chan"), 0, 0), ridge)
 

time: 42.4 us -> 41.9 us (0.988)
  waiting for transfers between devices: 4.95 us -> 4.5 us
    ppermute x6, waiting for transfers between devices: 3.41 us -> 2.95 us  [exchange(): return lax.ppermute(value, 'chan', [(i, i ^ flip) for i in range(count)])]
  transfers between devices with their start and end apart: 8 -> 8, of which waited for: 3 -> 2; matrix products, arithmetic and copies ran while one was open for 0% -> 0% of each run, Pallas kernels for 15% -> 15%
where the time goes in v9:
time: 41.9 us; the launch traced here: 41.7 us
  blocking collectives  12.9 us (31%)
  Pallas kernels  11.5 us (27%)
  starting transfers between devices  11.5 us (27%)
  waiting for transfers between devices  4.5 us (11%)
  between operations  0.7 us (2%)
  local copies, waits for them, and re-layouts  0.67 us (2%)
    all_to_all x1, blocking collectives, local_packed(): return final(lax.all_to_all(copies, ('rows', 'chan'), 0, 0), ridge)  12.9 us
    ppermute x6, starting transfers between devices, exchange(): return lax.ppermute(value, 'chan', [(i, i ^ flip) for i in range(count)])  8.37 us
    pallas_call x4, Pallas kernels, terms(): pl.pallas_call(kernel, out_shape=tuple((jax.ShapeDtypeStruct(*out) for ou...  7.09 us
    ppermute x2, starting transfers between devices, exchange_across(): return lax.ppermute(value, ('rows', 'chan'), pairs)  3.08 us
    ppermute x6, waiting for transfers between devices, exchange(): return lax.ppermute(value, 'chan', [(i, i ^ flip) for i in range(count)])  2.95 us
    pallas_call x1, Pallas kernels, final(): pl.pallas_call(final_kernel, out_shape=(out, out), in_specs=[vmem] * 2, o...  1.85 us
    pallas_call x1, Pallas kernels, prep(): pl.pallas_call(prep_kernel, out_shape=(full, full), in_specs=[pl.BlockSpe...  1.75 us
    ppermute x2, waiting for transfers between devices, exchange_across(): return lax.ppermute(value, ('rows', 'chan'), pairs)  1.55 us
  transfers between devices with their start and end apart: 8, of which 2 were waited for; matrix products, arithmetic and copies ran while one was open for 0% of the time, Pallas kernels for 15%

profile of v9, /device:TPU:0, one launch (start us, length us, event | category | flops | bytes accessed | tf_op | source)
XLA Modules:
  0.0 41.7 jit_solution(853325028623440808)
XLA Ops:
  0.6 0.6 %copy-done = s32[1,32]{1,0:T(1,128)S(1)} copy-done((s32[1,32]{1,0:T(1,128)S(1)}, s32[1,32]{1,0:T(1,128)}, u32[]{:S(2)}) %copy-start) | copy-done | bytes 152
  1.3 1.8 %prep.1 = (bf16[13,32,128]{2,1,0:T(8,128)(2,1)S(1)}, bf16[13,32,128]{2,1,0:T(8,128)(2,1)S(1)}) custom-call(s32[1,32]{1,0:T(1,128)S(1)} %copy-done, bf16[49,32,32]{2,1,0:T(8,128)(2,1)} %bitcast.5, bf16[32,32,49]{2,1,0:T(8,128)(2,1)} %g_hbm.1), custom_call_target="tpu_custom_call" | custom-call | tf_op jit(solution)/shard_map/prep/pallas_call | solution.py:67
  3.0 3.0 %collective-permute-start.1 = (bf16[13,32,128]{2,1,0:T(8,128)(2,1)S(1)}, bf16[13,32,128]{2,1,0:T(8,128)(2,1)S(1)}, u32[]{:S(2)}, u32[]{:S(2)}) collective-permute-start(bf16[13,32,128]{2,1,0:T(8,128)(2,1)S(1)} %get-tuple-element.12.refs_0_), channel_id=1, source_target_pairs={{0,2},{1,3},{2,0},{3,1},{4,6},{5,7},{6,4},{7,5},{8,10},{9,11},{10,... | collective-permute-start | bytes 319496 | tf_op jit(solution)/shard_map/ppermute | solution.py:272
  6.1 2.6 %collective-permute-start.5 = (bf16[13,32,128]{2,1,0:T(8,128)(2,1)S(1)}, bf16[13,32,128]{2,1,0:T(8,128)(2,1)S(1)}, u32[]{:S(2)}, u32[]{:S(2)}) collective-permute-start(bf16[13,32,128]{2,1,0:T(8,128)(2,1)S(1)} %get-tuple-element.13.refs_0_), channel_id=1, source_target_pairs={{0,8},{1,9},{2,10},{3,11},{4,12},{5,13},{6,14},{7,15},{8,0},{9,1},... | collective-permute-start | bytes 319496 | tf_op jit(solution)/shard_map/ppermute | solution.py:272
  8.7 1.6 %collective-permute-start.3 = (bf16[13,32,128]{2,1,0:T(8,128)(2,1)S(1)}, bf16[13,32,128]{2,1,0:T(8,128)(2,1)S(1)}, u32[]{:S(2)}, u32[]{:S(2)}) collective-permute-start(bf16[13,32,128]{2,1,0:T(8,128)(2,1)S(1)} %get-tuple-element.13.refs_0_), channel_id=1, source_target_pairs={{0,4},{1,5},{2,6},{3,7},{4,0},{5,1},{6,2},{7,3},{8,12},{9,13},{10,... | collective-permute-start | bytes 319496 | tf_op jit(solution)/shard_map/ppermute | solution.py:272
  10.2 0.0 collective-permute-start
  10.3 0.0 collective-permute-done.1.refs_2_
  10.3 0.5 %collective-permute-start.2 = (bf16[13,32,128]{2,1,0:T(8,128)(2,1)S(1)}, bf16[13,32,128]{2,1,0:T(8,128)(2,1)S(1)}, u32[]{:S(2)}, u32[]{:S(2)}) collective-permute-start(bf16[13,32,128]{2,1,0:T(8,128)(2,1)S(1)} %collective-permute-done.1.refs_2_), channel_id=1, source_target_pairs={{0,1},{1,0},{2,3},{3,2},{4,5},{5,4},{6,7},{7,6},{8,9},{9,8},{10,11... | collective-permute-start | bytes 319496 | tf_op jit(solution)/shard_map/ppermute | solution.py:272
  10.8 2.9 %collective-permute-done.5.refs_2_ = bf16[13,32,128]{2,1,0:T(8,128)(2,1)S(1)} collective-permute-done((bf16[13,32,128]{2,1,0:T(8,128)(2,1)S(1)}, bf16[13,32,128]{2,1,0:T(8,128)(2,1)S(1)}, u32[]{:S(2)}, u32[]{:S(2)}) %collective-permute-start.5) | collective-permute-done | bytes 106528 | tf_op jit(solution)/shard_map/ppermute | solution.py:272
  13.7 0.7 %collective-permute-start.6 = (bf16[13,32,128]{2,1,0:T(8,128)(2,1)S(1)}, bf16[13,32,128]{2,1,0:T(8,128)(2,1)S(1)}, u32[]{:S(2)}, u32[]{:S(2)}) collective-permute-start(bf16[13,32,128]{2,1,0:T(8,128)(2,1)S(1)} %collective-permute-done.5.refs_2_), channel_id=1, source_target_pairs={{0,4},{1,5},{2,6},{3,7},{4,0},{5,1},{6,2},{7,3},{8,12},{9,13},{10,... | collective-permute-start | bytes 319496 | tf_op jit(solution)/shard_map/ppermute | solution.py:272
  14.4 0.0 collective-permute-done.3.refs_4_.refs_1_
  14.4 0.4 %unpack_x.1 = (bf16[49,32,128]{2,1,0:T(8,128)(2,1)S(1)}, bf16[49,16,128]{2,1,0:T(8,128)(2,1)S(1)}) custom-call(bf16[13,32,128]{2,1,0:T(8,128)(2,1)S(1)} %get-tuple-element.12.refs_0_, bf16[13,32,128]{2,1,0:T(8,128)(2,1)S(1)} %collective-permute-done.refs_1_, bf16[13,32,128]{2,1,0:T(8,128)(2,1)S(1)} %collective-permute-done.1.refs_2_, ...), custom_call_target="tpu_custom_call" | custom-call | bytes 1048576 | tf_op jit(solution)/shard_map/unpack_x/pallas_call | solution.py:113
  14.8 1.6 %collective-permute-start.4 = (bf16[49,16,128]{2,1,0:T(8,128)(2,1)S(1)}, bf16[49,16,128]{2,1,0:T(8,128)(2,1)S(1)}, u32[]{:S(2)}, u32[]{:S(2)}) collective-permute-start(bf16[49,16,128]{2,1,0:T(8,128)(2,1)S(1)} %get-tuple-element.15.xp.refs_4_), channel_id=1, source_target_pairs={{0,16},{1,17},{2,18},{3,19},{4,20},{5,21},{6,22},{7,23},{8,24},{9,... | collective-permute-start | bytes 602120 | tf_op jit(solution)/shard_map/ppermute | solution.py:282
  16.4 2.1 %own_inputs.1 = (f32[7,224,896]{2,1,0:T(8,128)S(1)}, bf16[1568,384]{1,0:T(8,128)(2,1)S(1)}) custom-call(bf16[49,32,128]{2,1,0:T(8,128)(2,1)S(1)} %get-tuple-element.14.x, bf16[49,16,128]{2,1,0:T(8,128)(2,1)S(1)} %get-tuple-element.15.xp.refs_4_), custom_call_target="tpu_custom_call" | custom-call | flops 6000000000 | bytes 4194304 | tf_op jit(solution)/shard_map/own_inputs/pallas_call | solution.py:202
  18.4 0.4 %unpack_g.1 = (bf16[49,32,128]{2,1,0:T(8,128)(2,1)S(1)}, bf16[49,16,128]{2,1,0:T(8,128)(2,1)S(1)}) custom-call(bf16[13,32,128]{2,1,0:T(8,128)(2,1)S(1)} %get-tuple-element.13.refs_0_, bf16[13,32,128]{2,1,0:T(8,128)(2,1)S(1)} %collective-permute-done.3.refs_4_.refs_1_, bf16[13,32,128]{2,1,0:T(8,128)(2,1)S(1)} %collective-permute-done.5.refs_2_, ...), custom_call_target="tpu_custom_call" | custom-call | bytes 1048576 | tf_op jit(solution)/shard_map/unpack_g/pallas_call | solution.py:113
  18.9 1.5 %collective-permute-start.7 = (bf16[49,16,128]{2,1,0:T(8,128)(2,1)S(1)}, bf16[49,16,128]{2,1,0:T(8,128)(2,1)S(1)}, u32[]{:S(2)}, u32[]{:S(2)}) collective-permute-start(bf16[49,16,128]{2,1,0:T(8,128)(2,1)S(1)} %get-tuple-element.18.gp), channel_id=1, source_target_pairs={{0,16},{1,17},{2,18},{3,19},{4,20},{5,21},{6,22},{7,23},{8,24},{9,... | collective-permute-start | bytes 602120 | tf_op jit(solution)/shard_map/ppermute | solution.py:282
  20.4 1.4 %terms_own.1.own_ref = f32[32,128]{1,0:T(8,128)S(1)} custom-call(f32[7,224,896]{2,1,0:T(8,128)S(1)} %get-tuple-element.19.t, bf16[49,32,128]{2,1,0:T(8,128)(2,1)S(1)} %get-tuple-element.17.g, bf16[49,16,128]{2,1,0:T(8,128)(2,1)S(1)} %get-tuple-element.18.gp), custom_call_target="tpu_custom_call" | custom-call | flops 6000000000 | bytes 4194304 | tf_op jit(solution)/shard_map/terms_own/pallas_call | solution.py:202
  21.8 0.0 collective-permute-done.4.xp
  21.8 0.0 copy-start.1
  21.8 2.0 %cross_inputs.1.t = f32[7,224,896]{2,1,0:T(8,128)S(1)} custom-call(bf16[1568,384]{1,0:T(8,128)(2,1)S(1)} %get-tuple-element.16.lx, bf16[49,16,128]{2,1,0:T(8,128)(2,1)S(1)} %collective-permute-done.4.xp), custom_call_target="tpu_custom_call" | custom-call | flops 6000000000 | bytes 4194304 | tf_op jit(solution)/shard_map/cross_inputs/pallas_call | solution.py:202
  23.9 1.6 %collective-permute-done.7.gp = bf16[49,16,128]{2,1,0:T(8,128)(2,1)S(1)} collective-permute-done((bf16[49,16,128]{2,1,0:T(8,128)(2,1)S(1)}, bf16[49,16,128]{2,1,0:T(8,128)(2,1)S(1)}, u32[]{:S(2)}, u32[]{:S(2)}) %collective-permute-start.7) | collective-permute-done | bytes 200736 | tf_op jit(solution)/shard_map/ppermute | solution.py:282
  25.4 1.6 %terms_cross.1 = (f32[8,128]{1,0:T(8,128)S(1)}, f32[1,32]{1,0:T(1,128)S(1)}) custom-call(f32[7,224,896]{2,1,0:T(8,128)S(1)} %cross_inputs.1.t, bf16[49,32,128]{2,1,0:T(8,128)(2,1)S(1)} %get-tuple-element.17.g, bf16[49,16,128]{2,1,0:T(8,128)(2,1)S(1)} %collective-permute-done.7.gp, f32[32,128]{1,0:T(8,128)S(1)} %terms_own.1.own_ref, f32[1,32]{1,0:T(1,128)S(1)} %bitcast.4), custom_call_target="tpu_custom_call" | custom-call | flops 6000000000 | bytes 4194304 | tf_op jit(solution)/shard_map/terms_cross/pallas_call | solution.py:202
  27.0 12.9 %all_to_all.5.terms_ref = f32[32,8,128]{2,1,0:T(8,128)S(1)} all-to-all(f32[32,8,128]{2,1,0:T(8,128)S(1)} %broadcast_in_dim.3), channel_id=1, replica_groups=mesh['rows'=2,'chan'=16] {'rows','chan'}, dimensions={0} | all-to-all | bytes 262144 | tf_op jit(solution)/shard_map/all_to_all | solution.py:301
  39.9 1.8 %solve.1 = (f32[32,32]{1,0:T(8,128)}, f32[32,32]{1,0:T(8,128)}) custom-call(f32[32,8,128]{2,1,0:T(8,128)S(1)} %all_to_all.5.terms_ref, f32[1,32]{1,0:T(1,128)S(1)} %get-tuple-element.21.ridge_ref), custom_call_target="tpu_custom_call" | custom-call | tf_op jit(solution)/shard_map/solve/pallas_call | solution.py:261
  (6 shorter events, 0.0 us)
Async XLA Ops:
  0.6 0.7 %copy-start = (s32[1,32]{1,0:T(1,128)S(1)}, s32[1,32]{1,0:T(1,128)}, u32[]{:S(2)}) copy-start(s32[1,32]{1,0:T(1,128)} %order_hbm.1) | copy-start | bytes 388
  3.0 7.2 %collective-permute-start.1 = (bf16[13,32,128]{2,1,0:T(8,128)(2,1)S(1)}, bf16[13,32,128]{2,1,0:T(8,128)(2,1)S(1)}, u32[]{:S(2)}, u32[]{:S(2)}) collective-permute-start(bf16[13,32,128]{2,1,0:T(8,128)(2,1)S(1)} %get-tuple-element.12.refs_0_), channel_id=1, source_target_pairs={{0,2},{1,3},{2,0},{3,1},{4,6},{5,7},{6,4},{7,5},{8,10},{9,11},{10,... | collective-permute-start | bytes 319496 | tf_op jit(solution)/shard_map/ppermute | solution.py:272
  6.1 7.6 %collective-permute-start.5 = (bf16[13,32,128]{2,1,0:T(8,128)(2,1)S(1)}, bf16[13,32,128]{2,1,0:T(8,128)(2,1)S(1)}, u32[]{:S(2)}, u32[]{:S(2)}) collective-permute-start(bf16[13,32,128]{2,1,0:T(8,128)(2,1)S(1)} %get-tuple-element.13.refs_0_), channel_id=1, source_target_pairs={{0,8},{1,9},{2,10},{3,11},{4,12},{5,13},{6,14},{7,15},{8,0},{9,1},... | collective-permute-start | bytes 319496 | tf_op jit(solution)/shard_map/ppermute | solution.py:272
  8.7 5.7 %collective-permute-start.3 = (bf16[13,32,128]{2,1,0:T(8,128)(2,1)S(1)}, bf16[13,32,128]{2,1,0:T(8,128)(2,1)S(1)}, u32[]{:S(2)}, u32[]{:S(2)}) collective-permute-start(bf16[13,32,128]{2,1,0:T(8,128)(2,1)S(1)} %get-tuple-element.13.refs_0_), channel_id=1, source_target_pairs={{0,4},{1,5},{2,6},{3,7},{4,0},{5,1},{6,2},{7,3},{8,12},{9,13},{10,... | collective-permute-start | bytes 319496 | tf_op jit(solution)/shard_map/ppermute | solution.py:272
  10.2 4.1 %collective-permute-start = (bf16[13,32,128]{2,1,0:T(8,128)(2,1)S(1)}, bf16[13,32,128]{2,1,0:T(8,128)(2,1)S(1)}, u32[]{:S(2)}, u32[]{:S(2)}) collective-permute-start(bf16[13,32,128]{2,1,0:T(8,128)(2,1)S(1)} %get-tuple-element.12.refs_0_), channel_id=1, source_target_pairs={{0,1},{1,0},{2,3},{3,2},{4,5},{5,4},{6,7},{7,6},{8,9},{9,8},{10,11... | collective-permute-start | bytes 319496 | tf_op jit(solution)/shard_map/ppermute | solution.py:272
  10.3 4.1 %collective-permute-start.2 = (bf16[13,32,128]{2,1,0:T(8,128)(2,1)S(1)}, bf16[13,32,128]{2,1,0:T(8,128)(2,1)S(1)}, u32[]{:S(2)}, u32[]{:S(2)}) collective-permute-start(bf16[13,32,128]{2,1,0:T(8,128)(2,1)S(1)} %collective-permute-done.1.refs_2_), channel_id=1, source_target_pairs={{0,1},{1,0},{2,3},{3,2},{4,5},{5,4},{6,7},{7,6},{8,9},{9,8},{10,11... | collective-permute-start | bytes 319496 | tf_op jit(solution)/shard_map/ppermute | solution.py:272
  13.7 4.7 %collective-permute-start.6 = (bf16[13,32,128]{2,1,0:T(8,128)(2,1)S(1)}, bf16[13,32,128]{2,1,0:T(8,128)(2,1)S(1)}, u32[]{:S(2)}, u32[]{:S(2)}) collective-permute-start(bf16[13,32,128]{2,1,0:T(8,128)(2,1)S(1)} %collective-permute-done.5.refs_2_), channel_id=1, source_target_pairs={{0,4},{1,5},{2,6},{3,7},{4,0},{5,1},{6,2},{7,3},{8,12},{9,13},{10,... | collective-permute-start | bytes 319496 | tf_op jit(solution)/shard_map/ppermute | solution.py:272
  14.8 7.0 %collective-permute-start.4 = (bf16[49,16,128]{2,1,0:T(8,128)(2,1)S(1)}, bf16[49,16,128]{2,1,0:T(8,128)(2,1)S(1)}, u32[]{:S(2)}, u32[]{:S(2)}) collective-permute-start(bf16[49,16,128]{2,1,0:T(8,128)(2,1)S(1)} %get-tuple-element.15.xp.refs_4_), channel_id=1, source_target_pairs={{0,16},{1,17},{2,18},{3,19},{4,20},{5,21},{6,22},{7,23},{8,24},{9,... | collective-permute-start | bytes 602120 | tf_op jit(solution)/shard_map/ppermute | solution.py:282
  18.9 6.6 %collective-permute-start.7 = (bf16[49,16,128]{2,1,0:T(8,128)(2,1)S(1)}, bf16[49,16,128]{2,1,0:T(8,128)(2,1)S(1)}, u32[]{:S(2)}, u32[]{:S(2)}) collective-permute-start(bf16[49,16,128]{2,1,0:T(8,128)(2,1)S(1)} %get-tuple-element.18.gp), channel_id=1, source_target_pairs={{0,16},{1,17},{2,18},{3,19},{4,20},{5,21},{6,22},{7,23},{8,24},{9,... | collective-permute-start | bytes 602120 | tf_op jit(solution)/shard_map/ppermute | solution.py:282
  21.8 3.6 %copy-start.1 = (f32[32]{0:T(128)S(1)}, f32[32]{0:T(128)}, u32[]{:S(2)}) copy-start(f32[32]{0:T(128)} %param.7) | copy-start | bytes 388

commit v10 on v9

--- a/solution.py
+++ b/solution.py
@@ -286,7 +286,7 @@
     x = jnp.transpose(activations, (1, 2, 0, 3)).reshape(SPOTS, EX, CH)
     xo, go = prep(ordering, x, cotangents)
     own_g = gather(go, count, 8, 4)
-    x_all, x_piv = unpack(gather(xo, count, 2, 1), "unpack_x", (own_g[1],))
+    x_all, x_piv = unpack([xo] + [exchange(xo, count, f) for f in (1, 2, 3)], "unpack_x", (own_g[1], own_g[2]))
     x_cross = exchange_across(x_piv, count)
     g_all, g_piv = unpack(own_g, "unpack_g", (x_piv,))
     g_cross = exchange_across(g_piv, count)

time: 41.9 us -> 43.4 us (1.036)
  waiting for transfers between devices: 4.5 us -> 7.43 us
  blocking collectives: 12.9 us -> 12.2 us
  starting transfers between devices: 11.5 us -> 11 us
    ppermute x6, waiting for transfers between devices: 2.95 us -> 5.5 us  [exchange(): return lax.ppermute(value, 'chan', [(i, i ^ flip) for i in range(count)])]
    ppermute x2, starting transfers between devices: 3.08 us -> 2.15 us  [exchange_across(): return lax.ppermute(value, ('rows', 'chan'), pairs)]
    all_to_all x1, blocking collectives: 12.9 us -> 12.2 us  [local_packed(): return final(lax.all_to_all(copies, ('rows', 'chan'), 0, 0), ridge)]
    ppermute x6, starting transfers between devices: 8.37 us -> 8.81 us  [exchange(): return lax.ppermute(value, 'chan', [(i, i ^ flip) for i in range(count)])]
  transfers between devices with their start and end apart: 8 -> 8, of which waited for: 2 -> 6; matrix products, arithmetic and copies ran while one was open for 0% -> 0% of each run, Pallas kernels for 15% -> 14%
where the time goes in v10:
time: 43.4 us; the launch traced here: 43.3 us
  blocking collectives  12.2 us (28%)
  Pallas kernels  11.4 us (26%)
  starting transfers between devices  11 us (25%)
  waiting for transfers between devices  7.43 us (17%)
  between operations  0.69 us (2%)
  local copies, waits for them, and re-layouts  0.67 us (2%)
    all_to_all x1, blocking collectives, local_packed(): return final(lax.all_to_all(copies, ('rows', 'chan'), 0, 0), ridge)  12.2 us
    ppermute x6, starting transfers between devices, exchange(): return lax.ppermute(value, 'chan', [(i, i ^ flip) for i in range(count)])  8.81 us
    pallas_call x4, Pallas kernels, terms(): pl.pallas_call(kernel, out_shape=tuple((jax.ShapeDtypeStruct(*out) for ou...  6.91 us
    ppermute x6, waiting for transfers between devices, exchange(): return lax.ppermute(value, 'chan', [(i, i ^ flip) for i in range(count)])  5.5 us
    ppermute x2, starting transfers between devices, exchange_across(): return lax.ppermute(value, ('rows', 'chan'), pairs)  2.15 us
    ppermute x2, waiting for transfers between devices, exchange_across(): return lax.ppermute(value, ('rows', 'chan'), pairs)  1.93 us
    pallas_call x1, Pallas kernels, final(): pl.pallas_call(final_kernel, out_shape=(out, out), in_specs=[vmem] * 2, o...  1.85 us
    pallas_call x1, Pallas kernels, prep(): pl.pallas_call(prep_kernel, out_shape=(full, full), in_specs=[pl.BlockSpe...  1.75 us
  transfers between devices with their start and end apart: 8, of which 6 were waited for; matrix products, arithmetic and copies ran while one was open for 0% of the time, Pallas kernels for 14%

profile of v10, /device:TPU:0, one launch (start us, length us, event | category | flops | bytes accessed | tf_op | source)
XLA Modules:
  0.0 43.3 jit_solution(1026984143033273469)
XLA Ops:
  0.6 0.6 %copy-done = s32[1,32]{1,0:T(1,128)S(1)} copy-done((s32[1,32]{1,0:T(1,128)S(1)}, s32[1,32]{1,0:T(1,128)}, u32[]{:S(2)}) %copy-start) | copy-done | bytes 152
  1.3 1.8 %prep.1 = (bf16[13,32,128]{2,1,0:T(8,128)(2,1)S(1)}, bf16[13,32,128]{2,1,0:T(8,128)(2,1)S(1)}) custom-call(s32[1,32]{1,0:T(1,128)S(1)} %copy-done, bf16[49,32,32]{2,1,0:T(8,128)(2,1)} %bitcast.5, bf16[32,32,49]{2,1,0:T(8,128)(2,1)} %g_hbm.1), custom_call_target="tpu_custom_call" | custom-call | tf_op jit(solution)/shard_map/prep/pallas_call | solution.py:67
  3.0 4.1 %collective-permute-start.4 = (bf16[13,32,128]{2,1,0:T(8,128)(2,1)S(1)}, bf16[13,32,128]{2,1,0:T(8,128)(2,1)S(1)}, u32[]{:S(2)}, u32[]{:S(2)}) collective-permute-start(bf16[13,32,128]{2,1,0:T(8,128)(2,1)S(1)} %get-tuple-element.13.refs_0_), channel_id=1, source_target_pairs={{0,8},{1,9},{2,10},{3,11},{4,12},{5,13},{6,14},{7,15},{8,0},{9,1},... | collective-permute-start | bytes 319496 | tf_op jit(solution)/shard_map/ppermute | solution.py:272
  7.2 0.0 collective-permute-start
  7.2 1.5 %collective-permute-start.1 = (bf16[13,32,128]{2,1,0:T(8,128)(2,1)S(1)}, bf16[13,32,128]{2,1,0:T(8,128)(2,1)S(1)}, u32[]{:S(2)}, u32[]{:S(2)}) collective-permute-start(bf16[13,32,128]{2,1,0:T(8,128)(2,1)S(1)} %get-tuple-element.12.refs_0_), channel_id=1, source_target_pairs={{0,2},{1,3},{2,0},{3,1},{4,6},{5,7},{6,4},{7,5},{8,10},{9,11},{10,... | collective-permute-start | bytes 319496 | tf_op jit(solution)/shard_map/ppermute | solution.py:272
  8.7 0.3 collective-permute-start.2
  9.0 1.6 %collective-permute-start.3 = (bf16[13,32,128]{2,1,0:T(8,128)(2,1)S(1)}, bf16[13,32,128]{2,1,0:T(8,128)(2,1)S(1)}, u32[]{:S(2)}, u32[]{:S(2)}) collective-permute-start(bf16[13,32,128]{2,1,0:T(8,128)(2,1)S(1)} %get-tuple-element.13.refs_0_), channel_id=1, source_target_pairs={{0,4},{1,5},{2,6},{3,7},{4,0},{5,1},{6,2},{7,3},{8,12},{9,13},{10,... | collective-permute-start | bytes 319496 | tf_op jit(solution)/shard_map/ppermute | solution.py:272
  10.6 1.9 %collective-permute-done.4.refs_5_.refs_2_ = bf16[13,32,128]{2,1,0:T(8,128)(2,1)S(1)} collective-permute-done((bf16[13,32,128]{2,1,0:T(8,128)(2,1)S(1)}, bf16[13,32,128]{2,1,0:T(8,128)(2,1)S(1)}, u32[]{:S(2)}, u32[]{:S(2)}) %collective-permute-start.4) | collective-permute-done | bytes 106528 | tf_op jit(solution)/shard_map/ppermute | solution.py:272
  12.5 0.5 %collective-permute-done.1.refs_2_ = bf16[13,32,128]{2,1,0:T(8,128)(2,1)S(1)} collective-permute-done((bf16[13,32,128]{2,1,0:T(8,128)(2,1)S(1)}, bf16[13,32,128]{2,1,0:T(8,128)(2,1)S(1)}, u32[]{:S(2)}, u32[]{:S(2)}) %collective-permute-start.1) | collective-permute-done | bytes 106528 | tf_op jit(solution)/shard_map/ppermute | solution.py:272
  12.9 1.5 %collective-permute-done.2.refs_3_ = bf16[13,32,128]{2,1,0:T(8,128)(2,1)S(1)} collective-permute-done((bf16[13,32,128]{2,1,0:T(8,128)(2,1)S(1)}, bf16[13,32,128]{2,1,0:T(8,128)(2,1)S(1)}, u32[]{:S(2)}, u32[]{:S(2)}) %collective-permute-start.2) | collective-permute-done | bytes 106528 | tf_op jit(solution)/shard_map/ppermute | solution.py:272
  14.4 0.3 collective-permute-done.3.refs_4_.refs_1_
  14.7 0.4 unpack_x.1
  15.1 1.6 %collective-permute-start.5 = (bf16[49,16,128]{2,1,0:T(8,128)(2,1)S(1)}, bf16[49,16,128]{2,1,0:T(8,128)(2,1)S(1)}, u32[]{:S(2)}, u32[]{:S(2)}) collective-permute-start(bf16[49,16,128]{2,1,0:T(8,128)(2,1)S(1)} %get-tuple-element.15.xp.refs_4_), channel_id=1, source_target_pairs={{0,16},{1,17},{2,18},{3,19},{4,20},{5,21},{6,22},{7,23},{8,24},{9,... | collective-permute-start | bytes 602120 | tf_op jit(solution)/shard_map/ppermute | solution.py:282
  16.7 1.3 %collective-permute-start.6 = (bf16[13,32,128]{2,1,0:T(8,128)(2,1)S(1)}, bf16[13,32,128]{2,1,0:T(8,128)(2,1)S(1)}, u32[]{:S(2)}, u32[]{:S(2)}) collective-permute-start(bf16[13,32,128]{2,1,0:T(8,128)(2,1)S(1)} %collective-permute-done.4.refs_5_.refs_2_), channel_id=1, source_target_pairs={{0,4},{1,5},{2,6},{3,7},{4,0},{5,1},{6,2},{7,3},{8,12},{9,13},{10,... | collective-permute-start | bytes 319496 | tf_op jit(solution)/shard_map/ppermute | solution.py:272
  18.0 2.0 %own_inputs.1 = (f32[7,224,896]{2,1,0:T(8,128)S(1)}, bf16[1568,384]{1,0:T(8,128)(2,1)S(1)}) custom-call(bf16[49,32,128]{2,1,0:T(8,128)(2,1)S(1)} %get-tuple-element.14.x, bf16[49,16,128]{2,1,0:T(8,128)(2,1)S(1)} %get-tuple-element.15.xp.refs_4_), custom_call_target="tpu_custom_call" | custom-call | flops 6000000000 | bytes 4194304 | tf_op jit(solution)/shard_map/own_inputs/pallas_call | solution.py:202
  20.0 1.4 %collective-permute-done.6.refs_3_ = bf16[13,32,128]{2,1,0:T(8,128)(2,1)S(1)} collective-permute-done((bf16[13,32,128]{2,1,0:T(8,128)(2,1)S(1)}, bf16[13,32,128]{2,1,0:T(8,128)(2,1)S(1)}, u32[]{:S(2)}, u32[]{:S(2)}) %collective-permute-start.6) | collective-permute-done | bytes 106528 | tf_op jit(solution)/shard_map/ppermute | solution.py:272
  21.4 0.4 unpack_g.1
  21.9 0.5 %collective-permute-start.7 = (bf16[49,16,128]{2,1,0:T(8,128)(2,1)S(1)}, bf16[49,16,128]{2,1,0:T(8,128)(2,1)S(1)}, u32[]{:S(2)}, u32[]{:S(2)}) collective-permute-start(bf16[49,16,128]{2,1,0:T(8,128)(2,1)S(1)} %get-tuple-element.18.gp), channel_id=1, source_target_pairs={{0,16},{1,17},{2,18},{3,19},{4,20},{5,21},{6,22},{7,23},{8,24},{9,... | collective-permute-start | bytes 602120 | tf_op jit(solution)/shard_map/ppermute | solution.py:282
  22.4 1.4 %terms_own.1.own_ref = f32[32,128]{1,0:T(8,128)S(1)} custom-call(f32[7,224,896]{2,1,0:T(8,128)S(1)} %get-tuple-element.19.t, bf16[49,32,128]{2,1,0:T(8,128)(2,1)S(1)} %get-tuple-element.17.g, bf16[49,16,128]{2,1,0:T(8,128)(2,1)S(1)} %get-tuple-element.18.gp), custom_call_target="tpu_custom_call" | custom-call | flops 6000000000 | bytes 4194304 | tf_op jit(solution)/shard_map/terms_own/pallas_call | solution.py:202
  23.9 2.0 %cross_inputs.1.t = f32[7,224,896]{2,1,0:T(8,128)S(1)} custom-call(bf16[1568,384]{1,0:T(8,128)(2,1)S(1)} %get-tuple-element.16.lx, bf16[49,16,128]{2,1,0:T(8,128)(2,1)S(1)} %collective-permute-done.5.xp), custom_call_target="tpu_custom_call" | custom-call | flops 6000000000 | bytes 4194304 | tf_op jit(solution)/shard_map/cross_inputs/pallas_call | solution.py:202
  25.9 1.9 %collective-permute-done.7.gp = bf16[49,16,128]{2,1,0:T(8,128)(2,1)S(1)} collective-permute-done((bf16[49,16,128]{2,1,0:T(8,128)(2,1)S(1)}, bf16[49,16,128]{2,1,0:T(8,128)(2,1)S(1)}, u32[]{:S(2)}, u32[]{:S(2)}) %collective-permute-start.7) | collective-permute-done | bytes 200736 | tf_op jit(solution)/shard_map/ppermute | solution.py:282
  27.8 1.4 %terms_cross.1 = (f32[8,128]{1,0:T(8,128)S(1)}, f32[1,32]{1,0:T(1,128)S(1)}) custom-call(f32[7,224,896]{2,1,0:T(8,128)S(1)} %cross_inputs.1.t, bf16[49,32,128]{2,1,0:T(8,128)(2,1)S(1)} %get-tuple-element.17.g, bf16[49,16,128]{2,1,0:T(8,128)(2,1)S(1)} %collective-permute-done.7.gp, f32[32,128]{1,0:T(8,128)S(1)} %terms_own.1.own_ref, f32[1,32]{1,0:T(1,128)S(1)} %bitcast.4), custom_call_target="tpu_custom_call" | custom-call | flops 6000000000 | bytes 4194304 | tf_op jit(solution)/shard_map/terms_cross/pallas_call | solution.py:202
  29.3 12.2 %all_to_all.5.terms_ref = f32[32,8,128]{2,1,0:T(8,128)S(1)} all-to-all(f32[32,8,128]{2,1,0:T(8,128)S(1)} %broadcast_in_dim.3), channel_id=1, replica_groups=mesh['rows'=2,'chan'=16] {'rows','chan'}, dimensions={0} | all-to-all | bytes 262144 | tf_op jit(solution)/shard_map/all_to_all | solution.py:301
  41.4 1.8 %solve.1 = (f32[32,32]{1,0:T(8,128)}, f32[32,32]{1,0:T(8,128)}) custom-call(f32[32,8,128]{2,1,0:T(8,128)S(1)} %all_to_all.5.terms_ref, f32[1,32]{1,0:T(1,128)S(1)} %get-tuple-element.21.ridge_ref), custom_call_target="tpu_custom_call" | custom-call | tf_op jit(solution)/shard_map/solve/pallas_call | solution.py:261
  (6 shorter events, 0.0 us)
Async XLA Ops:
  0.6 0.7 %copy-start = (s32[1,32]{1,0:T(1,128)S(1)}, s32[1,32]{1,0:T(1,128)}, u32[]{:S(2)}) copy-start(s32[1,32]{1,0:T(1,128)} %order_hbm.1) | copy-start | bytes 388
  3.0 9.4 %collective-permute-start.4 = (bf16[13,32,128]{2,1,0:T(8,128)(2,1)S(1)}, bf16[13,32,128]{2,1,0:T(8,128)(2,1)S(1)}, u32[]{:S(2)}, u32[]{:S(2)}) collective-permute-start(bf16[13,32,128]{2,1,0:T(8,128)(2,1)S(1)} %get-tuple-element.13.refs_0_), channel_id=1, source_target_pairs={{0,8},{1,9},{2,10},{3,11},{4,12},{5,13},{6,14},{7,15},{8,0},{9,1},... | collective-permute-start | bytes 319496 | tf_op jit(solution)/shard_map/ppermute | solution.py:272
  7.2 5.3 %collective-permute-start = (bf16[13,32,128]{2,1,0:T(8,128)(2,1)S(1)}, bf16[13,32,128]{2,1,0:T(8,128)(2,1)S(1)}, u32[]{:S(2)}, u32[]{:S(2)}) collective-permute-start(bf16[13,32,128]{2,1,0:T(8,128)(2,1)S(1)} %get-tuple-element.12.refs_0_), channel_id=1, source_target_pairs={{0,1},{1,0},{2,3},{3,2},{4,5},{5,4},{6,7},{7,6},{8,9},{9,8},{10,11... | collective-permute-start | bytes 319496 | tf_op jit(solution)/shard_map/ppermute | solution.py:272
  7.2 5.8 %collective-permute-start.1 = (bf16[13,32,128]{2,1,0:T(8,128)(2,1)S(1)}, bf16[13,32,128]{2,1,0:T(8,128)(2,1)S(1)}, u32[]{:S(2)}, u32[]{:S(2)}) collective-permute-start(bf16[13,32,128]{2,1,0:T(8,128)(2,1)S(1)} %get-tuple-element.12.refs_0_), channel_id=1, source_target_pairs={{0,2},{1,3},{2,0},{3,1},{4,6},{5,7},{6,4},{7,5},{8,10},{9,11},{10,... | collective-permute-start | bytes 319496 | tf_op jit(solution)/shard_map/ppermute | solution.py:272
  8.7 5.8 %collective-permute-start.2 = (bf16[13,32,128]{2,1,0:T(8,128)(2,1)S(1)}, bf16[13,32,128]{2,1,0:T(8,128)(2,1)S(1)}, u32[]{:S(2)}, u32[]{:S(2)}) collective-permute-start(bf16[13,32,128]{2,1,0:T(8,128)(2,1)S(1)} %get-tuple-element.12.refs_0_), channel_id=1, source_target_pairs={{0,3},{1,2},{2,1},{3,0},{4,7},{5,6},{6,5},{7,4},{8,11},{9,10},{10,... | collective-permute-start | bytes 319496 | tf_op jit(solution)/shard_map/ppermute | solution.py:272
  9.0 5.7 %collective-permute-start.3 = (bf16[13,32,128]{2,1,0:T(8,128)(2,1)S(1)}, bf16[13,32,128]{2,1,0:T(8,128)(2,1)S(1)}, u32[]{:S(2)}, u32[]{:S(2)}) collective-permute-start(bf16[13,32,128]{2,1,0:T(8,128)(2,1)S(1)} %get-tuple-element.13.refs_0_), channel_id=1, source_target_pairs={{0,4},{1,5},{2,6},{3,7},{4,0},{5,1},{6,2},{7,3},{8,12},{9,13},{10,... | collective-permute-start | bytes 319496 | tf_op jit(solution)/shard_map/ppermute | solution.py:272
  15.1 8.7 %collective-permute-start.5 = (bf16[49,16,128]{2,1,0:T(8,128)(2,1)S(1)}, bf16[49,16,128]{2,1,0:T(8,128)(2,1)S(1)}, u32[]{:S(2)}, u32[]{:S(2)}) collective-permute-start(bf16[49,16,128]{2,1,0:T(8,128)(2,1)S(1)} %get-tuple-element.15.xp.refs_4_), channel_id=1, source_target_pairs={{0,16},{1,17},{2,18},{3,19},{4,20},{5,21},{6,22},{7,23},{8,24},{9,... | collective-permute-start | bytes 602120 | tf_op jit(solution)/shard_map/ppermute | solution.py:282
  16.7 4.7 %collective-permute-start.6 = (bf16[13,32,128]{2,1,0:T(8,128)(2,1)S(1)}, bf16[13,32,128]{2,1,0:T(8,128)(2,1)S(1)}, u32[]{:S(2)}, u32[]{:S(2)}) collective-permute-start(bf16[13,32,128]{2,1,0:T(8,128)(2,1)S(1)} %collective-permute-done.4.refs_5_.refs_2_), channel_id=1, source_target_pairs={{0,4},{1,5},{2,6},{3,7},{4,0},{5,1},{6,2},{7,3},{8,12},{9,13},{10,... | collective-permute-start | bytes 319496 | tf_op jit(solution)/shard_map/ppermute | solution.py:272
  21.9 5.9 %collective-permute-start.7 = (bf16[49,16,128]{2,1,0:T(8,128)(2,1)S(1)}, bf16[49,16,128]{2,1,0:T(8,128)(2,1)S(1)}, u32[]{:S(2)}, u32[]{:S(2)}) collective-permute-start(bf16[49,16,128]{2,1,0:T(8,128)(2,1)S(1)} %get-tuple-element.18.gp), channel_id=1, source_target_pairs={{0,16},{1,17},{2,18},{3,19},{4,20},{5,21},{6,22},{7,23},{8,24},{9,... | collective-permute-start | bytes 602120 | tf_op jit(solution)/shard_map/ppermute | solution.py:282
  23.9 3.9 %copy-start.1 = (f32[32]{0:T(128)S(1)}, f32[32]{0:T(128)}, u32[]{:S(2)}) copy-start(f32[32]{0:T(128)} %param.7) | copy-start | bytes 388

commit v11 on v10

--- a/solution.py
+++ b/solution.py
@@ -27,17 +27,11 @@
     return copies
 
 
-def prep_kernel(order_hbm, x_hbm, g_hbm, xo_ref, go_ref, order_ref, x_ref, g_ref, sems, gs, gt, gout):
-    copies = fetch((order_hbm, g_hbm, x_hbm), (order_ref, g_ref, x_ref), sems)
+def prep_kernel(x_hbm, g_hbm, xo_ref, go_ref, x_ref, g_ref, sems, gs, gt, gout):
+    copies = fetch((g_hbm, x_hbm), (g_ref, x_ref), sems)
     copies[0].wait()
-    copies[1].wait()
-    row_id = lax.broadcasted_iota(jnp.int32, (EX, EX), 0)
-    col_id = lax.broadcasted_iota(jnp.int32, (EX, EX), 1)
-    onehot = jnp.zeros((EX, EX), F32)
     for k in range(EX):
-        example = order_ref[0, k]
-        onehot = jnp.where((row_id == k) & (col_id == example), 1.0, onehot)
-        gs[k * CH:(k + 1) * CH, 0:SPOTS] = g_ref[example].astype(F32)
+        gs[k * CH:(k + 1) * CH, 0:SPOTS] = g_ref[k].astype(F32)
     gt[SPOTS:, :] = jnp.zeros((4 * GROUPS4 - SPOTS, LANES), F32)
     block_id = lax.broadcasted_iota(jnp.int32, (GROUPS4, LANES), 1) // CH
     for quad in range(EX // 4):
@@ -52,35 +46,32 @@
             gout[pl.ds(quad * 4 + e, GROUPS4, stride=EX), :] = merged
     for group in range(GROUPS4):
         go_ref[group] = gout[group * EX:(group + 1) * EX, :].astype(BF16)
-    copies[2].wait()
-    onehot = onehot.astype(BF16)
+    copies[1].wait()
     zero_block = jnp.zeros((EX, CH), BF16)
     for group in range(GROUPS4):
         spots = [4 * group + j for j in range(4)]
-        packed = jnp.concatenate([x_ref[p] if p < SPOTS else zero_block for p in spots], axis=1)
-        xo_ref[group] = jnp.dot(onehot, packed, preferred_element_type=F32).astype(BF16)
-
-
-def prep(order, x, g):
+        xo_ref[group] = jnp.concatenate([x_ref[p] if p < SPOTS else zero_block for p in spots], axis=1)
+
+
+def prep(x, g):
     full = jax.ShapeDtypeStruct((GROUPS4, EX, LANES), BF16)
     vmem = pl.BlockSpec(memory_space=pltpu.VMEM)
     return pl.pallas_call(
         prep_kernel,
         out_shape=(full, full),
-        in_specs=[pl.BlockSpec(memory_space=pltpu.HBM)] * 3,
+        in_specs=[pl.BlockSpec(memory_space=pltpu.HBM)] * 2,
         out_specs=(vmem,) * 2,
         scratch_shapes=[
-            pltpu.SMEM(order.shape, order.dtype),
             pltpu.VMEM(x.shape, x.dtype),
             pltpu.VMEM(g.shape, g.dtype),
-            pltpu.SemaphoreType.DMA((3,)),
+            pltpu.SemaphoreType.DMA((2,)),
             pltpu.VMEM((EX * CH, LANES), F32),
             pltpu.VMEM((4 * GROUPS4, LANES), F32),
             pltpu.VMEM((GROUPS4 * EX, LANES), F32),
         ],
         compiler_params=pltpu.CompilerParams(vmem_limit_bytes=54848 << 10),
         name="prep",
-    )(order, x, g)
+    )(x, g)
 
 
 ROWB = SIDE * EX
@@ -91,8 +82,14 @@
     return pl.CostEstimate(flops=flops, bytes_accessed=moved, transcendentals=0)
 
 
+def order_matrix(order):
+    example = lax.broadcasted_iota(jnp.int32, (EX, EX), 0)
+    return jnp.transpose(jnp.where(example == jnp.broadcast_to(order, (EX, EX)), 1.0, 0.0))
+
+
 def unpack_kernel(*refs):
-    packed, (all_ref, piv_ref) = refs[:4], refs[-2:]
+    packed, order_ref, (all_ref, piv_ref) = refs[:4], refs[4], refs[-2:]
+    pick = order_matrix(order_ref[...])[:PIV_DEV].astype(BF16)
     row = lax.broadcasted_iota(jnp.int32, (4 * LANES, 4 * LANES), 0)
     col = lax.broadcasted_iota(jnp.int32, (4 * LANES, 4 * LANES), 1)
     target = (row // CH) % 4 * LANES + row // LANES * CH + row % CH
@@ -100,25 +97,26 @@
     flat = jnp.concatenate([ref[...].reshape(GROUPS4 * EX, LANES) for ref in packed], axis=1)
     moved = jnp.dot(flat, move, preferred_element_type=F32).astype(BF16)
     for group in range(GROUPS4):
+        rows = moved[group * EX:(group + 1) * EX]
+        pivots = jnp.dot(pick, rows, preferred_element_type=F32).astype(BF16)
         for j in range(4):
             if 4 * group + j < SPOTS:
-                spot = moved[group * EX:(group + 1) * EX, j * LANES:(j + 1) * LANES]
-                all_ref[4 * group + j] = spot
-                piv_ref[4 * group + j] = spot[:PIV_DEV]
-
-
-def unpack(arrays, name, after=()):
+                all_ref[4 * group + j] = rows[:, j * LANES:(j + 1) * LANES]
+                piv_ref[4 * group + j] = pivots[:, j * LANES:(j + 1) * LANES]
+
+
+def unpack(arrays, order, name, after=()):
     vmem = pl.BlockSpec(memory_space=pltpu.VMEM)
     pivots = jax.ShapeDtypeStruct((SPOTS, PIV_DEV, LANES), BF16)
     return pl.pallas_call(
         unpack_kernel,
         out_shape=(jax.ShapeDtypeStruct((SPOTS, EX, LANES), BF16), pivots),
-        in_specs=[vmem] * 4 + [pl.BlockSpec(memory_space=pl.ANY)] * len(after),
+        in_specs=[vmem] * 5 + [pl.BlockSpec(memory_space=pl.ANY)] * len(after),
         out_specs=(vmem,) * 2,
         compiler_params=pltpu.CompilerParams(vmem_limit_bytes=12 << 20),
         cost_estimate=cost(0, 1 << 20),
         name=name,
-    )(*arrays, *after)
+    )(*arrays, order, *after)
 
 
 CONTRACT = (((1,), (1,)), ((), ()))
@@ -185,15 +183,15 @@
     out_ref[...] = panel_terms(g, gp, rg, t)
 
 
-def cross_kernel(t, g, gp, own_ref, ridge, out_ref, ridge_out, rg):
+def cross_kernel(t, g, gp, own_ref, order_ref, ridge, out_ref, ridge_out, rg):
     ridge_out[...] = ridge[...]
     across = panel_terms(g, gp, rg, t)
-    lane = lax.broadcasted_iota(jnp.int32, (8, LANES), 1)
-    is_own = (lane // PIV_DEV) % 2 == lax.axis_index("rows")
-    packed = jnp.zeros((8, LANES), F32)
-    for j in range(4):
-        rows = slice(8 * j, 8 * j + 8)
-        packed = jnp.where(lane // EX == j, jnp.where(is_own, own_ref[rows, :], across[rows]), packed)
+    lane = lax.broadcasted_iota(jnp.int32, (EX, LANES), 1)
+    both = jnp.where((lane // PIV_DEV) % 2 == lax.axis_index("rows"), own_ref[...], across)
+    both = jnp.dot(order_matrix(order_ref[...]), both, precision=lax.Precision.HIGHEST, preferred_element_type=F32)
+    packed = both[:8]
+    for j in range(1, 4):
+        packed = jnp.where(lane[:8] // EX == j, both[8 * j:8 * j + 8], packed)
     out_ref[...] = packed
 
 
@@ -234,7 +232,7 @@
     ridge = jnp.where(row_id == col_id, jnp.broadcast_to(ridge_ref[...], (EX, EX)), 0.0)
     system = 0.5 * (diag + jnp.transpose(diag)) + ridge
     factor = jnp.zeros((EX, EX), F32)
-    step = 4
+    step = 8
     for j in range(0, EX, step):
         sys_cols = [jnp.broadcast_to(system[:, j + k:j + k + 1], (EX, EX)) for k in range(step)]
         pan_cols = [jnp.broadcast_to(panel[:, j + k:j + k + 1], (EX, EX)) for k in range(step)]
@@ -284,18 +282,18 @@
 
 def local_packed(count, activations, cotangents, ordering, ridge):
     x = jnp.transpose(activations, (1, 2, 0, 3)).reshape(SPOTS, EX, CH)
-    xo, go = prep(ordering, x, cotangents)
+    xo, go = prep(x, cotangents)
     own_g = gather(go, count, 8, 4)
-    x_all, x_piv = unpack([xo] + [exchange(xo, count, f) for f in (1, 2, 3)], "unpack_x", (own_g[1], own_g[2]))
+    x_all, x_piv = unpack(gather(xo, count, 2, 1), ordering, "unpack_x", (own_g[1],))
     x_cross = exchange_across(x_piv, count)
-    g_all, g_piv = unpack(own_g, "unpack_g", (x_piv,))
+    g_all, g_piv = unpack(own_g, ordering, "unpack_g", (x_piv,))
     g_cross = exchange_across(g_piv, count)
     flops, product = 6 * 10**9, ((SIDE, ROWB, SIDE * COLB), F32)
     windows = ((SPOTS * EX, 3 * LANES), BF16)
     products, lx = terms(own_inputs_kernel, (x_all, x_piv), (product, windows), 3 * LANES, flops, "own_inputs")
     own_term, = terms(own_kernel, (products, g_all, g_piv), (((EX, LANES), F32),), LANES, flops, "terms_own")
     products, = terms(cross_inputs_kernel, (lx, x_cross), (product,), 3 * LANES, flops, "cross_inputs")
-    arrays = (products, g_all, g_cross, own_term, ridge.reshape(1, EX))
+    arrays = (products, g_all, g_cross, own_term, ordering, ridge.reshape(1, EX))
     term, ridge = terms(cross_kernel, arrays, (((8, LANES), F32), ((1, EX), F32)), LANES, flops, "terms_cross")
     copies = jnp.broadcast_to(term, (2 * count, 8, LANES))
     return final(lax.all_to_all(copies, ("rows", "chan"), 0, 0), ridge)

time: 43.4 us -> 41.8 us (0.963)
  waiting for transfers between devices: 7.43 us -> 5.17 us
  blocking collectives: 12.2 us -> 12.8 us
    ppermute x6, waiting for transfers between devices: 5.5 us -> 2.95 us  [exchange(): return lax.ppermute(value, 'chan', [(i, i ^ flip) for i in range(count)])]
    all_to_all x1, blocking collectives: 12.2 us -> 12.8 us  [local_packed(): return final(lax.all_to_all(copies, ('rows', 'chan'), 0, 0), ridge)]
    pallas_call x4, Pallas kernels: 6.91 us -> 7.37 us  [terms(): pl.pallas_call(kernel, out_shape=tuple((jax.ShapeDtypeStruct(*out) for ou...]
    ppermute x6, starting transfers between devices: 8.81 us -> 8.37 us  [exchange(): return lax.ppermute(value, 'chan', [(i, i ^ flip) for i in range(count)])]
  transfers between devices with their start and end apart: 8 -> 8, of which waited for: 6 -> 3; matrix products, arithmetic and copies ran while one was open for 0% -> 0% of each run, Pallas kernels for 14% -> 16%
where the time goes in v11:
time: 41.8 us; the launch traced here: 41.6 us
  blocking collectives  12.8 us (31%)
  Pallas kernels  11.5 us (28%)
  starting transfers between devices  10.7 us (26%)
  waiting for transfers between devices  5.17 us (12%)
  between operations  0.7 us (2%)
  local copies, waits for them, and re-layouts  0.69 us (2%)
    all_to_all x1, blocking collectives, local_packed(): return final(lax.all_to_all(copies, ('rows', 'chan'), 0, 0), ridge)  12.8 us
    ppermute x6, starting transfers between devices, exchange(): return lax.ppermute(value, 'chan', [(i, i ^ flip) for i in range(count)])  8.37 us
    pallas_call x4, Pallas kernels, terms(): pl.pallas_call(kernel, out_shape=tuple((jax.ShapeDtypeStruct(*out) for ou...  7.37 us
    ppermute x6, waiting for transfers between devices, exchange(): return lax.ppermute(value, 'chan', [(i, i ^ flip) for i in range(count)])  2.95 us
    ppermute x2, starting transfers between devices, exchange_across(): return lax.ppermute(value, ('rows', 'chan'), pairs)  2.29 us
    ppermute x2, waiting for transfers between devices, exchange_across(): return lax.ppermute(value, ('rows', 'chan'), pairs)  2.22 us
    pallas_call x1, Pallas kernels, prep(): pl.pallas_call(prep_kernel, out_shape=(full, full), in_specs=[pl.BlockSpe...  1.62 us
    pallas_call x1, Pallas kernels, final(): pl.pallas_call(final_kernel, out_shape=(out, out), in_specs=[vmem] * 2, o...  1.47 us
  transfers between devices with their start and end apart: 8, of which 3 were waited for; matrix products, arithmetic and copies ran while one was open for 0% of the time, Pallas kernels for 16%

profile of v11, /device:TPU:0, one launch (start us, length us, event | category | flops | bytes accessed | tf_op | source)
XLA Modules:
  0.0 41.6 jit_solution(3010740177092963273)
XLA Ops:
  0.6 1.6 %prep.1 = (bf16[13,32,128]{2,1,0:T(8,128)(2,1)S(1)}, bf16[13,32,128]{2,1,0:T(8,128)(2,1)S(1)}) custom-call(bf16[49,32,32]{2,1,0:T(8,128)(2,1)} %bitcast.5, bf16[32,32,49]{2,1,0:T(8,128)(2,1)} %g_hbm.1), custom_call_target="tpu_custom_call" | custom-call | tf_op jit(solution)/shard_map/prep/pallas_call | solution.py:59
  2.3 3.0 %collective-permute-start.1 = (bf16[13,32,128]{2,1,0:T(8,128)(2,1)S(1)}, bf16[13,32,128]{2,1,0:T(8,128)(2,1)S(1)}, u32[]{:S(2)}, u32[]{:S(2)}) collective-permute-start(bf16[13,32,128]{2,1,0:T(8,128)(2,1)S(1)} %get-tuple-element.12.refs_0_), channel_id=1, source_target_pairs={{0,2},{1,3},{2,0},{3,1},{4,6},{5,7},{6,4},{7,5},{8,10},{9,11},{10,... | collective-permute-start | bytes 319496 | tf_op jit(solution)/shard_map/ppermute | solution.py:270
  5.3 2.6 %collective-permute-start.5 = (bf16[13,32,128]{2,1,0:T(8,128)(2,1)S(1)}, bf16[13,32,128]{2,1,0:T(8,128)(2,1)S(1)}, u32[]{:S(2)}, u32[]{:S(2)}) collective-permute-start(bf16[13,32,128]{2,1,0:T(8,128)(2,1)S(1)} %get-tuple-element.13.refs_0_), channel_id=1, source_target_pairs={{0,8},{1,9},{2,10},{3,11},{4,12},{5,13},{6,14},{7,15},{8,0},{9,1},... | collective-permute-start | bytes 319496 | tf_op jit(solution)/shard_map/ppermute | solution.py:270
  7.9 1.6 %collective-permute-start.3 = (bf16[13,32,128]{2,1,0:T(8,128)(2,1)S(1)}, bf16[13,32,128]{2,1,0:T(8,128)(2,1)S(1)}, u32[]{:S(2)}, u32[]{:S(2)}) collective-permute-start(bf16[13,32,128]{2,1,0:T(8,128)(2,1)S(1)} %get-tuple-element.13.refs_0_), channel_id=1, source_target_pairs={{0,4},{1,5},{2,6},{3,7},{4,0},{5,1},{6,2},{7,3},{8,12},{9,13},{10,... | collective-permute-start | bytes 319496 | tf_op jit(solution)/shard_map/ppermute | solution.py:270
  9.5 0.0 collective-permute-done.1.refs_2_
  9.5 0.5 %collective-permute-start.2 = (bf16[13,32,128]{2,1,0:T(8,128)(2,1)S(1)}, bf16[13,32,128]{2,1,0:T(8,128)(2,1)S(1)}, u32[]{:S(2)}, u32[]{:S(2)}) collective-permute-start(bf16[13,32,128]{2,1,0:T(8,128)(2,1)S(1)} %collective-permute-done.1.refs_2_), channel_id=1, source_target_pairs={{0,1},{1,0},{2,3},{3,2},{4,5},{5,4},{6,7},{7,6},{8,9},{9,8},{10,11... | collective-permute-start | bytes 319496 | tf_op jit(solution)/shard_map/ppermute | solution.py:270
  10.0 2.9 %collective-permute-done.5.refs_2_ = bf16[13,32,128]{2,1,0:T(8,128)(2,1)S(1)} collective-permute-done((bf16[13,32,128]{2,1,0:T(8,128)(2,1)S(1)}, bf16[13,32,128]{2,1,0:T(8,128)(2,1)S(1)}, u32[]{:S(2)}, u32[]{:S(2)}) %collective-permute-start.5) | collective-permute-done | bytes 106528 | tf_op jit(solution)/shard_map/ppermute | solution.py:270
  12.9 0.7 %collective-permute-start.6 = (bf16[13,32,128]{2,1,0:T(8,128)(2,1)S(1)}, bf16[13,32,128]{2,1,0:T(8,128)(2,1)S(1)}, u32[]{:S(2)}, u32[]{:S(2)}) collective-permute-start(bf16[13,32,128]{2,1,0:T(8,128)(2,1)S(1)} %collective-permute-done.5.refs_2_), channel_id=1, source_target_pairs={{0,4},{1,5},{2,6},{3,7},{4,0},{5,1},{6,2},{7,3},{8,12},{9,13},{10,... | collective-permute-start | bytes 319496 | tf_op jit(solution)/shard_map/ppermute | solution.py:270
  13.6 0.0 collective-permute-done.3.refs_5_.refs_1_
  13.6 0.0 collective-permute-done.refs_1_
  13.6 0.0 copy-start
  13.6 0.6 %copy-done = s32[1,32]{1,0:T(1,128)S(1)} copy-done((s32[1,32]{1,0:T(1,128)S(1)}, s32[1,32]{1,0:T(1,128)}, u32[]{:S(2)}) %copy-start) | copy-done | bytes 152
  14.2 0.5 %unpack_x.1 = (bf16[49,32,128]{2,1,0:T(8,128)(2,1)S(1)}, bf16[49,16,128]{2,1,0:T(8,128)(2,1)S(1)}) custom-call(bf16[13,32,128]{2,1,0:T(8,128)(2,1)S(1)} %get-tuple-element.12.refs_0_, bf16[13,32,128]{2,1,0:T(8,128)(2,1)S(1)} %collective-permute-done.refs_1_, bf16[13,32,128]{2,1,0:T(8,128)(2,1)S(1)} %collective-permute-done.1.refs_2_, ...), custom_call_target="tpu_custom_call" | custom-call | bytes 1048576 | tf_op jit(solution)/shard_map/unpack_x/pallas_call | solution.py:111
  14.8 1.6 %collective-permute-start.4 = (bf16[49,16,128]{2,1,0:T(8,128)(2,1)S(1)}, bf16[49,16,128]{2,1,0:T(8,128)(2,1)S(1)}, u32[]{:S(2)}, u32[]{:S(2)}) collective-permute-start(bf16[49,16,128]{2,1,0:T(8,128)(2,1)S(1)} %get-tuple-element.15.xp.refs_5_), channel_id=1, source_target_pairs={{0,16},{1,17},{2,18},{3,19},{4,20},{5,21},{6,22},{7,23},{8,24},{9,... | collective-permute-start | bytes 602120 | tf_op jit(solution)/shard_map/ppermute | solution.py:280
  16.3 2.1 %own_inputs.1 = (f32[7,224,896]{2,1,0:T(8,128)S(1)}, bf16[1568,384]{1,0:T(8,128)(2,1)S(1)}) custom-call(bf16[49,32,128]{2,1,0:T(8,128)(2,1)S(1)} %get-tuple-element.14.x, bf16[49,16,128]{2,1,0:T(8,128)(2,1)S(1)} %get-tuple-element.15.xp.refs_5_), custom_call_target="tpu_custom_call" | custom-call | flops 6000000000 | bytes 4194304 | tf_op jit(solution)/shard_map/own_inputs/pallas_call | solution.py:200
  18.4 0.5 %unpack_g.1 = (bf16[49,32,128]{2,1,0:T(8,128)(2,1)S(1)}, bf16[49,16,128]{2,1,0:T(8,128)(2,1)S(1)}) custom-call(bf16[13,32,128]{2,1,0:T(8,128)(2,1)S(1)} %get-tuple-element.13.refs_0_, bf16[13,32,128]{2,1,0:T(8,128)(2,1)S(1)} %collective-permute-done.3.refs_5_.refs_1_, bf16[13,32,128]{2,1,0:T(8,128)(2,1)S(1)} %collective-permute-done.5.refs_2_, ...), custom_call_target="tpu_custom_call" | custom-call | bytes 1048576 | tf_op jit(solution)/shard_map/unpack_g/pallas_call | solution.py:111
  19.0 0.7 %collective-permute-start.7 = (bf16[49,16,128]{2,1,0:T(8,128)(2,1)S(1)}, bf16[49,16,128]{2,1,0:T(8,128)(2,1)S(1)}, u32[]{:S(2)}, u32[]{:S(2)}) collective-permute-start(bf16[49,16,128]{2,1,0:T(8,128)(2,1)S(1)} %get-tuple-element.18.gp), channel_id=1, source_target_pairs={{0,16},{1,17},{2,18},{3,19},{4,20},{5,21},{6,22},{7,23},{8,24},{9,... | collective-permute-start | bytes 602120 | tf_op jit(solution)/shard_map/ppermute | solution.py:280
  19.7 1.4 %terms_own.1.own_ref = f32[32,128]{1,0:T(8,128)S(1)} custom-call(f32[7,224,896]{2,1,0:T(8,128)S(1)} %get-tuple-element.19.t, bf16[49,32,128]{2,1,0:T(8,128)(2,1)S(1)} %get-tuple-element.17.g, bf16[49,16,128]{2,1,0:T(8,128)(2,1)S(1)} %get-tuple-element.18.gp), custom_call_target="tpu_custom_call" | custom-call | flops 6000000000 | bytes 4194304 | tf_op jit(solution)/shard_map/terms_own/pallas_call | solution.py:200
  21.1 0.3 collective-permute-done.4.xp
  21.4 2.0 %cross_inputs.1.t = f32[7,224,896]{2,1,0:T(8,128)S(1)} custom-call(bf16[1568,384]{1,0:T(8,128)(2,1)S(1)} %get-tuple-element.16.lx, bf16[49,16,128]{2,1,0:T(8,128)(2,1)S(1)} %collective-permute-done.4.xp), custom_call_target="tpu_custom_call" | custom-call | flops 6000000000 | bytes 4194304 | tf_op jit(solution)/shard_map/cross_inputs/pallas_call | solution.py:200
  23.5 1.9 %collective-permute-done.7.gp = bf16[49,16,128]{2,1,0:T(8,128)(2,1)S(1)} collective-permute-done((bf16[49,16,128]{2,1,0:T(8,128)(2,1)S(1)}, bf16[49,16,128]{2,1,0:T(8,128)(2,1)S(1)}, u32[]{:S(2)}, u32[]{:S(2)}) %collective-permute-start.7) | collective-permute-done | bytes 200736 | tf_op jit(solution)/shard_map/ppermute | solution.py:280
  25.4 1.8 %terms_cross.1 = (f32[8,128]{1,0:T(8,128)S(1)}, f32[1,32]{1,0:T(1,128)S(1)}) custom-call(f32[7,224,896]{2,1,0:T(8,128)S(1)} %cross_inputs.1.t, bf16[49,32,128]{2,1,0:T(8,128)(2,1)S(1)} %get-tuple-element.17.g, bf16[49,16,128]{2,1,0:T(8,128)(2,1)S(1)} %collective-permute-done.7.gp, f32[32,128]{1,0:T(8,128)S(1)} %terms_own.1.own_ref, s32[1,32]{1,0:T(1,128)S(1)} %copy-done.1, ...), custom_call_target="tpu_custom_call" | custom-call | flops 6000000000 | bytes 4194304 | tf_op jit(solution)/shard_map/terms_cross/pallas_call | solution.py:200
  27.3 12.8 %all_to_all.5.terms_ref = f32[32,8,128]{2,1,0:T(8,128)S(1)} all-to-all(f32[32,8,128]{2,1,0:T(8,128)S(1)} %broadcast_in_dim.3), channel_id=1, replica_groups=mesh['rows'=2,'chan'=16] {'rows','chan'}, dimensions={0} | all-to-all | bytes 262144 | tf_op jit(solution)/shard_map/all_to_all | solution.py:299
  40.1 1.5 %solve.1 = (f32[32,32]{1,0:T(8,128)}, f32[32,32]{1,0:T(8,128)}) custom-call(f32[32,8,128]{2,1,0:T(8,128)S(1)} %all_to_all.5.terms_ref, f32[1,32]{1,0:T(1,128)S(1)} %get-tuple-element.21.ridge_ref), custom_call_target="tpu_custom_call" | custom-call | tf_op jit(solution)/shard_map/solve/pallas_call | solution.py:259
  (8 shorter events, 0.0 us)
Async XLA Ops:
  2.3 7.2 %collective-permute-start.1 = (bf16[13,32,128]{2,1,0:T(8,128)(2,1)S(1)}, bf16[13,32,128]{2,1,0:T(8,128)(2,1)S(1)}, u32[]{:S(2)}, u32[]{:S(2)}) collective-permute-start(bf16[13,32,128]{2,1,0:T(8,128)(2,1)S(1)} %get-tuple-element.12.refs_0_), channel_id=1, source_target_pairs={{0,2},{1,3},{2,0},{3,1},{4,6},{5,7},{6,4},{7,5},{8,10},{9,11},{10,... | collective-permute-start | bytes 319496 | tf_op jit(solution)/shard_map/ppermute | solution.py:270
  5.3 7.6 %collective-permute-start.5 = (bf16[13,32,128]{2,1,0:T(8,128)(2,1)S(1)}, bf16[13,32,128]{2,1,0:T(8,128)(2,1)S(1)}, u32[]{:S(2)}, u32[]{:S(2)}) collective-permute-start(bf16[13,32,128]{2,1,0:T(8,128)(2,1)S(1)} %get-tuple-element.13.refs_0_), channel_id=1, source_target_pairs={{0,8},{1,9},{2,10},{3,11},{4,12},{5,13},{6,14},{7,15},{8,0},{9,1},... | collective-permute-start | bytes 319496 | tf_op jit(solution)/shard_map/ppermute | solution.py:270
  7.9 5.7 %collective-permute-start.3 = (bf16[13,32,128]{2,1,0:T(8,128)(2,1)S(1)}, bf16[13,32,128]{2,1,0:T(8,128)(2,1)S(1)}, u32[]{:S(2)}, u32[]{:S(2)}) collective-permute-start(bf16[13,32,128]{2,1,0:T(8,128)(2,1)S(1)} %get-tuple-element.13.refs_0_), channel_id=1, source_target_pairs={{0,4},{1,5},{2,6},{3,7},{4,0},{5,1},{6,2},{7,3},{8,12},{9,13},{10,... | collective-permute-start | bytes 319496 | tf_op jit(solution)/shard_map/ppermute | solution.py:270
  9.5 4.1 %collective-permute-start = (bf16[13,32,128]{2,1,0:T(8,128)(2,1)S(1)}, bf16[13,32,128]{2,1,0:T(8,128)(2,1)S(1)}, u32[]{:S(2)}, u32[]{:S(2)}) collective-permute-start(bf16[13,32,128]{2,1,0:T(8,128)(2,1)S(1)} %get-tuple-element.12.refs_0_), channel_id=1, source_target_pairs={{0,1},{1,0},{2,3},{3,2},{4,5},{5,4},{6,7},{7,6},{8,9},{9,8},{10,11... | collective-permute-start | bytes 319496 | tf_op jit(solution)/shard_map/ppermute | solution.py:270
  9.5 4.1 %collective-permute-start.2 = (bf16[13,32,128]{2,1,0:T(8,128)(2,1)S(1)}, bf16[13,32,128]{2,1,0:T(8,128)(2,1)S(1)}, u32[]{:S(2)}, u32[]{:S(2)}) collective-permute-start(bf16[13,32,128]{2,1,0:T(8,128)(2,1)S(1)} %collective-permute-done.1.refs_2_), channel_id=1, source_target_pairs={{0,1},{1,0},{2,3},{3,2},{4,5},{5,4},{6,7},{7,6},{8,9},{9,8},{10,11... | collective-permute-start | bytes 319496 | tf_op jit(solution)/shard_map/ppermute | solution.py:270
  12.9 5.5 %collective-permute-start.6 = (bf16[13,32,128]{2,1,0:T(8,128)(2,1)S(1)}, bf16[13,32,128]{2,1,0:T(8,128)(2,1)S(1)}, u32[]{:S(2)}, u32[]{:S(2)}) collective-permute-start(bf16[13,32,128]{2,1,0:T(8,128)(2,1)S(1)} %collective-permute-done.5.refs_2_), channel_id=1, source_target_pairs={{0,4},{1,5},{2,6},{3,7},{4,0},{5,1},{6,2},{7,3},{8,12},{9,13},{10,... | collective-permute-start | bytes 319496 | tf_op jit(solution)/shard_map/ppermute | solution.py:270
  13.6 0.7 %copy-start = (s32[1,32]{1,0:T(1,128)S(1)}, s32[1,32]{1,0:T(1,128)}, u32[]{:S(2)}) copy-start(s32[1,32]{1,0:T(1,128)} %order_ref.1) | copy-start | bytes 388
  14.8 6.6 %collective-permute-start.4 = (bf16[49,16,128]{2,1,0:T(8,128)(2,1)S(1)}, bf16[49,16,128]{2,1,0:T(8,128)(2,1)S(1)}, u32[]{:S(2)}, u32[]{:S(2)}) collective-permute-start(bf16[49,16,128]{2,1,0:T(8,128)(2,1)S(1)} %get-tuple-element.15.xp.refs_5_), channel_id=1, source_target_pairs={{0,16},{1,17},{2,18},{3,19},{4,20},{5,21},{6,22},{7,23},{8,24},{9,... | collective-permute-start | bytes 602120 | tf_op jit(solution)/shard_map/ppermute | solution.py:280
  16.3 2.1 %copy-start.1 = (s32[1,32]{1,0:T(1,128)S(1)}, s32[1,32]{1,0:T(1,128)}, u32[]{:S(2)}) copy-start(s32[1,32]{1,0:T(1,128)} %order_ref.1) | copy-start | bytes 388
  19.0 6.4 %collective-permute-start.7 = (bf16[49,16,128]{2,1,0:T(8,128)(2,1)S(1)}, bf16[49,16,128]{2,1,0:T(8,128)(2,1)S(1)}, u32[]{:S(2)}, u32[]{:S(2)}) collective-permute-start(bf16[49,16,128]{2,1,0:T(8,128)(2,1)S(1)} %get-tuple-element.18.gp), channel_id=1, source_target_pairs={{0,16},{1,17},{2,18},{3,19},{4,20},{5,21},{6,22},{7,23},{8,24},{9,... | collective-permute-start | bytes 602120 | tf_op jit(solution)/shard_map/ppermute | solution.py:280
  21.4 4.0 %copy-start.2 = (f32[32]{0:T(128)S(1)}, f32[32]{0:T(128)}, u32[]{:S(2)}) copy-start(f32[32]{0:T(128)} %param.7) | copy-start | bytes 388

commit v12 on v9

--- a/solution.py
+++ b/solution.py
@@ -234,7 +234,7 @@
     ridge = jnp.where(row_id == col_id, jnp.broadcast_to(ridge_ref[...], (EX, EX)), 0.0)
     system = 0.5 * (diag + jnp.transpose(diag)) + ridge
     factor = jnp.zeros((EX, EX), F32)
-    step = 4
+    step = 8
     for j in range(0, EX, step):
         sys_cols = [jnp.broadcast_to(system[:, j + k:j + k + 1], (EX, EX)) for k in range(step)]
         pan_cols = [jnp.broadcast_to(panel[:, j + k:j + k + 1], (EX, EX)) for k in range(step)]

time: 41.9 us -> 41.5 us (level)
  no operation moved by 1% of the time
where the time goes in v12:
time: 41.5 us; the launch traced here: 41.3 us
  blocking collectives  12.9 us (31%)
  starting transfers between devices  11.5 us (28%)
  Pallas kernels  11.2 us (27%)
  waiting for transfers between devices  4.5 us (11%)
  between operations  0.7 us (2%)
  local copies, waits for them, and re-layouts  0.67 us (2%)
    all_to_all x1, blocking collectives, local_packed(): return final(lax.all_to_all(copies, ('rows', 'chan'), 0, 0), ridge)  12.9 us
    ppermute x6, starting transfers between devices, exchange(): return lax.ppermute(value, 'chan', [(i, i ^ flip) for i in range(count)])  8.37 us
    pallas_call x4, Pallas kernels, terms(): pl.pallas_call(kernel, out_shape=tuple((jax.ShapeDtypeStruct(*out) for ou...  7.09 us
    ppermute x2, starting transfers between devices, exchange_across(): return lax.ppermute(value, ('rows', 'chan'), pairs)  3.08 us
    ppermute x6, waiting for transfers between devices, exchange(): return lax.ppermute(value, 'chan', [(i, i ^ flip) for i in range(count)])  2.95 us
    pallas_call x1, Pallas kernels, prep(): pl.pallas_call(prep_kernel, out_shape=(full, full), in_specs=[pl.BlockSpe...  1.75 us
    ppermute x2, waiting for transfers between devices, exchange_across(): return lax.ppermute(value, ('rows', 'chan'), pairs)  1.55 us
    pallas_call x1, Pallas kernels, final(): pl.pallas_call(final_kernel, out_shape=(out, out), in_specs=[vmem] * 2, o...  1.47 us
  transfers between devices with their start and end apart: 8, of which 2 were waited for; matrix products, arithmetic and copies ran while one was open for 0% of the time, Pallas kernels for 15%

profile of v12, /device:TPU:0, one launch (start us, length us, event | category | flops | bytes accessed | tf_op | source)
XLA Modules:
  0.0 41.3 jit_solution(2118583527478768195)
XLA Ops:
  0.6 0.6 %copy-done = s32[1,32]{1,0:T(1,128)S(1)} copy-done((s32[1,32]{1,0:T(1,128)S(1)}, s32[1,32]{1,0:T(1,128)}, u32[]{:S(2)}) %copy-start) | copy-done | bytes 152
  1.3 1.8 %prep.1 = (bf16[13,32,128]{2,1,0:T(8,128)(2,1)S(1)}, bf16[13,32,128]{2,1,0:T(8,128)(2,1)S(1)}) custom-call(s32[1,32]{1,0:T(1,128)S(1)} %copy-done, bf16[49,32,32]{2,1,0:T(8,128)(2,1)} %bitcast.5, bf16[32,32,49]{2,1,0:T(8,128)(2,1)} %g_hbm.1), custom_call_target="tpu_custom_call" | custom-call | tf_op jit(solution)/shard_map/prep/pallas_call | solution.py:67
  3.0 3.0 %collective-permute-start.1 = (bf16[13,32,128]{2,1,0:T(8,128)(2,1)S(1)}, bf16[13,32,128]{2,1,0:T(8,128)(2,1)S(1)}, u32[]{:S(2)}, u32[]{:S(2)}) collective-permute-start(bf16[13,32,128]{2,1,0:T(8,128)(2,1)S(1)} %get-tuple-element.12.refs_0_), channel_id=1, source_target_pairs={{0,2},{1,3},{2,0},{3,1},{4,6},{5,7},{6,4},{7,5},{8,10},{9,11},{10,... | collective-permute-start | bytes 319496 | tf_op jit(solution)/shard_map/ppermute | solution.py:272
  6.1 2.6 %collective-permute-start.5 = (bf16[13,32,128]{2,1,0:T(8,128)(2,1)S(1)}, bf16[13,32,128]{2,1,0:T(8,128)(2,1)S(1)}, u32[]{:S(2)}, u32[]{:S(2)}) collective-permute-start(bf16[13,32,128]{2,1,0:T(8,128)(2,1)S(1)} %get-tuple-element.13.refs_0_), channel_id=1, source_target_pairs={{0,8},{1,9},{2,10},{3,11},{4,12},{5,13},{6,14},{7,15},{8,0},{9,1},... | collective-permute-start | bytes 319496 | tf_op jit(solution)/shard_map/ppermute | solution.py:272
  8.7 1.6 %collective-permute-start.3 = (bf16[13,32,128]{2,1,0:T(8,128)(2,1)S(1)}, bf16[13,32,128]{2,1,0:T(8,128)(2,1)S(1)}, u32[]{:S(2)}, u32[]{:S(2)}) collective-permute-start(bf16[13,32,128]{2,1,0:T(8,128)(2,1)S(1)} %get-tuple-element.13.refs_0_), channel_id=1, source_target_pairs={{0,4},{1,5},{2,6},{3,7},{4,0},{5,1},{6,2},{7,3},{8,12},{9,13},{10,... | collective-permute-start | bytes 319496 | tf_op jit(solution)/shard_map/ppermute | solution.py:272
  10.2 0.0 collective-permute-start
  10.3 0.0 collective-permute-done.1.refs_2_
  10.3 0.5 %collective-permute-start.2 = (bf16[13,32,128]{2,1,0:T(8,128)(2,1)S(1)}, bf16[13,32,128]{2,1,0:T(8,128)(2,1)S(1)}, u32[]{:S(2)}, u32[]{:S(2)}) collective-permute-start(bf16[13,32,128]{2,1,0:T(8,128)(2,1)S(1)} %collective-permute-done.1.refs_2_), channel_id=1, source_target_pairs={{0,1},{1,0},{2,3},{3,2},{4,5},{5,4},{6,7},{7,6},{8,9},{9,8},{10,11... | collective-permute-start | bytes 319496 | tf_op jit(solution)/shard_map/ppermute | solution.py:272
  10.8 2.9 %collective-permute-done.5.refs_2_ = bf16[13,32,128]{2,1,0:T(8,128)(2,1)S(1)} collective-permute-done((bf16[13,32,128]{2,1,0:T(8,128)(2,1)S(1)}, bf16[13,32,128]{2,1,0:T(8,128)(2,1)S(1)}, u32[]{:S(2)}, u32[]{:S(2)}) %collective-permute-start.5) | collective-permute-done | bytes 106528 | tf_op jit(solution)/shard_map/ppermute | solution.py:272
  13.7 0.7 %collective-permute-start.6 = (bf16[13,32,128]{2,1,0:T(8,128)(2,1)S(1)}, bf16[13,32,128]{2,1,0:T(8,128)(2,1)S(1)}, u32[]{:S(2)}, u32[]{:S(2)}) collective-permute-start(bf16[13,32,128]{2,1,0:T(8,128)(2,1)S(1)} %collective-permute-done.5.refs_2_), channel_id=1, source_target_pairs={{0,4},{1,5},{2,6},{3,7},{4,0},{5,1},{6,2},{7,3},{8,12},{9,13},{10,... | collective-permute-start | bytes 319496 | tf_op jit(solution)/shard_map/ppermute | solution.py:272
  14.4 0.0 collective-permute-done.3.refs_4_.refs_1_
  14.4 0.4 %unpack_x.1 = (bf16[49,32,128]{2,1,0:T(8,128)(2,1)S(1)}, bf16[49,16,128]{2,1,0:T(8,128)(2,1)S(1)}) custom-call(bf16[13,32,128]{2,1,0:T(8,128)(2,1)S(1)} %get-tuple-element.12.refs_0_, bf16[13,32,128]{2,1,0:T(8,128)(2,1)S(1)} %collective-permute-done.refs_1_, bf16[13,32,128]{2,1,0:T(8,128)(2,1)S(1)} %collective-permute-done.1.refs_2_, ...), custom_call_target="tpu_custom_call" | custom-call | bytes 1048576 | tf_op jit(solution)/shard_map/unpack_x/pallas_call | solution.py:113
  14.8 1.6 %collective-permute-start.4 = (bf16[49,16,128]{2,1,0:T(8,128)(2,1)S(1)}, bf16[49,16,128]{2,1,0:T(8,128)(2,1)S(1)}, u32[]{:S(2)}, u32[]{:S(2)}) collective-permute-start(bf16[49,16,128]{2,1,0:T(8,128)(2,1)S(1)} %get-tuple-element.15.xp.refs_4_), channel_id=1, source_target_pairs={{0,16},{1,17},{2,18},{3,19},{4,20},{5,21},{6,22},{7,23},{8,24},{9,... | collective-permute-start | bytes 602120 | tf_op jit(solution)/shard_map/ppermute | solution.py:282
  16.4 2.1 %own_inputs.1 = (f32[7,224,896]{2,1,0:T(8,128)S(1)}, bf16[1568,384]{1,0:T(8,128)(2,1)S(1)}) custom-call(bf16[49,32,128]{2,1,0:T(8,128)(2,1)S(1)} %get-tuple-element.14.x, bf16[49,16,128]{2,1,0:T(8,128)(2,1)S(1)} %get-tuple-element.15.xp.refs_4_), custom_call_target="tpu_custom_call" | custom-call | flops 6000000000 | bytes 4194304 | tf_op jit(solution)/shard_map/own_inputs/pallas_call | solution.py:202
  18.4 0.4 %unpack_g.1 = (bf16[49,32,128]{2,1,0:T(8,128)(2,1)S(1)}, bf16[49,16,128]{2,1,0:T(8,128)(2,1)S(1)}) custom-call(bf16[13,32,128]{2,1,0:T(8,128)(2,1)S(1)} %get-tuple-element.13.refs_0_, bf16[13,32,128]{2,1,0:T(8,128)(2,1)S(1)} %collective-permute-done.3.refs_4_.refs_1_, bf16[13,32,128]{2,1,0:T(8,128)(2,1)S(1)} %collective-permute-done.5.refs_2_, ...), custom_call_target="tpu_custom_call" | custom-call | bytes 1048576 | tf_op jit(solution)/shard_map/unpack_g/pallas_call | solution.py:113
  18.9 1.5 %collective-permute-start.7 = (bf16[49,16,128]{2,1,0:T(8,128)(2,1)S(1)}, bf16[49,16,128]{2,1,0:T(8,128)(2,1)S(1)}, u32[]{:S(2)}, u32[]{:S(2)}) collective-permute-start(bf16[49,16,128]{2,1,0:T(8,128)(2,1)S(1)} %get-tuple-element.18.gp), channel_id=1, source_target_pairs={{0,16},{1,17},{2,18},{3,19},{4,20},{5,21},{6,22},{7,23},{8,24},{9,... | collective-permute-start | bytes 602120 | tf_op jit(solution)/shard_map/ppermute | solution.py:282
  20.4 1.4 %terms_own.1.own_ref = f32[32,128]{1,0:T(8,128)S(1)} custom-call(f32[7,224,896]{2,1,0:T(8,128)S(1)} %get-tuple-element.19.t, bf16[49,32,128]{2,1,0:T(8,128)(2,1)S(1)} %get-tuple-element.17.g, bf16[49,16,128]{2,1,0:T(8,128)(2,1)S(1)} %get-tuple-element.18.gp), custom_call_target="tpu_custom_call" | custom-call | flops 6000000000 | bytes 4194304 | tf_op jit(solution)/shard_map/terms_own/pallas_call | solution.py:202
  21.8 0.0 collective-permute-done.4.xp
  21.8 0.0 copy-start.1
  21.8 2.0 %cross_inputs.1.t = f32[7,224,896]{2,1,0:T(8,128)S(1)} custom-call(bf16[1568,384]{1,0:T(8,128)(2,1)S(1)} %get-tuple-element.16.lx, bf16[49,16,128]{2,1,0:T(8,128)(2,1)S(1)} %collective-permute-done.4.xp), custom_call_target="tpu_custom_call" | custom-call | flops 6000000000 | bytes 4194304 | tf_op jit(solution)/shard_map/cross_inputs/pallas_call | solution.py:202
  23.9 1.6 %collective-permute-done.7.gp = bf16[49,16,128]{2,1,0:T(8,128)(2,1)S(1)} collective-permute-done((bf16[49,16,128]{2,1,0:T(8,128)(2,1)S(1)}, bf16[49,16,128]{2,1,0:T(8,128)(2,1)S(1)}, u32[]{:S(2)}, u32[]{:S(2)}) %collective-permute-start.7) | collective-permute-done | bytes 200736 | tf_op jit(solution)/shard_map/ppermute | solution.py:282
  25.4 1.6 %terms_cross.1 = (f32[8,128]{1,0:T(8,128)S(1)}, f32[1,32]{1,0:T(1,128)S(1)}) custom-call(f32[7,224,896]{2,1,0:T(8,128)S(1)} %cross_inputs.1.t, bf16[49,32,128]{2,1,0:T(8,128)(2,1)S(1)} %get-tuple-element.17.g, bf16[49,16,128]{2,1,0:T(8,128)(2,1)S(1)} %collective-permute-done.7.gp, f32[32,128]{1,0:T(8,128)S(1)} %terms_own.1.own_ref, f32[1,32]{1,0:T(1,128)S(1)} %bitcast.4), custom_call_target="tpu_custom_call" | custom-call | flops 6000000000 | bytes 4194304 | tf_op jit(solution)/shard_map/terms_cross/pallas_call | solution.py:202
  27.0 12.9 %all_to_all.5.terms_ref = f32[32,8,128]{2,1,0:T(8,128)S(1)} all-to-all(f32[32,8,128]{2,1,0:T(8,128)S(1)} %broadcast_in_dim.3), channel_id=1, replica_groups=mesh['rows'=2,'chan'=16] {'rows','chan'}, dimensions={0} | all-to-all | bytes 262144 | tf_op jit(solution)/shard_map/all_to_all | solution.py:301
  39.9 1.5 %solve.1 = (f32[32,32]{1,0:T(8,128)}, f32[32,32]{1,0:T(8,128)}) custom-call(f32[32,8,128]{2,1,0:T(8,128)S(1)} %all_to_all.5.terms_ref, f32[1,32]{1,0:T(1,128)S(1)} %get-tuple-element.21.ridge_ref), custom_call_target="tpu_custom_call" | custom-call | tf_op jit(solution)/shard_map/solve/pallas_call | solution.py:261
  (6 shorter events, 0.0 us)
Async XLA Ops:
  0.6 0.7 %copy-start = (s32[1,32]{1,0:T(1,128)S(1)}, s32[1,32]{1,0:T(1,128)}, u32[]{:S(2)}) copy-start(s32[1,32]{1,0:T(1,128)} %order_hbm.1) | copy-start | bytes 388
  3.0 7.2 %collective-permute-start.1 = (bf16[13,32,128]{2,1,0:T(8,128)(2,1)S(1)}, bf16[13,32,128]{2,1,0:T(8,128)(2,1)S(1)}, u32[]{:S(2)}, u32[]{:S(2)}) collective-permute-start(bf16[13,32,128]{2,1,0:T(8,128)(2,1)S(1)} %get-tuple-element.12.refs_0_), channel_id=1, source_target_pairs={{0,2},{1,3},{2,0},{3,1},{4,6},{5,7},{6,4},{7,5},{8,10},{9,11},{10,... | collective-permute-start | bytes 319496 | tf_op jit(solution)/shard_map/ppermute | solution.py:272
  6.1 7.6 %collective-permute-start.5 = (bf16[13,32,128]{2,1,0:T(8,128)(2,1)S(1)}, bf16[13,32,128]{2,1,0:T(8,128)(2,1)S(1)}, u32[]{:S(2)}, u32[]{:S(2)}) collective-permute-start(bf16[13,32,128]{2,1,0:T(8,128)(2,1)S(1)} %get-tuple-element.13.refs_0_), channel_id=1, source_target_pairs={{0,8},{1,9},{2,10},{3,11},{4,12},{5,13},{6,14},{7,15},{8,0},{9,1},... | collective-permute-start | bytes 319496 | tf_op jit(solution)/shard_map/ppermute | solution.py:272
  8.7 5.7 %collective-permute-start.3 = (bf16[13,32,128]{2,1,0:T(8,128)(2,1)S(1)}, bf16[13,32,128]{2,1,0:T(8,128)(2,1)S(1)}, u32[]{:S(2)}, u32[]{:S(2)}) collective-permute-start(bf16[13,32,128]{2,1,0:T(8,128)(2,1)S(1)} %get-tuple-element.13.refs_0_), channel_id=1, source_target_pairs={{0,4},{1,5},{2,6},{3,7},{4,0},{5,1},{6,2},{7,3},{8,12},{9,13},{10,... | collective-permute-start | bytes 319496 | tf_op jit(solution)/shard_map/ppermute | solution.py:272
  10.2 4.1 %collective-permute-start = (bf16[13,32,128]{2,1,0:T(8,128)(2,1)S(1)}, bf16[13,32,128]{2,1,0:T(8,128)(2,1)S(1)}, u32[]{:S(2)}, u32[]{:S(2)}) collective-permute-start(bf16[13,32,128]{2,1,0:T(8,128)(2,1)S(1)} %get-tuple-element.12.refs_0_), channel_id=1, source_target_pairs={{0,1},{1,0},{2,3},{3,2},{4,5},{5,4},{6,7},{7,6},{8,9},{9,8},{10,11... | collective-permute-start | bytes 319496 | tf_op jit(solution)/shard_map/ppermute | solution.py:272
  10.3 4.1 %collective-permute-start.2 = (bf16[13,32,128]{2,1,0:T(8,128)(2,1)S(1)}, bf16[13,32,128]{2,1,0:T(8,128)(2,1)S(1)}, u32[]{:S(2)}, u32[]{:S(2)}) collective-permute-start(bf16[13,32,128]{2,1,0:T(8,128)(2,1)S(1)} %collective-permute-done.1.refs_2_), channel_id=1, source_target_pairs={{0,1},{1,0},{2,3},{3,2},{4,5},{5,4},{6,7},{7,6},{8,9},{9,8},{10,11... | collective-permute-start | bytes 319496 | tf_op jit(solution)/shard_map/ppermute | solution.py:272
  13.7 4.7 %collective-permute-start.6 = (bf16[13,32,128]{2,1,0:T(8,128)(2,1)S(1)}, bf16[13,32,128]{2,1,0:T(8,128)(2,1)S(1)}, u32[]{:S(2)}, u32[]{:S(2)}) collective-permute-start(bf16[13,32,128]{2,1,0:T(8,128)(2,1)S(1)} %collective-permute-done.5.refs_2_), channel_id=1, source_target_pairs={{0,4},{1,5},{2,6},{3,7},{4,0},{5,1},{6,2},{7,3},{8,12},{9,13},{10,... | collective-permute-start | bytes 319496 | tf_op jit(solution)/shard_map/ppermute | solution.py:272
  14.8 7.0 %collective-permute-start.4 = (bf16[49,16,128]{2,1,0:T(8,128)(2,1)S(1)}, bf16[49,16,128]{2,1,0:T(8,128)(2,1)S(1)}, u32[]{:S(2)}, u32[]{:S(2)}) collective-permute-start(bf16[49,16,128]{2,1,0:T(8,128)(2,1)S(1)} %get-tuple-element.15.xp.refs_4_), channel_id=1, source_target_pairs={{0,16},{1,17},{2,18},{3,19},{4,20},{5,21},{6,22},{7,23},{8,24},{9,... | collective-permute-start | bytes 602120 | tf_op jit(solution)/shard_map/ppermute | solution.py:282
  18.9 6.6 %collective-permute-start.7 = (bf16[49,16,128]{2,1,0:T(8,128)(2,1)S(1)}, bf16[49,16,128]{2,1,0:T(8,128)(2,1)S(1)}, u32[]{:S(2)}, u32[]{:S(2)}) collective-permute-start(bf16[49,16,128]{2,1,0:T(8,128)(2,1)S(1)} %get-tuple-element.18.gp), channel_id=1, source_target_pairs={{0,16},{1,17},{2,18},{3,19},{4,20},{5,21},{6,22},{7,23},{8,24},{9,... | collective-permute-start | bytes 602120 | tf_op jit(solution)/shard_map/ppermute | solution.py:282
  21.8 3.6 %copy-start.1 = (f32[32]{0:T(128)S(1)}, f32[32]{0:T(128)}, u32[]{:S(2)}) copy-start(f32[32]{0:T(128)} %param.7) | copy-start | bytes 388

commit v13 on v12

--- a/solution.py
+++ b/solution.py
@@ -170,7 +170,7 @@
     return acc + pltpu.roll(acc, 16, 1)
 
 
-def own_inputs_kernel(x, xp, t_out, lx_out, rx):
+def own_inputs_kernel(x, xp, after, t_out, lx_out, rx):
     place_windows(x, lx_out, SIDE)
     place_windows(xp, rx, PITCH)
     input_products(lx_out, rx, t_out)
@@ -292,7 +292,7 @@
     g_cross = exchange_across(g_piv, count)
     flops, product = 6 * 10**9, ((SIDE, ROWB, SIDE * COLB), F32)
     windows = ((SPOTS * EX, 3 * LANES), BF16)
-    products, lx = terms(own_inputs_kernel, (x_all, x_piv), (product, windows), 3 * LANES, flops, "own_inputs")
+    products, lx = terms(own_inputs_kernel, (x_all, x_piv, g_piv), (product, windows), 3 * LANES, flops, "own_inputs")
     own_term, = terms(own_kernel, (products, g_all, g_piv), (((EX, LANES), F32),), LANES, flops, "terms_own")
     products, = terms(cross_inputs_kernel, (lx, x_cross), (product,), 3 * LANES, flops, "cross_inputs")
     arrays = (products, g_all, g_cross, own_term, ridge.reshape(1, EX))

time: 41.5 us -> 41.6 us (level)
  waiting for transfers between devices: 4.5 us -> 5.51 us
  blocking collectives: 12.9 us -> 11.9 us
    ppermute x6, waiting for transfers between devices: 2.95 us -> 4.92 us  [exchange(): return lax.ppermute(value, 'chan', [(i, i ^ flip) for i in range(count)])]
    ppermute x2, waiting for transfers between devices: 1.55 us -> 0.6 us  [exchange_across(): return lax.ppermute(value, ('rows', 'chan'), pairs)]
    all_to_all x1, blocking collectives: 12.9 us -> 11.9 us  [local_packed(): return final(lax.all_to_all(copies, ('rows', 'chan'), 0, 0), ridge)]
  transfers between devices with their start and end apart: 8 -> 8, of which waited for: 2 -> 4; matrix products, arithmetic and copies ran while one was open for 0% -> 0% of each run, Pallas kernels for 15% -> 16%
where the time goes in v13:
time: 41.6 us; the launch traced here: 41.4 us
  blocking collectives  11.9 us (29%)
  starting transfers between devices  11.4 us (27%)
  Pallas kernels  11.2 us (27%)
  waiting for transfers between devices  5.51 us (13%)
  between operations  0.69 us (2%)
  local copies, waits for them, and re-layouts  0.67 us (2%)
    all_to_all x1, blocking collectives, local_packed(): return final(lax.all_to_all(copies, ('rows', 'chan'), 0, 0), ridge)  11.9 us
    ppermute x6, starting transfers between devices, exchange(): return lax.ppermute(value, 'chan', [(i, i ^ flip) for i in range(count)])  8.29 us
    pallas_call x4, Pallas kernels, terms(): pl.pallas_call(kernel, out_shape=tuple((jax.ShapeDtypeStruct(*out) for ou...  7.12 us
    ppermute x6, waiting for transfers between devices, exchange(): return lax.ppermute(value, 'chan', [(i, i ^ flip) for i in range(count)])  4.92 us
    ppermute x2, starting transfers between devices, exchange_across(): return lax.ppermute(value, ('rows', 'chan'), pairs)  3.11 us
    pallas_call x1, Pallas kernels, prep(): pl.pallas_call(prep_kernel, out_shape=(full, full), in_specs=[pl.BlockSpe...  1.76 us
    pallas_call x1, Pallas kernels, final(): pl.pallas_call(final_kernel, out_shape=(out, out), in_specs=[vmem] * 2, o...  1.47 us
    pallas_call x2, Pallas kernels, unpack(): pl.pallas_call(unpack_kernel, out_shape=(jax.ShapeDtypeStruct((SPOTS, EX,...  0.84 us
  transfers between devices with their start and end apart: 8, of which 4 were waited for; matrix products, arithmetic and copies ran while one was open for 0% of the time, Pallas kernels for 16%

profile of v13, /device:TPU:0, one launch (start us, length us, event | category | flops | bytes accessed | tf_op | source)
XLA Modules:
  0.0 41.4 jit_solution(1210631733390078968)
XLA Ops:
  0.6 0.6 %copy-done = s32[1,32]{1,0:T(1,128)S(1)} copy-done((s32[1,32]{1,0:T(1,128)S(1)}, s32[1,32]{1,0:T(1,128)}, u32[]{:S(2)}) %copy-start) | copy-done | bytes 152
  1.3 1.8 %prep.1 = (bf16[13,32,128]{2,1,0:T(8,128)(2,1)S(1)}, bf16[13,32,128]{2,1,0:T(8,128)(2,1)S(1)}) custom-call(s32[1,32]{1,0:T(1,128)S(1)} %copy-done, bf16[49,32,32]{2,1,0:T(8,128)(2,1)} %bitcast.5, bf16[32,32,49]{2,1,0:T(8,128)(2,1)} %g_hbm.1), custom_call_target="tpu_custom_call" | custom-call | tf_op jit(solution)/shard_map/prep/pallas_call | solution.py:67
  3.0 3.0 %collective-permute-start.1 = (bf16[13,32,128]{2,1,0:T(8,128)(2,1)S(1)}, bf16[13,32,128]{2,1,0:T(8,128)(2,1)S(1)}, u32[]{:S(2)}, u32[]{:S(2)}) collective-permute-start(bf16[13,32,128]{2,1,0:T(8,128)(2,1)S(1)} %get-tuple-element.12.refs_0_), channel_id=1, source_target_pairs={{0,2},{1,3},{2,0},{3,1},{4,6},{5,7},{6,4},{7,5},{8,10},{9,11},{10,... | collective-permute-start | bytes 319496 | tf_op jit(solution)/shard_map/ppermute | solution.py:272
  6.1 2.6 %collective-permute-start.4 = (bf16[13,32,128]{2,1,0:T(8,128)(2,1)S(1)}, bf16[13,32,128]{2,1,0:T(8,128)(2,1)S(1)}, u32[]{:S(2)}, u32[]{:S(2)}) collective-permute-start(bf16[13,32,128]{2,1,0:T(8,128)(2,1)S(1)} %get-tuple-element.13.refs_0_), channel_id=1, source_target_pairs={{0,8},{1,9},{2,10},{3,11},{4,12},{5,13},{6,14},{7,15},{8,0},{9,1},... | collective-permute-start | bytes 319496 | tf_op jit(solution)/shard_map/ppermute | solution.py:272
  8.7 0.0 collective-permute-start
  8.7 1.6 %collective-permute-start.3 = (bf16[13,32,128]{2,1,0:T(8,128)(2,1)S(1)}, bf16[13,32,128]{2,1,0:T(8,128)(2,1)S(1)}, u32[]{:S(2)}, u32[]{:S(2)}) collective-permute-start(bf16[13,32,128]{2,1,0:T(8,128)(2,1)S(1)} %get-tuple-element.13.refs_0_), channel_id=1, source_target_pairs={{0,4},{1,5},{2,6},{3,7},{4,0},{5,1},{6,2},{7,3},{8,12},{9,13},{10,... | collective-permute-start | bytes 319496 | tf_op jit(solution)/shard_map/ppermute | solution.py:272
  10.3 0.2 collective-permute-start.2
  10.5 3.1 %collective-permute-done.4.refs_2_ = bf16[13,32,128]{2,1,0:T(8,128)(2,1)S(1)} collective-permute-done((bf16[13,32,128]{2,1,0:T(8,128)(2,1)S(1)}, bf16[13,32,128]{2,1,0:T(8,128)(2,1)S(1)}, u32[]{:S(2)}, u32[]{:S(2)}) %collective-permute-start.4) | collective-permute-done | bytes 106528 | tf_op jit(solution)/shard_map/ppermute | solution.py:272
  13.5 0.9 %collective-permute-start.5 = (bf16[13,32,128]{2,1,0:T(8,128)(2,1)S(1)}, bf16[13,32,128]{2,1,0:T(8,128)(2,1)S(1)}, u32[]{:S(2)}, u32[]{:S(2)}) collective-permute-start(bf16[13,32,128]{2,1,0:T(8,128)(2,1)S(1)} %collective-permute-done.4.refs_2_), channel_id=1, source_target_pairs={{0,4},{1,5},{2,6},{3,7},{4,0},{5,1},{6,2},{7,3},{8,12},{9,13},{10,... | collective-permute-start | bytes 319496 | tf_op jit(solution)/shard_map/ppermute | solution.py:272
  14.4 0.5 %collective-permute-done.3.refs_4_.refs_1_ = bf16[13,32,128]{2,1,0:T(8,128)(2,1)S(1)} collective-permute-done((bf16[13,32,128]{2,1,0:T(8,128)(2,1)S(1)}, bf16[13,32,128]{2,1,0:T(8,128)(2,1)S(1)}, u32[]{:S(2)}, u32[]{:S(2)}) %collective-permute-start.3) | collective-permute-done | bytes 106528 | tf_op jit(solution)/shard_map/ppermute | solution.py:272
  14.9 0.4 %unpack_x.1 = (bf16[49,32,128]{2,1,0:T(8,128)(2,1)S(1)}, bf16[49,16,128]{2,1,0:T(8,128)(2,1)S(1)}) custom-call(bf16[13,32,128]{2,1,0:T(8,128)(2,1)S(1)} %get-tuple-element.12.refs_0_, bf16[13,32,128]{2,1,0:T(8,128)(2,1)S(1)} %collective-permute-done.refs_1_, bf16[13,32,128]{2,1,0:T(8,128)(2,1)S(1)} %collective-permute-done.1.refs_2_, ...), custom_call_target="tpu_custom_call" | custom-call | bytes 1048576 | tf_op jit(solution)/shard_map/unpack_x/pallas_call | solution.py:113
  15.4 1.6 %collective-permute-start.6 = (bf16[49,16,128]{2,1,0:T(8,128)(2,1)S(1)}, bf16[49,16,128]{2,1,0:T(8,128)(2,1)S(1)}, u32[]{:S(2)}, u32[]{:S(2)}) collective-permute-start(bf16[49,16,128]{2,1,0:T(8,128)(2,1)S(1)} %get-tuple-element.15.refs_4_.xp), channel_id=1, source_target_pairs={{0,16},{1,17},{2,18},{3,19},{4,20},{5,21},{6,22},{7,23},{8,24},{9,... | collective-permute-start | bytes 602120 | tf_op jit(solution)/shard_map/ppermute | solution.py:282
  16.9 1.3 %collective-permute-done.5.refs_3_ = bf16[13,32,128]{2,1,0:T(8,128)(2,1)S(1)} collective-permute-done((bf16[13,32,128]{2,1,0:T(8,128)(2,1)S(1)}, bf16[13,32,128]{2,1,0:T(8,128)(2,1)S(1)}, u32[]{:S(2)}, u32[]{:S(2)}) %collective-permute-start.5) | collective-permute-done | bytes 106528 | tf_op jit(solution)/shard_map/ppermute | solution.py:272
  18.3 0.4 %unpack_g.1 = (bf16[49,32,128]{2,1,0:T(8,128)(2,1)S(1)}, bf16[49,16,128]{2,1,0:T(8,128)(2,1)S(1)}) custom-call(bf16[13,32,128]{2,1,0:T(8,128)(2,1)S(1)} %get-tuple-element.13.refs_0_, bf16[13,32,128]{2,1,0:T(8,128)(2,1)S(1)} %collective-permute-done.3.refs_4_.refs_1_, bf16[13,32,128]{2,1,0:T(8,128)(2,1)S(1)} %collective-permute-done.4.refs_2_, ...), custom_call_target="tpu_custom_call" | custom-call | bytes 1048576 | tf_op jit(solution)/shard_map/unpack_g/pallas_call | solution.py:113
  18.7 1.6 %collective-permute-start.7 = (bf16[49,16,128]{2,1,0:T(8,128)(2,1)S(1)}, bf16[49,16,128]{2,1,0:T(8,128)(2,1)S(1)}, u32[]{:S(2)}, u32[]{:S(2)}) collective-permute-start(bf16[49,16,128]{2,1,0:T(8,128)(2,1)S(1)} %get-tuple-element.16.after.gp), channel_id=1, source_target_pairs={{0,16},{1,17},{2,18},{3,19},{4,20},{5,21},{6,22},{7,23},{8,24},{9,... | collective-permute-start | bytes 602120 | tf_op jit(solution)/shard_map/ppermute | solution.py:282
  20.2 2.0 %own_inputs.1 = (f32[7,224,896]{2,1,0:T(8,128)S(1)}, bf16[1568,384]{1,0:T(8,128)(2,1)S(1)}) custom-call(bf16[49,32,128]{2,1,0:T(8,128)(2,1)S(1)} %get-tuple-element.14.x, bf16[49,16,128]{2,1,0:T(8,128)(2,1)S(1)} %get-tuple-element.15.refs_4_.xp, bf16[49,16,128]{2,1,0:T(8,128)(2,1)S(1)} %get-tuple-element.16.after.gp), custom_call_target="tpu_custom_call" | custom-call | flops 6000000000 | bytes 4194304 | tf_op jit(solution)/shard_map/own_inputs/pallas_call | solution.py:202
  22.3 1.6 %terms_own.1.own_ref = f32[32,128]{1,0:T(8,128)S(1)} custom-call(f32[7,224,896]{2,1,0:T(8,128)S(1)} %get-tuple-element.19.t, bf16[49,32,128]{2,1,0:T(8,128)(2,1)S(1)} %get-tuple-element.18.g, bf16[49,16,128]{2,1,0:T(8,128)(2,1)S(1)} %get-tuple-element.16.after.gp), custom_call_target="tpu_custom_call" | custom-call | flops 6000000000 | bytes 4194304 | tf_op jit(solution)/shard_map/terms_own/pallas_call | solution.py:202
  23.9 0.0 collective-permute-done.6.xp
  23.9 0.0 copy-start.1
  23.9 2.0 %cross_inputs.1.t = f32[7,224,896]{2,1,0:T(8,128)S(1)} custom-call(bf16[1568,384]{1,0:T(8,128)(2,1)S(1)} %get-tuple-element.17.lx, bf16[49,16,128]{2,1,0:T(8,128)(2,1)S(1)} %collective-permute-done.6.xp), custom_call_target="tpu_custom_call" | custom-call | flops 6000000000 | bytes 4194304 | tf_op jit(solution)/shard_map/cross_inputs/pallas_call | solution.py:202
  25.9 0.6 %collective-permute-done.7.gp = bf16[49,16,128]{2,1,0:T(8,128)(2,1)S(1)} collective-permute-done((bf16[49,16,128]{2,1,0:T(8,128)(2,1)S(1)}, bf16[49,16,128]{2,1,0:T(8,128)(2,1)S(1)}, u32[]{:S(2)}, u32[]{:S(2)}) %collective-permute-start.7) | collective-permute-done | bytes 200736 | tf_op jit(solution)/shard_map/ppermute | solution.py:282
  26.5 1.4 %terms_cross.1 = (f32[8,128]{1,0:T(8,128)S(1)}, f32[1,32]{1,0:T(1,128)S(1)}) custom-call(f32[7,224,896]{2,1,0:T(8,128)S(1)} %cross_inputs.1.t, bf16[49,32,128]{2,1,0:T(8,128)(2,1)S(1)} %get-tuple-element.18.g, bf16[49,16,128]{2,1,0:T(8,128)(2,1)S(1)} %collective-permute-done.7.gp, f32[32,128]{1,0:T(8,128)S(1)} %terms_own.1.own_ref, f32[1,32]{1,0:T(1,128)S(1)} %bitcast.4), custom_call_target="tpu_custom_call" | custom-call | flops 6000000000 | bytes 4194304 | tf_op jit(solution)/shard_map/terms_cross/pallas_call | solution.py:202
  28.0 11.9 %all_to_all.5.terms_ref = f32[32,8,128]{2,1,0:T(8,128)S(1)} all-to-all(f32[32,8,128]{2,1,0:T(8,128)S(1)} %broadcast_in_dim.3), channel_id=1, replica_groups=mesh['rows'=2,'chan'=16] {'rows','chan'}, dimensions={0} | all-to-all | bytes 262144 | tf_op jit(solution)/shard_map/all_to_all | solution.py:301
  39.9 1.5 %solve.1 = (f32[32,32]{1,0:T(8,128)}, f32[32,32]{1,0:T(8,128)}) custom-call(f32[32,8,128]{2,1,0:T(8,128)S(1)} %all_to_all.5.terms_ref, f32[1,32]{1,0:T(1,128)S(1)} %get-tuple-element.21.ridge_ref), custom_call_target="tpu_custom_call" | custom-call | tf_op jit(solution)/shard_map/solve/pallas_call | solution.py:261
  (6 shorter events, 0.0 us)
Async XLA Ops:
  0.6 0.7 %copy-start = (s32[1,32]{1,0:T(1,128)S(1)}, s32[1,32]{1,0:T(1,128)}, u32[]{:S(2)}) copy-start(s32[1,32]{1,0:T(1,128)} %order_hbm.1) | copy-start | bytes 388
  3.0 7.2 %collective-permute-start.1 = (bf16[13,32,128]{2,1,0:T(8,128)(2,1)S(1)}, bf16[13,32,128]{2,1,0:T(8,128)(2,1)S(1)}, u32[]{:S(2)}, u32[]{:S(2)}) collective-permute-start(bf16[13,32,128]{2,1,0:T(8,128)(2,1)S(1)} %get-tuple-element.12.refs_0_), channel_id=1, source_target_pairs={{0,2},{1,3},{2,0},{3,1},{4,6},{5,7},{6,4},{7,5},{8,10},{9,11},{10,... | collective-permute-start | bytes 319496 | tf_op jit(solution)/shard_map/ppermute | solution.py:272
  6.1 7.5 %collective-permute-start.4 = (bf16[13,32,128]{2,1,0:T(8,128)(2,1)S(1)}, bf16[13,32,128]{2,1,0:T(8,128)(2,1)S(1)}, u32[]{:S(2)}, u32[]{:S(2)}) collective-permute-start(bf16[13,32,128]{2,1,0:T(8,128)(2,1)S(1)} %get-tuple-element.13.refs_0_), channel_id=1, source_target_pairs={{0,8},{1,9},{2,10},{3,11},{4,12},{5,13},{6,14},{7,15},{8,0},{9,1},... | collective-permute-start | bytes 319496 | tf_op jit(solution)/shard_map/ppermute | solution.py:272
  8.7 5.7 %collective-permute-start = (bf16[13,32,128]{2,1,0:T(8,128)(2,1)S(1)}, bf16[13,32,128]{2,1,0:T(8,128)(2,1)S(1)}, u32[]{:S(2)}, u32[]{:S(2)}) collective-permute-start(bf16[13,32,128]{2,1,0:T(8,128)(2,1)S(1)} %get-tuple-element.12.refs_0_), channel_id=1, source_target_pairs={{0,1},{1,0},{2,3},{3,2},{4,5},{5,4},{6,7},{7,6},{8,9},{9,8},{10,11... | collective-permute-start | bytes 319496 | tf_op jit(solution)/shard_map/ppermute | solution.py:272
  8.7 6.3 %collective-permute-start.3 = (bf16[13,32,128]{2,1,0:T(8,128)(2,1)S(1)}, bf16[13,32,128]{2,1,0:T(8,128)(2,1)S(1)}, u32[]{:S(2)}, u32[]{:S(2)}) collective-permute-start(bf16[13,32,128]{2,1,0:T(8,128)(2,1)S(1)} %get-tuple-element.13.refs_0_), channel_id=1, source_target_pairs={{0,4},{1,5},{2,6},{3,7},{4,0},{5,1},{6,2},{7,3},{8,12},{9,13},{10,... | collective-permute-start | bytes 319496 | tf_op jit(solution)/shard_map/ppermute | solution.py:272
  10.3 4.7 %collective-permute-start.2 = (bf16[13,32,128]{2,1,0:T(8,128)(2,1)S(1)}, bf16[13,32,128]{2,1,0:T(8,128)(2,1)S(1)}, u32[]{:S(2)}, u32[]{:S(2)}) collective-permute-start(bf16[13,32,128]{2,1,0:T(8,128)(2,1)S(1)} %collective-permute-done.1.refs_2_), channel_id=1, source_target_pairs={{0,1},{1,0},{2,3},{3,2},{4,5},{5,4},{6,7},{7,6},{8,9},{9,8},{10,11... | collective-permute-start | bytes 319496 | tf_op jit(solution)/shard_map/ppermute | solution.py:272
  13.5 4.7 %collective-permute-start.5 = (bf16[13,32,128]{2,1,0:T(8,128)(2,1)S(1)}, bf16[13,32,128]{2,1,0:T(8,128)(2,1)S(1)}, u32[]{:S(2)}, u32[]{:S(2)}) collective-permute-start(bf16[13,32,128]{2,1,0:T(8,128)(2,1)S(1)} %collective-permute-done.4.refs_2_), channel_id=1, source_target_pairs={{0,4},{1,5},{2,6},{3,7},{4,0},{5,1},{6,2},{7,3},{8,12},{9,13},{10,... | collective-permute-start | bytes 319496 | tf_op jit(solution)/shard_map/ppermute | solution.py:272
  15.4 8.5 %collective-permute-start.6 = (bf16[49,16,128]{2,1,0:T(8,128)(2,1)S(1)}, bf16[49,16,128]{2,1,0:T(8,128)(2,1)S(1)}, u32[]{:S(2)}, u32[]{:S(2)}) collective-permute-start(bf16[49,16,128]{2,1,0:T(8,128)(2,1)S(1)} %get-tuple-element.15.refs_4_.xp), channel_id=1, source_target_pairs={{0,16},{1,17},{2,18},{3,19},{4,20},{5,21},{6,22},{7,23},{8,24},{9,... | collective-permute-start | bytes 602120 | tf_op jit(solution)/shard_map/ppermute | solution.py:282
  18.7 7.8 %collective-permute-start.7 = (bf16[49,16,128]{2,1,0:T(8,128)(2,1)S(1)}, bf16[49,16,128]{2,1,0:T(8,128)(2,1)S(1)}, u32[]{:S(2)}, u32[]{:S(2)}) collective-permute-start(bf16[49,16,128]{2,1,0:T(8,128)(2,1)S(1)} %get-tuple-element.16.after.gp), channel_id=1, source_target_pairs={{0,16},{1,17},{2,18},{3,19},{4,20},{5,21},{6,22},{7,23},{8,24},{9,... | collective-permute-start | bytes 602120 | tf_op jit(solution)/shard_map/ppermute | solution.py:282
  23.9 2.7 %copy-start.1 = (f32[32]{0:T(128)S(1)}, f32[32]{0:T(128)}, u32[]{:S(2)}) copy-start(f32[32]{0:T(128)} %param.7) | copy-start | bytes 388

commit v14 on v11

--- a/solution.py
+++ b/solution.py
@@ -168,7 +168,7 @@
     return acc + pltpu.roll(acc, 16, 1)
 
 
-def own_inputs_kernel(x, xp, t_out, lx_out, rx):
+def own_inputs_kernel(x, xp, after, t_out, lx_out, rx):
     place_windows(x, lx_out, SIDE)
     place_windows(xp, rx, PITCH)
     input_products(lx_out, rx, t_out)
@@ -290,7 +290,7 @@
     g_cross = exchange_across(g_piv, count)
     flops, product = 6 * 10**9, ((SIDE, ROWB, SIDE * COLB), F32)
     windows = ((SPOTS * EX, 3 * LANES), BF16)
-    products, lx = terms(own_inputs_kernel, (x_all, x_piv), (product, windows), 3 * LANES, flops, "own_inputs")
+    products, lx = terms(own_inputs_kernel, (x_all, x_piv, g_piv), (product, windows), 3 * LANES, flops, "own_inputs")
     own_term, = terms(own_kernel, (products, g_all, g_piv), (((EX, LANES), F32),), LANES, flops, "terms_own")
     products, = terms(cross_inputs_kernel, (lx, x_cross), (product,), 3 * LANES, flops, "cross_inputs")
     arrays = (products, g_all, g_cross, own_term, ordering, ridge.reshape(1, EX))

time: 41.8 us -> 41.8 us (level)
  blocking collectives: 12.8 us -> 11.9 us
  starting transfers between devices: 10.7 us -> 11.4 us
    ppermute x6, waiting for transfers between devices: 2.95 us -> 4.15 us  [exchange(): return lax.ppermute(value, 'chan', [(i, i ^ flip) for i in range(count)])]
    all_to_all x1, blocking collectives: 12.8 us -> 11.9 us  [local_packed(): return final(lax.all_to_all(copies, ('rows', 'chan'), 0, 0), ridge)]
    ppermute x2, waiting for transfers between devices: 2.22 us -> 1.31 us  [exchange_across(): return lax.ppermute(value, ('rows', 'chan'), pairs)]
    ppermute x2, starting transfers between devices: 2.29 us -> 3.12 us  [exchange_across(): return lax.ppermute(value, ('rows', 'chan'), pairs)]
  transfers between devices with their start and end apart: 8 -> 8, of which waited for: 3 -> 5; matrix products, arithmetic and copies ran while one was open for 0% -> 0% of each run, Pallas kernels for 16% -> 16%
where the time goes in v14:
time: 41.8 us; the launch traced here: 41.6 us
  blocking collectives  11.9 us (28%)
  Pallas kernels  11.4 us (27%)
  starting transfers between devices  11.4 us (27%)
  waiting for transfers between devices  5.46 us (13%)
  local copies, waits for them, and re-layouts  0.7 us (2%)
  between operations  0.68 us (2%)
    all_to_all x1, blocking collectives, local_packed(): return final(lax.all_to_all(copies, ('rows', 'chan'), 0, 0), ridge)  11.9 us
    ppermute x6, starting transfers between devices, exchange(): return lax.ppermute(value, 'chan', [(i, i ^ flip) for i in range(count)])  8.29 us
    pallas_call x4, Pallas kernels, terms(): pl.pallas_call(kernel, out_shape=tuple((jax.ShapeDtypeStruct(*out) for ou...  7.26 us
    ppermute x6, waiting for transfers between devices, exchange(): return lax.ppermute(value, 'chan', [(i, i ^ flip) for i in range(count)])  4.15 us
    ppermute x2, starting transfers between devices, exchange_across(): return lax.ppermute(value, ('rows', 'chan'), pairs)  3.12 us
    pallas_call x1, Pallas kernels, prep(): pl.pallas_call(prep_kernel, out_shape=(full, full), in_specs=[pl.BlockSpe...  1.62 us
    pallas_call x1, Pallas kernels, final(): pl.pallas_call(final_kernel, out_shape=(out, out), in_specs=[vmem] * 2, o...  1.47 us
    ppermute x2, waiting for transfers between devices, exchange_across(): return lax.ppermute(value, ('rows', 'chan'), pairs)  1.31 us
  transfers between devices with their start and end apart: 8, of which 5 were waited for; matrix products, arithmetic and copies ran while one was open for 0% of the time, Pallas kernels for 16%

profile of v14, /device:TPU:0, one launch (start us, length us, event | category | flops | bytes accessed | tf_op | source)
XLA Modules:
  0.0 41.6 jit_solution(18228863950766325862)
XLA Ops:
  0.6 1.6 %prep.1 = (bf16[13,32,128]{2,1,0:T(8,128)(2,1)S(1)}, bf16[13,32,128]{2,1,0:T(8,128)(2,1)S(1)}) custom-call(bf16[49,32,32]{2,1,0:T(8,128)(2,1)} %bitcast.5, bf16[32,32,49]{2,1,0:T(8,128)(2,1)} %g_hbm.1), custom_call_target="tpu_custom_call" | custom-call | tf_op jit(solution)/shard_map/prep/pallas_call | solution.py:59
  2.3 3.0 %collective-permute-start.1 = (bf16[13,32,128]{2,1,0:T(8,128)(2,1)S(1)}, bf16[13,32,128]{2,1,0:T(8,128)(2,1)S(1)}, u32[]{:S(2)}, u32[]{:S(2)}) collective-permute-start(bf16[13,32,128]{2,1,0:T(8,128)(2,1)S(1)} %get-tuple-element.12.refs_0_), channel_id=1, source_target_pairs={{0,2},{1,3},{2,0},{3,1},{4,6},{5,7},{6,4},{7,5},{8,10},{9,11},{10,... | collective-permute-start | bytes 319496 | tf_op jit(solution)/shard_map/ppermute | solution.py:270
  5.3 2.6 %collective-permute-start.4 = (bf16[13,32,128]{2,1,0:T(8,128)(2,1)S(1)}, bf16[13,32,128]{2,1,0:T(8,128)(2,1)S(1)}, u32[]{:S(2)}, u32[]{:S(2)}) collective-permute-start(bf16[13,32,128]{2,1,0:T(8,128)(2,1)S(1)} %get-tuple-element.13.refs_0_), channel_id=1, source_target_pairs={{0,8},{1,9},{2,10},{3,11},{4,12},{5,13},{6,14},{7,15},{8,0},{9,1},... | collective-permute-start | bytes 319496 | tf_op jit(solution)/shard_map/ppermute | solution.py:270
  7.9 0.0 collective-permute-start
  7.9 1.6 %collective-permute-start.3 = (bf16[13,32,128]{2,1,0:T(8,128)(2,1)S(1)}, bf16[13,32,128]{2,1,0:T(8,128)(2,1)S(1)}, u32[]{:S(2)}, u32[]{:S(2)}) collective-permute-start(bf16[13,32,128]{2,1,0:T(8,128)(2,1)S(1)} %get-tuple-element.13.refs_0_), channel_id=1, source_target_pairs={{0,4},{1,5},{2,6},{3,7},{4,0},{5,1},{6,2},{7,3},{8,12},{9,13},{10,... | collective-permute-start | bytes 319496 | tf_op jit(solution)/shard_map/ppermute | solution.py:270
  9.5 0.0 collective-permute-done.1.refs_2_
  9.5 0.2 collective-permute-start.2
  9.7 3.1 %collective-permute-done.4.refs_2_ = bf16[13,32,128]{2,1,0:T(8,128)(2,1)S(1)} collective-permute-done((bf16[13,32,128]{2,1,0:T(8,128)(2,1)S(1)}, bf16[13,32,128]{2,1,0:T(8,128)(2,1)S(1)}, u32[]{:S(2)}, u32[]{:S(2)}) %collective-permute-start.4) | collective-permute-done | bytes 106528 | tf_op jit(solution)/shard_map/ppermute | solution.py:270
  12.8 0.9 %collective-permute-start.5 = (bf16[13,32,128]{2,1,0:T(8,128)(2,1)S(1)}, bf16[13,32,128]{2,1,0:T(8,128)(2,1)S(1)}, u32[]{:S(2)}, u32[]{:S(2)}) collective-permute-start(bf16[13,32,128]{2,1,0:T(8,128)(2,1)S(1)} %collective-permute-done.4.refs_2_), channel_id=1, source_target_pairs={{0,4},{1,5},{2,6},{3,7},{4,0},{5,1},{6,2},{7,3},{8,12},{9,13},{10,... | collective-permute-start | bytes 319496 | tf_op jit(solution)/shard_map/ppermute | solution.py:270
  13.6 0.5 %collective-permute-done.3.refs_5_.refs_1_ = bf16[13,32,128]{2,1,0:T(8,128)(2,1)S(1)} collective-permute-done((bf16[13,32,128]{2,1,0:T(8,128)(2,1)S(1)}, bf16[13,32,128]{2,1,0:T(8,128)(2,1)S(1)}, u32[]{:S(2)}, u32[]{:S(2)}) %collective-permute-start.3) | collective-permute-done | bytes 106528 | tf_op jit(solution)/shard_map/ppermute | solution.py:270
  14.2 0.7 %copy-done = s32[1,32]{1,0:T(1,128)S(1)} copy-done((s32[1,32]{1,0:T(1,128)S(1)}, s32[1,32]{1,0:T(1,128)}, u32[]{:S(2)}) %copy-start) | copy-done | bytes 152
  14.8 0.5 %unpack_x.1 = (bf16[49,32,128]{2,1,0:T(8,128)(2,1)S(1)}, bf16[49,16,128]{2,1,0:T(8,128)(2,1)S(1)}) custom-call(bf16[13,32,128]{2,1,0:T(8,128)(2,1)S(1)} %get-tuple-element.12.refs_0_, bf16[13,32,128]{2,1,0:T(8,128)(2,1)S(1)} %collective-permute-done.refs_1_, bf16[13,32,128]{2,1,0:T(8,128)(2,1)S(1)} %collective-permute-done.1.refs_2_, ...), custom_call_target="tpu_custom_call" | custom-call | bytes 1048576 | tf_op jit(solution)/shard_map/unpack_x/pallas_call | solution.py:111
  15.3 1.6 %collective-permute-start.6 = (bf16[49,16,128]{2,1,0:T(8,128)(2,1)S(1)}, bf16[49,16,128]{2,1,0:T(8,128)(2,1)S(1)}, u32[]{:S(2)}, u32[]{:S(2)}) collective-permute-start(bf16[49,16,128]{2,1,0:T(8,128)(2,1)S(1)} %get-tuple-element.15.refs_5_.xp), channel_id=1, source_target_pairs={{0,16},{1,17},{2,18},{3,19},{4,20},{5,21},{6,22},{7,23},{8,24},{9,... | collective-permute-start | bytes 602120 | tf_op jit(solution)/shard_map/ppermute | solution.py:280
  16.9 0.5 %collective-permute-done.5.refs_3_ = bf16[13,32,128]{2,1,0:T(8,128)(2,1)S(1)} collective-permute-done((bf16[13,32,128]{2,1,0:T(8,128)(2,1)S(1)}, bf16[13,32,128]{2,1,0:T(8,128)(2,1)S(1)}, u32[]{:S(2)}, u32[]{:S(2)}) %collective-permute-start.5) | collective-permute-done | bytes 106528 | tf_op jit(solution)/shard_map/ppermute | solution.py:270
  17.5 0.5 %unpack_g.1 = (bf16[49,32,128]{2,1,0:T(8,128)(2,1)S(1)}, bf16[49,16,128]{2,1,0:T(8,128)(2,1)S(1)}) custom-call(bf16[13,32,128]{2,1,0:T(8,128)(2,1)S(1)} %get-tuple-element.13.refs_0_, bf16[13,32,128]{2,1,0:T(8,128)(2,1)S(1)} %collective-permute-done.3.refs_5_.refs_1_, bf16[13,32,128]{2,1,0:T(8,128)(2,1)S(1)} %collective-permute-done.4.refs_2_, ...), custom_call_target="tpu_custom_call" | custom-call | bytes 1048576 | tf_op jit(solution)/shard_map/unpack_g/pallas_call | solution.py:111
  18.0 1.6 %collective-permute-start.7 = (bf16[49,16,128]{2,1,0:T(8,128)(2,1)S(1)}, bf16[49,16,128]{2,1,0:T(8,128)(2,1)S(1)}, u32[]{:S(2)}, u32[]{:S(2)}) collective-permute-start(bf16[49,16,128]{2,1,0:T(8,128)(2,1)S(1)} %get-tuple-element.16.after.gp), channel_id=1, source_target_pairs={{0,16},{1,17},{2,18},{3,19},{4,20},{5,21},{6,22},{7,23},{8,24},{9,... | collective-permute-start | bytes 602120 | tf_op jit(solution)/shard_map/ppermute | solution.py:280
  19.6 2.0 %own_inputs.1 = (f32[7,224,896]{2,1,0:T(8,128)S(1)}, bf16[1568,384]{1,0:T(8,128)(2,1)S(1)}) custom-call(bf16[49,32,128]{2,1,0:T(8,128)(2,1)S(1)} %get-tuple-element.14.x, bf16[49,16,128]{2,1,0:T(8,128)(2,1)S(1)} %get-tuple-element.15.refs_5_.xp, bf16[49,16,128]{2,1,0:T(8,128)(2,1)S(1)} %get-tuple-element.16.after.gp), custom_call_target="tpu_custom_call" | custom-call | flops 6000000000 | bytes 4194304 | tf_op jit(solution)/shard_map/own_inputs/pallas_call | solution.py:200
  21.6 1.6 %terms_own.1.own_ref = f32[32,128]{1,0:T(8,128)S(1)} custom-call(f32[7,224,896]{2,1,0:T(8,128)S(1)} %get-tuple-element.19.t, bf16[49,32,128]{2,1,0:T(8,128)(2,1)S(1)} %get-tuple-element.18.g, bf16[49,16,128]{2,1,0:T(8,128)(2,1)S(1)} %get-tuple-element.16.after.gp), custom_call_target="tpu_custom_call" | custom-call | flops 6000000000 | bytes 4194304 | tf_op jit(solution)/shard_map/terms_own/pallas_call | solution.py:200
  23.2 0.1 collective-permute-done.6.xp
  23.3 2.0 %cross_inputs.1.t = f32[7,224,896]{2,1,0:T(8,128)S(1)} custom-call(bf16[1568,384]{1,0:T(8,128)(2,1)S(1)} %get-tuple-element.17.lx, bf16[49,16,128]{2,1,0:T(8,128)(2,1)S(1)} %collective-permute-done.6.xp), custom_call_target="tpu_custom_call" | custom-call | flops 6000000000 | bytes 4194304 | tf_op jit(solution)/shard_map/cross_inputs/pallas_call | solution.py:200
  25.3 1.2 %collective-permute-done.7.gp = bf16[49,16,128]{2,1,0:T(8,128)(2,1)S(1)} collective-permute-done((bf16[49,16,128]{2,1,0:T(8,128)(2,1)S(1)}, bf16[49,16,128]{2,1,0:T(8,128)(2,1)S(1)}, u32[]{:S(2)}, u32[]{:S(2)}) %collective-permute-start.7) | collective-permute-done | bytes 200736 | tf_op jit(solution)/shard_map/ppermute | solution.py:280
  26.5 1.6 %terms_cross.1 = (f32[8,128]{1,0:T(8,128)S(1)}, f32[1,32]{1,0:T(1,128)S(1)}) custom-call(f32[7,224,896]{2,1,0:T(8,128)S(1)} %cross_inputs.1.t, bf16[49,32,128]{2,1,0:T(8,128)(2,1)S(1)} %get-tuple-element.18.g, bf16[49,16,128]{2,1,0:T(8,128)(2,1)S(1)} %collective-permute-done.7.gp, f32[32,128]{1,0:T(8,128)S(1)} %terms_own.1.own_ref, s32[1,32]{1,0:T(1,128)S(1)} %copy-done.1, ...), custom_call_target="tpu_custom_call" | custom-call | flops 6000000000 | bytes 4194304 | tf_op jit(solution)/shard_map/terms_cross/pallas_call | solution.py:200
  28.2 11.9 %all_to_all.5.terms_ref = f32[32,8,128]{2,1,0:T(8,128)S(1)} all-to-all(f32[32,8,128]{2,1,0:T(8,128)S(1)} %broadcast_in_dim.3), channel_id=1, replica_groups=mesh['rows'=2,'chan'=16] {'rows','chan'}, dimensions={0} | all-to-all | bytes 262144 | tf_op jit(solution)/shard_map/all_to_all | solution.py:299
  40.1 1.5 %solve.1 = (f32[32,32]{1,0:T(8,128)}, f32[32,32]{1,0:T(8,128)}) custom-call(f32[32,8,128]{2,1,0:T(8,128)S(1)} %all_to_all.5.terms_ref, f32[1,32]{1,0:T(1,128)S(1)} %get-tuple-element.21.ridge_ref), custom_call_target="tpu_custom_call" | custom-call | tf_op jit(solution)/shard_map/solve/pallas_call | solution.py:259
  (8 shorter events, 0.0 us)
Async XLA Ops:
  2.3 7.2 %collective-permute-start.1 = (bf16[13,32,128]{2,1,0:T(8,128)(2,1)S(1)}, bf16[13,32,128]{2,1,0:T(8,128)(2,1)S(1)}, u32[]{:S(2)}, u32[]{:S(2)}) collective-permute-start(bf16[13,32,128]{2,1,0:T(8,128)(2,1)S(1)} %get-tuple-element.12.refs_0_), channel_id=1, source_target_pairs={{0,2},{1,3},{2,0},{3,1},{4,6},{5,7},{6,4},{7,5},{8,10},{9,11},{10,... | collective-permute-start | bytes 319496 | tf_op jit(solution)/shard_map/ppermute | solution.py:270
  5.3 7.5 %collective-permute-start.4 = (bf16[13,32,128]{2,1,0:T(8,128)(2,1)S(1)}, bf16[13,32,128]{2,1,0:T(8,128)(2,1)S(1)}, u32[]{:S(2)}, u32[]{:S(2)}) collective-permute-start(bf16[13,32,128]{2,1,0:T(8,128)(2,1)S(1)} %get-tuple-element.13.refs_0_), channel_id=1, source_target_pairs={{0,8},{1,9},{2,10},{3,11},{4,12},{5,13},{6,14},{7,15},{8,0},{9,1},... | collective-permute-start | bytes 319496 | tf_op jit(solution)/shard_map/ppermute | solution.py:270
  7.9 5.7 %collective-permute-start = (bf16[13,32,128]{2,1,0:T(8,128)(2,1)S(1)}, bf16[13,32,128]{2,1,0:T(8,128)(2,1)S(1)}, u32[]{:S(2)}, u32[]{:S(2)}) collective-permute-start(bf16[13,32,128]{2,1,0:T(8,128)(2,1)S(1)} %get-tuple-element.12.refs_0_), channel_id=1, source_target_pairs={{0,1},{1,0},{2,3},{3,2},{4,5},{5,4},{6,7},{7,6},{8,9},{9,8},{10,11... | collective-permute-start | bytes 319496 | tf_op jit(solution)/shard_map/ppermute | solution.py:270
  7.9 6.3 %collective-permute-start.3 = (bf16[13,32,128]{2,1,0:T(8,128)(2,1)S(1)}, bf16[13,32,128]{2,1,0:T(8,128)(2,1)S(1)}, u32[]{:S(2)}, u32[]{:S(2)}) collective-permute-start(bf16[13,32,128]{2,1,0:T(8,128)(2,1)S(1)} %get-tuple-element.13.refs_0_), channel_id=1, source_target_pairs={{0,4},{1,5},{2,6},{3,7},{4,0},{5,1},{6,2},{7,3},{8,12},{9,13},{10,... | collective-permute-start | bytes 319496 | tf_op jit(solution)/shard_map/ppermute | solution.py:270
  9.5 4.7 %collective-permute-start.2 = (bf16[13,32,128]{2,1,0:T(8,128)(2,1)S(1)}, bf16[13,32,128]{2,1,0:T(8,128)(2,1)S(1)}, u32[]{:S(2)}, u32[]{:S(2)}) collective-permute-start(bf16[13,32,128]{2,1,0:T(8,128)(2,1)S(1)} %collective-permute-done.1.refs_2_), channel_id=1, source_target_pairs={{0,1},{1,0},{2,3},{3,2},{4,5},{5,4},{6,7},{7,6},{8,9},{9,8},{10,11... | collective-permute-start | bytes 319496 | tf_op jit(solution)/shard_map/ppermute | solution.py:270
  12.8 4.7 %collective-permute-start.5 = (bf16[13,32,128]{2,1,0:T(8,128)(2,1)S(1)}, bf16[13,32,128]{2,1,0:T(8,128)(2,1)S(1)}, u32[]{:S(2)}, u32[]{:S(2)}) collective-permute-start(bf16[13,32,128]{2,1,0:T(8,128)(2,1)S(1)} %collective-permute-done.4.refs_2_), channel_id=1, source_target_pairs={{0,4},{1,5},{2,6},{3,7},{4,0},{5,1},{6,2},{7,3},{8,12},{9,13},{10,... | collective-permute-start | bytes 319496 | tf_op jit(solution)/shard_map/ppermute | solution.py:270
  14.2 0.7 %copy-start = (s32[1,32]{1,0:T(1,128)S(1)}, s32[1,32]{1,0:T(1,128)}, u32[]{:S(2)}) copy-start(s32[1,32]{1,0:T(1,128)} %order_ref.1) | copy-start | bytes 388
  15.3 7.9 %collective-permute-start.6 = (bf16[49,16,128]{2,1,0:T(8,128)(2,1)S(1)}, bf16[49,16,128]{2,1,0:T(8,128)(2,1)S(1)}, u32[]{:S(2)}, u32[]{:S(2)}) collective-permute-start(bf16[49,16,128]{2,1,0:T(8,128)(2,1)S(1)} %get-tuple-element.15.refs_5_.xp), channel_id=1, source_target_pairs={{0,16},{1,17},{2,18},{3,19},{4,20},{5,21},{6,22},{7,23},{8,24},{9,... | collective-permute-start | bytes 602120 | tf_op jit(solution)/shard_map/ppermute | solution.py:280
  18.0 8.5 %collective-permute-start.7 = (bf16[49,16,128]{2,1,0:T(8,128)(2,1)S(1)}, bf16[49,16,128]{2,1,0:T(8,128)(2,1)S(1)}, u32[]{:S(2)}, u32[]{:S(2)}) collective-permute-start(bf16[49,16,128]{2,1,0:T(8,128)(2,1)S(1)} %get-tuple-element.16.after.gp), channel_id=1, source_target_pairs={{0,16},{1,17},{2,18},{3,19},{4,20},{5,21},{6,22},{7,23},{8,24},{9,... | collective-permute-start | bytes 602120 | tf_op jit(solution)/shard_map/ppermute | solution.py:280
  23.3 3.2 %copy-start.1 = (s32[1,32]{1,0:T(1,128)S(1)}, s32[1,32]{1,0:T(1,128)}, u32[]{:S(2)}) copy-start(s32[1,32]{1,0:T(1,128)} %order_ref.1) | copy-start | bytes 388
  23.3 3.2 %copy-start.2 = (f32[32]{0:T(128)S(1)}, f32[32]{0:T(128)}, u32[]{:S(2)}) copy-start(f32[32]{0:T(128)} %param.7) | copy-start | bytes 388

commit v15 on v12

--- a/solution.py
+++ b/solution.py
@@ -234,7 +234,7 @@
     ridge = jnp.where(row_id == col_id, jnp.broadcast_to(ridge_ref[...], (EX, EX)), 0.0)
     system = 0.5 * (diag + jnp.transpose(diag)) + ridge
     factor = jnp.zeros((EX, EX), F32)
-    step = 8
+    step = 16
     for j in range(0, EX, step):
         sys_cols = [jnp.broadcast_to(system[:, j + k:j + k + 1], (EX, EX)) for k in range(step)]
         pan_cols = [jnp.broadcast_to(panel[:, j + k:j + k + 1], (EX, EX)) for k in range(step)]

time: 41.5 us -> 41.5 us (level)
  no operation moved by 1% of the time
where the time goes in v15:
time: 41.5 us; the launch traced here: 41.4 us
  blocking collectives  12.9 us (31%)
  starting transfers between devices  11.4 us (27%)
  Pallas kernels  11.2 us (27%)
  waiting for transfers between devices  4.5 us (11%)
  between operations  0.7 us (2%)
  local copies, waits for them, and re-layouts  0.67 us (2%)
    all_to_all x1, blocking collectives, local_packed(): return final(lax.all_to_all(copies, ('rows', 'chan'), 0, 0), ridge)  12.9 us
    ppermute x6, starting transfers between devices, exchange(): return lax.ppermute(value, 'chan', [(i, i ^ flip) for i in range(count)])  8.37 us
    pallas_call x4, Pallas kernels, terms(): pl.pallas_call(kernel, out_shape=tuple((jax.ShapeDtypeStruct(*out) for ou...  7.11 us
    ppermute x2, starting transfers between devices, exchange_across(): return lax.ppermute(value, ('rows', 'chan'), pairs)  3.07 us
    ppermute x6, waiting for transfers between devices, exchange(): return lax.ppermute(value, 'chan', [(i, i ^ flip) for i in range(count)])  2.95 us
    pallas_call x1, Pallas kernels, prep(): pl.pallas_call(prep_kernel, out_shape=(full, full), in_specs=[pl.BlockSpe...  1.75 us
    ppermute x2, waiting for transfers between devices, exchange_across(): return lax.ppermute(value, ('rows', 'chan'), pairs)  1.55 us
    pallas_call x1, Pallas kernels, final(): pl.pallas_call(final_kernel, out_shape=(out, out), in_specs=[vmem] * 2, o...  1.48 us
  transfers between devices with their start and end apart: 8, of which 2 were waited for; matrix products, arithmetic and copies ran while one was open for 0% of the time, Pallas kernels for 15%

profile of v15, /device:TPU:0, one launch (start us, length us, event | category | flops | bytes accessed | tf_op | source)
XLA Modules:
  0.0 41.4 jit_solution(13669470110250139869)
XLA Ops:
  0.6 0.6 %copy-done = s32[1,32]{1,0:T(1,128)S(1)} copy-done((s32[1,32]{1,0:T(1,128)S(1)}, s32[1,32]{1,0:T(1,128)}, u32[]{:S(2)}) %copy-start) | copy-done | bytes 152
  1.3 1.8 %prep.1 = (bf16[13,32,128]{2,1,0:T(8,128)(2,1)S(1)}, bf16[13,32,128]{2,1,0:T(8,128)(2,1)S(1)}) custom-call(s32[1,32]{1,0:T(1,128)S(1)} %copy-done, bf16[49,32,32]{2,1,0:T(8,128)(2,1)} %bitcast.5, bf16[32,32,49]{2,1,0:T(8,128)(2,1)} %g_hbm.1), custom_call_target="tpu_custom_call" | custom-call | tf_op jit(solution)/shard_map/prep/pallas_call | solution.py:67
  3.0 3.0 %collective-permute-start.1 = (bf16[13,32,128]{2,1,0:T(8,128)(2,1)S(1)}, bf16[13,32,128]{2,1,0:T(8,128)(2,1)S(1)}, u32[]{:S(2)}, u32[]{:S(2)}) collective-permute-start(bf16[13,32,128]{2,1,0:T(8,128)(2,1)S(1)} %get-tuple-element.12.refs_0_), channel_id=1, source_target_pairs={{0,2},{1,3},{2,0},{3,1},{4,6},{5,7},{6,4},{7,5},{8,10},{9,11},{10,... | collective-permute-start | bytes 319496 | tf_op jit(solution)/shard_map/ppermute | solution.py:272
  6.1 2.6 %collective-permute-start.5 = (bf16[13,32,128]{2,1,0:T(8,128)(2,1)S(1)}, bf16[13,32,128]{2,1,0:T(8,128)(2,1)S(1)}, u32[]{:S(2)}, u32[]{:S(2)}) collective-permute-start(bf16[13,32,128]{2,1,0:T(8,128)(2,1)S(1)} %get-tuple-element.13.refs_0_), channel_id=1, source_target_pairs={{0,8},{1,9},{2,10},{3,11},{4,12},{5,13},{6,14},{7,15},{8,0},{9,1},... | collective-permute-start | bytes 319496 | tf_op jit(solution)/shard_map/ppermute | solution.py:272
  8.7 1.6 %collective-permute-start.3 = (bf16[13,32,128]{2,1,0:T(8,128)(2,1)S(1)}, bf16[13,32,128]{2,1,0:T(8,128)(2,1)S(1)}, u32[]{:S(2)}, u32[]{:S(2)}) collective-permute-start(bf16[13,32,128]{2,1,0:T(8,128)(2,1)S(1)} %get-tuple-element.13.refs_0_), channel_id=1, source_target_pairs={{0,4},{1,5},{2,6},{3,7},{4,0},{5,1},{6,2},{7,3},{8,12},{9,13},{10,... | collective-permute-start | bytes 319496 | tf_op jit(solution)/shard_map/ppermute | solution.py:272
  10.2 0.0 collective-permute-start
  10.3 0.0 collective-permute-done.1.refs_2_
  10.3 0.5 %collective-permute-start.2 = (bf16[13,32,128]{2,1,0:T(8,128)(2,1)S(1)}, bf16[13,32,128]{2,1,0:T(8,128)(2,1)S(1)}, u32[]{:S(2)}, u32[]{:S(2)}) collective-permute-start(bf16[13,32,128]{2,1,0:T(8,128)(2,1)S(1)} %collective-permute-done.1.refs_2_), channel_id=1, source_target_pairs={{0,1},{1,0},{2,3},{3,2},{4,5},{5,4},{6,7},{7,6},{8,9},{9,8},{10,11... | collective-permute-start | bytes 319496 | tf_op jit(solution)/shard_map/ppermute | solution.py:272
  10.8 2.9 %collective-permute-done.5.refs_2_ = bf16[13,32,128]{2,1,0:T(8,128)(2,1)S(1)} collective-permute-done((bf16[13,32,128]{2,1,0:T(8,128)(2,1)S(1)}, bf16[13,32,128]{2,1,0:T(8,128)(2,1)S(1)}, u32[]{:S(2)}, u32[]{:S(2)}) %collective-permute-start.5) | collective-permute-done | bytes 106528 | tf_op jit(solution)/shard_map/ppermute | solution.py:272
  13.7 0.7 %collective-permute-start.6 = (bf16[13,32,128]{2,1,0:T(8,128)(2,1)S(1)}, bf16[13,32,128]{2,1,0:T(8,128)(2,1)S(1)}, u32[]{:S(2)}, u32[]{:S(2)}) collective-permute-start(bf16[13,32,128]{2,1,0:T(8,128)(2,1)S(1)} %collective-permute-done.5.refs_2_), channel_id=1, source_target_pairs={{0,4},{1,5},{2,6},{3,7},{4,0},{5,1},{6,2},{7,3},{8,12},{9,13},{10,... | collective-permute-start | bytes 319496 | tf_op jit(solution)/shard_map/ppermute | solution.py:272
  14.4 0.4 %unpack_x.1 = (bf16[49,32,128]{2,1,0:T(8,128)(2,1)S(1)}, bf16[49,16,128]{2,1,0:T(8,128)(2,1)S(1)}) custom-call(bf16[13,32,128]{2,1,0:T(8,128)(2,1)S(1)} %get-tuple-element.12.refs_0_, bf16[13,32,128]{2,1,0:T(8,128)(2,1)S(1)} %collective-permute-done.refs_1_, bf16[13,32,128]{2,1,0:T(8,128)(2,1)S(1)} %collective-permute-done.1.refs_2_, ...), custom_call_target="tpu_custom_call" | custom-call | bytes 1048576 | tf_op jit(solution)/shard_map/unpack_x/pallas_call | solution.py:113
  14.8 1.6 %collective-permute-start.4 = (bf16[49,16,128]{2,1,0:T(8,128)(2,1)S(1)}, bf16[49,16,128]{2,1,0:T(8,128)(2,1)S(1)}, u32[]{:S(2)}, u32[]{:S(2)}) collective-permute-start(bf16[49,16,128]{2,1,0:T(8,128)(2,1)S(1)} %get-tuple-element.15.xp.refs_4_), channel_id=1, source_target_pairs={{0,16},{1,17},{2,18},{3,19},{4,20},{5,21},{6,22},{7,23},{8,24},{9,... | collective-permute-start | bytes 602120 | tf_op jit(solution)/shard_map/ppermute | solution.py:282
  16.4 2.1 %own_inputs.1 = (f32[7,224,896]{2,1,0:T(8,128)S(1)}, bf16[1568,384]{1,0:T(8,128)(2,1)S(1)}) custom-call(bf16[49,32,128]{2,1,0:T(8,128)(2,1)S(1)} %get-tuple-element.14.x, bf16[49,16,128]{2,1,0:T(8,128)(2,1)S(1)} %get-tuple-element.15.xp.refs_4_), custom_call_target="tpu_custom_call" | custom-call | flops 6000000000 | bytes 4194304 | tf_op jit(solution)/shard_map/own_inputs/pallas_call | solution.py:202
  18.4 0.0 collective-permute-done.6.refs_3_
  18.4 0.4 %unpack_g.1 = (bf16[49,32,128]{2,1,0:T(8,128)(2,1)S(1)}, bf16[49,16,128]{2,1,0:T(8,128)(2,1)S(1)}) custom-call(bf16[13,32,128]{2,1,0:T(8,128)(2,1)S(1)} %get-tuple-element.13.refs_0_, bf16[13,32,128]{2,1,0:T(8,128)(2,1)S(1)} %collective-permute-done.3.refs_4_.refs_1_, bf16[13,32,128]{2,1,0:T(8,128)(2,1)S(1)} %collective-permute-done.5.refs_2_, ...), custom_call_target="tpu_custom_call" | custom-call | bytes 1048576 | tf_op jit(solution)/shard_map/unpack_g/pallas_call | solution.py:113
  18.9 1.5 %collective-permute-start.7 = (bf16[49,16,128]{2,1,0:T(8,128)(2,1)S(1)}, bf16[49,16,128]{2,1,0:T(8,128)(2,1)S(1)}, u32[]{:S(2)}, u32[]{:S(2)}) collective-permute-start(bf16[49,16,128]{2,1,0:T(8,128)(2,1)S(1)} %get-tuple-element.18.gp), channel_id=1, source_target_pairs={{0,16},{1,17},{2,18},{3,19},{4,20},{5,21},{6,22},{7,23},{8,24},{9,... | collective-permute-start | bytes 602120 | tf_op jit(solution)/shard_map/ppermute | solution.py:282
  20.4 1.4 %terms_own.1.own_ref = f32[32,128]{1,0:T(8,128)S(1)} custom-call(f32[7,224,896]{2,1,0:T(8,128)S(1)} %get-tuple-element.19.t, bf16[49,32,128]{2,1,0:T(8,128)(2,1)S(1)} %get-tuple-element.17.g, bf16[49,16,128]{2,1,0:T(8,128)(2,1)S(1)} %get-tuple-element.18.gp), custom_call_target="tpu_custom_call" | custom-call | flops 6000000000 | bytes 4194304 | tf_op jit(solution)/shard_map/terms_own/pallas_call | solution.py:202
  21.8 0.0 collective-permute-done.4.xp
  21.8 0.0 copy-start.1
  21.8 2.0 %cross_inputs.1.t = f32[7,224,896]{2,1,0:T(8,128)S(1)} custom-call(bf16[1568,384]{1,0:T(8,128)(2,1)S(1)} %get-tuple-element.16.lx, bf16[49,16,128]{2,1,0:T(8,128)(2,1)S(1)} %collective-permute-done.4.xp), custom_call_target="tpu_custom_call" | custom-call | flops 6000000000 | bytes 4194304 | tf_op jit(solution)/shard_map/cross_inputs/pallas_call | solution.py:202
  23.9 1.6 %collective-permute-done.7.gp = bf16[49,16,128]{2,1,0:T(8,128)(2,1)S(1)} collective-permute-done((bf16[49,16,128]{2,1,0:T(8,128)(2,1)S(1)}, bf16[49,16,128]{2,1,0:T(8,128)(2,1)S(1)}, u32[]{:S(2)}, u32[]{:S(2)}) %collective-permute-start.7) | collective-permute-done | bytes 200736 | tf_op jit(solution)/shard_map/ppermute | solution.py:282
  25.4 1.6 %terms_cross.1 = (f32[8,128]{1,0:T(8,128)S(1)}, f32[1,32]{1,0:T(1,128)S(1)}) custom-call(f32[7,224,896]{2,1,0:T(8,128)S(1)} %cross_inputs.1.t, bf16[49,32,128]{2,1,0:T(8,128)(2,1)S(1)} %get-tuple-element.17.g, bf16[49,16,128]{2,1,0:T(8,128)(2,1)S(1)} %collective-permute-done.7.gp, f32[32,128]{1,0:T(8,128)S(1)} %terms_own.1.own_ref, f32[1,32]{1,0:T(1,128)S(1)} %bitcast.4), custom_call_target="tpu_custom_call" | custom-call | flops 6000000000 | bytes 4194304 | tf_op jit(solution)/shard_map/terms_cross/pallas_call | solution.py:202
  27.0 12.9 %all_to_all.5.terms_ref = f32[32,8,128]{2,1,0:T(8,128)S(1)} all-to-all(f32[32,8,128]{2,1,0:T(8,128)S(1)} %broadcast_in_dim.3), channel_id=1, replica_groups=mesh['rows'=2,'chan'=16] {'rows','chan'}, dimensions={0} | all-to-all | bytes 262144 | tf_op jit(solution)/shard_map/all_to_all | solution.py:301
  39.9 1.5 %solve.1 = (f32[32,32]{1,0:T(8,128)}, f32[32,32]{1,0:T(8,128)}) custom-call(f32[32,8,128]{2,1,0:T(8,128)S(1)} %all_to_all.5.terms_ref, f32[1,32]{1,0:T(1,128)S(1)} %get-tuple-element.21.ridge_ref), custom_call_target="tpu_custom_call" | custom-call | tf_op jit(solution)/shard_map/solve/pallas_call | solution.py:261
  (6 shorter events, 0.0 us)
Async XLA Ops:
  0.6 0.7 %copy-start = (s32[1,32]{1,0:T(1,128)S(1)}, s32[1,32]{1,0:T(1,128)}, u32[]{:S(2)}) copy-start(s32[1,32]{1,0:T(1,128)} %order_hbm.1) | copy-start | bytes 388
  3.0 7.2 %collective-permute-start.1 = (bf16[13,32,128]{2,1,0:T(8,128)(2,1)S(1)}, bf16[13,32,128]{2,1,0:T(8,128)(2,1)S(1)}, u32[]{:S(2)}, u32[]{:S(2)}) collective-permute-start(bf16[13,32,128]{2,1,0:T(8,128)(2,1)S(1)} %get-tuple-element.12.refs_0_), channel_id=1, source_target_pairs={{0,2},{1,3},{2,0},{3,1},{4,6},{5,7},{6,4},{7,5},{8,10},{9,11},{10,... | collective-permute-start | bytes 319496 | tf_op jit(solution)/shard_map/ppermute | solution.py:272
  6.1 7.6 %collective-permute-start.5 = (bf16[13,32,128]{2,1,0:T(8,128)(2,1)S(1)}, bf16[13,32,128]{2,1,0:T(8,128)(2,1)S(1)}, u32[]{:S(2)}, u32[]{:S(2)}) collective-permute-start(bf16[13,32,128]{2,1,0:T(8,128)(2,1)S(1)} %get-tuple-element.13.refs_0_), channel_id=1, source_target_pairs={{0,8},{1,9},{2,10},{3,11},{4,12},{5,13},{6,14},{7,15},{8,0},{9,1},... | collective-permute-start | bytes 319496 | tf_op jit(solution)/shard_map/ppermute | solution.py:272
  8.7 5.7 %collective-permute-start.3 = (bf16[13,32,128]{2,1,0:T(8,128)(2,1)S(1)}, bf16[13,32,128]{2,1,0:T(8,128)(2,1)S(1)}, u32[]{:S(2)}, u32[]{:S(2)}) collective-permute-start(bf16[13,32,128]{2,1,0:T(8,128)(2,1)S(1)} %get-tuple-element.13.refs_0_), channel_id=1, source_target_pairs={{0,4},{1,5},{2,6},{3,7},{4,0},{5,1},{6,2},{7,3},{8,12},{9,13},{10,... | collective-permute-start | bytes 319496 | tf_op jit(solution)/shard_map/ppermute | solution.py:272
  10.2 4.1 %collective-permute-start = (bf16[13,32,128]{2,1,0:T(8,128)(2,1)S(1)}, bf16[13,32,128]{2,1,0:T(8,128)(2,1)S(1)}, u32[]{:S(2)}, u32[]{:S(2)}) collective-permute-start(bf16[13,32,128]{2,1,0:T(8,128)(2,1)S(1)} %get-tuple-element.12.refs_0_), channel_id=1, source_target_pairs={{0,1},{1,0},{2,3},{3,2},{4,5},{5,4},{6,7},{7,6},{8,9},{9,8},{10,11... | collective-permute-start | bytes 319496 | tf_op jit(solution)/shard_map/ppermute | solution.py:272
  10.3 4.1 %collective-permute-start.2 = (bf16[13,32,128]{2,1,0:T(8,128)(2,1)S(1)}, bf16[13,32,128]{2,1,0:T(8,128)(2,1)S(1)}, u32[]{:S(2)}, u32[]{:S(2)}) collective-permute-start(bf16[13,32,128]{2,1,0:T(8,128)(2,1)S(1)} %collective-permute-done.1.refs_2_), channel_id=1, source_target_pairs={{0,1},{1,0},{2,3},{3,2},{4,5},{5,4},{6,7},{7,6},{8,9},{9,8},{10,11... | collective-permute-start | bytes 319496 | tf_op jit(solution)/shard_map/ppermute | solution.py:272
  13.7 4.7 %collective-permute-start.6 = (bf16[13,32,128]{2,1,0:T(8,128)(2,1)S(1)}, bf16[13,32,128]{2,1,0:T(8,128)(2,1)S(1)}, u32[]{:S(2)}, u32[]{:S(2)}) collective-permute-start(bf16[13,32,128]{2,1,0:T(8,128)(2,1)S(1)} %collective-permute-done.5.refs_2_), channel_id=1, source_target_pairs={{0,4},{1,5},{2,6},{3,7},{4,0},{5,1},{6,2},{7,3},{8,12},{9,13},{10,... | collective-permute-start | bytes 319496 | tf_op jit(solution)/shard_map/ppermute | solution.py:272
  14.8 7.0 %collective-permute-start.4 = (bf16[49,16,128]{2,1,0:T(8,128)(2,1)S(1)}, bf16[49,16,128]{2,1,0:T(8,128)(2,1)S(1)}, u32[]{:S(2)}, u32[]{:S(2)}) collective-permute-start(bf16[49,16,128]{2,1,0:T(8,128)(2,1)S(1)} %get-tuple-element.15.xp.refs_4_), channel_id=1, source_target_pairs={{0,16},{1,17},{2,18},{3,19},{4,20},{5,21},{6,22},{7,23},{8,24},{9,... | collective-permute-start | bytes 602120 | tf_op jit(solution)/shard_map/ppermute | solution.py:282
  18.9 6.6 %collective-permute-start.7 = (bf16[49,16,128]{2,1,0:T(8,128)(2,1)S(1)}, bf16[49,16,128]{2,1,0:T(8,128)(2,1)S(1)}, u32[]{:S(2)}, u32[]{:S(2)}) collective-permute-start(bf16[49,16,128]{2,1,0:T(8,128)(2,1)S(1)} %get-tuple-element.18.gp), channel_id=1, source_target_pairs={{0,16},{1,17},{2,18},{3,19},{4,20},{5,21},{6,22},{7,23},{8,24},{9,... | collective-permute-start | bytes 602120 | tf_op jit(solution)/shard_map/ppermute | solution.py:282
  21.8 3.6 %copy-start.1 = (f32[32]{0:T(128)S(1)}, f32[32]{0:T(128)}, u32[]{:S(2)}) copy-start(f32[32]{0:T(128)} %param.7) | copy-start | bytes 388
